TPU v7x, 32 devices: a whole 2x2x4 slice. The times are simulated.
32 devices in a mesh: sector: 4 (over x, core), term: 8 (over z, y).
Axes of the slice: x: 2, y: 2, z: 4, core: 2. Of those that a mesh axis runs over, the one named last changes fastest.
Arguments:
- lanczos_vector: float32 [8, 512, 512], P('sector'), may hold values from -6 to 6
- left_block: bfloat16 [8, 32, 512, 512], P('sector', 'term'), may hold values from -0.375 to 0.375
- right_block: bfloat16 [8, 32, 512, 512], P('sector', 'term'), may hold values from -0.25 to 0.25
- left_energy: float32 [8, 512], P('sector'), may hold values from 0.5 to 4
- right_energy: float32 [8, 512], P('sector'), may hold values from 0.5 to 4
- sector_shifts: int32 [32], P('term'), may hold values from -1 to 1
- sector_sizes: int32 [8], P('sector'), may hold values from 128 to 512, as said below
Outputs:
- next_vector: float32 [8, 512, 512], P('sector', 'term')
- next_sigma: float32 [8, 512, 512], P('sector', 'term')
Inputs may be any that keep to these rules, and one draw needn't show every extreme that they name: `sector_sizes`: each value is a multiple of 128; some sector has exactly 512.
All inputs are finite; a program needn't handle non-finite values.
Results may differ from a plain program's by a relative error of at most 0.0023.
Values may be sent and summed in bfloat16 or wider, within the bound.
No kernel may reach another device: no remote copies, remote signals or barrier semaphores. Data moves between devices by JAX's collectives and lax.ppermute only.
A program may use at most 64 MiB of HBM per device.

v0:
```python
import functools
import jax
import jax.numpy as jnp
from jax import lax
from jax.experimental import pallas as pl
from jax.experimental.pallas import tpu as pltpu
from jax.sharding import PartitionSpec as P

epsilon = 1e-06
NT = (((1,), (1,)), ((), ()))
GUESS = 4.5


def other(hi, step, count):
    return hi ^ step if count & (count - 1) == 0 else (step - hi) % count


def traced_other(hi, step, count):
    return hi ^ step if count & (count - 1) == 0 else lax.rem(step - hi + count, count)


def pairs_low(size):
    return [(i, i ^ 1) for i in range(size)]


def pairs_high(size, low, step):
    count = size // low
    return [(i, other(i // low, step, count) * low + i % low) for i in range(size)]


def row_finder(count, low, span):
    rank = lax.axis_index("term")
    hi, lo = rank // low, lax.rem(rank, low)

    def row_of(step, far):
        digit = 1 - lo if far else lo
        return pl.multiple_of((traced_other(hi, step, count) * low + digit) * span, span)

    return row_of


def add_pair(acc, left, right, block):
    mixed = jnp.dot(left[...], block[...], preferred_element_type=jnp.float32)
    acc[...] += lax.dot_general(
        mixed.astype(jnp.bfloat16), right[...], NT, preferred_element_type=jnp.float32
    )


def sector_at(turn, sectors):
    odd = lax.rem(lax.axis_index("sector"), 2)
    return odd * turn + (1 - odd) * (sectors - 1 - turn)


def halos_at(turn, sectors):
    return ([0] if turn == 0 else []) + ([1] if turn == sectors - 1 else [])


def halo_side(halo):
    here, groups = lax.axis_index("sector"), lax.axis_size("sector")
    side = (1 - 2 * lax.rem(here, 2)) * (1 - 2 * halo)
    return side, (here + side >= 0) & (here + side < groups)


def add_inner(dims, s, shift_ref, acc, left, right, wb, before_term=lambda t: None):
    sectors, terms = dims[:2]
    for t in range(terms):
        before_term(t)
        partner = s + shift_ref[t]

        @pl.when((partner >= 0) & (partner < sectors))
        def _():
            add_pair(acc, left.at[s, t], right.at[s, t], wb.at[partner])


def place_rows(dims, wb, pieces):
    sectors, terms, size, count, low, span = dims
    row_of = row_finder(count, low, span)
    for far in range(low):
        for step in range(count):
            wb[pl.ds(row_of(step, far), span), :] = pieces[far][step]


def add_outer(dims, turn, gathered, shift_ref, acc, left, right, blocks, wb):
    sectors, terms = dims[:2]
    s = sector_at(turn, sectors)
    for block, halo in zip(blocks, halos_at(turn, sectors)):
        if gathered:
            place_rows(dims, wb, [block.at[0], block.at[1]])
            held = wb
        else:
            held = block
        side, there = halo_side(halo)
        for t in range(terms):

            @pl.when((shift_ref[t] == side) & there)
            def _():
                add_pair(acc, left.at[s, t], right.at[s, t], held)


def cut(dims, acc, send_ref, keep_ref):
    sectors, terms, size, count, low, span = dims
    row_of = row_finder(count, low, span)
    for step in range(count):
        if low > 1:
            send_ref[step] = acc[pl.ds(row_of(step, 1), span), :].astype(jnp.bfloat16)
        keep_ref[step] = acc[pl.ds(row_of(step, 0), span), :]


def live_tile(shape, first_row, limit):
    row = first_row + lax.broadcasted_iota(jnp.int32, shape, 0)
    return (row < limit) & (lax.broadcasted_iota(jnp.int32, shape, 1) < limit)


def energy_rows(left_row, right_row, s, first, span):
    shape = (span, left_row.shape[1])
    row = first + lax.broadcasted_iota(jnp.int32, shape, 0)
    here = row == lax.broadcasted_iota(jnp.int32, shape, 1)
    left = jnp.sum(jnp.where(here, left_row[pl.ds(s, 1), :], 0.0), axis=1, keepdims=True)
    return left + right_row[pl.ds(s, 1), :]


def round_kernel(size_hbm, vector_hbm, rounded, edge, other_edge, vector, sizes, sems):
    sectors, size = vector.shape[:2]
    parts = sems.shape[0] // sectors
    rows = size // parts
    tile = min(64, rows)
    limits = pltpu.make_async_copy(size_hbm, sizes, sems.at[sectors * parts])
    limits.start()
    copies = [
        pltpu.make_async_copy(
            vector_hbm.at[sector_at(turn, sectors), pl.ds(n * rows, rows), :],
            vector.at[turn, pl.ds(n * rows, rows), :],
            sems.at[turn * parts + n],
        )
        for turn in range(sectors)
        for n in range(parts)
    ]
    for copy in copies:
        copy.start()
    limits.wait()
    for turn in range(sectors):
        s = sector_at(turn, sectors)
        for n in range(parts):
            copies[turn * parts + n].wait()

            @pl.loop(0, rows // tile)
            def _(k):
                first = pl.multiple_of(n * rows + k * tile, tile)
                part = pl.ds(first, tile)
                live = live_tile((tile, size), first, sizes[s])
                value = jnp.where(live, vector[turn, part, :], 0.0).astype(jnp.bfloat16)
                rounded[s, part, :] = value
                if turn == 0:
                    edge[part, :] = value
                if turn == sectors - 1:
                    other_edge[part, :] = value


def load_kernel(
    dims, wb, shift_hbm, size_hbm, left_hbm, right_hbm, vector_hbm,
    acc, left, right, start, shift_ref, size_ref, sems, row_sems, scalar_sems,
):
    sectors, terms, size, count, low, span = dims
    scalars = [
        pltpu.make_async_copy(shift_hbm, shift_ref, scalar_sems.at[0]),
        pltpu.make_async_copy(size_hbm, size_ref, scalar_sems.at[1]),
    ]
    for copy in scalars:
        copy.start()
    first = row_finder(count, low, span)(0, 0)
    rows = [
        pltpu.make_async_copy(vector_hbm.at[s, pl.ds(first, span), :], start.at[s], row_sems.at[s])
        for s in range(sectors)
    ]
    copies = {
        (turn, t): [
            pltpu.make_async_copy(
                hbm.at[sector_at(turn, sectors), t],
                vmem.at[sector_at(turn, sectors), t],
                sems.at[k, turn, t],
            )
            for k, (hbm, vmem) in enumerate(((left_hbm, left), (right_hbm, right)))
        ]
        for turn in range(sectors)
        for t in range(terms)
    }
    for pair in copies.values():
        for copy in pair:
            copy.start()
    for copy in rows:
        copy.start()
    acc[...] = jnp.zeros_like(acc)
    for copy in scalars:
        copy.wait()

    def arrived(t):
        for copy in copies[0, t]:
            copy.wait()

    add_inner(dims, sector_at(0, sectors), shift_ref, acc, left, right, wb, arrived)
    for s in range(sectors):
        rows[s].wait()
        live = live_tile((span, size), first, size_ref[s])
        start[s] = jnp.where(live, start[s], 0.0)
    for turn in range(1, sectors):
        for t in range(terms):
            for copy in copies[turn, t]:
                copy.wait()


def outer_kernel(dims, gathered, shift_ref, acc_ref, left, right, *refs):
    blocks, (send_ref, keep_ref, acc, wb) = refs[:-4], refs[-4:]
    acc[...] = acc_ref[...]
    add_outer(dims, 0, gathered, shift_ref, acc, left, right, blocks, wb)
    cut(dims, acc, send_ref, keep_ref)


def self_kernel(dims, shift_ref, left, right, mine, theirs, acc, own):
    s = sector_at(0, dims[0])
    acc[...] = jnp.zeros_like(acc)
    place_rows(dims, own, [mine, theirs])
    for t in range(dims[1]):

        @pl.when(shift_ref[t] == 0)
        def _():
            add_pair(acc, left.at[s, t], right.at[s, t], own)


def inner_kernel(dims, shift_ref, acc_ref, first_block, left, right, *refs):
    sectors, terms = dims[:2]
    pieces, (acc, own) = refs[:-2], refs[-2:]
    acc[...] = acc_ref[...]
    s = sector_at(0, sectors)
    own[s] = first_block[...]
    for turn in range(1, sectors):
        place_rows(dims, own.at[sector_at(turn, sectors)], pieces[2 * turn - 2 : 2 * turn])
    for t in range(terms):
        partner = s + shift_ref[t]

        @pl.when((shift_ref[t] != 0) & (partner >= 0) & (partner < sectors))
        def _():
            add_pair(acc, left.at[s, t], right.at[s, t], own.at[partner])


def full_kernel(dims, turn, gathered, shift_ref, own, left, right, *refs):
    blocks, (send_ref, keep_ref, acc, wb) = refs[:-4], refs[-4:]
    acc[...] = jnp.zeros_like(acc)
    add_inner(dims, sector_at(turn, dims[0]), shift_ref, acc, left, right, own)
    add_outer(dims, turn, gathered, shift_ref, acc, left, right, blocks, wb)
    cut(dims, acc, send_ref, keep_ref)


def sums_kernel(dims, size_ref, vector_ref, wb, sums):
    sectors, size = dims[0], dims[2]
    sums[...] = jnp.zeros_like(sums)
    tile = min(64, size)
    for s in range(sectors):

        @pl.loop(0, size // tile)
        def _(n):
            first = pl.multiple_of(n * tile, tile)
            rows = pl.ds(first, tile)
            live = live_tile((tile, size), first, size_ref[s])
            start = jnp.where(live, vector_ref[s, rows, :], 0.0)
            shifted = wb[s, rows, :].astype(jnp.float32)
            for k, term in enumerate((shifted * shifted, shifted * start, start * start)):
                sums[k : k + 1, :] += jnp.sum(term, 0, keepdims=True)


def shift_kernel(dims, turn, scale, size_ref, start, left_row, right_row, *refs):
    sectors, terms, size, count, low, span = dims
    parts, (held_ref, shifted_ref, plus_ref, minus_ref) = refs[:-4], refs[-4:]
    s = sector_at(turn, sectors)
    first = row_finder(count, low, span)(0, 0)
    total = parts[0][...]
    for part in parts[1:]:
        total += part[...].astype(jnp.float32)
    mixed = jnp.where(live_tile((span, size), first, size_ref[s]), scale * total, 0.0)
    energy = energy_rows(left_row, right_row, s, first, span)
    begin = start[s]
    shifted = mixed + (energy - GUESS) * begin
    held_ref[...] = shifted.astype(jnp.bfloat16)
    shifted_ref[...] = shifted
    plus_ref[...] = energy * shifted
    minus_ref[...] = energy * begin + mixed


def finish_kernel(dims, cells, scale, size_ref, start, *refs):
    sectors, terms, size, count, low, span = dims
    shifted, plus, minus = [refs[k * sectors : (k + 1) * sectors] for k in range(3)]
    parts, refs = refs[3 * sectors : 3 * sectors + count * sectors], refs[3 * sectors + count * sectors :]
    tables, (next_ref, sigma_ref) = refs[:-2], refs[-2:]
    first = row_finder(count, low, span)(0, 0)
    sums = sum(table[...] for table in tables)
    shifted_sq, overlap, norm_sq = [
        jnp.sum(sums[k : k + 1, :], axis=1, keepdims=True) for k in range(3)
    ]
    correlation = overlap + GUESS * norm_sq
    ritz = (correlation / cells) / (norm_sq / cells + epsilon)
    delta = ritz - GUESS
    res_sq = shifted_sq - 2.0 * delta * overlap + delta * delta * norm_sq
    inverse = lax.rsqrt(res_sq / cells + epsilon)
    for turn in range(sectors):
        s = sector_at(turn, sectors)
        next_ref[s] = (shifted[turn][...] - delta * start[s]) * inverse
        total = parts[turn * count][...]
        for part in parts[turn * count + 1 : (turn + 1) * count]:
            total += part[...].astype(jnp.float32)
        mixed = jnp.where(live_tile((span, size), first, size_ref[s]), scale * total, 0.0)
        sigma_ref[s] = (plus[turn][...] - delta * minus[turn][...] + mixed) * inverse


SMEM = pl.BlockSpec(memory_space=pltpu.SMEM)
VMEM = pl.BlockSpec(memory_space=pltpu.VMEM)
HBM = pl.BlockSpec(memory_space=pltpu.HBM)
LIMIT = pltpu.CompilerParams(vmem_limit_bytes=24 * 2**20)


def call(kernel, out_shape, scalars, arrays, matrices=(), scratch=(), flops=2**20):
    matrices = [pltpu.with_memory_space_constraint(m, pltpu.HBM) for m in matrices]
    return pl.pallas_call(
        kernel,
        out_shape=out_shape,
        in_specs=[SMEM] * len(scalars) + [VMEM] * len(arrays) + [HBM] * len(matrices),
        out_specs=[VMEM] * len(out_shape),
        scratch_shapes=scratch,
        compiler_params=LIMIT,
        cost_estimate=pl.CostEstimate(flops=flops, bytes_accessed=flops // 256, transcendentals=0),
    )(*scalars, *arrays, *matrices)


def after_all(value, *others):
    return lax.optimization_barrier((value, *others))[0]


def on_device(
    lanczos_vector, left_block, right_block, left_energy, right_energy, sector_shifts, sector_sizes
):
    sectors, size = lanczos_vector.shape[:2]
    terms, ranks = left_block.shape[1], lax.axis_size("term")
    groups = lax.axis_size("sector")
    scale = float(terms * ranks) ** (-0.5)
    cells = float(sectors * groups * size * size)
    span = size // ranks
    low = 2 if ranks % 2 == 0 else 1
    count = ranks // low
    dims = (sectors, terms, size, count, low, span)
    turns = range(sectors)
    pair_flops = 4 * size**3
    rows = pltpu.VMEM((sectors, span, size), jnp.float32)
    square = pltpu.VMEM((size, size), jnp.float32)
    square_low = pltpu.VMEM((size, size), jnp.bfloat16)
    cut_shapes = [jax.ShapeDtypeStruct((count, span, size), d) for d in (jnp.bfloat16, jnp.float32)]
    pairs = [
        [p for i in range(start, groups - 1, 2) for p in ((i, i + 1), (i + 1, i))]
        for start in range(2)
    ]

    def halo(edge, which):
        return lax.ppermute(edge, "sector", pairs[which]) if pairs[which] else edge

    def low_sum(send, keep):
        if low == 1:
            return keep
        return keep + lax.ppermute(send, "term", pairs_low(ranks)).astype(jnp.float32)

    hops = range(count - 1, 0, -1)

    def high_parts(total):
        return [total[0]] + [
            lax.ppermute(total[k].astype(jnp.bfloat16), "term", pairs_high(ranks, low, k))
            for k in hops
        ]

    def gather_high(held, following):
        got = {
            k: lax.ppermute(
                after_all(held, following) if k == 1 else held, "term", pairs_high(ranks, low, k)
            )
            for k in hops
        }
        return jnp.concatenate([held] + [got[k] for k in range(1, count)])

    def first_cut(acc, halos, gathered):
        return call(
            functools.partial(outer_kernel, dims, gathered),
            cut_shapes,
            (sector_shifts,),
            (acc, left, right, *[halos[h] for h in halos_at(0, sectors)]),
            scratch=[square, square_low],
            flops=terms * pair_flops // 3,
        )

    def later_cut(turn, own, halos, gathered):
        return call(
            functools.partial(full_kernel, dims, turn, gathered),
            cut_shapes,
            (sector_shifts,),
            (own, left, right, *[halos[h] for h in halos_at(turn, sectors)]),
            scratch=[square, square_low],
            flops=terms * pair_flops,
        )

    with jax.named_scope("first"):
        parts = 2 if size % 256 == 0 else 1
        block = jax.ShapeDtypeStruct((size, size), jnp.bfloat16)
        rounded, *edges = call(
            round_kernel,
            [pltpu.VMEM(lanczos_vector.shape, jnp.bfloat16), block, block],
            (),
            (),
            (sector_sizes, lanczos_vector),
            [
                pltpu.VMEM(lanczos_vector.shape, jnp.float32),
                pltpu.SMEM((sectors,), jnp.int32),
                pltpu.SemaphoreType.DMA((sectors * parts + 1,)),
            ],
        )
        halos = [halo(edge, which) for which, edge in enumerate(edges)]
        matrices = pltpu.VMEM(left_block.shape, jnp.bfloat16)
        acc, left, right, start = call(
            functools.partial(load_kernel, dims),
            [square, matrices, matrices, rows],
            (),
            (rounded,),
            (sector_shifts, sector_sizes, left_block, right_block, lanczos_vector),
            [
                pltpu.SMEM((terms,), jnp.int32),
                pltpu.SMEM((sectors,), jnp.int32),
                pltpu.SemaphoreType.DMA((2, sectors, terms)),
                pltpu.SemaphoreType.DMA((sectors,)),
                pltpu.SemaphoreType.DMA((2,)),
            ],
            terms * pair_flops,
        )
        cuts = [first_cut(acc, halos, False)]
        cuts += [later_cut(turn, rounded, halos, False) for turn in turns[1:]]
        totals = [low_sum(*c) for c in cuts]

    with jax.named_scope("gather"):
        shifted, plus, minus, pieces = [[None] * sectors for _ in range(4)]
        row = pltpu.VMEM((span, size), jnp.float32)
        parts = [high_parts(total) for total in totals]
        held = [None] * sectors
        for turn in turns:
            held[turn], shifted[turn], plus[turn], minus[turn] = call(
                functools.partial(shift_kernel, dims, turn, scale),
                [jax.ShapeDtypeStruct((span, size), jnp.bfloat16), row, row, row],
                (sector_sizes,),
                (start, left_energy, right_energy, *parts[turn]),
            )
        for turn in turns:
            mine = gather_high(held[turn][None], held[min(turn + 1, sectors - 1)])
            theirs = lax.ppermute(mine, "term", pairs_low(ranks)) if low > 1 else mine
            pieces[turn] = [mine, theirs]

    with jax.named_scope("second"):
        acc, block = call(
            functools.partial(self_kernel, dims),
            [square, square_low],
            (sector_shifts,),
            (left, right, *pieces[0]),
            flops=terms * pair_flops // 3,
        )
        whole = after_all(jnp.stack(pieces[0]), pieces[-1][1], acc)
        halos = [halo(edge, n) for n, edge in enumerate((whole, jnp.stack(pieces[-1])))]
        acc, own = call(
            functools.partial(inner_kernel, dims),
            [square, pltpu.VMEM((sectors, size, size), jnp.bfloat16)],
            (sector_shifts,),
            (acc, block, left, right, *[piece for both in pieces[1:] for piece in both]),
            flops=terms * pair_flops // 3,
        )
        cuts = [first_cut(acc, halos, True)]
        (sums,) = call(
            functools.partial(sums_kernel, dims),
            [jax.ShapeDtypeStruct((8, size), jnp.float32)],
            (sector_sizes,),
            (lanczos_vector, after_all(own, *cuts[0])),
        )
        own = after_all(own, sums)
        cuts += [later_cut(turn, own, halos, True) for turn in turns[1:]]
        totals = [low_sum(*c) for c in cuts]

    with jax.named_scope("scalars"):
        parts = [high_parts(total) for total in totals]
        sums = after_all(sums, totals[-1], parts[0][-1])
        tables, reach = [sums], 1
        while reach < groups:
            if groups & (groups - 1):
                tables, reach = [lax.psum(sums, "sector")], groups
            else:
                sums, width = sum(tables), min(4, groups // reach)
                tables = [sums] + [
                    lax.ppermute(sums, "sector", [(i, i ^ (reach * k)) for i in range(groups)])
                    for k in range(1, width)
                ]
                reach *= width
        out = jax.ShapeDtypeStruct((sectors, span, size), jnp.float32)
        flat = [part for each in parts for part in each]
        return call(
            functools.partial(finish_kernel, dims, cells, scale),
            [out, out],
            (sector_sizes,),
            (start, *shifted, *plus, *minus, *flat, *tables),
        )


def solution(mesh):
    return jax.shard_map(
        on_device,
        mesh=mesh,
        in_specs=(
            P("sector", None, None),
            P("sector", "term", None, None),
            P("sector", "term", None, None),
            P("sector", None),
            P("sector", None),
            P("term"),
            P("sector"),
        ),
        out_specs=(P("sector", "term", None), P("sector", "term", None)),
        check_vma=False,
    )
```

profile of v0, /device:TPU:0, one launch (start us, length us, event | category | flops | bytes accessed | tf_op | source)
XLA Modules:
  0.0 91.2 jit_solution(11720990441258050394)
XLA Ops:
  0.6 1.6 %first.4 = (bf16[2,512,512]{2,1,0:T(8,128)(2,1)S(1)}, bf16[512,512]{1,0:T(8,128)(2,1)S(1)}, bf16[512,512]{1,0:T(8,128)(2,1)S(1)}) custom-call(s32[2]{0:T(128)} %size_ref.7, f32[2,512,512]{2,1,0:T(8,128)} %vector_ref.1), custom_call_target="tpu_custom_call" | custom-call | flops 1048576 | bytes 4096 | tf_op jit(solution)/shard_map/first/pallas_call | solution.py:321
  2.3 0.5 collective-permute-start
  2.8 0.7 collective-permute-start.5
  3.5 3.6 %first.5 = (f32[512,512]{1,0:T(8,128)S(1)}, bf16[2,4,512,512]{3,2,1,0:T(8,128)(2,1)S(1)}, bf16[2,4,512,512]{3,2,1,0:T(8,128)(2,1)S(1)}, f32[2,64,512]{2,1,0:T(8,128)S(1)}) custom-call(bf16[2,512,512]{2,1,0:T(8,128)(2,1)S(1)} %get-tuple-element.35.wb.own, s32[4]{0:T(128)} %shift_ref.11, s32[2]{0:T(128)} %size_ref.7, bf16[2,4,512,512]{3,2,1,0:T(8,128)(2,1)} %left_hbm.1, ...), custom_call_target="tpu_custom_call" | custom-call | flops 2147483648 | bytes 8388608 | tf_op jit(solution)/shard_map/first/pallas_call | solution.py:321
  7.2 2.1 %first.6 = (bf16[4,64,512]{2,1,0:T(8,128)(2,1)S(1)}, f32[4,64,512]{2,1,0:T(8,128)S(1)}) custom-call(s32[4]{0:T(128)S(1)} %copy-done.1, f32[512,512]{1,0:T(8,128)S(1)} %get-tuple-element.37.acc_ref, bf16[2,4,512,512]{3,2,1,0:T(8,128)(2,1)S(1)} %get-tuple-element.38.left, bf16[2,4,512,512]{3,2,1,0:T(8,128)(2,1)S(1)} %get-tuple-element.39.right, ...), custom_call_target="tpu_custom_call" | custom-call | flops 715827904 | bytes 2796202 | tf_op jit(solution)/shard_map/first/pallas_call | solution.py:321
  9.3 1.9 %collective-permute-start.1 = (bf16[4,64,512]{2,1,0:T(8,128)(2,1)S(1)}, bf16[4,64,512]{2,1,0:T(8,128)(2,1)S(1)}, u32[]{:S(2)}, u32[]{:S(2)}) collective-permute-start(bf16[4,64,512]{2,1,0:T(8,128)(2,1)S(1)} %get-tuple-element.42), channel_id=1, source_target_pairs={{0,1},{1,0},{2,3},{3,2},{4,5},{5,4},{6,7},{7,6},{8,9},{9,8},{10,11... | collective-permute-start | bytes 786440 | tf_op jit(solution)/shard_map/first/ppermute | solution.py:365
  11.2 3.6 %first.7 = (bf16[4,64,512]{2,1,0:T(8,128)(2,1)S(1)}, f32[4,64,512]{2,1,0:T(8,128)S(1)}) custom-call(s32[4]{0:T(128)S(1)} %copy-done.1, bf16[2,512,512]{2,1,0:T(8,128)(2,1)S(1)} %get-tuple-element.35.wb.own, bf16[2,4,512,512]{3,2,1,0:T(8,128)(2,1)S(1)} %get-tuple-element.38.left, bf16[2,4,512,512]{3,2,1,0:T(8,128)(2,1)S(1)} %get-tuple-element.39.right, ...), custom_call_target="tpu_custom_call" | custom-call | flops 2147483648 | bytes 8388608 | tf_op jit(solution)/shard_map/first/pallas_call | solution.py:321
  14.9 0.9 %collective-permute-done.1 = bf16[4,64,512]{2,1,0:T(8,128)(2,1)S(1)} collective-permute-done((bf16[4,64,512]{2,1,0:T(8,128)(2,1)S(1)}, bf16[4,64,512]{2,1,0:T(8,128)(2,1)S(1)}, u32[]{:S(2)}, u32[]{:S(2)}) %collective-permute-start.1) | collective-permute-done | bytes 262176 | tf_op jit(solution)/shard_map/first/ppermute | solution.py:365
  15.9 4.8 %collective-permute-start.2 = (bf16[64,512]{1,0:T(8,128)(2,1)S(1)}, bf16[64,512]{1,0:T(8,128)(2,1)S(1)}, u32[]{:S(2)}, u32[]{:S(2)}) collective-permute-start(bf16[64,512]{1,0:T(8,128)(2,1)S(1)} %get-tuple-element.91), channel_id=1, source_target_pairs={{0,6},{1,7},{2,4},{3,5},{4,2},{5,3},{6,0},{7,1},{8,14},{9,15},{10,... | collective-permute-start | bytes 196616 | tf_op jit(solution)/shard_map/gather/ppermute | solution.py:371
  20.8 0.8 collective-permute-start.3
  21.6 0.5 collective-permute-start.4
  22.2 4.0 %collective-permute-start.7 = (bf16[64,512]{1,0:T(8,128)(2,1)S(1)}, bf16[64,512]{1,0:T(8,128)(2,1)S(1)}, u32[]{:S(2)}, u32[]{:S(2)}) collective-permute-start(bf16[64,512]{1,0:T(8,128)(2,1)S(1)} %get-tuple-element.88), channel_id=1, source_target_pairs={{0,6},{1,7},{2,4},{3,5},{4,2},{5,3},{6,0},{7,1},{8,14},{9,15},{10,... | collective-permute-start | bytes 196616 | tf_op jit(solution)/shard_map/gather/ppermute | solution.py:371
  26.2 0.4 collective-permute-start.8
  26.6 0.5 collective-permute-start.9
  27.1 2.2 %collective-permute-done.3.refs_2_ = bf16[64,512]{1,0:T(8,128)(2,1)S(1)} collective-permute-done((bf16[64,512]{1,0:T(8,128)(2,1)S(1)}, bf16[64,512]{1,0:T(8,128)(2,1)S(1)}, u32[]{:S(2)}, u32[]{:S(2)}) %collective-permute-start.3) | collective-permute-done | bytes 65568 | tf_op jit(solution)/shard_map/gather/ppermute | solution.py:371
  29.3 0.7 gather.2
  30.0 1.5 %collective-permute-start.12 = (bf16[1,64,512]{2,1,0:T(8,128)(2,1)S(1)}, bf16[1,64,512]{2,1,0:T(8,128)(2,1)S(1)}, u32[]{:S(2)}, u32[]{:S(2)}) collective-permute-start(bf16[1,64,512]{2,1,0:T(8,128)(2,1)S(1)} %bitcast.46), channel_id=1, source_target_pairs={{0,6},{1,7},{2,4},{3,5},{4,2},{5,3},{6,0},{7,1},{8,14},{9,15},{10,... | collective-permute-start | bytes 196616 | tf_op jit(solution)/shard_map/gather/ppermute | solution.py:377
  31.5 2.7 %collective-permute-done.8.refs_2_ = bf16[64,512]{1,0:T(8,128)(2,1)S(1)} collective-permute-done((bf16[64,512]{1,0:T(8,128)(2,1)S(1)}, bf16[64,512]{1,0:T(8,128)(2,1)S(1)}, u32[]{:S(2)}, u32[]{:S(2)}) %collective-permute-start.8) | collective-permute-done | bytes 65568 | tf_op jit(solution)/shard_map/gather/ppermute | solution.py:371
  34.2 0.7 gather.3
  35.2 1.0 %collective-permute-done.12 = bf16[1,64,512]{2,1,0:T(8,128)(2,1)S(1)} collective-permute-done((bf16[1,64,512]{2,1,0:T(8,128)(2,1)S(1)}, bf16[1,64,512]{2,1,0:T(8,128)(2,1)S(1)}, u32[]{:S(2)}, u32[]{:S(2)}) %collective-permute-start.12) | collective-permute-done | bytes 65568 | tf_op jit(solution)/shard_map/gather/ppermute | solution.py:377
  36.3 2.9 %collective-permute-done.11 = bf16[1,64,512]{2,1,0:T(8,128)(2,1)S(1)} collective-permute-done((bf16[1,64,512]{2,1,0:T(8,128)(2,1)S(1)}, bf16[1,64,512]{2,1,0:T(8,128)(2,1)S(1)}, u32[]{:S(2)}, u32[]{:S(2)}) %collective-permute-start.11) | collective-permute-done | bytes 65568 | tf_op jit(solution)/shard_map/gather/ppermute | solution.py:377
  39.2 1.2 %collective-permute-done.10 = bf16[1,64,512]{2,1,0:T(8,128)(2,1)S(1)} collective-permute-done((bf16[1,64,512]{2,1,0:T(8,128)(2,1)S(1)}, bf16[1,64,512]{2,1,0:T(8,128)(2,1)S(1)}, u32[]{:S(2)}, u32[]{:S(2)}) %collective-permute-start.10) | collective-permute-done | bytes 65568 | tf_op jit(solution)/shard_map/gather/ppermute | solution.py:377
  40.4 2.2 %collective-permute-start.13 = (bf16[4,64,512]{2,1,0:T(8,128)(2,1)S(1)}, bf16[4,64,512]{2,1,0:T(8,128)(2,1)S(1)}, u32[]{:S(2)}, u32[]{:S(2)}) collective-permute-start(bf16[4,64,512]{2,1,0:T(8,128)(2,1)S(1)} %get-tuple-element.85.mine), channel_id=1, source_target_pairs={{0,1},{1,0},{2,3},{3,2},{4,5},{5,4},{6,7},{7,6},{8,9},{9,8},{10,11... | collective-permute-start | bytes 786440 | tf_op jit(solution)/shard_map/gather/ppermute | solution.py:454
  42.6 2.8 %collective-permute-start.16 = (bf16[1,64,512]{2,1,0:T(8,128)(2,1)S(1)}, bf16[1,64,512]{2,1,0:T(8,128)(2,1)S(1)}, u32[]{:S(2)}, u32[]{:S(2)}) collective-permute-start(bf16[1,64,512]{2,1,0:T(8,128)(2,1)S(1)} %bitcast.42), channel_id=1, source_target_pairs={{0,6},{1,7},{2,4},{3,5},{4,2},{5,3},{6,0},{7,1},{8,14},{9,15},{10,... | collective-permute-start | bytes 196616 | tf_op jit(solution)/shard_map/gather/ppermute | solution.py:377
  45.4 1.6 %collective-permute-start.14 = (bf16[1,64,512]{2,1,0:T(8,128)(2,1)S(1)}, bf16[1,64,512]{2,1,0:T(8,128)(2,1)S(1)}, u32[]{:S(2)}, u32[]{:S(2)}) collective-permute-start(bf16[1,64,512]{2,1,0:T(8,128)(2,1)S(1)} %bitcast.44), channel_id=1, source_target_pairs={{0,2},{1,3},{2,0},{3,1},{4,6},{5,7},{6,4},{7,5},{8,10},{9,11},{10,... | collective-permute-start | bytes 196616 | tf_op jit(solution)/shard_map/gather/ppermute | solution.py:377
  47.0 1.8 %collective-permute-done.16 = bf16[1,64,512]{2,1,0:T(8,128)(2,1)S(1)} collective-permute-done((bf16[1,64,512]{2,1,0:T(8,128)(2,1)S(1)}, bf16[1,64,512]{2,1,0:T(8,128)(2,1)S(1)}, u32[]{:S(2)}, u32[]{:S(2)}) %collective-permute-start.16) | collective-permute-done | bytes 65568 | tf_op jit(solution)/shard_map/gather/ppermute | solution.py:377
  48.7 2.1 %collective-permute-done.15 = bf16[1,64,512]{2,1,0:T(8,128)(2,1)S(1)} collective-permute-done((bf16[1,64,512]{2,1,0:T(8,128)(2,1)S(1)}, bf16[1,64,512]{2,1,0:T(8,128)(2,1)S(1)}, u32[]{:S(2)}, u32[]{:S(2)}) %collective-permute-start.15) | collective-permute-done | bytes 65568 | tf_op jit(solution)/shard_map/gather/ppermute | solution.py:377
  51.1 0.8 collective-permute-start.17
  51.9 2.1 %second.5 = (f32[512,512]{1,0:T(8,128)S(1)}, bf16[512,512]{1,0:T(8,128)(2,1)S(1)}) custom-call(s32[4]{0:T(128)S(1)} %copy-done.1, bf16[2,4,512,512]{3,2,1,0:T(8,128)(2,1)S(1)} %get-tuple-element.38.left, bf16[2,4,512,512]{3,2,1,0:T(8,128)(2,1)S(1)} %get-tuple-element.39.right, bf16[4,64,512]{2,1,0:T(8,128)(2,1)S(1)} %get-tuple-element.85.mine, ...), custom_call_target="tpu_custom_call" | custom-call | flops 715827904 | bytes 2796202 | tf_op jit(solution)/shard_map/second/pallas_call | solution.py:321
  54.0 4.6 %collective-permute-done.17.refs_1_ = bf16[4,64,512]{2,1,0:T(8,128)(2,1)S(1)} collective-permute-done((bf16[4,64,512]{2,1,0:T(8,128)(2,1)S(1)}, bf16[4,64,512]{2,1,0:T(8,128)(2,1)S(1)}, u32[]{:S(2)}, u32[]{:S(2)}) %collective-permute-start.17) | collective-permute-done | bytes 262176 | tf_op jit(solution)/shard_map/gather/ppermute | solution.py:454
  58.7 0.9 collective-permute-start.23
  59.6 0.7 second.6
  60.5 2.2 %second.7 = (bf16[4,64,512]{2,1,0:T(8,128)(2,1)S(1)}, f32[4,64,512]{2,1,0:T(8,128)S(1)}) custom-call(s32[4]{0:T(128)S(1)} %copy-done.1, f32[512,512]{1,0:T(8,128)S(1)} %get-tuple-element.58.acc_ref, bf16[2,4,512,512]{3,2,1,0:T(8,128)(2,1)S(1)} %get-tuple-element.38.left, bf16[2,4,512,512]{3,2,1,0:T(8,128)(2,1)S(1)} %get-tuple-element.39.right, ...), custom_call_target="tpu_custom_call" | custom-call | flops 715827904 | bytes 2796202 | tf_op jit(solution)/shard_map/second/pallas_call | solution.py:321
  62.7 2.1 %collective-permute-start.19 = (bf16[4,64,512]{2,1,0:T(8,128)(2,1)S(1)}, bf16[4,64,512]{2,1,0:T(8,128)(2,1)S(1)}, u32[]{:S(2)}, u32[]{:S(2)}) collective-permute-start(bf16[4,64,512]{2,1,0:T(8,128)(2,1)S(1)} %get-tuple-element.61), channel_id=1, source_target_pairs={{0,1},{1,0},{2,3},{3,2},{4,5},{5,4},{6,7},{7,6},{8,9},{9,8},{10,11... | collective-permute-start | bytes 786440 | tf_op jit(solution)/shard_map/second/ppermute | solution.py:365
  64.7 1.4 %second.8.refs_14_ = f32[8,512]{1,0:T(8,128)S(1)} custom-call(s32[2]{0:T(128)S(1)} %copy-done.2, f32[2,512,512]{2,1,0:T(8,128)S(1)} %copy-done, bf16[2,512,512]{2,1,0:T(8,128)(2,1)S(1)} %get-tuple-element.64.wb.own), custom_call_target="tpu_custom_call" | custom-call | flops 1048576 | bytes 4096 | tf_op jit(solution)/shard_map/second/pallas_call | solution.py:321
  66.2 3.6 %second.9 = (bf16[4,64,512]{2,1,0:T(8,128)(2,1)S(1)}, f32[4,64,512]{2,1,0:T(8,128)S(1)}) custom-call(s32[4]{0:T(128)S(1)} %copy-done.1, bf16[2,512,512]{2,1,0:T(8,128)(2,1)S(1)} %get-tuple-element.64.wb.own, bf16[2,4,512,512]{3,2,1,0:T(8,128)(2,1)S(1)} %get-tuple-element.38.left, bf16[2,4,512,512]{3,2,1,0:T(8,128)(2,1)S(1)} %get-tuple-element.39.right, ...), custom_call_target="tpu_custom_call" | custom-call | flops 2147483648 | bytes 8388608 | tf_op jit(solution)/shard_map/second/pallas_call | solution.py:321
  70.0 1.9 %collective-permute-start.20 = (bf16[64,512]{1,0:T(8,128)(2,1)S(1)}, bf16[64,512]{1,0:T(8,128)(2,1)S(1)}, u32[]{:S(2)}, u32[]{:S(2)}) collective-permute-start(bf16[64,512]{1,0:T(8,128)(2,1)S(1)} %get-tuple-element.83), channel_id=1, source_target_pairs={{0,6},{1,7},{2,4},{3,5},{4,2},{5,3},{6,0},{7,1},{8,14},{9,15},{10,... | collective-permute-start | bytes 196616 | tf_op jit(solution)/shard_map/scalars/ppermute | solution.py:371
  71.9 0.9 collective-permute-start.21
  72.8 1.7 %collective-permute-start.22 = (bf16[64,512]{1,0:T(8,128)(2,1)S(1)}, bf16[64,512]{1,0:T(8,128)(2,1)S(1)}, u32[]{:S(2)}, u32[]{:S(2)}) collective-permute-start(bf16[64,512]{1,0:T(8,128)(2,1)S(1)} %get-tuple-element.81), channel_id=1, source_target_pairs={{0,2},{1,3},{2,0},{3,1},{4,6},{5,7},{6,4},{7,5},{8,10},{9,11},{10,... | collective-permute-start | bytes 196616 | tf_op jit(solution)/shard_map/scalars/ppermute | solution.py:371
  74.5 2.0 %collective-permute-done.24 = bf16[4,64,512]{2,1,0:T(8,128)(2,1)S(1)} collective-permute-done((bf16[4,64,512]{2,1,0:T(8,128)(2,1)S(1)}, bf16[4,64,512]{2,1,0:T(8,128)(2,1)S(1)}, u32[]{:S(2)}, u32[]{:S(2)}) %collective-permute-start.24) | collective-permute-done | bytes 262176 | tf_op jit(solution)/shard_map/second/ppermute | solution.py:365
  76.6 0.7 collective-permute-start.25
  77.3 1.1 %collective-permute-start.26 = (bf16[64,512]{1,0:T(8,128)(2,1)S(1)}, bf16[64,512]{1,0:T(8,128)(2,1)S(1)}, u32[]{:S(2)}, u32[]{:S(2)}) collective-permute-start(bf16[64,512]{1,0:T(8,128)(2,1)S(1)} %get-tuple-element.77), channel_id=1, source_target_pairs={{0,4},{1,5},{2,6},{3,7},{4,0},{5,1},{6,2},{7,3},{8,12},{9,13},{10,... | collective-permute-start | bytes 196616 | tf_op jit(solution)/shard_map/scalars/ppermute | solution.py:371
  78.4 2.7 %collective-permute-start.27 = (bf16[64,512]{1,0:T(8,128)(2,1)S(1)}, bf16[64,512]{1,0:T(8,128)(2,1)S(1)}, u32[]{:S(2)}, u32[]{:S(2)}) collective-permute-start(bf16[64,512]{1,0:T(8,128)(2,1)S(1)} %get-tuple-element.76), channel_id=1, source_target_pairs={{0,2},{1,3},{2,0},{3,1},{4,6},{5,7},{6,4},{7,5},{8,10},{9,11},{10,... | collective-permute-start | bytes 196616 | tf_op jit(solution)/shard_map/scalars/ppermute | solution.py:371
  81.1 1.6 %collective-permute-start.28 = (f32[8,512]{1,0:T(8,128)S(1)}, f32[8,512]{1,0:T(8,128)S(1)}, u32[]{:S(2)}, u32[]{:S(2)}) collective-permute-start(f32[8,512]{1,0:T(8,128)S(1)} %second.8.refs_14_), channel_id=1, source_target_pairs={{0,8},{8,0},{16,24},{24,16},{1,9},{9,1},{17,25},{25,17},{2,10},{10... | collective-permute-start | bytes 49160 | tf_op jit(solution)/shard_map/scalars/ppermute | solution.py:495
  82.7 3.6 %collective-permute-start.29 = (f32[8,512]{1,0:T(8,128)S(1)}, f32[8,512]{1,0:T(8,128)S(1)}, u32[]{:S(2)}, u32[]{:S(2)}) collective-permute-start(f32[8,512]{1,0:T(8,128)S(1)} %second.8.refs_14_), channel_id=1, source_target_pairs={{0,16},{8,24},{16,0},{24,8},{1,17},{9,25},{17,1},{25,9},{2,18},{10... | collective-permute-start | bytes 49160 | tf_op jit(solution)/shard_map/scalars/ppermute | solution.py:495
  86.4 1.7 %collective-permute-done.29.refs_16_ = f32[8,512]{1,0:T(8,128)S(1)} collective-permute-done((f32[8,512]{1,0:T(8,128)S(1)}, f32[8,512]{1,0:T(8,128)S(1)}, u32[]{:S(2)}, u32[]{:S(2)}) %collective-permute-start.29) | collective-permute-done | bytes 16416 | tf_op jit(solution)/shard_map/scalars/ppermute | solution.py:495
  88.0 1.6 %collective-permute-done.30.refs_17_ = f32[8,512]{1,0:T(8,128)S(1)} collective-permute-done((f32[8,512]{1,0:T(8,128)S(1)}, f32[8,512]{1,0:T(8,128)S(1)}, u32[]{:S(2)}, u32[]{:S(2)}) %collective-permute-start.30) | collective-permute-done | bytes 16416 | tf_op jit(solution)/shard_map/scalars/ppermute | solution.py:495
  89.6 1.5 %scalars.1 = (f32[2,64,512]{2,1,0:T(8,128)}, f32[2,64,512]{2,1,0:T(8,128)}) custom-call(s32[2]{0:T(128)S(1)} %copy-done.2, f32[2,64,512]{2,1,0:T(8,128)S(1)} %get-tuple-element.36.start, f32[64,512]{1,0:T(8,128)S(1)} %get-tuple-element.43.refs_0_, f32[64,512]{1,0:T(8,128)S(1)} %get-tuple-element.47.refs_1_, f32[64,512]{1,0:T(8,128)S(1)} %get-tuple-element.48.refs_2_, ...), custom_call_target="tpu_custom_call" | custom-call | flops 1048576 | bytes 4096 | tf_op jit(solution)/shard_map/scalars/pallas_call | solution.py:321
  (52 shorter events, 1.6 us)
Async XLA Ops:
  2.3 4.9 %collective-permute-start = (bf16[512,512]{1,0:T(8,128)(2,1)S(1)}, bf16[512,512]{1,0:T(8,128)(2,1)S(1)}, u32[]{:S(2)}, u32[]{:S(2)}) collective-permute-start(bf16[512,512]{1,0:T(8,128)(2,1)S(1)} %get-tuple-element.40), channel_id=1, source_target_pairs={{0,8},{8,0},{16,24},{24,16},{1,9},{9,1},{17,25},{25,17},{2,10},{10... | collective-permute-start | bytes 1572872 | tf_op jit(solution)/shard_map/first/ppermute | solution.py:360
  2.8 8.4 %collective-permute-start.5 = (bf16[512,512]{1,0:T(8,128)(2,1)S(1)}, bf16[512,512]{1,0:T(8,128)(2,1)S(1)}, u32[]{:S(2)}, u32[]{:S(2)}) collective-permute-start(bf16[512,512]{1,0:T(8,128)(2,1)S(1)} %get-tuple-element.44), channel_id=1, source_target_pairs={{8,16},{16,8},{9,17},{17,9},{10,18},{18,10},{11,19},{19,11},{12,20... | collective-permute-start | bytes 1572872 | tf_op jit(solution)/shard_map/first/ppermute | solution.py:360
  3.5 3.7 %copy-start.1 = (s32[4]{0:T(128)S(1)}, s32[4]{0:T(128)}, u32[]{:S(2)}) copy-start(s32[4]{0:T(128)} %shift_ref.11) | copy-start | bytes 52
  9.3 6.5 %collective-permute-start.1 = (bf16[4,64,512]{2,1,0:T(8,128)(2,1)S(1)}, bf16[4,64,512]{2,1,0:T(8,128)(2,1)S(1)}, u32[]{:S(2)}, u32[]{:S(2)}) collective-permute-start(bf16[4,64,512]{2,1,0:T(8,128)(2,1)S(1)} %get-tuple-element.42), channel_id=1, source_target_pairs={{0,1},{1,0},{2,3},{3,2},{4,5},{5,4},{6,7},{7,6},{8,9},{9,8},{10,11... | collective-permute-start | bytes 786440 | tf_op jit(solution)/shard_map/first/ppermute | solution.py:365
  14.8 14.6 %copy-start.2 = (s32[2]{0:T(128)S(1)}, s32[2]{0:T(128)}, u32[]{:S(2)}) copy-start(s32[2]{0:T(128)} %size_ref.7) | copy-start | bytes 28
  14.8 14.6 %copy-start.3 = (f32[2,512]{1,0:T(2,128)S(1)}, f32[2,512]{1,0:T(2,128)}, u32[]{:S(2)}) copy-start(f32[2,512]{1,0:T(2,128)} %left_row.3) | copy-start | bytes 12292
  14.8 14.6 %copy-start.4 = (f32[2,512]{1,0:T(2,128)S(1)}, f32[2,512]{1,0:T(2,128)}, u32[]{:S(2)}) copy-start(f32[2,512]{1,0:T(2,128)} %right_row.3) | copy-start | bytes 12292
  14.8 7.3 %collective-permute-start.6 = (bf16[4,64,512]{2,1,0:T(8,128)(2,1)S(1)}, bf16[4,64,512]{2,1,0:T(8,128)(2,1)S(1)}, u32[]{:S(2)}, u32[]{:S(2)}) collective-permute-start(bf16[4,64,512]{2,1,0:T(8,128)(2,1)S(1)} %get-tuple-element.46), channel_id=1, source_target_pairs={{0,1},{1,0},{2,3},{3,2},{4,5},{5,4},{6,7},{7,6},{8,9},{9,8},{10,11... | collective-permute-start | bytes 786440 | tf_op jit(solution)/shard_map/first/ppermute | solution.py:365
  15.9 10.7 %collective-permute-start.2 = (bf16[64,512]{1,0:T(8,128)(2,1)S(1)}, bf16[64,512]{1,0:T(8,128)(2,1)S(1)}, u32[]{:S(2)}, u32[]{:S(2)}) collective-permute-start(bf16[64,512]{1,0:T(8,128)(2,1)S(1)} %get-tuple-element.91), channel_id=1, source_target_pairs={{0,6},{1,7},{2,4},{3,5},{4,2},{5,3},{6,0},{7,1},{8,14},{9,15},{10,... | collective-permute-start | bytes 196616 | tf_op jit(solution)/shard_map/gather/ppermute | solution.py:371
  20.8 8.6 %collective-permute-start.3 = (bf16[64,512]{1,0:T(8,128)(2,1)S(1)}, bf16[64,512]{1,0:T(8,128)(2,1)S(1)}, u32[]{:S(2)}, u32[]{:S(2)}) collective-permute-start(bf16[64,512]{1,0:T(8,128)(2,1)S(1)} %get-tuple-element.90), channel_id=1, source_target_pairs={{0,4},{1,5},{2,6},{3,7},{4,0},{5,1},{6,2},{7,3},{8,12},{9,13},{10,... | collective-permute-start | bytes 196616 | tf_op jit(solution)/shard_map/gather/ppermute | solution.py:371
  21.6 7.7 %collective-permute-start.4 = (bf16[64,512]{1,0:T(8,128)(2,1)S(1)}, bf16[64,512]{1,0:T(8,128)(2,1)S(1)}, u32[]{:S(2)}, u32[]{:S(2)}) collective-permute-start(bf16[64,512]{1,0:T(8,128)(2,1)S(1)} %get-tuple-element.89), channel_id=1, source_target_pairs={{0,2},{1,3},{2,0},{3,1},{4,6},{5,7},{6,4},{7,5},{8,10},{9,11},{10,... | collective-permute-start | bytes 196616 | tf_op jit(solution)/shard_map/gather/ppermute | solution.py:371
  22.2 9.3 %collective-permute-start.7 = (bf16[64,512]{1,0:T(8,128)(2,1)S(1)}, bf16[64,512]{1,0:T(8,128)(2,1)S(1)}, u32[]{:S(2)}, u32[]{:S(2)}) collective-permute-start(bf16[64,512]{1,0:T(8,128)(2,1)S(1)} %get-tuple-element.88), channel_id=1, source_target_pairs={{0,6},{1,7},{2,4},{3,5},{4,2},{5,3},{6,0},{7,1},{8,14},{9,15},{10,... | collective-permute-start | bytes 196616 | tf_op jit(solution)/shard_map/gather/ppermute | solution.py:371
  26.2 8.0 %collective-permute-start.8 = (bf16[64,512]{1,0:T(8,128)(2,1)S(1)}, bf16[64,512]{1,0:T(8,128)(2,1)S(1)}, u32[]{:S(2)}, u32[]{:S(2)}) collective-permute-start(bf16[64,512]{1,0:T(8,128)(2,1)S(1)} %get-tuple-element.87), channel_id=1, source_target_pairs={{0,4},{1,5},{2,6},{3,7},{4,0},{5,1},{6,2},{7,3},{8,12},{9,13},{10,... | collective-permute-start | bytes 196616 | tf_op jit(solution)/shard_map/gather/ppermute | solution.py:371
  26.6 7.6 %collective-permute-start.9 = (bf16[64,512]{1,0:T(8,128)(2,1)S(1)}, bf16[64,512]{1,0:T(8,128)(2,1)S(1)}, u32[]{:S(2)}, u32[]{:S(2)}) collective-permute-start(bf16[64,512]{1,0:T(8,128)(2,1)S(1)} %get-tuple-element.86), channel_id=1, source_target_pairs={{0,2},{1,3},{2,0},{3,1},{4,6},{5,7},{6,4},{7,5},{8,10},{9,11},{10,... | collective-permute-start | bytes 196616 | tf_op jit(solution)/shard_map/gather/ppermute | solution.py:371
  30.0 6.2 %collective-permute-start.12 = (bf16[1,64,512]{2,1,0:T(8,128)(2,1)S(1)}, bf16[1,64,512]{2,1,0:T(8,128)(2,1)S(1)}, u32[]{:S(2)}, u32[]{:S(2)}) collective-permute-start(bf16[1,64,512]{2,1,0:T(8,128)(2,1)S(1)} %bitcast.46), channel_id=1, source_target_pairs={{0,6},{1,7},{2,4},{3,5},{4,2},{5,3},{6,0},{7,1},{8,14},{9,15},{10,... | collective-permute-start | bytes 196616 | tf_op jit(solution)/shard_map/gather/ppermute | solution.py:377
  31.5 7.7 %collective-permute-start.11 = (bf16[1,64,512]{2,1,0:T(8,128)(2,1)S(1)}, bf16[1,64,512]{2,1,0:T(8,128)(2,1)S(1)}, u32[]{:S(2)}, u32[]{:S(2)}) collective-permute-start(bf16[1,64,512]{2,1,0:T(8,128)(2,1)S(1)} %bitcast.47), channel_id=1, source_target_pairs={{0,4},{1,5},{2,6},{3,7},{4,0},{5,1},{6,2},{7,3},{8,12},{9,13},{10,... | collective-permute-start | bytes 196616 | tf_op jit(solution)/shard_map/gather/ppermute | solution.py:377
  34.9 5.4 %collective-permute-start.10 = (bf16[1,64,512]{2,1,0:T(8,128)(2,1)S(1)}, bf16[1,64,512]{2,1,0:T(8,128)(2,1)S(1)}, u32[]{:S(2)}, u32[]{:S(2)}) collective-permute-start(bf16[1,64,512]{2,1,0:T(8,128)(2,1)S(1)} %bitcast.48), channel_id=1, source_target_pairs={{0,2},{1,3},{2,0},{3,1},{4,6},{5,7},{6,4},{7,5},{8,10},{9,11},{10,... | collective-permute-start | bytes 196616 | tf_op jit(solution)/shard_map/gather/ppermute | solution.py:377
  40.4 11.5 %collective-permute-start.13 = (bf16[4,64,512]{2,1,0:T(8,128)(2,1)S(1)}, bf16[4,64,512]{2,1,0:T(8,128)(2,1)S(1)}, u32[]{:S(2)}, u32[]{:S(2)}) collective-permute-start(bf16[4,64,512]{2,1,0:T(8,128)(2,1)S(1)} %get-tuple-element.85.mine), channel_id=1, source_target_pairs={{0,1},{1,0},{2,3},{3,2},{4,5},{5,4},{6,7},{7,6},{8,9},{9,8},{10,11... | collective-permute-start | bytes 786440 | tf_op jit(solution)/shard_map/gather/ppermute | solution.py:454
  42.6 6.1 %collective-permute-start.16 = (bf16[1,64,512]{2,1,0:T(8,128)(2,1)S(1)}, bf16[1,64,512]{2,1,0:T(8,128)(2,1)S(1)}, u32[]{:S(2)}, u32[]{:S(2)}) collective-permute-start(bf16[1,64,512]{2,1,0:T(8,128)(2,1)S(1)} %bitcast.42), channel_id=1, source_target_pairs={{0,6},{1,7},{2,4},{3,5},{4,2},{5,3},{6,0},{7,1},{8,14},{9,15},{10,... | collective-permute-start | bytes 196616 | tf_op jit(solution)/shard_map/gather/ppermute | solution.py:377
  45.4 5.4 %collective-permute-start.15 = (bf16[1,64,512]{2,1,0:T(8,128)(2,1)S(1)}, bf16[1,64,512]{2,1,0:T(8,128)(2,1)S(1)}, u32[]{:S(2)}, u32[]{:S(2)}) collective-permute-start(bf16[1,64,512]{2,1,0:T(8,128)(2,1)S(1)} %bitcast.43), channel_id=1, source_target_pairs={{0,4},{1,5},{2,6},{3,7},{4,0},{5,1},{6,2},{7,3},{8,12},{9,13},{10,... | collective-permute-start | bytes 196616 | tf_op jit(solution)/shard_map/gather/ppermute | solution.py:377
  45.4 5.6 %collective-permute-start.14 = (bf16[1,64,512]{2,1,0:T(8,128)(2,1)S(1)}, bf16[1,64,512]{2,1,0:T(8,128)(2,1)S(1)}, u32[]{:S(2)}, u32[]{:S(2)}) collective-permute-start(bf16[1,64,512]{2,1,0:T(8,128)(2,1)S(1)} %bitcast.44), channel_id=1, source_target_pairs={{0,2},{1,3},{2,0},{3,1},{4,6},{5,7},{6,4},{7,5},{8,10},{9,11},{10,... | collective-permute-start | bytes 196616 | tf_op jit(solution)/shard_map/gather/ppermute | solution.py:377
  51.1 7.6 %collective-permute-start.17 = (bf16[4,64,512]{2,1,0:T(8,128)(2,1)S(1)}, bf16[4,64,512]{2,1,0:T(8,128)(2,1)S(1)}, u32[]{:S(2)}, u32[]{:S(2)}) collective-permute-start(bf16[4,64,512]{2,1,0:T(8,128)(2,1)S(1)} %get-tuple-element.80.refs_0_), channel_id=1, source_target_pairs={{0,1},{1,0},{2,3},{3,2},{4,5},{5,4},{6,7},{7,6},{8,9},{9,8},{10,11... | collective-permute-start | bytes 786440 | tf_op jit(solution)/shard_map/gather/ppermute | solution.py:454
  58.6 1.9 %collective-permute-start.18 = (bf16[2,4,64,512]{3,2,1,0:T(8,128)(2,1)S(1)}, bf16[2,4,64,512]{3,2,1,0:T(8,128)(2,1)S(1)}, u32[]{:S(2)}, u32[]{:S(2)}) collective-permute-start(bf16[2,4,64,512]{3,2,1,0:T(8,128)(2,1)S(1)} %pad_maximum_fusion), channel_id=1, source_target_pairs={{0,8},{8,0},{16,24},{24,16},{1,9},{9,1},{17,25},{25,17},{2,10},{10... | collective-permute-start | bytes 1572872 | tf_op jit(solution)/shard_map/second/ppermute | solution.py:360
  58.7 7.5 %collective-permute-start.23 = (bf16[2,4,64,512]{3,2,1,0:T(8,128)(2,1)S(1)}, bf16[2,4,64,512]{3,2,1,0:T(8,128)(2,1)S(1)}, u32[]{:S(2)}, u32[]{:S(2)}) collective-permute-start(bf16[2,4,64,512]{3,2,1,0:T(8,128)(2,1)S(1)} %pad_maximum_fusion.1), channel_id=1, source_target_pairs={{8,16},{16,8},{9,17},{17,9},{10,18},{18,10},{11,19},{19,11},{12,20... | collective-permute-start | bytes 1572872 | tf_op jit(solution)/shard_map/second/ppermute | solution.py:360
  60.5 4.2 %copy-start = (f32[2,512,512]{2,1,0:T(8,128)S(1)}, f32[2,512,512]{2,1,0:T(8,128)}, u32[]{:S(2)}) copy-start(f32[2,512,512]{2,1,0:T(8,128)} %vector_ref.1) | copy-start | bytes 6291460
  62.7 7.2 %collective-permute-start.19 = (bf16[4,64,512]{2,1,0:T(8,128)(2,1)S(1)}, bf16[4,64,512]{2,1,0:T(8,128)(2,1)S(1)}, u32[]{:S(2)}, u32[]{:S(2)}) collective-permute-start(bf16[4,64,512]{2,1,0:T(8,128)(2,1)S(1)} %get-tuple-element.61), channel_id=1, source_target_pairs={{0,1},{1,0},{2,3},{3,2},{4,5},{5,4},{6,7},{7,6},{8,9},{9,8},{10,11... | collective-permute-start | bytes 786440 | tf_op jit(solution)/shard_map/second/ppermute | solution.py:365
  69.8 6.7 %collective-permute-start.24 = (bf16[4,64,512]{2,1,0:T(8,128)(2,1)S(1)}, bf16[4,64,512]{2,1,0:T(8,128)(2,1)S(1)}, u32[]{:S(2)}, u32[]{:S(2)}) collective-permute-start(bf16[4,64,512]{2,1,0:T(8,128)(2,1)S(1)} %get-tuple-element.66), channel_id=1, source_target_pairs={{0,1},{1,0},{2,3},{3,2},{4,5},{5,4},{6,7},{7,6},{8,9},{9,8},{10,11... | collective-permute-start | bytes 786440 | tf_op jit(solution)/shard_map/second/ppermute | solution.py:365
  70.0 11.1 %collective-permute-start.20 = (bf16[64,512]{1,0:T(8,128)(2,1)S(1)}, bf16[64,512]{1,0:T(8,128)(2,1)S(1)}, u32[]{:S(2)}, u32[]{:S(2)}) collective-permute-start(bf16[64,512]{1,0:T(8,128)(2,1)S(1)} %get-tuple-element.83), channel_id=1, source_target_pairs={{0,6},{1,7},{2,4},{3,5},{4,2},{5,3},{6,0},{7,1},{8,14},{9,15},{10,... | collective-permute-start | bytes 196616 | tf_op jit(solution)/shard_map/scalars/ppermute | solution.py:371
  71.9 10.8 %collective-permute-start.21 = (bf16[64,512]{1,0:T(8,128)(2,1)S(1)}, bf16[64,512]{1,0:T(8,128)(2,1)S(1)}, u32[]{:S(2)}, u32[]{:S(2)}) collective-permute-start(bf16[64,512]{1,0:T(8,128)(2,1)S(1)} %get-tuple-element.82), channel_id=1, source_target_pairs={{0,4},{1,5},{2,6},{3,7},{4,0},{5,1},{6,2},{7,3},{8,12},{9,13},{10,... | collective-permute-start | bytes 196616 | tf_op jit(solution)/shard_map/scalars/ppermute | solution.py:371
  72.8 5.6 %collective-permute-start.22 = (bf16[64,512]{1,0:T(8,128)(2,1)S(1)}, bf16[64,512]{1,0:T(8,128)(2,1)S(1)}, u32[]{:S(2)}, u32[]{:S(2)}) collective-permute-start(bf16[64,512]{1,0:T(8,128)(2,1)S(1)} %get-tuple-element.81), channel_id=1, source_target_pairs={{0,2},{1,3},{2,0},{3,1},{4,6},{5,7},{6,4},{7,5},{8,10},{9,11},{10,... | collective-permute-start | bytes 196616 | tf_op jit(solution)/shard_map/scalars/ppermute | solution.py:371
  76.6 9.7 %collective-permute-start.25 = (bf16[64,512]{1,0:T(8,128)(2,1)S(1)}, bf16[64,512]{1,0:T(8,128)(2,1)S(1)}, u32[]{:S(2)}, u32[]{:S(2)}) collective-permute-start(bf16[64,512]{1,0:T(8,128)(2,1)S(1)} %get-tuple-element.78), channel_id=1, source_target_pairs={{0,6},{1,7},{2,4},{3,5},{4,2},{5,3},{6,0},{7,1},{8,14},{9,15},{10,... | collective-permute-start | bytes 196616 | tf_op jit(solution)/shard_map/scalars/ppermute | solution.py:371
  77.3 9.0 %collective-permute-start.26 = (bf16[64,512]{1,0:T(8,128)(2,1)S(1)}, bf16[64,512]{1,0:T(8,128)(2,1)S(1)}, u32[]{:S(2)}, u32[]{:S(2)}) collective-permute-start(bf16[64,512]{1,0:T(8,128)(2,1)S(1)} %get-tuple-element.77), channel_id=1, source_target_pairs={{0,4},{1,5},{2,6},{3,7},{4,0},{5,1},{6,2},{7,3},{8,12},{9,13},{10,... | collective-permute-start | bytes 196616 | tf_op jit(solution)/shard_map/scalars/ppermute | solution.py:371
  78.4 7.9 %collective-permute-start.27 = (bf16[64,512]{1,0:T(8,128)(2,1)S(1)}, bf16[64,512]{1,0:T(8,128)(2,1)S(1)}, u32[]{:S(2)}, u32[]{:S(2)}) collective-permute-start(bf16[64,512]{1,0:T(8,128)(2,1)S(1)} %get-tuple-element.76), channel_id=1, source_target_pairs={{0,2},{1,3},{2,0},{3,1},{4,6},{5,7},{6,4},{7,5},{8,10},{9,11},{10,... | collective-permute-start | bytes 196616 | tf_op jit(solution)/shard_map/scalars/ppermute | solution.py:371
  81.1 5.2 %collective-permute-start.28 = (f32[8,512]{1,0:T(8,128)S(1)}, f32[8,512]{1,0:T(8,128)S(1)}, u32[]{:S(2)}, u32[]{:S(2)}) collective-permute-start(f32[8,512]{1,0:T(8,128)S(1)} %second.8.refs_14_), channel_id=1, source_target_pairs={{0,8},{8,0},{16,24},{24,16},{1,9},{9,1},{17,25},{25,17},{2,10},{10... | collective-permute-start | bytes 49160 | tf_op jit(solution)/shard_map/scalars/ppermute | solution.py:495
  82.7 5.3 %collective-permute-start.29 = (f32[8,512]{1,0:T(8,128)S(1)}, f32[8,512]{1,0:T(8,128)S(1)}, u32[]{:S(2)}, u32[]{:S(2)}) collective-permute-start(f32[8,512]{1,0:T(8,128)S(1)} %second.8.refs_14_), channel_id=1, source_target_pairs={{0,16},{8,24},{16,0},{24,8},{1,17},{9,25},{17,1},{25,9},{2,18},{10... | collective-permute-start | bytes 49160 | tf_op jit(solution)/shard_map/scalars/ppermute | solution.py:495
  86.3 3.3 %collective-permute-start.30 = (f32[8,512]{1,0:T(8,128)S(1)}, f32[8,512]{1,0:T(8,128)S(1)}, u32[]{:S(2)}, u32[]{:S(2)}) collective-permute-start(f32[8,512]{1,0:T(8,128)S(1)} %second.8.refs_14_), channel_id=1, source_target_pairs={{0,24},{8,16},{16,8},{24,0},{1,25},{9,17},{17,9},{25,1},{2,26},{10... | collective-permute-start | bytes 49160 | tf_op jit(solution)/shard_map/scalars/ppermute | solution.py:495
where the time goes:
time: 91.1 us; the launch traced here: 91.2 us
  starting transfers between devices  40.6 us (45%)
  waiting for transfers between devices  25.1 us (28%)
  Pallas kernels  23.8 us (26%)
  between operations  0.97 us (1%)
    pallas_call x12, Pallas kernels, call(): pl.pallas_call(kernel, out_shape=out_shape, in_specs=[SMEM] * len(scalars...  23.8 us
    ppermute x12, starting transfers between devices, high_parts(): lax.ppermute(total[k].astype(jnp.bfloat16), 'term', pairs_high(ranks, low...  20 us
    ppermute x6, waiting for transfers between devices, gather_high(): lax.ppermute(after_all(held, following) if k == 1 else held, 'term', pair...  9.11 us
    ppermute x6, starting transfers between devices, gather_high(): lax.ppermute(after_all(held, following) if k == 1 else held, 'term', pair...  6.2 us
    ppermute x3, starting transfers between devices, on_device(): lax.ppermute(sums, 'sector', [(i, i ^ reach * k) for i in range(groups)])  5.18 us
    ppermute x12, waiting for transfers between devices, high_parts(): lax.ppermute(total[k].astype(jnp.bfloat16), 'term', pairs_high(ranks, low...  4.94 us
    ppermute x2, waiting for transfers between devices, on_device(): theirs = lax.ppermute(mine, 'term', pairs_low(ranks)) if low > 1 else mine  4.61 us
    ppermute x4, starting transfers between devices, low_sum(): lax.ppermute(send, 'term', pairs_low(ranks)).astype(jnp.float32)  4.1 us
  transfers between devices with their start and end apart: 31, of which 14 were waited for; matrix products, arithmetic and copies ran while one was open for 1% of the time, Pallas kernels for 23%

commit v1 on v0

--- a/solution.py
+++ b/solution.py
@@ -372,13 +372,8 @@
             for k in hops
         ]
 
-    def gather_high(held, following):
-        got = {
-            k: lax.ppermute(
-                after_all(held, following) if k == 1 else held, "term", pairs_high(ranks, low, k)
-            )
-            for k in hops
-        }
+    def gather_high(held):
+        got = {k: lax.ppermute(held, "term", pairs_high(ranks, low, k)) for k in hops}
         return jnp.concatenate([held] + [got[k] for k in range(1, count)])
 
     def first_cut(acc, halos, gathered):
@@ -441,26 +436,23 @@
         shifted, plus, minus, pieces = [[None] * sectors for _ in range(4)]
         row = pltpu.VMEM((span, size), jnp.float32)
         parts = [high_parts(total) for total in totals]
-        held = [None] * sectors
         for turn in turns:
-            held[turn], shifted[turn], plus[turn], minus[turn] = call(
+            held, shifted[turn], plus[turn], minus[turn] = call(
                 functools.partial(shift_kernel, dims, turn, scale),
                 [jax.ShapeDtypeStruct((span, size), jnp.bfloat16), row, row, row],
                 (sector_sizes,),
                 (start, left_energy, right_energy, *parts[turn]),
             )
-        for turn in turns:
-            mine = gather_high(held[turn][None], held[min(turn + 1, sectors - 1)])
+            mine = gather_high(held[None])
             theirs = lax.ppermute(mine, "term", pairs_low(ranks)) if low > 1 else mine
             pieces[turn] = [mine, theirs]
-
     with jax.named_scope("second"):
         acc, block = call(
             functools.partial(self_kernel, dims),
             [square, square_low],
             (sector_shifts,),
             (left, right, *pieces[0]),
-            flops=terms * pair_flops // 3,
+            flops=1,
         )
         whole = after_all(jnp.stack(pieces[0]), pieces[-1][1], acc)
         halos = [halo(edge, n) for n, edge in enumerate((whole, jnp.stack(pieces[-1])))]

time: 91.1 us -> 87.9 us (0.965)
  Pallas kernels: 23.8 us -> 21 us
    ppermute x2, waiting for transfers between devices: 4.61 us -> 8.68 us  [on_device(): theirs = lax.ppermute(mine, 'term', pairs_low(ranks)) if low > 1 else mine]
    ppermute x6, waiting for transfers between devices: 9.11 us -> 5.85 us  [gather_high(): lax.ppermute(held, 'term', pairs_high(ranks, low, k))]
    ppermute x3, waiting for transfers between devices: 3.28 us -> 0.26 us  [on_device(): lax.ppermute(sums, 'sector', [(i, i ^ reach * k) for i in range(groups)])]
    ppermute x4, starting transfers between devices: 4.1 us -> 6.96 us  [low_sum(): lax.ppermute(send, 'term', pairs_low(ranks)).astype(jnp.float32)]
    pallas_call x12, Pallas kernels: 23.8 us -> 21 us  [call(): pl.pallas_call(kernel, out_shape=out_shape, in_specs=[SMEM] * len(scalars...]
    ppermute x6, starting transfers between devices: 6.2 us -> 8.97 us  [gather_high(): lax.ppermute(held, 'term', pairs_high(ranks, low, k))]
    ppermute x12, starting transfers between devices: 20 us -> 17.3 us  [high_parts(): lax.ppermute(total[k].astype(jnp.bfloat16), 'term', pairs_high(ranks, low...]
    ppermute x3, starting transfers between devices: 5.18 us -> 3.02 us  [on_device(): lax.ppermute(sums, 'sector', [(i, i ^ reach * k) for i in range(groups)])]
  transfers between devices with their start and end apart: 31 -> 31, of which waited for: 14 -> 11; matrix products, arithmetic and copies ran while one was open for 1% -> 1% of each run, Pallas kernels for 23% -> 20%
where the time goes in v1:
time: 87.9 us; the launch traced here: 88.6 us
  starting transfers between devices  40.2 us (46%)
  waiting for transfers between devices  25.7 us (29%)
  Pallas kernels  21 us (24%)
  between operations  0.97 us (1%)
    pallas_call x12, Pallas kernels, call(): pl.pallas_call(kernel, out_shape=out_shape, in_specs=[SMEM] * len(scalars...  21 us
    ppermute x12, starting transfers between devices, high_parts(): lax.ppermute(total[k].astype(jnp.bfloat16), 'term', pairs_high(ranks, low...  17.3 us
    ppermute x6, starting transfers between devices, gather_high(): lax.ppermute(held, 'term', pairs_high(ranks, low, k))  8.97 us
    ppermute x2, waiting for transfers between devices, on_device(): theirs = lax.ppermute(mine, 'term', pairs_low(ranks)) if low > 1 else mine  8.68 us
    ppermute x4, starting transfers between devices, low_sum(): lax.ppermute(send, 'term', pairs_low(ranks)).astype(jnp.float32)  6.96 us
    ppermute x12, waiting for transfers between devices, high_parts(): lax.ppermute(total[k].astype(jnp.bfloat16), 'term', pairs_high(ranks, low...  5.88 us
    ppermute x6, waiting for transfers between devices, gather_high(): lax.ppermute(held, 'term', pairs_high(ranks, low, k))  5.85 us
    ppermute x4, waiting for transfers between devices, low_sum(): lax.ppermute(send, 'term', pairs_low(ranks)).astype(jnp.float32)  5.06 us
  transfers between devices with their start and end apart: 31, of which 11 were waited for; matrix products, arithmetic and copies ran while one was open for 1% of the time, Pallas kernels for 20%

profile of v1, /device:TPU:0, one launch (start us, length us, event | category | flops | bytes accessed | tf_op | source)
XLA Modules:
  0.0 88.6 jit_solution(12136483034413891429)
XLA Ops:
  0.6 1.6 %first.4 = (bf16[2,512,512]{2,1,0:T(8,128)(2,1)S(1)}, bf16[512,512]{1,0:T(8,128)(2,1)S(1)}, bf16[512,512]{1,0:T(8,128)(2,1)S(1)}) custom-call(s32[2]{0:T(128)} %size_ref.7, f32[2,512,512]{2,1,0:T(8,128)} %vector_ref.1), custom_call_target="tpu_custom_call" | custom-call | flops 1048576 | bytes 4096 | tf_op jit(solution)/shard_map/first/pallas_call | solution.py:321
  2.3 0.5 collective-permute-start
  2.8 0.7 collective-permute-start.5
  3.5 3.6 %first.5 = (f32[512,512]{1,0:T(8,128)S(1)}, bf16[2,4,512,512]{3,2,1,0:T(8,128)(2,1)S(1)}, bf16[2,4,512,512]{3,2,1,0:T(8,128)(2,1)S(1)}, f32[2,64,512]{2,1,0:T(8,128)S(1)}) custom-call(bf16[2,512,512]{2,1,0:T(8,128)(2,1)S(1)} %get-tuple-element.33.wb.own, s32[4]{0:T(128)} %shift_ref.11, s32[2]{0:T(128)} %size_ref.7, bf16[2,4,512,512]{3,2,1,0:T(8,128)(2,1)} %left_hbm.1, ...), custom_call_target="tpu_custom_call" | custom-call | flops 2147483648 | bytes 8388608 | tf_op jit(solution)/shard_map/first/pallas_call | solution.py:321
  7.2 2.1 %first.6 = (bf16[4,64,512]{2,1,0:T(8,128)(2,1)S(1)}, f32[4,64,512]{2,1,0:T(8,128)S(1)}) custom-call(s32[4]{0:T(128)S(1)} %copy-done.1, f32[512,512]{1,0:T(8,128)S(1)} %get-tuple-element.35.acc_ref, bf16[2,4,512,512]{3,2,1,0:T(8,128)(2,1)S(1)} %get-tuple-element.36.left, bf16[2,4,512,512]{3,2,1,0:T(8,128)(2,1)S(1)} %get-tuple-element.37.right, ...), custom_call_target="tpu_custom_call" | custom-call | flops 715827904 | bytes 2796202 | tf_op jit(solution)/shard_map/first/pallas_call | solution.py:321
  9.3 3.3 %collective-permute-start.1 = (bf16[4,64,512]{2,1,0:T(8,128)(2,1)S(1)}, bf16[4,64,512]{2,1,0:T(8,128)(2,1)S(1)}, u32[]{:S(2)}, u32[]{:S(2)}) collective-permute-start(bf16[4,64,512]{2,1,0:T(8,128)(2,1)S(1)} %get-tuple-element.40), channel_id=1, source_target_pairs={{0,1},{1,0},{2,3},{3,2},{4,5},{5,4},{6,7},{7,6},{8,9},{9,8},{10,11... | collective-permute-start | bytes 786440 | tf_op jit(solution)/shard_map/first/ppermute | solution.py:365
  12.6 2.1 %first.7 = (bf16[4,64,512]{2,1,0:T(8,128)(2,1)S(1)}, f32[4,64,512]{2,1,0:T(8,128)S(1)}) custom-call(s32[4]{0:T(128)S(1)} %copy-done.1, bf16[2,512,512]{2,1,0:T(8,128)(2,1)S(1)} %get-tuple-element.33.wb.own, bf16[2,4,512,512]{3,2,1,0:T(8,128)(2,1)S(1)} %get-tuple-element.36.left, bf16[2,4,512,512]{3,2,1,0:T(8,128)(2,1)S(1)} %get-tuple-element.37.right, ...), custom_call_target="tpu_custom_call" | custom-call | flops 2147483648 | bytes 8388608 | tf_op jit(solution)/shard_map/first/pallas_call | solution.py:321
  14.8 0.8 collective-permute-start.6
  15.6 3.0 %collective-permute-done.1 = bf16[4,64,512]{2,1,0:T(8,128)(2,1)S(1)} collective-permute-done((bf16[4,64,512]{2,1,0:T(8,128)(2,1)S(1)}, bf16[4,64,512]{2,1,0:T(8,128)(2,1)S(1)}, u32[]{:S(2)}, u32[]{:S(2)}) %collective-permute-start.1) | collective-permute-done | bytes 262176 | tf_op jit(solution)/shard_map/first/ppermute | solution.py:365
  18.8 4.7 %collective-permute-start.2 = (bf16[64,512]{1,0:T(8,128)(2,1)S(1)}, bf16[64,512]{1,0:T(8,128)(2,1)S(1)}, u32[]{:S(2)}, u32[]{:S(2)}) collective-permute-start(bf16[64,512]{1,0:T(8,128)(2,1)S(1)} %get-tuple-element.87), channel_id=1, source_target_pairs={{0,6},{1,7},{2,4},{3,5},{4,2},{5,3},{6,0},{7,1},{8,14},{9,15},{10,... | collective-permute-start | bytes 196616 | tf_op jit(solution)/shard_map/gather/ppermute | solution.py:371
  23.5 0.6 collective-permute-start.4
  24.1 0.1 fusion.4
  24.3 4.7 %collective-permute-start.7 = (bf16[64,512]{1,0:T(8,128)(2,1)S(1)}, bf16[64,512]{1,0:T(8,128)(2,1)S(1)}, u32[]{:S(2)}, u32[]{:S(2)}) collective-permute-start(bf16[64,512]{1,0:T(8,128)(2,1)S(1)} %get-tuple-element.84), channel_id=1, source_target_pairs={{0,6},{1,7},{2,4},{3,5},{4,2},{5,3},{6,0},{7,1},{8,14},{9,15},{10,... | collective-permute-start | bytes 196616 | tf_op jit(solution)/shard_map/gather/ppermute | solution.py:371
  29.0 0.6 collective-permute-start.9
  29.6 0.7 gather.2
  30.3 3.9 %collective-permute-start.12 = (bf16[1,64,512]{2,1,0:T(8,128)(2,1)S(1)}, bf16[1,64,512]{2,1,0:T(8,128)(2,1)S(1)}, u32[]{:S(2)}, u32[]{:S(2)}) collective-permute-start(bf16[1,64,512]{2,1,0:T(8,128)(2,1)S(1)} %bitcast.42), channel_id=1, source_target_pairs={{0,6},{1,7},{2,4},{3,5},{4,2},{5,3},{6,0},{7,1},{8,14},{9,15},{10,... | collective-permute-start | bytes 196616 | tf_op jit(solution)/shard_map/gather/ppermute | solution.py:376
  34.2 0.6 collective-permute-start.10
  34.9 0.4 collective-permute-done.8.refs_2_
  35.3 0.7 gather.3
  36.0 3.3 %collective-permute-start.16 = (bf16[1,64,512]{2,1,0:T(8,128)(2,1)S(1)}, bf16[1,64,512]{2,1,0:T(8,128)(2,1)S(1)}, u32[]{:S(2)}, u32[]{:S(2)}) collective-permute-start(bf16[1,64,512]{2,1,0:T(8,128)(2,1)S(1)} %bitcast.46), channel_id=1, source_target_pairs={{0,6},{1,7},{2,4},{3,5},{4,2},{5,3},{6,0},{7,1},{8,14},{9,15},{10,... | collective-permute-start | bytes 196616 | tf_op jit(solution)/shard_map/gather/ppermute | solution.py:376
  39.4 1.1 %collective-permute-start.14 = (bf16[1,64,512]{2,1,0:T(8,128)(2,1)S(1)}, bf16[1,64,512]{2,1,0:T(8,128)(2,1)S(1)}, u32[]{:S(2)}, u32[]{:S(2)}) collective-permute-start(bf16[1,64,512]{2,1,0:T(8,128)(2,1)S(1)} %bitcast.48), channel_id=1, source_target_pairs={{0,2},{1,3},{2,0},{3,1},{4,6},{5,7},{6,4},{7,5},{8,10},{9,11},{10,... | collective-permute-start | bytes 196616 | tf_op jit(solution)/shard_map/gather/ppermute | solution.py:376
  40.5 3.2 %collective-permute-done.11 = bf16[1,64,512]{2,1,0:T(8,128)(2,1)S(1)} collective-permute-done((bf16[1,64,512]{2,1,0:T(8,128)(2,1)S(1)}, bf16[1,64,512]{2,1,0:T(8,128)(2,1)S(1)}, u32[]{:S(2)}, u32[]{:S(2)}) %collective-permute-start.11) | collective-permute-done | bytes 65568 | tf_op jit(solution)/shard_map/gather/ppermute | solution.py:376
  43.8 2.7 %collective-permute-done.15 = bf16[1,64,512]{2,1,0:T(8,128)(2,1)S(1)} collective-permute-done((bf16[1,64,512]{2,1,0:T(8,128)(2,1)S(1)}, bf16[1,64,512]{2,1,0:T(8,128)(2,1)S(1)}, u32[]{:S(2)}, u32[]{:S(2)}) %collective-permute-start.15) | collective-permute-done | bytes 65568 | tf_op jit(solution)/shard_map/gather/ppermute | solution.py:376
  46.5 1.8 %collective-permute-start.17 = (bf16[4,64,512]{2,1,0:T(8,128)(2,1)S(1)}, bf16[4,64,512]{2,1,0:T(8,128)(2,1)S(1)}, u32[]{:S(2)}, u32[]{:S(2)}) collective-permute-start(bf16[4,64,512]{2,1,0:T(8,128)(2,1)S(1)} %get-tuple-element.76.refs_0_), channel_id=1, source_target_pairs={{0,1},{1,0},{2,3},{3,2},{4,5},{5,4},{6,7},{7,6},{8,9},{9,8},{10,11... | collective-permute-start | bytes 786440 | tf_op jit(solution)/shard_map/gather/ppermute | solution.py:447
  48.3 4.6 %collective-permute-done.13.theirs = bf16[4,64,512]{2,1,0:T(8,128)(2,1)S(1)} collective-permute-done((bf16[4,64,512]{2,1,0:T(8,128)(2,1)S(1)}, bf16[4,64,512]{2,1,0:T(8,128)(2,1)S(1)}, u32[]{:S(2)}, u32[]{:S(2)}) %collective-permute-start.13) | collective-permute-done | bytes 262176 | tf_op jit(solution)/shard_map/gather/ppermute | solution.py:447
  52.9 0.7 second.5
  53.7 4.0 %collective-permute-done.17.refs_1_ = bf16[4,64,512]{2,1,0:T(8,128)(2,1)S(1)} collective-permute-done((bf16[4,64,512]{2,1,0:T(8,128)(2,1)S(1)}, bf16[4,64,512]{2,1,0:T(8,128)(2,1)S(1)}, u32[]{:S(2)}, u32[]{:S(2)}) %collective-permute-start.17) | collective-permute-done | bytes 262176 | tf_op jit(solution)/shard_map/gather/ppermute | solution.py:447
  57.8 0.9 collective-permute-start.23
  58.7 2.1 %second.6 = (f32[512,512]{1,0:T(8,128)S(1)}, bf16[2,512,512]{2,1,0:T(8,128)(2,1)S(1)}) custom-call(s32[4]{0:T(128)S(1)} %copy-done.1, f32[512,512]{1,0:T(8,128)S(1)} %get-tuple-element.51.acc_ref, bf16[512,512]{1,0:T(8,128)(2,1)S(1)} %get-tuple-element.52.first_block, bf16[2,4,512,512]{3,2,1,0:T(8,128)(2,1)S(1)} %get-tuple-element.36.left, ...), custom_call_target="tpu_custom_call" | custom-call | flops 715827904 | bytes 2796202 | tf_op jit(solution)/shard_map/second/pallas_call | solution.py:321
  60.8 2.2 %second.7 = (bf16[4,64,512]{2,1,0:T(8,128)(2,1)S(1)}, f32[4,64,512]{2,1,0:T(8,128)S(1)}) custom-call(s32[4]{0:T(128)S(1)} %copy-done.1, f32[512,512]{1,0:T(8,128)S(1)} %get-tuple-element.54.acc_ref, bf16[2,4,512,512]{3,2,1,0:T(8,128)(2,1)S(1)} %get-tuple-element.36.left, bf16[2,4,512,512]{3,2,1,0:T(8,128)(2,1)S(1)} %get-tuple-element.37.right, ...), custom_call_target="tpu_custom_call" | custom-call | flops 715827904 | bytes 2796202 | tf_op jit(solution)/shard_map/second/pallas_call | solution.py:321
  63.0 0.4 collective-permute-start.19
  63.3 1.4 %second.8.refs_14_ = f32[8,512]{1,0:T(8,128)S(1)} custom-call(s32[2]{0:T(128)S(1)} %copy-done.2, f32[2,512,512]{2,1,0:T(8,128)S(1)} %copy-done, bf16[2,512,512]{2,1,0:T(8,128)(2,1)S(1)} %get-tuple-element.60.wb.own), custom_call_target="tpu_custom_call" | custom-call | flops 1048576 | bytes 4096 | tf_op jit(solution)/shard_map/second/pallas_call | solution.py:321
  64.8 2.2 %second.9 = (bf16[4,64,512]{2,1,0:T(8,128)(2,1)S(1)}, f32[4,64,512]{2,1,0:T(8,128)S(1)}) custom-call(s32[4]{0:T(128)S(1)} %copy-done.1, bf16[2,512,512]{2,1,0:T(8,128)(2,1)S(1)} %get-tuple-element.60.wb.own, bf16[2,4,512,512]{3,2,1,0:T(8,128)(2,1)S(1)} %get-tuple-element.36.left, bf16[2,4,512,512]{3,2,1,0:T(8,128)(2,1)S(1)} %get-tuple-element.37.right, ...), custom_call_target="tpu_custom_call" | custom-call | flops 2147483648 | bytes 8388608 | tf_op jit(solution)/shard_map/second/pallas_call | solution.py:321
  67.0 2.5 %collective-permute-start.24 = (bf16[4,64,512]{2,1,0:T(8,128)(2,1)S(1)}, bf16[4,64,512]{2,1,0:T(8,128)(2,1)S(1)}, u32[]{:S(2)}, u32[]{:S(2)}) collective-permute-start(bf16[4,64,512]{2,1,0:T(8,128)(2,1)S(1)} %get-tuple-element.62), channel_id=1, source_target_pairs={{0,1},{1,0},{2,3},{3,2},{4,5},{5,4},{6,7},{7,6},{8,9},{9,8},{10,11... | collective-permute-start | bytes 786440 | tf_op jit(solution)/shard_map/second/ppermute | solution.py:365
  69.5 2.0 %collective-permute-done.19 = bf16[4,64,512]{2,1,0:T(8,128)(2,1)S(1)} collective-permute-done((bf16[4,64,512]{2,1,0:T(8,128)(2,1)S(1)}, bf16[4,64,512]{2,1,0:T(8,128)(2,1)S(1)}, u32[]{:S(2)}, u32[]{:S(2)}) %collective-permute-start.19) | collective-permute-done | bytes 262176 | tf_op jit(solution)/shard_map/second/ppermute | solution.py:365
  71.6 1.3 %collective-permute-start.20 = (bf16[64,512]{1,0:T(8,128)(2,1)S(1)}, bf16[64,512]{1,0:T(8,128)(2,1)S(1)}, u32[]{:S(2)}, u32[]{:S(2)}) collective-permute-start(bf16[64,512]{1,0:T(8,128)(2,1)S(1)} %get-tuple-element.79), channel_id=1, source_target_pairs={{0,6},{1,7},{2,4},{3,5},{4,2},{5,3},{6,0},{7,1},{8,14},{9,15},{10,... | collective-permute-start | bytes 196616 | tf_op jit(solution)/shard_map/scalars/ppermute | solution.py:371
  72.9 3.2 %collective-permute-start.22 = (bf16[64,512]{1,0:T(8,128)(2,1)S(1)}, bf16[64,512]{1,0:T(8,128)(2,1)S(1)}, u32[]{:S(2)}, u32[]{:S(2)}) collective-permute-start(bf16[64,512]{1,0:T(8,128)(2,1)S(1)} %get-tuple-element.77), channel_id=1, source_target_pairs={{0,2},{1,3},{2,0},{3,1},{4,6},{5,7},{6,4},{7,5},{8,10},{9,11},{10,... | collective-permute-start | bytes 196616 | tf_op jit(solution)/shard_map/scalars/ppermute | solution.py:371
  76.1 0.1 fusion.2
  76.2 1.3 %collective-permute-start.25 = (bf16[64,512]{1,0:T(8,128)(2,1)S(1)}, bf16[64,512]{1,0:T(8,128)(2,1)S(1)}, u32[]{:S(2)}, u32[]{:S(2)}) collective-permute-start(bf16[64,512]{1,0:T(8,128)(2,1)S(1)} %get-tuple-element.74), channel_id=1, source_target_pairs={{0,6},{1,7},{2,4},{3,5},{4,2},{5,3},{6,0},{7,1},{8,14},{9,15},{10,... | collective-permute-start | bytes 196616 | tf_op jit(solution)/shard_map/scalars/ppermute | solution.py:371
  77.5 0.3 collective-permute-start.26
  77.8 2.6 %collective-permute-done.22.refs_9_ = bf16[64,512]{1,0:T(8,128)(2,1)S(1)} collective-permute-done((bf16[64,512]{1,0:T(8,128)(2,1)S(1)}, bf16[64,512]{1,0:T(8,128)(2,1)S(1)}, u32[]{:S(2)}, u32[]{:S(2)}) %collective-permute-start.22) | collective-permute-done | bytes 65568 | tf_op jit(solution)/shard_map/scalars/ppermute | solution.py:371
  80.4 0.6 collective-permute-start.27
  81.0 1.1 %collective-permute-start.28 = (f32[8,512]{1,0:T(8,128)S(1)}, f32[8,512]{1,0:T(8,128)S(1)}, u32[]{:S(2)}, u32[]{:S(2)}) collective-permute-start(f32[8,512]{1,0:T(8,128)S(1)} %second.8.refs_14_), channel_id=1, source_target_pairs={{0,8},{8,0},{16,24},{24,16},{1,9},{9,1},{17,25},{25,17},{2,10},{10... | collective-permute-start | bytes 49160 | tf_op jit(solution)/shard_map/scalars/ppermute | solution.py:487
  82.1 1.8 %collective-permute-start.29 = (f32[8,512]{1,0:T(8,128)S(1)}, f32[8,512]{1,0:T(8,128)S(1)}, u32[]{:S(2)}, u32[]{:S(2)}) collective-permute-start(f32[8,512]{1,0:T(8,128)S(1)} %second.8.refs_14_), channel_id=1, source_target_pairs={{0,16},{8,24},{16,0},{24,8},{1,17},{9,25},{17,1},{25,9},{2,18},{10... | collective-permute-start | bytes 49160 | tf_op jit(solution)/shard_map/scalars/ppermute | solution.py:487
  83.9 0.1 collective-permute-start.30
  84.0 2.8 %collective-permute-done.26.refs_12_ = bf16[64,512]{1,0:T(8,128)(2,1)S(1)} collective-permute-done((bf16[64,512]{1,0:T(8,128)(2,1)S(1)}, bf16[64,512]{1,0:T(8,128)(2,1)S(1)}, u32[]{:S(2)}, u32[]{:S(2)}) %collective-permute-start.26) | collective-permute-done | bytes 65568 | tf_op jit(solution)/shard_map/scalars/ppermute | solution.py:371
  86.8 0.3 collective-permute-done.30.refs_17_
  87.1 1.5 %scalars.1 = (f32[2,64,512]{2,1,0:T(8,128)}, f32[2,64,512]{2,1,0:T(8,128)}) custom-call(s32[2]{0:T(128)S(1)} %copy-done.2, f32[2,64,512]{2,1,0:T(8,128)S(1)} %get-tuple-element.34.start, f32[64,512]{1,0:T(8,128)S(1)} %get-tuple-element.41.refs_0_, f32[64,512]{1,0:T(8,128)S(1)} %get-tuple-element.45.refs_1_, f32[64,512]{1,0:T(8,128)S(1)} %get-tuple-element.46.refs_2_, ...), custom_call_target="tpu_custom_call" | custom-call | flops 1048576 | bytes 4096 | tf_op jit(solution)/shard_map/scalars/pallas_call | solution.py:321
  (52 shorter events, 0.8 us)
Async XLA Ops:
  2.3 4.9 %collective-permute-start = (bf16[512,512]{1,0:T(8,128)(2,1)S(1)}, bf16[512,512]{1,0:T(8,128)(2,1)S(1)}, u32[]{:S(2)}, u32[]{:S(2)}) collective-permute-start(bf16[512,512]{1,0:T(8,128)(2,1)S(1)} %get-tuple-element.38), channel_id=1, source_target_pairs={{0,8},{8,0},{16,24},{24,16},{1,9},{9,1},{17,25},{25,17},{2,10},{10... | collective-permute-start | bytes 1572872 | tf_op jit(solution)/shard_map/first/ppermute | solution.py:360
  2.8 9.8 %collective-permute-start.5 = (bf16[512,512]{1,0:T(8,128)(2,1)S(1)}, bf16[512,512]{1,0:T(8,128)(2,1)S(1)}, u32[]{:S(2)}, u32[]{:S(2)}) collective-permute-start(bf16[512,512]{1,0:T(8,128)(2,1)S(1)} %get-tuple-element.42), channel_id=1, source_target_pairs={{8,16},{16,8},{9,17},{17,9},{10,18},{18,10},{11,19},{19,11},{12,20... | collective-permute-start | bytes 1572872 | tf_op jit(solution)/shard_map/first/ppermute | solution.py:360
  3.5 3.7 %copy-start.1 = (s32[4]{0:T(128)S(1)}, s32[4]{0:T(128)}, u32[]{:S(2)}) copy-start(s32[4]{0:T(128)} %shift_ref.11) | copy-start | bytes 52
  9.3 9.3 %collective-permute-start.1 = (bf16[4,64,512]{2,1,0:T(8,128)(2,1)S(1)}, bf16[4,64,512]{2,1,0:T(8,128)(2,1)S(1)}, u32[]{:S(2)}, u32[]{:S(2)}) collective-permute-start(bf16[4,64,512]{2,1,0:T(8,128)(2,1)S(1)} %get-tuple-element.40), channel_id=1, source_target_pairs={{0,1},{1,0},{2,3},{3,2},{4,5},{5,4},{6,7},{7,6},{8,9},{9,8},{10,11... | collective-permute-start | bytes 786440 | tf_op jit(solution)/shard_map/first/ppermute | solution.py:365
  14.8 14.9 %copy-start.2 = (s32[2]{0:T(128)S(1)}, s32[2]{0:T(128)}, u32[]{:S(2)}) copy-start(s32[2]{0:T(128)} %size_ref.7) | copy-start | bytes 28
  14.8 14.8 %copy-start.3 = (f32[2,512]{1,0:T(2,128)S(1)}, f32[2,512]{1,0:T(2,128)}, u32[]{:S(2)}) copy-start(f32[2,512]{1,0:T(2,128)} %left_row.3) | copy-start | bytes 12292
  14.8 14.8 %copy-start.4 = (f32[2,512]{1,0:T(2,128)S(1)}, f32[2,512]{1,0:T(2,128)}, u32[]{:S(2)}) copy-start(f32[2,512]{1,0:T(2,128)} %right_row.3) | copy-start | bytes 12292
  14.8 9.3 %collective-permute-start.6 = (bf16[4,64,512]{2,1,0:T(8,128)(2,1)S(1)}, bf16[4,64,512]{2,1,0:T(8,128)(2,1)S(1)}, u32[]{:S(2)}, u32[]{:S(2)}) collective-permute-start(bf16[4,64,512]{2,1,0:T(8,128)(2,1)S(1)} %get-tuple-element.44), channel_id=1, source_target_pairs={{0,1},{1,0},{2,3},{3,2},{4,5},{5,4},{6,7},{7,6},{8,9},{9,8},{10,11... | collective-permute-start | bytes 786440 | tf_op jit(solution)/shard_map/first/ppermute | solution.py:365
  18.8 10.3 %collective-permute-start.2 = (bf16[64,512]{1,0:T(8,128)(2,1)S(1)}, bf16[64,512]{1,0:T(8,128)(2,1)S(1)}, u32[]{:S(2)}, u32[]{:S(2)}) collective-permute-start(bf16[64,512]{1,0:T(8,128)(2,1)S(1)} %get-tuple-element.87), channel_id=1, source_target_pairs={{0,6},{1,7},{2,4},{3,5},{4,2},{5,3},{6,0},{7,1},{8,14},{9,15},{10,... | collective-permute-start | bytes 196616 | tf_op jit(solution)/shard_map/gather/ppermute | solution.py:371
  23.5 6.1 %collective-permute-start.3 = (bf16[64,512]{1,0:T(8,128)(2,1)S(1)}, bf16[64,512]{1,0:T(8,128)(2,1)S(1)}, u32[]{:S(2)}, u32[]{:S(2)}) collective-permute-start(bf16[64,512]{1,0:T(8,128)(2,1)S(1)} %get-tuple-element.86), channel_id=1, source_target_pairs={{0,4},{1,5},{2,6},{3,7},{4,0},{5,1},{6,2},{7,3},{8,12},{9,13},{10,... | collective-permute-start | bytes 196616 | tf_op jit(solution)/shard_map/gather/ppermute | solution.py:371
  23.5 6.1 %collective-permute-start.4 = (bf16[64,512]{1,0:T(8,128)(2,1)S(1)}, bf16[64,512]{1,0:T(8,128)(2,1)S(1)}, u32[]{:S(2)}, u32[]{:S(2)}) collective-permute-start(bf16[64,512]{1,0:T(8,128)(2,1)S(1)} %get-tuple-element.85), channel_id=1, source_target_pairs={{0,2},{1,3},{2,0},{3,1},{4,6},{5,7},{6,4},{7,5},{8,10},{9,11},{10,... | collective-permute-start | bytes 196616 | tf_op jit(solution)/shard_map/gather/ppermute | solution.py:371
  24.3 9.9 %collective-permute-start.7 = (bf16[64,512]{1,0:T(8,128)(2,1)S(1)}, bf16[64,512]{1,0:T(8,128)(2,1)S(1)}, u32[]{:S(2)}, u32[]{:S(2)}) collective-permute-start(bf16[64,512]{1,0:T(8,128)(2,1)S(1)} %get-tuple-element.84), channel_id=1, source_target_pairs={{0,6},{1,7},{2,4},{3,5},{4,2},{5,3},{6,0},{7,1},{8,14},{9,15},{10,... | collective-permute-start | bytes 196616 | tf_op jit(solution)/shard_map/gather/ppermute | solution.py:371
  29.0 6.3 %collective-permute-start.8 = (bf16[64,512]{1,0:T(8,128)(2,1)S(1)}, bf16[64,512]{1,0:T(8,128)(2,1)S(1)}, u32[]{:S(2)}, u32[]{:S(2)}) collective-permute-start(bf16[64,512]{1,0:T(8,128)(2,1)S(1)} %get-tuple-element.83), channel_id=1, source_target_pairs={{0,4},{1,5},{2,6},{3,7},{4,0},{5,1},{6,2},{7,3},{8,12},{9,13},{10,... | collective-permute-start | bytes 196616 | tf_op jit(solution)/shard_map/gather/ppermute | solution.py:371
  29.0 6.3 %collective-permute-start.9 = (bf16[64,512]{1,0:T(8,128)(2,1)S(1)}, bf16[64,512]{1,0:T(8,128)(2,1)S(1)}, u32[]{:S(2)}, u32[]{:S(2)}) collective-permute-start(bf16[64,512]{1,0:T(8,128)(2,1)S(1)} %get-tuple-element.82), channel_id=1, source_target_pairs={{0,2},{1,3},{2,0},{3,1},{4,6},{5,7},{6,4},{7,5},{8,10},{9,11},{10,... | collective-permute-start | bytes 196616 | tf_op jit(solution)/shard_map/gather/ppermute | solution.py:371
  30.3 9.1 %collective-permute-start.12 = (bf16[1,64,512]{2,1,0:T(8,128)(2,1)S(1)}, bf16[1,64,512]{2,1,0:T(8,128)(2,1)S(1)}, u32[]{:S(2)}, u32[]{:S(2)}) collective-permute-start(bf16[1,64,512]{2,1,0:T(8,128)(2,1)S(1)} %bitcast.42), channel_id=1, source_target_pairs={{0,6},{1,7},{2,4},{3,5},{4,2},{5,3},{6,0},{7,1},{8,14},{9,15},{10,... | collective-permute-start | bytes 196616 | tf_op jit(solution)/shard_map/gather/ppermute | solution.py:376
  34.2 9.5 %collective-permute-start.11 = (bf16[1,64,512]{2,1,0:T(8,128)(2,1)S(1)}, bf16[1,64,512]{2,1,0:T(8,128)(2,1)S(1)}, u32[]{:S(2)}, u32[]{:S(2)}) collective-permute-start(bf16[1,64,512]{2,1,0:T(8,128)(2,1)S(1)} %bitcast.43), channel_id=1, source_target_pairs={{0,4},{1,5},{2,6},{3,7},{4,0},{5,1},{6,2},{7,3},{8,12},{9,13},{10,... | collective-permute-start | bytes 196616 | tf_op jit(solution)/shard_map/gather/ppermute | solution.py:376
  34.2 9.5 %collective-permute-start.10 = (bf16[1,64,512]{2,1,0:T(8,128)(2,1)S(1)}, bf16[1,64,512]{2,1,0:T(8,128)(2,1)S(1)}, u32[]{:S(2)}, u32[]{:S(2)}) collective-permute-start(bf16[1,64,512]{2,1,0:T(8,128)(2,1)S(1)} %bitcast.44), channel_id=1, source_target_pairs={{0,2},{1,3},{2,0},{3,1},{4,6},{5,7},{6,4},{7,5},{8,10},{9,11},{10,... | collective-permute-start | bytes 196616 | tf_op jit(solution)/shard_map/gather/ppermute | solution.py:376
  36.0 7.8 %collective-permute-start.16 = (bf16[1,64,512]{2,1,0:T(8,128)(2,1)S(1)}, bf16[1,64,512]{2,1,0:T(8,128)(2,1)S(1)}, u32[]{:S(2)}, u32[]{:S(2)}) collective-permute-start(bf16[1,64,512]{2,1,0:T(8,128)(2,1)S(1)} %bitcast.46), channel_id=1, source_target_pairs={{0,6},{1,7},{2,4},{3,5},{4,2},{5,3},{6,0},{7,1},{8,14},{9,15},{10,... | collective-permute-start | bytes 196616 | tf_op jit(solution)/shard_map/gather/ppermute | solution.py:376
  39.4 7.1 %collective-permute-start.15 = (bf16[1,64,512]{2,1,0:T(8,128)(2,1)S(1)}, bf16[1,64,512]{2,1,0:T(8,128)(2,1)S(1)}, u32[]{:S(2)}, u32[]{:S(2)}) collective-permute-start(bf16[1,64,512]{2,1,0:T(8,128)(2,1)S(1)} %bitcast.47), channel_id=1, source_target_pairs={{0,4},{1,5},{2,6},{3,7},{4,0},{5,1},{6,2},{7,3},{8,12},{9,13},{10,... | collective-permute-start | bytes 196616 | tf_op jit(solution)/shard_map/gather/ppermute | solution.py:376
  39.4 7.1 %collective-permute-start.14 = (bf16[1,64,512]{2,1,0:T(8,128)(2,1)S(1)}, bf16[1,64,512]{2,1,0:T(8,128)(2,1)S(1)}, u32[]{:S(2)}, u32[]{:S(2)}) collective-permute-start(bf16[1,64,512]{2,1,0:T(8,128)(2,1)S(1)} %bitcast.48), channel_id=1, source_target_pairs={{0,2},{1,3},{2,0},{3,1},{4,6},{5,7},{6,4},{7,5},{8,10},{9,11},{10,... | collective-permute-start | bytes 196616 | tf_op jit(solution)/shard_map/gather/ppermute | solution.py:376
  43.7 9.2 %collective-permute-start.13 = (bf16[4,64,512]{2,1,0:T(8,128)(2,1)S(1)}, bf16[4,64,512]{2,1,0:T(8,128)(2,1)S(1)}, u32[]{:S(2)}, u32[]{:S(2)}) collective-permute-start(bf16[4,64,512]{2,1,0:T(8,128)(2,1)S(1)} %get-tuple-element.81.mine), channel_id=1, source_target_pairs={{0,1},{1,0},{2,3},{3,2},{4,5},{5,4},{6,7},{7,6},{8,9},{9,8},{10,11... | collective-permute-start | bytes 786440 | tf_op jit(solution)/shard_map/gather/ppermute | solution.py:447
  46.5 11.2 %collective-permute-start.17 = (bf16[4,64,512]{2,1,0:T(8,128)(2,1)S(1)}, bf16[4,64,512]{2,1,0:T(8,128)(2,1)S(1)}, u32[]{:S(2)}, u32[]{:S(2)}) collective-permute-start(bf16[4,64,512]{2,1,0:T(8,128)(2,1)S(1)} %get-tuple-element.76.refs_0_), channel_id=1, source_target_pairs={{0,1},{1,0},{2,3},{3,2},{4,5},{5,4},{6,7},{7,6},{8,9},{9,8},{10,11... | collective-permute-start | bytes 786440 | tf_op jit(solution)/shard_map/gather/ppermute | solution.py:447
  57.7 3.1 %collective-permute-start.18 = (bf16[2,4,64,512]{3,2,1,0:T(8,128)(2,1)S(1)}, bf16[2,4,64,512]{3,2,1,0:T(8,128)(2,1)S(1)}, u32[]{:S(2)}, u32[]{:S(2)}) collective-permute-start(bf16[2,4,64,512]{3,2,1,0:T(8,128)(2,1)S(1)} %pad_maximum_fusion), channel_id=1, source_target_pairs={{0,8},{8,0},{16,24},{24,16},{1,9},{9,1},{17,25},{25,17},{2,10},{10... | collective-permute-start | bytes 1572872 | tf_op jit(solution)/shard_map/second/ppermute | solution.py:360
  57.8 7.0 %collective-permute-start.23 = (bf16[2,4,64,512]{3,2,1,0:T(8,128)(2,1)S(1)}, bf16[2,4,64,512]{3,2,1,0:T(8,128)(2,1)S(1)}, u32[]{:S(2)}, u32[]{:S(2)}) collective-permute-start(bf16[2,4,64,512]{3,2,1,0:T(8,128)(2,1)S(1)} %pad_maximum_fusion.1), channel_id=1, source_target_pairs={{8,16},{16,8},{9,17},{17,9},{10,18},{18,10},{11,19},{19,11},{12,20... | collective-permute-start | bytes 1572872 | tf_op jit(solution)/shard_map/second/ppermute | solution.py:360
  60.8 2.5 %copy-start = (f32[2,512,512]{2,1,0:T(8,128)S(1)}, f32[2,512,512]{2,1,0:T(8,128)}, u32[]{:S(2)}) copy-start(f32[2,512,512]{2,1,0:T(8,128)} %vector_ref.1) | copy-start | bytes 6291460
  63.0 8.5 %collective-permute-start.19 = (bf16[4,64,512]{2,1,0:T(8,128)(2,1)S(1)}, bf16[4,64,512]{2,1,0:T(8,128)(2,1)S(1)}, u32[]{:S(2)}, u32[]{:S(2)}) collective-permute-start(bf16[4,64,512]{2,1,0:T(8,128)(2,1)S(1)} %get-tuple-element.57), channel_id=1, source_target_pairs={{0,1},{1,0},{2,3},{3,2},{4,5},{5,4},{6,7},{7,6},{8,9},{9,8},{10,11... | collective-permute-start | bytes 786440 | tf_op jit(solution)/shard_map/second/ppermute | solution.py:365
  67.0 9.1 %collective-permute-start.24 = (bf16[4,64,512]{2,1,0:T(8,128)(2,1)S(1)}, bf16[4,64,512]{2,1,0:T(8,128)(2,1)S(1)}, u32[]{:S(2)}, u32[]{:S(2)}) collective-permute-start(bf16[4,64,512]{2,1,0:T(8,128)(2,1)S(1)} %get-tuple-element.62), channel_id=1, source_target_pairs={{0,1},{1,0},{2,3},{3,2},{4,5},{5,4},{6,7},{7,6},{8,9},{9,8},{10,11... | collective-permute-start | bytes 786440 | tf_op jit(solution)/shard_map/second/ppermute | solution.py:365
  71.6 9.4 %collective-permute-start.20 = (bf16[64,512]{1,0:T(8,128)(2,1)S(1)}, bf16[64,512]{1,0:T(8,128)(2,1)S(1)}, u32[]{:S(2)}, u32[]{:S(2)}) collective-permute-start(bf16[64,512]{1,0:T(8,128)(2,1)S(1)} %get-tuple-element.79), channel_id=1, source_target_pairs={{0,6},{1,7},{2,4},{3,5},{4,2},{5,3},{6,0},{7,1},{8,14},{9,15},{10,... | collective-permute-start | bytes 196616 | tf_op jit(solution)/shard_map/scalars/ppermute | solution.py:371
  72.9 9.2 %collective-permute-start.21 = (bf16[64,512]{1,0:T(8,128)(2,1)S(1)}, bf16[64,512]{1,0:T(8,128)(2,1)S(1)}, u32[]{:S(2)}, u32[]{:S(2)}) collective-permute-start(bf16[64,512]{1,0:T(8,128)(2,1)S(1)} %get-tuple-element.78), channel_id=1, source_target_pairs={{0,4},{1,5},{2,6},{3,7},{4,0},{5,1},{6,2},{7,3},{8,12},{9,13},{10,... | collective-permute-start | bytes 196616 | tf_op jit(solution)/shard_map/scalars/ppermute | solution.py:371
  72.9 7.5 %collective-permute-start.22 = (bf16[64,512]{1,0:T(8,128)(2,1)S(1)}, bf16[64,512]{1,0:T(8,128)(2,1)S(1)}, u32[]{:S(2)}, u32[]{:S(2)}) collective-permute-start(bf16[64,512]{1,0:T(8,128)(2,1)S(1)} %get-tuple-element.77), channel_id=1, source_target_pairs={{0,2},{1,3},{2,0},{3,1},{4,6},{5,7},{6,4},{7,5},{8,10},{9,11},{10,... | collective-permute-start | bytes 196616 | tf_op jit(solution)/shard_map/scalars/ppermute | solution.py:371
  76.2 7.7 %collective-permute-start.25 = (bf16[64,512]{1,0:T(8,128)(2,1)S(1)}, bf16[64,512]{1,0:T(8,128)(2,1)S(1)}, u32[]{:S(2)}, u32[]{:S(2)}) collective-permute-start(bf16[64,512]{1,0:T(8,128)(2,1)S(1)} %get-tuple-element.74), channel_id=1, source_target_pairs={{0,6},{1,7},{2,4},{3,5},{4,2},{5,3},{6,0},{7,1},{8,14},{9,15},{10,... | collective-permute-start | bytes 196616 | tf_op jit(solution)/shard_map/scalars/ppermute | solution.py:371
  77.5 9.3 %collective-permute-start.26 = (bf16[64,512]{1,0:T(8,128)(2,1)S(1)}, bf16[64,512]{1,0:T(8,128)(2,1)S(1)}, u32[]{:S(2)}, u32[]{:S(2)}) collective-permute-start(bf16[64,512]{1,0:T(8,128)(2,1)S(1)} %get-tuple-element.73), channel_id=1, source_target_pairs={{0,4},{1,5},{2,6},{3,7},{4,0},{5,1},{6,2},{7,3},{8,12},{9,13},{10,... | collective-permute-start | bytes 196616 | tf_op jit(solution)/shard_map/scalars/ppermute | solution.py:371
  80.4 6.4 %collective-permute-start.27 = (bf16[64,512]{1,0:T(8,128)(2,1)S(1)}, bf16[64,512]{1,0:T(8,128)(2,1)S(1)}, u32[]{:S(2)}, u32[]{:S(2)}) collective-permute-start(bf16[64,512]{1,0:T(8,128)(2,1)S(1)} %get-tuple-element.72), channel_id=1, source_target_pairs={{0,2},{1,3},{2,0},{3,1},{4,6},{5,7},{6,4},{7,5},{8,10},{9,11},{10,... | collective-permute-start | bytes 196616 | tf_op jit(solution)/shard_map/scalars/ppermute | solution.py:371
  81.0 5.8 %collective-permute-start.28 = (f32[8,512]{1,0:T(8,128)S(1)}, f32[8,512]{1,0:T(8,128)S(1)}, u32[]{:S(2)}, u32[]{:S(2)}) collective-permute-start(f32[8,512]{1,0:T(8,128)S(1)} %second.8.refs_14_), channel_id=1, source_target_pairs={{0,8},{8,0},{16,24},{24,16},{1,9},{9,1},{17,25},{25,17},{2,10},{10... | collective-permute-start | bytes 49160 | tf_op jit(solution)/shard_map/scalars/ppermute | solution.py:487
  82.1 4.7 %collective-permute-start.29 = (f32[8,512]{1,0:T(8,128)S(1)}, f32[8,512]{1,0:T(8,128)S(1)}, u32[]{:S(2)}, u32[]{:S(2)}) collective-permute-start(f32[8,512]{1,0:T(8,128)S(1)} %second.8.refs_14_), channel_id=1, source_target_pairs={{0,16},{8,24},{16,0},{24,8},{1,17},{9,25},{17,1},{25,9},{2,18},{10... | collective-permute-start | bytes 49160 | tf_op jit(solution)/shard_map/scalars/ppermute | solution.py:487
  83.9 3.2 %collective-permute-start.30 = (f32[8,512]{1,0:T(8,128)S(1)}, f32[8,512]{1,0:T(8,128)S(1)}, u32[]{:S(2)}, u32[]{:S(2)}) collective-permute-start(f32[8,512]{1,0:T(8,128)S(1)} %second.8.refs_14_), channel_id=1, source_target_pairs={{0,24},{8,16},{16,8},{24,0},{1,25},{9,17},{17,9},{25,1},{2,26},{10... | collective-permute-start | bytes 49160 | tf_op jit(solution)/shard_map/scalars/ppermute | solution.py:487

commit v2 on v1

--- a/solution.py
+++ b/solution.py
@@ -28,6 +28,17 @@
     return [(i, other(i // low, step, count) * low + i % low) for i in range(size)]
 
 
+def gather_steps(count):
+    return [1 << b for b in reversed(range(count.bit_length() - 1))] if count & (count - 1) == 0 else None
+
+
+def gather_order(count):
+    order = [0]
+    for step in gather_steps(count) or ():
+        order += [o ^ step for o in order]
+    return order if gather_steps(count) else list(range(count))
+
+
 def row_finder(count, low, span):
     rank = lax.axis_index("term")
     hi, lo = rank // low, lax.rem(rank, low)
@@ -76,8 +87,8 @@
     sectors, terms, size, count, low, span = dims
     row_of = row_finder(count, low, span)
     for far in range(low):
-        for step in range(count):
-            wb[pl.ds(row_of(step, far), span), :] = pieces[far][step]
+        for n, step in enumerate(gather_order(count)):
+            wb[pl.ds(row_of(step, far), span), :] = pieces[far][n]
 
 
 def add_outer(dims, turn, gathered, shift_ref, acc, left, right, blocks, wb):
@@ -373,8 +384,14 @@
         ]
 
     def gather_high(held):
-        got = {k: lax.ppermute(held, "term", pairs_high(ranks, low, k)) for k in hops}
-        return jnp.concatenate([held] + [got[k] for k in range(1, count)])
+        steps = gather_steps(count)
+        if steps is None:
+            got = [lax.ppermute(held, "term", pairs_high(ranks, low, k)) for k in range(1, count)]
+            return jnp.concatenate([held, *got])
+        for step in steps:
+            got = lax.ppermute(held, "term", pairs_high(ranks, low, step))
+            held = jnp.concatenate([held, got])
+        return held
 
     def first_cut(acc, halos, gathered):
         return call(

time: 87.9 us -> 89.4 us (1.017)
  Pallas kernels: 21 us -> 22.6 us
  waiting for transfers between devices: 25.7 us -> 24.1 us
    ppermute x6 -> x4, starting transfers between devices: 8.97 us -> 4.08 us  [gather_high(): got = lax.ppermute(held, 'term', pairs_high(ranks, low, step))]
    ppermute x3, starting transfers between devices: 3.02 us -> 6.27 us  [on_device(): lax.ppermute(sums, 'sector', [(i, i ^ reach * k) for i in range(groups)])]
    ppermute x12, starting transfers between devices: 17.3 us -> 20.5 us  [high_parts(): lax.ppermute(total[k].astype(jnp.bfloat16), 'term', pairs_high(ranks, low...]
    ppermute x4, starting transfers between devices: 6.96 us -> 4.11 us  [low_sum(): lax.ppermute(send, 'term', pairs_low(ranks)).astype(jnp.float32)]
    ppermute x12, waiting for transfers between devices: 5.88 us -> 3.49 us  [high_parts(): lax.ppermute(total[k].astype(jnp.bfloat16), 'term', pairs_high(ranks, low...]
    ppermute x2, starting transfers between devices: 1.86 us -> 4.12 us  [on_device(): theirs = lax.ppermute(mine, 'term', pairs_low(ranks)) if low > 1 else mine]
    ppermute x6 -> x4, waiting for transfers between devices: 5.85 us -> 7.6 us  [gather_high(): got = lax.ppermute(held, 'term', pairs_high(ranks, low, step))]
    pallas_call x12, Pallas kernels: 21 us -> 22.6 us  [call(): pl.pallas_call(kernel, out_shape=out_shape, in_specs=[SMEM] * len(scalars...]
  transfers between devices with their start and end apart: 31 -> 29, of which waited for: 11 -> 11; matrix products, arithmetic and copies ran while one was open for 1% -> 1% of each run, Pallas kernels for 20% -> 22%
where the time goes in v2:
time: 89.4 us
  starting transfers between devices  40.9 us (46%)
  waiting for transfers between devices  24.1 us (27%)
  Pallas kernels  22.6 us (25%)
  between operations  1.02 us (1%)
    pallas_call x12, Pallas kernels, call(): pl.pallas_call(kernel, out_shape=out_shape, in_specs=[SMEM] * len(scalars...  22.6 us
    ppermute x12, starting transfers between devices, high_parts(): lax.ppermute(total[k].astype(jnp.bfloat16), 'term', pairs_high(ranks, low...  20.5 us
    ppermute x2, waiting for transfers between devices, on_device(): theirs = lax.ppermute(mine, 'term', pairs_low(ranks)) if low > 1 else mine  7.65 us
    ppermute x4, waiting for transfers between devices, gather_high(): got = lax.ppermute(held, 'term', pairs_high(ranks, low, step))  7.6 us
    ppermute x3, starting transfers between devices, on_device(): lax.ppermute(sums, 'sector', [(i, i ^ reach * k) for i in range(groups)])  6.27 us
    ppermute x2, starting transfers between devices, on_device(): theirs = lax.ppermute(mine, 'term', pairs_low(ranks)) if low > 1 else mine  4.12 us
    ppermute x4, starting transfers between devices, low_sum(): lax.ppermute(send, 'term', pairs_low(ranks)).astype(jnp.float32)  4.11 us
    ppermute x4, starting transfers between devices, gather_high(): got = lax.ppermute(held, 'term', pairs_high(ranks, low, step))  4.08 us
  transfers between devices with their start and end apart: 29, of which 11 were waited for; matrix products, arithmetic and copies ran while one was open for 1% of the time, Pallas kernels for 22%

profile of v2, /device:TPU:0, one launch (start us, length us, event | category | flops | bytes accessed | tf_op | source)
XLA Modules:
  0.0 89.4 jit_solution(3604179935349399961)
XLA Ops:
  0.6 1.6 %first.4 = (bf16[2,512,512]{2,1,0:T(8,128)(2,1)S(1)}, bf16[512,512]{1,0:T(8,128)(2,1)S(1)}, bf16[512,512]{1,0:T(8,128)(2,1)S(1)}) custom-call(s32[2]{0:T(128)} %size_ref.7, f32[2,512,512]{2,1,0:T(8,128)} %vector_ref.1), custom_call_target="tpu_custom_call" | custom-call | flops 1048576 | bytes 4096 | tf_op jit(solution)/shard_map/first/pallas_call | solution.py:332
  2.3 0.5 collective-permute-start
  2.8 0.7 collective-permute-start.5
  3.5 3.6 %first.5 = (f32[512,512]{1,0:T(8,128)S(1)}, bf16[2,4,512,512]{3,2,1,0:T(8,128)(2,1)S(1)}, bf16[2,4,512,512]{3,2,1,0:T(8,128)(2,1)S(1)}, f32[2,64,512]{2,1,0:T(8,128)S(1)}) custom-call(bf16[2,512,512]{2,1,0:T(8,128)(2,1)S(1)} %get-tuple-element.33.wb.own, s32[4]{0:T(128)} %shift_ref.11, s32[2]{0:T(128)} %size_ref.7, bf16[2,4,512,512]{3,2,1,0:T(8,128)(2,1)} %left_hbm.1, ...), custom_call_target="tpu_custom_call" | custom-call | flops 2147483648 | bytes 8388608 | tf_op jit(solution)/shard_map/first/pallas_call | solution.py:332
  7.2 2.1 %first.6 = (bf16[4,64,512]{2,1,0:T(8,128)(2,1)S(1)}, f32[4,64,512]{2,1,0:T(8,128)S(1)}) custom-call(s32[4]{0:T(128)S(1)} %copy-done.1, f32[512,512]{1,0:T(8,128)S(1)} %get-tuple-element.35.acc_ref, bf16[2,4,512,512]{3,2,1,0:T(8,128)(2,1)S(1)} %get-tuple-element.36.left, bf16[2,4,512,512]{3,2,1,0:T(8,128)(2,1)S(1)} %get-tuple-element.37.right, ...), custom_call_target="tpu_custom_call" | custom-call | flops 715827904 | bytes 2796202 | tf_op jit(solution)/shard_map/first/pallas_call | solution.py:332
  9.3 2.2 %collective-permute-start.1 = (bf16[4,64,512]{2,1,0:T(8,128)(2,1)S(1)}, bf16[4,64,512]{2,1,0:T(8,128)(2,1)S(1)}, u32[]{:S(2)}, u32[]{:S(2)}) collective-permute-start(bf16[4,64,512]{2,1,0:T(8,128)(2,1)S(1)} %get-tuple-element.40), channel_id=1, source_target_pairs={{0,1},{1,0},{2,3},{3,2},{4,5},{5,4},{6,7},{7,6},{8,9},{9,8},{10,11... | collective-permute-start | bytes 786440 | tf_op jit(solution)/shard_map/first/ppermute | solution.py:376
  11.5 2.9 %first.7 = (bf16[4,64,512]{2,1,0:T(8,128)(2,1)S(1)}, f32[4,64,512]{2,1,0:T(8,128)S(1)}) custom-call(s32[4]{0:T(128)S(1)} %copy-done.1, bf16[2,512,512]{2,1,0:T(8,128)(2,1)S(1)} %get-tuple-element.33.wb.own, bf16[2,4,512,512]{3,2,1,0:T(8,128)(2,1)S(1)} %get-tuple-element.36.left, bf16[2,4,512,512]{3,2,1,0:T(8,128)(2,1)S(1)} %get-tuple-element.37.right, ...), custom_call_target="tpu_custom_call" | custom-call | flops 2147483648 | bytes 8388608 | tf_op jit(solution)/shard_map/first/pallas_call | solution.py:332
  14.4 1.5 %collective-permute-done.1 = bf16[4,64,512]{2,1,0:T(8,128)(2,1)S(1)} collective-permute-done((bf16[4,64,512]{2,1,0:T(8,128)(2,1)S(1)}, bf16[4,64,512]{2,1,0:T(8,128)(2,1)S(1)}, u32[]{:S(2)}, u32[]{:S(2)}) %collective-permute-start.1) | collective-permute-done | bytes 262176 | tf_op jit(solution)/shard_map/first/ppermute | solution.py:376
  16.0 0.1 fusion.5
  16.1 6.1 %collective-permute-start.2 = (bf16[64,512]{1,0:T(8,128)(2,1)S(1)}, bf16[64,512]{1,0:T(8,128)(2,1)S(1)}, u32[]{:S(2)}, u32[]{:S(2)}) collective-permute-start(bf16[64,512]{1,0:T(8,128)(2,1)S(1)} %get-tuple-element.87), channel_id=1, source_target_pairs={{0,6},{1,7},{2,4},{3,5},{4,2},{5,3},{6,0},{7,1},{8,14},{9,15},{10,... | collective-permute-start | bytes 196616 | tf_op jit(solution)/shard_map/gather/ppermute | solution.py:382
  22.2 0.6 collective-permute-start.4
  22.9 0.1 fusion.4
  23.0 4.1 %collective-permute-start.7 = (bf16[64,512]{1,0:T(8,128)(2,1)S(1)}, bf16[64,512]{1,0:T(8,128)(2,1)S(1)}, u32[]{:S(2)}, u32[]{:S(2)}) collective-permute-start(bf16[64,512]{1,0:T(8,128)(2,1)S(1)} %get-tuple-element.84), channel_id=1, source_target_pairs={{0,6},{1,7},{2,4},{3,5},{4,2},{5,3},{6,0},{7,1},{8,14},{9,15},{10,... | collective-permute-start | bytes 196616 | tf_op jit(solution)/shard_map/gather/ppermute | solution.py:382
  27.1 0.6 collective-permute-start.9
  27.8 0.5 collective-permute-done.3.refs_2_
  28.3 0.7 gather.2
  28.9 1.9 %collective-permute-start.10 = (bf16[1,64,512]{2,1,0:T(8,128)(2,1)S(1)}, bf16[1,64,512]{2,1,0:T(8,128)(2,1)S(1)}, u32[]{:S(2)}, u32[]{:S(2)}) collective-permute-start(bf16[1,64,512]{2,1,0:T(8,128)(2,1)S(1)} %bitcast.42), channel_id=1, source_target_pairs={{0,4},{1,5},{2,6},{3,7},{4,0},{5,1},{6,2},{7,3},{8,12},{9,13},{10,... | collective-permute-start | bytes 196616 | tf_op jit(solution)/shard_map/gather/ppermute | solution.py:392
  30.9 3.0 %collective-permute-done.8.refs_2_ = bf16[64,512]{1,0:T(8,128)(2,1)S(1)} collective-permute-done((bf16[64,512]{1,0:T(8,128)(2,1)S(1)}, bf16[64,512]{1,0:T(8,128)(2,1)S(1)}, u32[]{:S(2)}, u32[]{:S(2)}) %collective-permute-start.8) | collective-permute-done | bytes 65568 | tf_op jit(solution)/shard_map/gather/ppermute | solution.py:382
  33.8 0.7 gather.3
  34.5 0.9 collective-permute-start.13
  35.4 1.3 %collective-permute-done.10 = bf16[1,64,512]{2,1,0:T(8,128)(2,1)S(1)} collective-permute-done((bf16[1,64,512]{2,1,0:T(8,128)(2,1)S(1)}, bf16[1,64,512]{2,1,0:T(8,128)(2,1)S(1)}, u32[]{:S(2)}, u32[]{:S(2)}) %collective-permute-start.10) | collective-permute-done | bytes 65568 | tf_op jit(solution)/shard_map/gather/ppermute | solution.py:392
  36.7 1.3 %collective-permute-start.11 = (bf16[2,64,512]{2,1,0:T(8,128)(2,1)S(1)}, bf16[2,64,512]{2,1,0:T(8,128)(2,1)S(1)}, u32[]{:S(2)}, u32[]{:S(2)}) collective-permute-start(bf16[2,64,512]{2,1,0:T(8,128)(2,1)S(1)} %pad_maximum_fusion.4), channel_id=1, source_target_pairs={{0,2},{1,3},{2,0},{3,1},{4,6},{5,7},{6,4},{7,5},{8,10},{9,11},{10,... | collective-permute-start | bytes 393224 | tf_op jit(solution)/shard_map/gather/ppermute | solution.py:392
  37.9 2.3 %collective-permute-done.13 = bf16[1,64,512]{2,1,0:T(8,128)(2,1)S(1)} collective-permute-done((bf16[1,64,512]{2,1,0:T(8,128)(2,1)S(1)}, bf16[1,64,512]{2,1,0:T(8,128)(2,1)S(1)}, u32[]{:S(2)}, u32[]{:S(2)}) %collective-permute-start.13) | collective-permute-done | bytes 65568 | tf_op jit(solution)/shard_map/gather/ppermute | solution.py:392
  40.3 3.2 %collective-permute-done.11 = bf16[2,64,512]{2,1,0:T(8,128)(2,1)S(1)} collective-permute-done((bf16[2,64,512]{2,1,0:T(8,128)(2,1)S(1)}, bf16[2,64,512]{2,1,0:T(8,128)(2,1)S(1)}, u32[]{:S(2)}, u32[]{:S(2)}) %collective-permute-start.11) | collective-permute-done | bytes 131104 | tf_op jit(solution)/shard_map/gather/ppermute | solution.py:392
  43.6 1.9 %collective-permute-start.12 = (bf16[4,64,512]{2,1,0:T(8,128)(2,1)S(1)}, bf16[4,64,512]{2,1,0:T(8,128)(2,1)S(1)}, u32[]{:S(2)}, u32[]{:S(2)}) collective-permute-start(bf16[4,64,512]{2,1,0:T(8,128)(2,1)S(1)} %get-tuple-element.81.mine), channel_id=1, source_target_pairs={{0,1},{1,0},{2,3},{3,2},{4,5},{5,4},{6,7},{7,6},{8,9},{9,8},{10,11... | collective-permute-start | bytes 786440 | tf_op jit(solution)/shard_map/gather/ppermute | solution.py:464
  45.4 0.8 collective-permute-done.14
  46.3 2.2 %collective-permute-start.15 = (bf16[4,64,512]{2,1,0:T(8,128)(2,1)S(1)}, bf16[4,64,512]{2,1,0:T(8,128)(2,1)S(1)}, u32[]{:S(2)}, u32[]{:S(2)}) collective-permute-start(bf16[4,64,512]{2,1,0:T(8,128)(2,1)S(1)} %get-tuple-element.76.refs_0_), channel_id=1, source_target_pairs={{0,1},{1,0},{2,3},{3,2},{4,5},{5,4},{6,7},{7,6},{8,9},{9,8},{10,11... | collective-permute-start | bytes 786440 | tf_op jit(solution)/shard_map/gather/ppermute | solution.py:464
  48.6 4.2 %collective-permute-done.12.theirs = bf16[4,64,512]{2,1,0:T(8,128)(2,1)S(1)} collective-permute-done((bf16[4,64,512]{2,1,0:T(8,128)(2,1)S(1)}, bf16[4,64,512]{2,1,0:T(8,128)(2,1)S(1)}, u32[]{:S(2)}, u32[]{:S(2)}) %collective-permute-start.12) | collective-permute-done | bytes 262176 | tf_op jit(solution)/shard_map/gather/ppermute | solution.py:464
  52.8 1.4 %second.5 = (f32[512,512]{1,0:T(8,128)S(1)}, bf16[512,512]{1,0:T(8,128)(2,1)S(1)}) custom-call(s32[4]{0:T(128)S(1)} %copy-done.1, bf16[2,4,512,512]{3,2,1,0:T(8,128)(2,1)S(1)} %get-tuple-element.36.left, bf16[2,4,512,512]{3,2,1,0:T(8,128)(2,1)S(1)} %get-tuple-element.37.right, bf16[4,64,512]{2,1,0:T(8,128)(2,1)S(1)} %get-tuple-element.81.mine, ...), custom_call_target="tpu_custom_call" | custom-call | flops 1 | tf_op jit(solution)/shard_map/second/pallas_call | solution.py:332
  54.2 3.4 %collective-permute-done.15.refs_1_ = bf16[4,64,512]{2,1,0:T(8,128)(2,1)S(1)} collective-permute-done((bf16[4,64,512]{2,1,0:T(8,128)(2,1)S(1)}, bf16[4,64,512]{2,1,0:T(8,128)(2,1)S(1)}, u32[]{:S(2)}, u32[]{:S(2)}) %collective-permute-start.15) | collective-permute-done | bytes 262176 | tf_op jit(solution)/shard_map/gather/ppermute | solution.py:464
  57.7 0.7 collective-permute-start.21
  58.4 1.6 %second.6 = (f32[512,512]{1,0:T(8,128)S(1)}, bf16[2,512,512]{2,1,0:T(8,128)(2,1)S(1)}) custom-call(s32[4]{0:T(128)S(1)} %copy-done.1, f32[512,512]{1,0:T(8,128)S(1)} %get-tuple-element.51.acc_ref, bf16[512,512]{1,0:T(8,128)(2,1)S(1)} %get-tuple-element.52.first_block, bf16[2,4,512,512]{3,2,1,0:T(8,128)(2,1)S(1)} %get-tuple-element.36.left, ...), custom_call_target="tpu_custom_call" | custom-call | flops 715827904 | bytes 2796202 | tf_op jit(solution)/shard_map/second/pallas_call | solution.py:332
  60.0 2.2 %second.7 = (bf16[4,64,512]{2,1,0:T(8,128)(2,1)S(1)}, f32[4,64,512]{2,1,0:T(8,128)S(1)}) custom-call(s32[4]{0:T(128)S(1)} %copy-done.1, f32[512,512]{1,0:T(8,128)S(1)} %get-tuple-element.54.acc_ref, bf16[2,4,512,512]{3,2,1,0:T(8,128)(2,1)S(1)} %get-tuple-element.36.left, bf16[2,4,512,512]{3,2,1,0:T(8,128)(2,1)S(1)} %get-tuple-element.37.right, ...), custom_call_target="tpu_custom_call" | custom-call | flops 715827904 | bytes 2796202 | tf_op jit(solution)/shard_map/second/pallas_call | solution.py:332
  62.2 1.8 %collective-permute-start.17 = (bf16[4,64,512]{2,1,0:T(8,128)(2,1)S(1)}, bf16[4,64,512]{2,1,0:T(8,128)(2,1)S(1)}, u32[]{:S(2)}, u32[]{:S(2)}) collective-permute-start(bf16[4,64,512]{2,1,0:T(8,128)(2,1)S(1)} %get-tuple-element.57), channel_id=1, source_target_pairs={{0,1},{1,0},{2,3},{3,2},{4,5},{5,4},{6,7},{7,6},{8,9},{9,8},{10,11... | collective-permute-start | bytes 786440 | tf_op jit(solution)/shard_map/second/ppermute | solution.py:376
  64.0 1.4 %second.8.refs_14_ = f32[8,512]{1,0:T(8,128)S(1)} custom-call(s32[2]{0:T(128)S(1)} %copy-done.2, f32[2,512,512]{2,1,0:T(8,128)S(1)} %copy-done, bf16[2,512,512]{2,1,0:T(8,128)(2,1)S(1)} %get-tuple-element.60.wb.own), custom_call_target="tpu_custom_call" | custom-call | flops 1048576 | bytes 4096 | tf_op jit(solution)/shard_map/second/pallas_call | solution.py:332
  65.5 2.9 %second.9 = (bf16[4,64,512]{2,1,0:T(8,128)(2,1)S(1)}, f32[4,64,512]{2,1,0:T(8,128)S(1)}) custom-call(s32[4]{0:T(128)S(1)} %copy-done.1, bf16[2,512,512]{2,1,0:T(8,128)(2,1)S(1)} %get-tuple-element.60.wb.own, bf16[2,4,512,512]{3,2,1,0:T(8,128)(2,1)S(1)} %get-tuple-element.36.left, bf16[2,4,512,512]{3,2,1,0:T(8,128)(2,1)S(1)} %get-tuple-element.37.right, ...), custom_call_target="tpu_custom_call" | custom-call | flops 2147483648 | bytes 8388608 | tf_op jit(solution)/shard_map/second/pallas_call | solution.py:332
  68.4 2.3 %collective-permute-done.17 = bf16[4,64,512]{2,1,0:T(8,128)(2,1)S(1)} collective-permute-done((bf16[4,64,512]{2,1,0:T(8,128)(2,1)S(1)}, bf16[4,64,512]{2,1,0:T(8,128)(2,1)S(1)}, u32[]{:S(2)}, u32[]{:S(2)}) %collective-permute-start.17) | collective-permute-done | bytes 262176 | tf_op jit(solution)/shard_map/second/ppermute | solution.py:376
  70.7 0.1 fusion.3
  70.8 2.9 %collective-permute-start.18 = (bf16[64,512]{1,0:T(8,128)(2,1)S(1)}, bf16[64,512]{1,0:T(8,128)(2,1)S(1)}, u32[]{:S(2)}, u32[]{:S(2)}) collective-permute-start(bf16[64,512]{1,0:T(8,128)(2,1)S(1)} %get-tuple-element.79), channel_id=1, source_target_pairs={{0,6},{1,7},{2,4},{3,5},{4,2},{5,3},{6,0},{7,1},{8,14},{9,15},{10,... | collective-permute-start | bytes 196616 | tf_op jit(solution)/shard_map/scalars/ppermute | solution.py:382
  73.8 1.5 %collective-permute-start.20 = (bf16[64,512]{1,0:T(8,128)(2,1)S(1)}, bf16[64,512]{1,0:T(8,128)(2,1)S(1)}, u32[]{:S(2)}, u32[]{:S(2)}) collective-permute-start(bf16[64,512]{1,0:T(8,128)(2,1)S(1)} %get-tuple-element.77), channel_id=1, source_target_pairs={{0,2},{1,3},{2,0},{3,1},{4,6},{5,7},{6,4},{7,5},{8,10},{9,11},{10,... | collective-permute-start | bytes 196616 | tf_op jit(solution)/shard_map/scalars/ppermute | solution.py:382
  75.3 0.1 fusion.2
  75.4 2.9 %collective-permute-start.23 = (bf16[64,512]{1,0:T(8,128)(2,1)S(1)}, bf16[64,512]{1,0:T(8,128)(2,1)S(1)}, u32[]{:S(2)}, u32[]{:S(2)}) collective-permute-start(bf16[64,512]{1,0:T(8,128)(2,1)S(1)} %get-tuple-element.74), channel_id=1, source_target_pairs={{0,6},{1,7},{2,4},{3,5},{4,2},{5,3},{6,0},{7,1},{8,14},{9,15},{10,... | collective-permute-start | bytes 196616 | tf_op jit(solution)/shard_map/scalars/ppermute | solution.py:382
  78.4 1.5 %collective-permute-start.25 = (bf16[64,512]{1,0:T(8,128)(2,1)S(1)}, bf16[64,512]{1,0:T(8,128)(2,1)S(1)}, u32[]{:S(2)}, u32[]{:S(2)}) collective-permute-start(bf16[64,512]{1,0:T(8,128)(2,1)S(1)} %get-tuple-element.72), channel_id=1, source_target_pairs={{0,2},{1,3},{2,0},{3,1},{4,6},{5,7},{6,4},{7,5},{8,10},{9,11},{10,... | collective-permute-start | bytes 196616 | tf_op jit(solution)/shard_map/scalars/ppermute | solution.py:382
  80.0 2.0 %collective-permute-start.26 = (f32[8,512]{1,0:T(8,128)S(1)}, f32[8,512]{1,0:T(8,128)S(1)}, u32[]{:S(2)}, u32[]{:S(2)}) collective-permute-start(f32[8,512]{1,0:T(8,128)S(1)} %second.8.refs_14_), channel_id=1, source_target_pairs={{0,8},{8,0},{16,24},{24,16},{1,9},{9,1},{17,25},{25,17},{2,10},{10... | collective-permute-start | bytes 49160 | tf_op jit(solution)/shard_map/scalars/ppermute | solution.py:504
  82.0 1.9 %collective-permute-start.27 = (f32[8,512]{1,0:T(8,128)S(1)}, f32[8,512]{1,0:T(8,128)S(1)}, u32[]{:S(2)}, u32[]{:S(2)}) collective-permute-start(f32[8,512]{1,0:T(8,128)S(1)} %second.8.refs_14_), channel_id=1, source_target_pairs={{0,16},{8,24},{16,0},{24,8},{1,17},{9,25},{17,1},{25,9},{2,18},{10... | collective-permute-start | bytes 49160 | tf_op jit(solution)/shard_map/scalars/ppermute | solution.py:504
  83.9 2.3 %collective-permute-start.28 = (f32[8,512]{1,0:T(8,128)S(1)}, f32[8,512]{1,0:T(8,128)S(1)}, u32[]{:S(2)}, u32[]{:S(2)}) collective-permute-start(f32[8,512]{1,0:T(8,128)S(1)} %second.8.refs_14_), channel_id=1, source_target_pairs={{0,24},{8,16},{16,8},{24,0},{1,25},{9,17},{17,9},{25,1},{2,26},{10... | collective-permute-start | bytes 49160 | tf_op jit(solution)/shard_map/scalars/ppermute | solution.py:504
  86.3 1.5 %collective-permute-done.28.refs_17_ = f32[8,512]{1,0:T(8,128)S(1)} collective-permute-done((f32[8,512]{1,0:T(8,128)S(1)}, f32[8,512]{1,0:T(8,128)S(1)}, u32[]{:S(2)}, u32[]{:S(2)}) %collective-permute-start.28) | collective-permute-done | bytes 16416 | tf_op jit(solution)/shard_map/scalars/ppermute | solution.py:504
  87.8 1.5 %scalars.1 = (f32[2,64,512]{2,1,0:T(8,128)}, f32[2,64,512]{2,1,0:T(8,128)}) custom-call(s32[2]{0:T(128)S(1)} %copy-done.2, f32[2,64,512]{2,1,0:T(8,128)S(1)} %get-tuple-element.34.start, f32[64,512]{1,0:T(8,128)S(1)} %get-tuple-element.41.refs_0_, f32[64,512]{1,0:T(8,128)S(1)} %get-tuple-element.45.refs_1_, f32[64,512]{1,0:T(8,128)S(1)} %get-tuple-element.46.refs_2_, ...), custom_call_target="tpu_custom_call" | custom-call | flops 1048576 | bytes 4096 | tf_op jit(solution)/shard_map/scalars/pallas_call | solution.py:332
  (50 shorter events, 0.7 us)
Async XLA Ops:
  2.3 4.9 %collective-permute-start = (bf16[512,512]{1,0:T(8,128)(2,1)S(1)}, bf16[512,512]{1,0:T(8,128)(2,1)S(1)}, u32[]{:S(2)}, u32[]{:S(2)}) collective-permute-start(bf16[512,512]{1,0:T(8,128)(2,1)S(1)} %get-tuple-element.38), channel_id=1, source_target_pairs={{0,8},{8,0},{16,24},{24,16},{1,9},{9,1},{17,25},{25,17},{2,10},{10... | collective-permute-start | bytes 1572872 | tf_op jit(solution)/shard_map/first/ppermute | solution.py:371
  2.8 8.7 %collective-permute-start.5 = (bf16[512,512]{1,0:T(8,128)(2,1)S(1)}, bf16[512,512]{1,0:T(8,128)(2,1)S(1)}, u32[]{:S(2)}, u32[]{:S(2)}) collective-permute-start(bf16[512,512]{1,0:T(8,128)(2,1)S(1)} %get-tuple-element.42), channel_id=1, source_target_pairs={{8,16},{16,8},{9,17},{17,9},{10,18},{18,10},{11,19},{19,11},{12,20... | collective-permute-start | bytes 1572872 | tf_op jit(solution)/shard_map/first/ppermute | solution.py:371
  3.5 3.7 %copy-start.1 = (s32[4]{0:T(128)S(1)}, s32[4]{0:T(128)}, u32[]{:S(2)}) copy-start(s32[4]{0:T(128)} %shift_ref.11) | copy-start | bytes 52
  9.3 6.7 %collective-permute-start.1 = (bf16[4,64,512]{2,1,0:T(8,128)(2,1)S(1)}, bf16[4,64,512]{2,1,0:T(8,128)(2,1)S(1)}, u32[]{:S(2)}, u32[]{:S(2)}) collective-permute-start(bf16[4,64,512]{2,1,0:T(8,128)(2,1)S(1)} %get-tuple-element.40), channel_id=1, source_target_pairs={{0,1},{1,0},{2,3},{3,2},{4,5},{5,4},{6,7},{7,6},{8,9},{9,8},{10,11... | collective-permute-start | bytes 786440 | tf_op jit(solution)/shard_map/first/ppermute | solution.py:376
  14.3 13.9 %copy-start.2 = (s32[2]{0:T(128)S(1)}, s32[2]{0:T(128)}, u32[]{:S(2)}) copy-start(s32[2]{0:T(128)} %size_ref.7) | copy-start | bytes 28
  14.3 13.9 %copy-start.3 = (f32[2,512]{1,0:T(2,128)S(1)}, f32[2,512]{1,0:T(2,128)}, u32[]{:S(2)}) copy-start(f32[2,512]{1,0:T(2,128)} %left_row.3) | copy-start | bytes 12292
  14.3 13.9 %copy-start.4 = (f32[2,512]{1,0:T(2,128)S(1)}, f32[2,512]{1,0:T(2,128)}, u32[]{:S(2)}) copy-start(f32[2,512]{1,0:T(2,128)} %right_row.3) | copy-start | bytes 12292
  14.4 8.5 %collective-permute-start.6 = (bf16[4,64,512]{2,1,0:T(8,128)(2,1)S(1)}, bf16[4,64,512]{2,1,0:T(8,128)(2,1)S(1)}, u32[]{:S(2)}, u32[]{:S(2)}) collective-permute-start(bf16[4,64,512]{2,1,0:T(8,128)(2,1)S(1)} %get-tuple-element.44), channel_id=1, source_target_pairs={{0,1},{1,0},{2,3},{3,2},{4,5},{5,4},{6,7},{7,6},{8,9},{9,8},{10,11... | collective-permute-start | bytes 786440 | tf_op jit(solution)/shard_map/first/ppermute | solution.py:376
  16.1 11.0 %collective-permute-start.2 = (bf16[64,512]{1,0:T(8,128)(2,1)S(1)}, bf16[64,512]{1,0:T(8,128)(2,1)S(1)}, u32[]{:S(2)}, u32[]{:S(2)}) collective-permute-start(bf16[64,512]{1,0:T(8,128)(2,1)S(1)} %get-tuple-element.87), channel_id=1, source_target_pairs={{0,6},{1,7},{2,4},{3,5},{4,2},{5,3},{6,0},{7,1},{8,14},{9,15},{10,... | collective-permute-start | bytes 196616 | tf_op jit(solution)/shard_map/gather/ppermute | solution.py:382
  22.2 6.0 %collective-permute-start.3 = (bf16[64,512]{1,0:T(8,128)(2,1)S(1)}, bf16[64,512]{1,0:T(8,128)(2,1)S(1)}, u32[]{:S(2)}, u32[]{:S(2)}) collective-permute-start(bf16[64,512]{1,0:T(8,128)(2,1)S(1)} %get-tuple-element.86), channel_id=1, source_target_pairs={{0,4},{1,5},{2,6},{3,7},{4,0},{5,1},{6,2},{7,3},{8,12},{9,13},{10,... | collective-permute-start | bytes 196616 | tf_op jit(solution)/shard_map/gather/ppermute | solution.py:382
  22.2 6.0 %collective-permute-start.4 = (bf16[64,512]{1,0:T(8,128)(2,1)S(1)}, bf16[64,512]{1,0:T(8,128)(2,1)S(1)}, u32[]{:S(2)}, u32[]{:S(2)}) collective-permute-start(bf16[64,512]{1,0:T(8,128)(2,1)S(1)} %get-tuple-element.85), channel_id=1, source_target_pairs={{0,2},{1,3},{2,0},{3,1},{4,6},{5,7},{6,4},{7,5},{8,10},{9,11},{10,... | collective-permute-start | bytes 196616 | tf_op jit(solution)/shard_map/gather/ppermute | solution.py:382
  23.0 7.9 %collective-permute-start.7 = (bf16[64,512]{1,0:T(8,128)(2,1)S(1)}, bf16[64,512]{1,0:T(8,128)(2,1)S(1)}, u32[]{:S(2)}, u32[]{:S(2)}) collective-permute-start(bf16[64,512]{1,0:T(8,128)(2,1)S(1)} %get-tuple-element.84), channel_id=1, source_target_pairs={{0,6},{1,7},{2,4},{3,5},{4,2},{5,3},{6,0},{7,1},{8,14},{9,15},{10,... | collective-permute-start | bytes 196616 | tf_op jit(solution)/shard_map/gather/ppermute | solution.py:382
  27.1 6.7 %collective-permute-start.8 = (bf16[64,512]{1,0:T(8,128)(2,1)S(1)}, bf16[64,512]{1,0:T(8,128)(2,1)S(1)}, u32[]{:S(2)}, u32[]{:S(2)}) collective-permute-start(bf16[64,512]{1,0:T(8,128)(2,1)S(1)} %get-tuple-element.83), channel_id=1, source_target_pairs={{0,4},{1,5},{2,6},{3,7},{4,0},{5,1},{6,2},{7,3},{8,12},{9,13},{10,... | collective-permute-start | bytes 196616 | tf_op jit(solution)/shard_map/gather/ppermute | solution.py:382
  27.1 6.7 %collective-permute-start.9 = (bf16[64,512]{1,0:T(8,128)(2,1)S(1)}, bf16[64,512]{1,0:T(8,128)(2,1)S(1)}, u32[]{:S(2)}, u32[]{:S(2)}) collective-permute-start(bf16[64,512]{1,0:T(8,128)(2,1)S(1)} %get-tuple-element.82), channel_id=1, source_target_pairs={{0,2},{1,3},{2,0},{3,1},{4,6},{5,7},{6,4},{7,5},{8,10},{9,11},{10,... | collective-permute-start | bytes 196616 | tf_op jit(solution)/shard_map/gather/ppermute | solution.py:382
  28.9 7.7 %collective-permute-start.10 = (bf16[1,64,512]{2,1,0:T(8,128)(2,1)S(1)}, bf16[1,64,512]{2,1,0:T(8,128)(2,1)S(1)}, u32[]{:S(2)}, u32[]{:S(2)}) collective-permute-start(bf16[1,64,512]{2,1,0:T(8,128)(2,1)S(1)} %bitcast.42), channel_id=1, source_target_pairs={{0,4},{1,5},{2,6},{3,7},{4,0},{5,1},{6,2},{7,3},{8,12},{9,13},{10,... | collective-permute-start | bytes 196616 | tf_op jit(solution)/shard_map/gather/ppermute | solution.py:392
  34.5 5.7 %collective-permute-start.13 = (bf16[1,64,512]{2,1,0:T(8,128)(2,1)S(1)}, bf16[1,64,512]{2,1,0:T(8,128)(2,1)S(1)}, u32[]{:S(2)}, u32[]{:S(2)}) collective-permute-start(bf16[1,64,512]{2,1,0:T(8,128)(2,1)S(1)} %bitcast.45), channel_id=1, source_target_pairs={{0,4},{1,5},{2,6},{3,7},{4,0},{5,1},{6,2},{7,3},{8,12},{9,13},{10,... | collective-permute-start | bytes 196616 | tf_op jit(solution)/shard_map/gather/ppermute | solution.py:392
  36.7 6.9 %collective-permute-start.11 = (bf16[2,64,512]{2,1,0:T(8,128)(2,1)S(1)}, bf16[2,64,512]{2,1,0:T(8,128)(2,1)S(1)}, u32[]{:S(2)}, u32[]{:S(2)}) collective-permute-start(bf16[2,64,512]{2,1,0:T(8,128)(2,1)S(1)} %pad_maximum_fusion.4), channel_id=1, source_target_pairs={{0,2},{1,3},{2,0},{3,1},{4,6},{5,7},{6,4},{7,5},{8,10},{9,11},{10,... | collective-permute-start | bytes 393224 | tf_op jit(solution)/shard_map/gather/ppermute | solution.py:392
  40.2 6.0 %collective-permute-start.14 = (bf16[2,64,512]{2,1,0:T(8,128)(2,1)S(1)}, bf16[2,64,512]{2,1,0:T(8,128)(2,1)S(1)}, u32[]{:S(2)}, u32[]{:S(2)}) collective-permute-start(bf16[2,64,512]{2,1,0:T(8,128)(2,1)S(1)} %pad_maximum_fusion.5), channel_id=1, source_target_pairs={{0,2},{1,3},{2,0},{3,1},{4,6},{5,7},{6,4},{7,5},{8,10},{9,11},{10,... | collective-permute-start | bytes 393224 | tf_op jit(solution)/shard_map/gather/ppermute | solution.py:392
  43.6 9.2 %collective-permute-start.12 = (bf16[4,64,512]{2,1,0:T(8,128)(2,1)S(1)}, bf16[4,64,512]{2,1,0:T(8,128)(2,1)S(1)}, u32[]{:S(2)}, u32[]{:S(2)}) collective-permute-start(bf16[4,64,512]{2,1,0:T(8,128)(2,1)S(1)} %get-tuple-element.81.mine), channel_id=1, source_target_pairs={{0,1},{1,0},{2,3},{3,2},{4,5},{5,4},{6,7},{7,6},{8,9},{9,8},{10,11... | collective-permute-start | bytes 786440 | tf_op jit(solution)/shard_map/gather/ppermute | solution.py:464
  46.3 11.3 %collective-permute-start.15 = (bf16[4,64,512]{2,1,0:T(8,128)(2,1)S(1)}, bf16[4,64,512]{2,1,0:T(8,128)(2,1)S(1)}, u32[]{:S(2)}, u32[]{:S(2)}) collective-permute-start(bf16[4,64,512]{2,1,0:T(8,128)(2,1)S(1)} %get-tuple-element.76.refs_0_), channel_id=1, source_target_pairs={{0,1},{1,0},{2,3},{3,2},{4,5},{5,4},{6,7},{7,6},{8,9},{9,8},{10,11... | collective-permute-start | bytes 786440 | tf_op jit(solution)/shard_map/gather/ppermute | solution.py:464
  57.6 2.4 %collective-permute-start.16 = (bf16[2,4,64,512]{3,2,1,0:T(8,128)(2,1)S(1)}, bf16[2,4,64,512]{3,2,1,0:T(8,128)(2,1)S(1)}, u32[]{:S(2)}, u32[]{:S(2)}) collective-permute-start(bf16[2,4,64,512]{3,2,1,0:T(8,128)(2,1)S(1)} %pad_maximum_fusion), channel_id=1, source_target_pairs={{0,8},{8,0},{16,24},{24,16},{1,9},{9,1},{17,25},{25,17},{2,10},{10... | collective-permute-start | bytes 1572872 | tf_op jit(solution)/shard_map/second/ppermute | solution.py:371
  57.7 7.8 %collective-permute-start.21 = (bf16[2,4,64,512]{3,2,1,0:T(8,128)(2,1)S(1)}, bf16[2,4,64,512]{3,2,1,0:T(8,128)(2,1)S(1)}, u32[]{:S(2)}, u32[]{:S(2)}) collective-permute-start(bf16[2,4,64,512]{3,2,1,0:T(8,128)(2,1)S(1)} %pad_maximum_fusion.1), channel_id=1, source_target_pairs={{8,16},{16,8},{9,17},{17,9},{10,18},{18,10},{11,19},{19,11},{12,20... | collective-permute-start | bytes 1572872 | tf_op jit(solution)/shard_map/second/ppermute | solution.py:371
  60.0 4.0 %copy-start = (f32[2,512,512]{2,1,0:T(8,128)S(1)}, f32[2,512,512]{2,1,0:T(8,128)}, u32[]{:S(2)}) copy-start(f32[2,512,512]{2,1,0:T(8,128)} %vector_ref.1) | copy-start | bytes 6291460
  62.2 8.5 %collective-permute-start.17 = (bf16[4,64,512]{2,1,0:T(8,128)(2,1)S(1)}, bf16[4,64,512]{2,1,0:T(8,128)(2,1)S(1)}, u32[]{:S(2)}, u32[]{:S(2)}) collective-permute-start(bf16[4,64,512]{2,1,0:T(8,128)(2,1)S(1)} %get-tuple-element.57), channel_id=1, source_target_pairs={{0,1},{1,0},{2,3},{3,2},{4,5},{5,4},{6,7},{7,6},{8,9},{9,8},{10,11... | collective-permute-start | bytes 786440 | tf_op jit(solution)/shard_map/second/ppermute | solution.py:376
  68.4 6.9 %collective-permute-start.22 = (bf16[4,64,512]{2,1,0:T(8,128)(2,1)S(1)}, bf16[4,64,512]{2,1,0:T(8,128)(2,1)S(1)}, u32[]{:S(2)}, u32[]{:S(2)}) collective-permute-start(bf16[4,64,512]{2,1,0:T(8,128)(2,1)S(1)} %get-tuple-element.62), channel_id=1, source_target_pairs={{0,1},{1,0},{2,3},{3,2},{4,5},{5,4},{6,7},{7,6},{8,9},{9,8},{10,11... | collective-permute-start | bytes 786440 | tf_op jit(solution)/shard_map/second/ppermute | solution.py:376
  70.8 9.1 %collective-permute-start.18 = (bf16[64,512]{1,0:T(8,128)(2,1)S(1)}, bf16[64,512]{1,0:T(8,128)(2,1)S(1)}, u32[]{:S(2)}, u32[]{:S(2)}) collective-permute-start(bf16[64,512]{1,0:T(8,128)(2,1)S(1)} %get-tuple-element.79), channel_id=1, source_target_pairs={{0,6},{1,7},{2,4},{3,5},{4,2},{5,3},{6,0},{7,1},{8,14},{9,15},{10,... | collective-permute-start | bytes 196616 | tf_op jit(solution)/shard_map/scalars/ppermute | solution.py:382
  73.8 8.2 %collective-permute-start.19 = (bf16[64,512]{1,0:T(8,128)(2,1)S(1)}, bf16[64,512]{1,0:T(8,128)(2,1)S(1)}, u32[]{:S(2)}, u32[]{:S(2)}) collective-permute-start(bf16[64,512]{1,0:T(8,128)(2,1)S(1)} %get-tuple-element.78), channel_id=1, source_target_pairs={{0,4},{1,5},{2,6},{3,7},{4,0},{5,1},{6,2},{7,3},{8,12},{9,13},{10,... | collective-permute-start | bytes 196616 | tf_op jit(solution)/shard_map/scalars/ppermute | solution.py:382
  73.8 4.7 %collective-permute-start.20 = (bf16[64,512]{1,0:T(8,128)(2,1)S(1)}, bf16[64,512]{1,0:T(8,128)(2,1)S(1)}, u32[]{:S(2)}, u32[]{:S(2)}) collective-permute-start(bf16[64,512]{1,0:T(8,128)(2,1)S(1)} %get-tuple-element.77), channel_id=1, source_target_pairs={{0,2},{1,3},{2,0},{3,1},{4,6},{5,7},{6,4},{7,5},{8,10},{9,11},{10,... | collective-permute-start | bytes 196616 | tf_op jit(solution)/shard_map/scalars/ppermute | solution.py:382
  75.4 8.5 %collective-permute-start.23 = (bf16[64,512]{1,0:T(8,128)(2,1)S(1)}, bf16[64,512]{1,0:T(8,128)(2,1)S(1)}, u32[]{:S(2)}, u32[]{:S(2)}) collective-permute-start(bf16[64,512]{1,0:T(8,128)(2,1)S(1)} %get-tuple-element.74), channel_id=1, source_target_pairs={{0,6},{1,7},{2,4},{3,5},{4,2},{5,3},{6,0},{7,1},{8,14},{9,15},{10,... | collective-permute-start | bytes 196616 | tf_op jit(solution)/shard_map/scalars/ppermute | solution.py:382
  78.4 7.9 %collective-permute-start.24 = (bf16[64,512]{1,0:T(8,128)(2,1)S(1)}, bf16[64,512]{1,0:T(8,128)(2,1)S(1)}, u32[]{:S(2)}, u32[]{:S(2)}) collective-permute-start(bf16[64,512]{1,0:T(8,128)(2,1)S(1)} %get-tuple-element.73), channel_id=1, source_target_pairs={{0,4},{1,5},{2,6},{3,7},{4,0},{5,1},{6,2},{7,3},{8,12},{9,13},{10,... | collective-permute-start | bytes 196616 | tf_op jit(solution)/shard_map/scalars/ppermute | solution.py:382
  78.4 7.8 %collective-permute-start.25 = (bf16[64,512]{1,0:T(8,128)(2,1)S(1)}, bf16[64,512]{1,0:T(8,128)(2,1)S(1)}, u32[]{:S(2)}, u32[]{:S(2)}) collective-permute-start(bf16[64,512]{1,0:T(8,128)(2,1)S(1)} %get-tuple-element.72), channel_id=1, source_target_pairs={{0,2},{1,3},{2,0},{3,1},{4,6},{5,7},{6,4},{7,5},{8,10},{9,11},{10,... | collective-permute-start | bytes 196616 | tf_op jit(solution)/shard_map/scalars/ppermute | solution.py:382
  80.0 6.3 %collective-permute-start.26 = (f32[8,512]{1,0:T(8,128)S(1)}, f32[8,512]{1,0:T(8,128)S(1)}, u32[]{:S(2)}, u32[]{:S(2)}) collective-permute-start(f32[8,512]{1,0:T(8,128)S(1)} %second.8.refs_14_), channel_id=1, source_target_pairs={{0,8},{8,0},{16,24},{24,16},{1,9},{9,1},{17,25},{25,17},{2,10},{10... | collective-permute-start | bytes 49160 | tf_op jit(solution)/shard_map/scalars/ppermute | solution.py:504
  82.0 4.3 %collective-permute-start.27 = (f32[8,512]{1,0:T(8,128)S(1)}, f32[8,512]{1,0:T(8,128)S(1)}, u32[]{:S(2)}, u32[]{:S(2)}) collective-permute-start(f32[8,512]{1,0:T(8,128)S(1)} %second.8.refs_14_), channel_id=1, source_target_pairs={{0,16},{8,24},{16,0},{24,8},{1,17},{9,25},{17,1},{25,9},{2,18},{10... | collective-permute-start | bytes 49160 | tf_op jit(solution)/shard_map/scalars/ppermute | solution.py:504
  83.9 3.9 %collective-permute-start.28 = (f32[8,512]{1,0:T(8,128)S(1)}, f32[8,512]{1,0:T(8,128)S(1)}, u32[]{:S(2)}, u32[]{:S(2)}) collective-permute-start(f32[8,512]{1,0:T(8,128)S(1)} %second.8.refs_14_), channel_id=1, source_target_pairs={{0,24},{8,16},{16,8},{24,0},{1,25},{9,17},{17,9},{25,1},{2,26},{10... | collective-permute-start | bytes 49160 | tf_op jit(solution)/shard_map/scalars/ppermute | solution.py:504

commit v3 on v1

--- a/solution.py
+++ b/solution.py
@@ -61,15 +61,27 @@
     return side, (here + side >= 0) & (here + side < groups)
 
 
-def add_inner(dims, s, shift_ref, acc, left, right, wb, before_term=lambda t: None):
+def add_pairs(dims, turn, shift_ref, acc, left, right, own, halos, arrived=None, skip_own=False):
     sectors, terms = dims[:2]
+    s = sector_at(turn, sectors)
     for t in range(terms):
-        before_term(t)
+        if arrived is not None:
+            arrived(t)
         partner = s + shift_ref[t]
-
-        @pl.when((partner >= 0) & (partner < sectors))
+        inside = (partner >= 0) & (partner < sectors)
+        if skip_own:
+            inside &= shift_ref[t] != 0
+
+        @pl.when(inside)
         def _():
-            add_pair(acc, left.at[s, t], right.at[s, t], wb.at[partner])
+            add_pair(acc, left.at[t], right.at[t], own.at[partner])
+
+        for block, halo in zip(halos, halos_at(turn, sectors)):
+            side, there = halo_side(halo)
+
+            @pl.when((shift_ref[t] == side) & there)
+            def _():
+                add_pair(acc, left.at[t], right.at[t], block)
 
 
 def place_rows(dims, wb, pieces):
@@ -78,23 +90,6 @@
     for far in range(low):
         for step in range(count):
             wb[pl.ds(row_of(step, far), span), :] = pieces[far][step]
-
-
-def add_outer(dims, turn, gathered, shift_ref, acc, left, right, blocks, wb):
-    sectors, terms = dims[:2]
-    s = sector_at(turn, sectors)
-    for block, halo in zip(blocks, halos_at(turn, sectors)):
-        if gathered:
-            place_rows(dims, wb, [block.at[0], block.at[1]])
-            held = wb
-        else:
-            held = block
-        side, there = halo_side(halo)
-        for t in range(terms):
-
-            @pl.when((shift_ref[t] == side) & there)
-            def _():
-                add_pair(acc, left.at[s, t], right.at[s, t], held)
 
 
 def cut(dims, acc, send_ref, keep_ref):
@@ -156,35 +151,32 @@
                     other_edge[part, :] = value
 
 
-def load_kernel(
-    dims, wb, shift_hbm, size_hbm, left_hbm, right_hbm, vector_hbm,
-    acc, left, right, start, shift_ref, size_ref, sems, row_sems, scalar_sems,
-):
+def load_kernel(dims, turn, own, *refs):
     sectors, terms, size, count, low, span = dims
+    blocks, refs = refs[: len(halos_at(turn, sectors))], refs[len(halos_at(turn, sectors)) :]
+    shift_hbm, size_hbm, left_hbm, right_hbm, vector_hbm, send_ref, keep_ref, left, right, *refs = refs
+    start, refs = (refs[0], refs[1:]) if turn == 0 else (None, refs)
+    acc, shift_ref, size_ref, sems, row_sems, scalar_sems = refs
+    s = sector_at(turn, sectors)
     scalars = [
         pltpu.make_async_copy(shift_hbm, shift_ref, scalar_sems.at[0]),
         pltpu.make_async_copy(size_hbm, size_ref, scalar_sems.at[1]),
     ]
+    copies = [
+        [
+            pltpu.make_async_copy(hbm.at[s, t], vmem.at[t], sems.at[k, t])
+            for k, (hbm, vmem) in enumerate(((left_hbm, left), (right_hbm, right)))
+        ]
+        for t in range(terms)
+    ]
+    first = row_finder(count, low, span)(0, 0)
+    rows = [
+        pltpu.make_async_copy(vector_hbm.at[e, pl.ds(first, span), :], start.at[e], row_sems.at[e])
+        for e in range(sectors if turn == 0 else 0)
+    ]
     for copy in scalars:
         copy.start()
-    first = row_finder(count, low, span)(0, 0)
-    rows = [
-        pltpu.make_async_copy(vector_hbm.at[s, pl.ds(first, span), :], start.at[s], row_sems.at[s])
-        for s in range(sectors)
-    ]
-    copies = {
-        (turn, t): [
-            pltpu.make_async_copy(
-                hbm.at[sector_at(turn, sectors), t],
-                vmem.at[sector_at(turn, sectors), t],
-                sems.at[k, turn, t],
-            )
-            for k, (hbm, vmem) in enumerate(((left_hbm, left), (right_hbm, right)))
-        ]
-        for turn in range(sectors)
-        for t in range(terms)
-    }
-    for pair in copies.values():
+    for pair in copies:
         for copy in pair:
             copy.start()
     for copy in rows:
@@ -194,77 +186,67 @@
         copy.wait()
 
     def arrived(t):
-        for copy in copies[0, t]:
+        for copy in copies[t]:
             copy.wait()
 
-    add_inner(dims, sector_at(0, sectors), shift_ref, acc, left, right, wb, arrived)
-    for s in range(sectors):
-        rows[s].wait()
-        live = live_tile((span, size), first, size_ref[s])
-        start[s] = jnp.where(live, start[s], 0.0)
-    for turn in range(1, sectors):
-        for t in range(terms):
-            for copy in copies[turn, t]:
-                copy.wait()
-
-
-def outer_kernel(dims, gathered, shift_ref, acc_ref, left, right, *refs):
-    blocks, (send_ref, keep_ref, acc, wb) = refs[:-4], refs[-4:]
-    acc[...] = acc_ref[...]
-    add_outer(dims, 0, gathered, shift_ref, acc, left, right, blocks, wb)
+    add_pairs(dims, turn, shift_ref, acc, left, right, own, blocks, arrived)
     cut(dims, acc, send_ref, keep_ref)
+    for e, copy in enumerate(rows):
+        copy.wait()
+        live = live_tile((span, size), first, size_ref[e])
+        start[e] = jnp.where(live, start[e], 0.0)
 
 
 def self_kernel(dims, shift_ref, left, right, mine, theirs, acc, own):
-    s = sector_at(0, dims[0])
     acc[...] = jnp.zeros_like(acc)
     place_rows(dims, own, [mine, theirs])
     for t in range(dims[1]):
 
         @pl.when(shift_ref[t] == 0)
         def _():
-            add_pair(acc, left.at[s, t], right.at[s, t], own)
-
-
-def inner_kernel(dims, shift_ref, acc_ref, first_block, left, right, *refs):
-    sectors, terms = dims[:2]
-    pieces, (acc, own) = refs[:-2], refs[-2:]
+            add_pair(acc, left.at[t], right.at[t], own)
+
+
+def rest_kernel(dims, shift_ref, acc_ref, first_block, left, right, *refs):
+    sectors = dims[0]
+    pieces, refs = refs[: 2 * sectors - 2], refs[2 * sectors - 2 :]
+    halos, (send_ref, keep_ref, own, acc, wb) = refs[:-5], refs[-5:]
     acc[...] = acc_ref[...]
-    s = sector_at(0, sectors)
-    own[s] = first_block[...]
+    own[sector_at(0, sectors)] = first_block[...]
     for turn in range(1, sectors):
         place_rows(dims, own.at[sector_at(turn, sectors)], pieces[2 * turn - 2 : 2 * turn])
-    for t in range(terms):
-        partner = s + shift_ref[t]
-
-        @pl.when((shift_ref[t] != 0) & (partner >= 0) & (partner < sectors))
-        def _():
-            add_pair(acc, left.at[s, t], right.at[s, t], own.at[partner])
-
-
-def full_kernel(dims, turn, gathered, shift_ref, own, left, right, *refs):
-    blocks, (send_ref, keep_ref, acc, wb) = refs[:-4], refs[-4:]
+    for n, halo in enumerate(halos):
+        place_rows(dims, wb.at[n], [halo.at[0], halo.at[1]])
+    blocks = [wb.at[n] for n in range(len(halos))]
+    add_pairs(dims, 0, shift_ref, acc, left, right, own, blocks, skip_own=True)
+    cut(dims, acc, send_ref, keep_ref)
+
+
+def full_kernel(dims, turn, shift_ref, own, left, right, *refs):
+    halos, (send_ref, keep_ref, acc, wb) = refs[:-4], refs[-4:]
     acc[...] = jnp.zeros_like(acc)
-    add_inner(dims, sector_at(turn, dims[0]), shift_ref, acc, left, right, own)
-    add_outer(dims, turn, gathered, shift_ref, acc, left, right, blocks, wb)
+    for n, halo in enumerate(halos):
+        place_rows(dims, wb.at[n], [halo.at[0], halo.at[1]])
+    blocks = [wb.at[n] for n in range(len(halos))]
+    add_pairs(dims, turn, shift_ref, acc, left, right, own, blocks)
     cut(dims, acc, send_ref, keep_ref)
 
 
-def sums_kernel(dims, size_ref, vector_ref, wb, sums):
-    sectors, size = dims[0], dims[2]
+def sums_kernel(dims, turn, size_ref, vector_ref, block, sums):
+    size = dims[2]
+    s = sector_at(turn, dims[0])
     sums[...] = jnp.zeros_like(sums)
     tile = min(64, size)
-    for s in range(sectors):
-
-        @pl.loop(0, size // tile)
-        def _(n):
-            first = pl.multiple_of(n * tile, tile)
-            rows = pl.ds(first, tile)
-            live = live_tile((tile, size), first, size_ref[s])
-            start = jnp.where(live, vector_ref[s, rows, :], 0.0)
-            shifted = wb[s, rows, :].astype(jnp.float32)
-            for k, term in enumerate((shifted * shifted, shifted * start, start * start)):
-                sums[k : k + 1, :] += jnp.sum(term, 0, keepdims=True)
+
+    @pl.loop(0, size // tile)
+    def _(n):
+        first = pl.multiple_of(n * tile, tile)
+        rows = pl.ds(first, tile)
+        live = live_tile((tile, size), first, size_ref[s])
+        start = jnp.where(live, vector_ref[s, rows, :], 0.0)
+        shifted = (block[rows, :] if turn == 0 else block[s, rows, :]).astype(jnp.float32)
+        for k, term in enumerate((shifted * shifted, shifted * start, start * start)):
+            sums[k : k + 1, :] += jnp.sum(term, 0, keepdims=True)
 
 
 def shift_kernel(dims, turn, scale, size_ref, start, left_row, right_row, *refs):
@@ -376,26 +358,6 @@
         got = {k: lax.ppermute(held, "term", pairs_high(ranks, low, k)) for k in hops}
         return jnp.concatenate([held] + [got[k] for k in range(1, count)])
 
-    def first_cut(acc, halos, gathered):
-        return call(
-            functools.partial(outer_kernel, dims, gathered),
-            cut_shapes,
-            (sector_shifts,),
-            (acc, left, right, *[halos[h] for h in halos_at(0, sectors)]),
-            scratch=[square, square_low],
-            flops=terms * pair_flops // 3,
-        )
-
-    def later_cut(turn, own, halos, gathered):
-        return call(
-            functools.partial(full_kernel, dims, turn, gathered),
-            cut_shapes,
-            (sector_shifts,),
-            (own, left, right, *[halos[h] for h in halos_at(turn, sectors)]),
-            scratch=[square, square_low],
-            flops=terms * pair_flops,
-        )
-
     with jax.named_scope("first"):
         parts = 2 if size % 256 == 0 else 1
         block = jax.ShapeDtypeStruct((size, size), jnp.bfloat16)
@@ -412,24 +374,27 @@
             ],
         )
         halos = [halo(edge, which) for which, edge in enumerate(edges)]
-        matrices = pltpu.VMEM(left_block.shape, jnp.bfloat16)
-        acc, left, right, start = call(
-            functools.partial(load_kernel, dims),
-            [square, matrices, matrices, rows],
-            (),
-            (rounded,),
-            (sector_shifts, sector_sizes, left_block, right_block, lanczos_vector),
-            [
-                pltpu.SMEM((terms,), jnp.int32),
-                pltpu.SMEM((sectors,), jnp.int32),
-                pltpu.SemaphoreType.DMA((2, sectors, terms)),
-                pltpu.SemaphoreType.DMA((sectors,)),
-                pltpu.SemaphoreType.DMA((2,)),
-            ],
-            terms * pair_flops,
-        )
-        cuts = [first_cut(acc, halos, False)]
-        cuts += [later_cut(turn, rounded, halos, False) for turn in turns[1:]]
+        matrices = pltpu.VMEM((terms, size, size), jnp.bfloat16)
+        cuts, left, right = [], [None] * sectors, [None] * sectors
+        for turn in turns:
+            send, keep, left[turn], right[turn], *more = call(
+                functools.partial(load_kernel, dims, turn),
+                [*cut_shapes, matrices, matrices] + ([rows] if turn == 0 else []),
+                (),
+                (rounded, *[halos[h] for h in halos_at(turn, sectors)]),
+                (sector_shifts, sector_sizes, left_block, right_block, lanczos_vector),
+                [
+                    square,
+                    pltpu.SMEM((terms,), jnp.int32),
+                    pltpu.SMEM((sectors,), jnp.int32),
+                    pltpu.SemaphoreType.DMA((2, terms)),
+                    pltpu.SemaphoreType.DMA((sectors,)),
+                    pltpu.SemaphoreType.DMA((2,)),
+                ],
+                terms * pair_flops,
+            )
+            cuts.append((send, keep))
+            start = more[0] if turn == 0 else start
         totals = [low_sum(*c) for c in cuts]
 
     with jax.named_scope("gather"):
@@ -446,37 +411,61 @@
             mine = gather_high(held[None])
             theirs = lax.ppermute(mine, "term", pairs_low(ranks)) if low > 1 else mine
             pieces[turn] = [mine, theirs]
+    def sector_sums(turn, block):
+        return call(
+            functools.partial(sums_kernel, dims, turn),
+            [jax.ShapeDtypeStruct((8, size), jnp.float32)],
+            (sector_sizes,),
+            (lanczos_vector, block),
+            flops=1,
+        )[0]
+
     with jax.named_scope("second"):
         acc, block = call(
             functools.partial(self_kernel, dims),
             [square, square_low],
             (sector_shifts,),
-            (left, right, *pieces[0]),
+            (left[0], right[0], *pieces[0]),
             flops=1,
         )
-        whole = after_all(jnp.stack(pieces[0]), pieces[-1][1], acc)
+        sums = [sector_sums(0, block)]
+        whole = after_all(jnp.stack(pieces[0]), pieces[-1][1], acc, sums[0])
         halos = [halo(edge, n) for n, edge in enumerate((whole, jnp.stack(pieces[-1])))]
-        acc, own = call(
-            functools.partial(inner_kernel, dims),
-            [square, pltpu.VMEM((sectors, size, size), jnp.bfloat16)],
+        *first_cut, own = call(
+            functools.partial(rest_kernel, dims),
+            [*cut_shapes, pltpu.VMEM((sectors, size, size), jnp.bfloat16)],
             (sector_shifts,),
-            (acc, block, left, right, *[piece for both in pieces[1:] for piece in both]),
-            flops=terms * pair_flops // 3,
+            (
+                acc,
+                block,
+                left[0],
+                right[0],
+                *[piece for both in pieces[1:] for piece in both],
+                *[halos[h] for h in halos_at(0, sectors)],
+            ),
+            scratch=[square, pltpu.VMEM((2, size, size), jnp.bfloat16)],
+            flops=terms * pair_flops // 2,
         )
-        cuts = [first_cut(acc, halos, True)]
-        (sums,) = call(
-            functools.partial(sums_kernel, dims),
-            [jax.ShapeDtypeStruct((8, size), jnp.float32)],
-            (sector_sizes,),
-            (lanczos_vector, after_all(own, *cuts[0])),
-        )
-        own = after_all(own, sums)
-        cuts += [later_cut(turn, own, halos, True) for turn in turns[1:]]
+        cuts = [first_cut]
+        for turn in turns[1:]:
+            sums.append(sector_sums(turn, after_all(own, *first_cut)))
+        own = after_all(own, *sums)
+        for turn in turns[1:]:
+            cuts.append(
+                call(
+                    functools.partial(full_kernel, dims, turn),
+                    cut_shapes,
+                    (sector_shifts,),
+                    (own, left[turn], right[turn], *[halos[h] for h in halos_at(turn, sectors)]),
+                    scratch=[square, pltpu.VMEM((2, size, size), jnp.bfloat16)],
+                    flops=terms * pair_flops,
+                )
+            )
         totals = [low_sum(*c) for c in cuts]
 
     with jax.named_scope("scalars"):
         parts = [high_parts(total) for total in totals]
-        sums = after_all(sums, totals[-1], parts[0][-1])
+        sums = after_all(sum(sums), totals[-1], parts[0][-1])
         tables, reach = [sums], 1
         while reach < groups:
             if groups & (groups - 1):

time: 87.9 us -> 86.1 us (0.980)
  waiting for transfers between devices: 25.7 us -> 22.9 us
  starting transfers between devices: 40.2 us -> 41.6 us
  Pallas kernels: 21 us -> 19.7 us
    ppermute x2, waiting for transfers between devices: 8.68 us -> 5.17 us  [on_device(): theirs = lax.ppermute(mine, 'term', pairs_low(ranks)) if low > 1 else mine]
    ppermute x4, waiting for transfers between devices: 0.01 us -> 1.78 us  [halo(): return lax.ppermute(edge, 'sector', pairs[which]) if pairs[which] else edge]
    pallas_call x12 -> x11, Pallas kernels: 21 us -> 19.7 us  [call(): pl.pallas_call(kernel, out_shape=out_shape, in_specs=[SMEM] * len(scalars...]
    ppermute x6, waiting for transfers between devices: 5.85 us -> 4.64 us  [gather_high(): lax.ppermute(held, 'term', pairs_high(ranks, low, k))]
    ppermute x2, starting transfers between devices: 1.86 us -> 2.81 us  [on_device(): theirs = lax.ppermute(mine, 'term', pairs_low(ranks)) if low > 1 else mine]
  transfers between devices with their start and end apart: 31 -> 31, of which waited for: 11 -> 13; matrix products, arithmetic and copies ran while one was open for 1% -> 1% of each run, Pallas kernels for 20% -> 19%
where the time goes in v3:
time: 86.1 us; the launch traced here: 86 us
  starting transfers between devices  41.6 us (48%)
  waiting for transfers between devices  22.9 us (27%)
  Pallas kernels  19.7 us (23%)
  between operations  0.91 us (1%)
    pallas_call x11, Pallas kernels, call(): pl.pallas_call(kernel, out_shape=out_shape, in_specs=[SMEM] * len(scalars...  19.7 us
    ppermute x12, starting transfers between devices, high_parts(): lax.ppermute(total[k].astype(jnp.bfloat16), 'term', pairs_high(ranks, low...  18 us
    ppermute x6, starting transfers between devices, gather_high(): lax.ppermute(held, 'term', pairs_high(ranks, low, k))  8.91 us
    ppermute x4, starting transfers between devices, low_sum(): lax.ppermute(send, 'term', pairs_low(ranks)).astype(jnp.float32)  7.47 us
    ppermute x12, waiting for transfers between devices, high_parts(): lax.ppermute(total[k].astype(jnp.bfloat16), 'term', pairs_high(ranks, low...  6.15 us
    ppermute x4, waiting for transfers between devices, low_sum(): lax.ppermute(send, 'term', pairs_low(ranks)).astype(jnp.float32)  5.19 us
    ppermute x2, waiting for transfers between devices, on_device(): theirs = lax.ppermute(mine, 'term', pairs_low(ranks)) if low > 1 else mine  5.17 us
    ppermute x6, waiting for transfers between devices, gather_high(): lax.ppermute(held, 'term', pairs_high(ranks, low, k))  4.64 us
  transfers between devices with their start and end apart: 31, of which 13 were waited for; matrix products, arithmetic and copies ran while one was open for 1% of the time, Pallas kernels for 19%

profile of v3, /device:TPU:0, one launch (start us, length us, event | category | flops | bytes accessed | tf_op | source)
XLA Modules:
  0.0 86.0 jit_solution(915685693266012057)
XLA Ops:
  0.6 1.6 %first.3 = (bf16[2,512,512]{2,1,0:T(8,128)(2,1)S(1)}, bf16[512,512]{1,0:T(8,128)(2,1)S(1)}, bf16[512,512]{1,0:T(8,128)(2,1)S(1)}) custom-call(s32[2]{0:T(128)} %size_ref.9, f32[2,512,512]{2,1,0:T(8,128)} %vector_ref.3), custom_call_target="tpu_custom_call" | custom-call | flops 1048576 | bytes 4096 | tf_op jit(solution)/shard_map/first/pallas_call | solution.py:303
  2.3 0.5 collective-permute-start
  2.8 0.7 collective-permute-start.5
  3.5 0.8 collective-permute-done.refs_0_
  4.3 4.3 %first.4 = (bf16[4,64,512]{2,1,0:T(8,128)(2,1)S(1)}, f32[4,64,512]{2,1,0:T(8,128)S(1)}, bf16[4,512,512]{2,1,0:T(8,128)(2,1)S(1)}, bf16[4,512,512]{2,1,0:T(8,128)(2,1)S(1)}, f32[2,64,512]{2,1,0:T(8,128)S(1)}) custom-call(bf16[2,512,512]{2,1,0:T(8,128)(2,1)S(1)} %get-tuple-element.33.own, bf16[512,512]{1,0:T(8,128)(2,1)S(1)} %collective-permute-done.refs_0_, ...), custom_call_target="tpu_custom_call" | custom-call | flops 2147483648 | bytes 8388608 | tf_op jit(solution)/shard_map/first/pallas_call | solution.py:303
  8.6 3.0 %collective-permute-start.1 = (bf16[4,64,512]{2,1,0:T(8,128)(2,1)S(1)}, bf16[4,64,512]{2,1,0:T(8,128)(2,1)S(1)}, u32[]{:S(2)}, u32[]{:S(2)}) collective-permute-start(bf16[4,64,512]{2,1,0:T(8,128)(2,1)S(1)} %get-tuple-element.37), channel_id=1, source_target_pairs={{0,1},{1,0},{2,3},{3,2},{4,5},{5,4},{6,7},{7,6},{8,9},{9,8},{10,11... | collective-permute-start | bytes 786440 | tf_op jit(solution)/shard_map/first/ppermute | solution.py:347
  11.6 3.1 %first.5 = (bf16[4,64,512]{2,1,0:T(8,128)(2,1)S(1)}, f32[4,64,512]{2,1,0:T(8,128)S(1)}, bf16[4,512,512]{2,1,0:T(8,128)(2,1)S(1)}, bf16[4,512,512]{2,1,0:T(8,128)(2,1)S(1)}) custom-call(bf16[2,512,512]{2,1,0:T(8,128)(2,1)S(1)} %get-tuple-element.33.own, bf16[512,512]{1,0:T(8,128)(2,1)S(1)} %collective-permute-done.5.refs_0_, s32[4]{0:T(128)} %shift_ref.5, ...), custom_call_target="tpu_custom_call" | custom-call | flops 2147483648 | bytes 8388608 | tf_op jit(solution)/shard_map/first/pallas_call | solution.py:303
  14.7 0.9 %collective-permute-start.6 = (bf16[4,64,512]{2,1,0:T(8,128)(2,1)S(1)}, bf16[4,64,512]{2,1,0:T(8,128)(2,1)S(1)}, u32[]{:S(2)}, u32[]{:S(2)}) collective-permute-start(bf16[4,64,512]{2,1,0:T(8,128)(2,1)S(1)} %get-tuple-element.41), channel_id=1, source_target_pairs={{0,1},{1,0},{2,3},{3,2},{4,5},{5,4},{6,7},{7,6},{8,9},{9,8},{10,11... | collective-permute-start | bytes 786440 | tf_op jit(solution)/shard_map/first/ppermute | solution.py:347
  15.6 2.1 %collective-permute-done.1 = bf16[4,64,512]{2,1,0:T(8,128)(2,1)S(1)} collective-permute-done((bf16[4,64,512]{2,1,0:T(8,128)(2,1)S(1)}, bf16[4,64,512]{2,1,0:T(8,128)(2,1)S(1)}, u32[]{:S(2)}, u32[]{:S(2)}) %collective-permute-start.1) | collective-permute-done | bytes 262176 | tf_op jit(solution)/shard_map/first/ppermute | solution.py:347
  17.8 4.6 %collective-permute-start.2 = (bf16[64,512]{1,0:T(8,128)(2,1)S(1)}, bf16[64,512]{1,0:T(8,128)(2,1)S(1)}, u32[]{:S(2)}, u32[]{:S(2)}) collective-permute-start(bf16[64,512]{1,0:T(8,128)(2,1)S(1)} %get-tuple-element.87), channel_id=1, source_target_pairs={{0,6},{1,7},{2,4},{3,5},{4,2},{5,3},{6,0},{7,1},{8,14},{9,15},{10,... | collective-permute-start | bytes 196616 | tf_op jit(solution)/shard_map/gather/ppermute | solution.py:353
  22.4 0.6 collective-permute-start.4
  23.2 3.8 %collective-permute-start.7 = (bf16[64,512]{1,0:T(8,128)(2,1)S(1)}, bf16[64,512]{1,0:T(8,128)(2,1)S(1)}, u32[]{:S(2)}, u32[]{:S(2)}) collective-permute-start(bf16[64,512]{1,0:T(8,128)(2,1)S(1)} %get-tuple-element.84), channel_id=1, source_target_pairs={{0,6},{1,7},{2,4},{3,5},{4,2},{5,3},{6,0},{7,1},{8,14},{9,15},{10,... | collective-permute-start | bytes 196616 | tf_op jit(solution)/shard_map/gather/ppermute | solution.py:353
  27.1 0.6 collective-permute-start.9
  27.7 1.2 %collective-permute-done.3.refs_2_ = bf16[64,512]{1,0:T(8,128)(2,1)S(1)} collective-permute-done((bf16[64,512]{1,0:T(8,128)(2,1)S(1)}, bf16[64,512]{1,0:T(8,128)(2,1)S(1)}, u32[]{:S(2)}, u32[]{:S(2)}) %collective-permute-start.3) | collective-permute-done | bytes 65568 | tf_op jit(solution)/shard_map/gather/ppermute | solution.py:353
  29.0 0.7 gather.2
  29.7 2.6 %collective-permute-start.12 = (bf16[1,64,512]{2,1,0:T(8,128)(2,1)S(1)}, bf16[1,64,512]{2,1,0:T(8,128)(2,1)S(1)}, u32[]{:S(2)}, u32[]{:S(2)}) collective-permute-start(bf16[1,64,512]{2,1,0:T(8,128)(2,1)S(1)} %bitcast.42), channel_id=1, source_target_pairs={{0,6},{1,7},{2,4},{3,5},{4,2},{5,3},{6,0},{7,1},{8,14},{9,15},{10,... | collective-permute-start | bytes 196616 | tf_op jit(solution)/shard_map/gather/ppermute | solution.py:358
  32.3 1.8 %collective-permute-start.10 = (bf16[1,64,512]{2,1,0:T(8,128)(2,1)S(1)}, bf16[1,64,512]{2,1,0:T(8,128)(2,1)S(1)}, u32[]{:S(2)}, u32[]{:S(2)}) collective-permute-start(bf16[1,64,512]{2,1,0:T(8,128)(2,1)S(1)} %bitcast.44), channel_id=1, source_target_pairs={{0,2},{1,3},{2,0},{3,1},{4,6},{5,7},{6,4},{7,5},{8,10},{9,11},{10,... | collective-permute-start | bytes 196616 | tf_op jit(solution)/shard_map/gather/ppermute | solution.py:358
  34.1 0.4 collective-permute-done.8.refs_2_
  34.6 0.7 gather.3
  35.3 2.3 %collective-permute-start.16 = (bf16[1,64,512]{2,1,0:T(8,128)(2,1)S(1)}, bf16[1,64,512]{2,1,0:T(8,128)(2,1)S(1)}, u32[]{:S(2)}, u32[]{:S(2)}) collective-permute-start(bf16[1,64,512]{2,1,0:T(8,128)(2,1)S(1)} %bitcast.46), channel_id=1, source_target_pairs={{0,6},{1,7},{2,4},{3,5},{4,2},{5,3},{6,0},{7,1},{8,14},{9,15},{10,... | collective-permute-start | bytes 196616 | tf_op jit(solution)/shard_map/gather/ppermute | solution.py:358
  37.6 2.2 %collective-permute-start.14 = (bf16[1,64,512]{2,1,0:T(8,128)(2,1)S(1)}, bf16[1,64,512]{2,1,0:T(8,128)(2,1)S(1)}, u32[]{:S(2)}, u32[]{:S(2)}) collective-permute-start(bf16[1,64,512]{2,1,0:T(8,128)(2,1)S(1)} %bitcast.48), channel_id=1, source_target_pairs={{0,2},{1,3},{2,0},{3,1},{4,6},{5,7},{6,4},{7,5},{8,10},{9,11},{10,... | collective-permute-start | bytes 196616 | tf_op jit(solution)/shard_map/gather/ppermute | solution.py:358
  39.7 0.5 collective-permute-done.11
  40.2 1.4 %collective-permute-start.13 = (bf16[4,64,512]{2,1,0:T(8,128)(2,1)S(1)}, bf16[4,64,512]{2,1,0:T(8,128)(2,1)S(1)}, u32[]{:S(2)}, u32[]{:S(2)}) collective-permute-start(bf16[4,64,512]{2,1,0:T(8,128)(2,1)S(1)} %get-tuple-element.81.mine), channel_id=1, source_target_pairs={{0,1},{1,0},{2,3},{3,2},{4,5},{5,4},{6,7},{7,6},{8,9},{9,8},{10,11... | collective-permute-start | bytes 786440 | tf_op jit(solution)/shard_map/gather/ppermute | solution.py:412
  41.7 0.3 collective-permute-done.16
  42.0 3.9 %collective-permute-done.15 = bf16[1,64,512]{2,1,0:T(8,128)(2,1)S(1)} collective-permute-done((bf16[1,64,512]{2,1,0:T(8,128)(2,1)S(1)}, bf16[1,64,512]{2,1,0:T(8,128)(2,1)S(1)}, u32[]{:S(2)}, u32[]{:S(2)}) %collective-permute-start.15) | collective-permute-done | bytes 65568 | tf_op jit(solution)/shard_map/gather/ppermute | solution.py:358
  45.9 1.4 %collective-permute-start.17 = (bf16[4,64,512]{2,1,0:T(8,128)(2,1)S(1)}, bf16[4,64,512]{2,1,0:T(8,128)(2,1)S(1)}, u32[]{:S(2)}, u32[]{:S(2)}) collective-permute-start(bf16[4,64,512]{2,1,0:T(8,128)(2,1)S(1)} %get-tuple-element.76.refs_0_), channel_id=1, source_target_pairs={{0,1},{1,0},{2,3},{3,2},{4,5},{5,4},{6,7},{7,6},{8,9},{9,8},{10,11... | collective-permute-start | bytes 786440 | tf_op jit(solution)/shard_map/gather/ppermute | solution.py:412
  47.3 1.9 %collective-permute-done.13.theirs = bf16[4,64,512]{2,1,0:T(8,128)(2,1)S(1)} collective-permute-done((bf16[4,64,512]{2,1,0:T(8,128)(2,1)S(1)}, bf16[4,64,512]{2,1,0:T(8,128)(2,1)S(1)}, u32[]{:S(2)}, u32[]{:S(2)}) %collective-permute-start.13) | collective-permute-done | bytes 262176 | tf_op jit(solution)/shard_map/gather/ppermute | solution.py:412
  49.2 1.4 %second.5 = (f32[512,512]{1,0:T(8,128)S(1)}, bf16[512,512]{1,0:T(8,128)(2,1)S(1)}) custom-call(s32[4]{0:T(128)S(1)} %copy-done.4, bf16[4,512,512]{2,1,0:T(8,128)(2,1)S(1)} %get-tuple-element.47.left, bf16[4,512,512]{2,1,0:T(8,128)(2,1)S(1)} %get-tuple-element.48.right, bf16[4,64,512]{2,1,0:T(8,128)(2,1)S(1)} %get-tuple-element.81.mine, ...), custom_call_target="tpu_custom_call" | custom-call | flops 1 | tf_op jit(solution)/shard_map/second/pallas_call | solution.py:303
  50.6 0.2 copy-done
  50.8 1.0 %second.6 = f32[8,512]{1,0:T(8,128)S(1)} custom-call(s32[2]{0:T(128)S(1)} %copy-done.1, f32[2,512,512]{2,1,0:T(8,128)S(1)} %copy-done, bf16[512,512]{1,0:T(8,128)(2,1)S(1)} %get-tuple-element.51.block.first_block), custom_call_target="tpu_custom_call" | custom-call | flops 1 | tf_op jit(solution)/shard_map/second/pallas_call | solution.py:303
  51.9 3.3 %collective-permute-done.17.refs_1_ = bf16[4,64,512]{2,1,0:T(8,128)(2,1)S(1)} collective-permute-done((bf16[4,64,512]{2,1,0:T(8,128)(2,1)S(1)}, bf16[4,64,512]{2,1,0:T(8,128)(2,1)S(1)}, u32[]{:S(2)}, u32[]{:S(2)}) %collective-permute-start.17) | collective-permute-done | bytes 262176 | tf_op jit(solution)/shard_map/gather/ppermute | solution.py:412
  55.2 0.9 %collective-permute-start.23 = (bf16[2,4,64,512]{3,2,1,0:T(8,128)(2,1)S(1)}, bf16[2,4,64,512]{3,2,1,0:T(8,128)(2,1)S(1)}, u32[]{:S(2)}, u32[]{:S(2)}) collective-permute-start(bf16[2,4,64,512]{3,2,1,0:T(8,128)(2,1)S(1)} %pad_maximum_fusion.1), channel_id=1, source_target_pairs={{8,16},{16,8},{9,17},{17,9},{10,18},{18,10},{11,19},{19,11},{12,20... | collective-permute-start | bytes 1572872 | tf_op jit(solution)/shard_map/second/ppermute | solution.py:342
  56.1 0.9 %collective-permute-done.18.refs_2_ = bf16[2,4,64,512]{3,2,1,0:T(8,128)(2,1)S(1)} collective-permute-done((bf16[2,4,64,512]{3,2,1,0:T(8,128)(2,1)S(1)}, bf16[2,4,64,512]{3,2,1,0:T(8,128)(2,1)S(1)}, u32[]{:S(2)}, u32[]{:S(2)}) %collective-permute-start.18) | collective-permute-done | bytes 524320 | tf_op jit(solution)/shard_map/second/ppermute | solution.py:342
  57.0 3.0 %second.7 = (bf16[4,64,512]{2,1,0:T(8,128)(2,1)S(1)}, f32[4,64,512]{2,1,0:T(8,128)S(1)}, bf16[2,512,512]{2,1,0:T(8,128)(2,1)S(1)}) custom-call(s32[4]{0:T(128)S(1)} %copy-done.4, f32[512,512]{1,0:T(8,128)S(1)} %get-tuple-element.50.acc_ref, bf16[512,512]{1,0:T(8,128)(2,1)S(1)} %get-tuple-element.51.block.first_block, ...), custom_call_target="tpu_custom_call" | custom-call | flops 1073741824 | bytes 4194304 | tf_op jit(solution)/shard_map/second/pallas_call | solution.py:303
  60.0 2.1 %collective-permute-start.19 = (bf16[4,64,512]{2,1,0:T(8,128)(2,1)S(1)}, bf16[4,64,512]{2,1,0:T(8,128)(2,1)S(1)}, u32[]{:S(2)}, u32[]{:S(2)}) collective-permute-start(bf16[4,64,512]{2,1,0:T(8,128)(2,1)S(1)} %get-tuple-element.55), channel_id=1, source_target_pairs={{0,1},{1,0},{2,3},{3,2},{4,5},{5,4},{6,7},{7,6},{8,9},{9,8},{10,11... | collective-permute-start | bytes 786440 | tf_op jit(solution)/shard_map/second/ppermute | solution.py:347
  62.1 1.0 %second.8 = f32[8,512]{1,0:T(8,128)S(1)} custom-call(s32[2]{0:T(128)S(1)} %copy-done.1, f32[2,512,512]{2,1,0:T(8,128)S(1)} %copy-done, bf16[2,512,512]{2,1,0:T(8,128)(2,1)S(1)} %get-tuple-element.58.block.own), custom_call_target="tpu_custom_call" | custom-call | flops 1 | tf_op jit(solution)/shard_map/second/pallas_call | solution.py:303
  63.1 1.5 %second.9 = (bf16[4,64,512]{2,1,0:T(8,128)(2,1)S(1)}, f32[4,64,512]{2,1,0:T(8,128)S(1)}) custom-call(s32[4]{0:T(128)S(1)} %copy-done.4, bf16[2,512,512]{2,1,0:T(8,128)(2,1)S(1)} %get-tuple-element.58.block.own, bf16[4,512,512]{2,1,0:T(8,128)(2,1)S(1)} %get-tuple-element.59.left, bf16[4,512,512]{2,1,0:T(8,128)(2,1)S(1)} %get-tuple-element.60.right, ...), custom_call_target="tpu_custom_call" | custom-call | flops 2147483648 | bytes 8388608 | tf_op jit(solution)/shard_map/second/pallas_call | solution.py:303
  64.6 1.5 %collective-permute-start.24 = (bf16[4,64,512]{2,1,0:T(8,128)(2,1)S(1)}, bf16[4,64,512]{2,1,0:T(8,128)(2,1)S(1)}, u32[]{:S(2)}, u32[]{:S(2)}) collective-permute-start(bf16[4,64,512]{2,1,0:T(8,128)(2,1)S(1)} %get-tuple-element.62), channel_id=1, source_target_pairs={{0,1},{1,0},{2,3},{3,2},{4,5},{5,4},{6,7},{7,6},{8,9},{9,8},{10,11... | collective-permute-start | bytes 786440 | tf_op jit(solution)/shard_map/second/ppermute | solution.py:347
  66.1 3.1 %collective-permute-done.19 = bf16[4,64,512]{2,1,0:T(8,128)(2,1)S(1)} collective-permute-done((bf16[4,64,512]{2,1,0:T(8,128)(2,1)S(1)}, bf16[4,64,512]{2,1,0:T(8,128)(2,1)S(1)}, u32[]{:S(2)}, u32[]{:S(2)}) %collective-permute-start.19) | collective-permute-done | bytes 262176 | tf_op jit(solution)/shard_map/second/ppermute | solution.py:347
  69.3 2.2 %collective-permute-start.20 = (bf16[64,512]{1,0:T(8,128)(2,1)S(1)}, bf16[64,512]{1,0:T(8,128)(2,1)S(1)}, u32[]{:S(2)}, u32[]{:S(2)}) collective-permute-start(bf16[64,512]{1,0:T(8,128)(2,1)S(1)} %get-tuple-element.79), channel_id=1, source_target_pairs={{0,6},{1,7},{2,4},{3,5},{4,2},{5,3},{6,0},{7,1},{8,14},{9,15},{10,... | collective-permute-start | bytes 196616 | tf_op jit(solution)/shard_map/scalars/ppermute | solution.py:353
  71.5 2.3 %collective-permute-start.22 = (bf16[64,512]{1,0:T(8,128)(2,1)S(1)}, bf16[64,512]{1,0:T(8,128)(2,1)S(1)}, u32[]{:S(2)}, u32[]{:S(2)}) collective-permute-start(bf16[64,512]{1,0:T(8,128)(2,1)S(1)} %get-tuple-element.77), channel_id=1, source_target_pairs={{0,2},{1,3},{2,0},{3,1},{4,6},{5,7},{6,4},{7,5},{8,10},{9,11},{10,... | collective-permute-start | bytes 196616 | tf_op jit(solution)/shard_map/scalars/ppermute | solution.py:353
  73.9 2.2 %collective-permute-start.25 = (bf16[64,512]{1,0:T(8,128)(2,1)S(1)}, bf16[64,512]{1,0:T(8,128)(2,1)S(1)}, u32[]{:S(2)}, u32[]{:S(2)}) collective-permute-start(bf16[64,512]{1,0:T(8,128)(2,1)S(1)} %get-tuple-element.74), channel_id=1, source_target_pairs={{0,6},{1,7},{2,4},{3,5},{4,2},{5,3},{6,0},{7,1},{8,14},{9,15},{10,... | collective-permute-start | bytes 196616 | tf_op jit(solution)/shard_map/scalars/ppermute | solution.py:353
  76.1 1.0 %collective-permute-done.22.refs_9_ = bf16[64,512]{1,0:T(8,128)(2,1)S(1)} collective-permute-done((bf16[64,512]{1,0:T(8,128)(2,1)S(1)}, bf16[64,512]{1,0:T(8,128)(2,1)S(1)}, u32[]{:S(2)}, u32[]{:S(2)}) %collective-permute-start.22) | collective-permute-done | bytes 65568 | tf_op jit(solution)/shard_map/scalars/ppermute | solution.py:353
  77.1 1.6 %collective-permute-start.27 = (bf16[64,512]{1,0:T(8,128)(2,1)S(1)}, bf16[64,512]{1,0:T(8,128)(2,1)S(1)}, u32[]{:S(2)}, u32[]{:S(2)}) collective-permute-start(bf16[64,512]{1,0:T(8,128)(2,1)S(1)} %get-tuple-element.72), channel_id=1, source_target_pairs={{0,2},{1,3},{2,0},{3,1},{4,6},{5,7},{6,4},{7,5},{8,10},{9,11},{10,... | collective-permute-start | bytes 196616 | tf_op jit(solution)/shard_map/scalars/ppermute | solution.py:353
  78.7 0.8 collective-permute-start.28
  79.5 1.4 %collective-permute-start.29 = (f32[8,512]{1,0:T(8,128)S(1)}, f32[8,512]{1,0:T(8,128)S(1)}, u32[]{:S(2)}, u32[]{:S(2)}) collective-permute-start(f32[8,512]{1,0:T(8,128)S(1)} %add.19.refs_14_), channel_id=1, source_target_pairs={{0,16},{8,24},{16,0},{24,8},{1,17},{9,25},{17,1},{25,9},{2,18},{10... | collective-permute-start | bytes 49160 | tf_op jit(solution)/shard_map/scalars/ppermute | solution.py:476
  81.0 3.5 %collective-permute-done.26.refs_12_ = bf16[64,512]{1,0:T(8,128)(2,1)S(1)} collective-permute-done((bf16[64,512]{1,0:T(8,128)(2,1)S(1)}, bf16[64,512]{1,0:T(8,128)(2,1)S(1)}, u32[]{:S(2)}, u32[]{:S(2)}) %collective-permute-start.26) | collective-permute-done | bytes 65568 | tf_op jit(solution)/shard_map/scalars/ppermute | solution.py:353
  84.5 1.5 %scalars.1 = (f32[2,64,512]{2,1,0:T(8,128)}, f32[2,64,512]{2,1,0:T(8,128)}) custom-call(s32[2]{0:T(128)S(1)} %copy-done.1, f32[2,64,512]{2,1,0:T(8,128)S(1)} %get-tuple-element.35.start, f32[64,512]{1,0:T(8,128)S(1)} %get-tuple-element.38.refs_0_, f32[64,512]{1,0:T(8,128)S(1)} %get-tuple-element.42.refs_1_, f32[64,512]{1,0:T(8,128)S(1)} %get-tuple-element.43.refs_2_, ...), custom_call_target="tpu_custom_call" | custom-call | flops 1048576 | bytes 4096 | tf_op jit(solution)/shard_map/scalars/pallas_call | solution.py:303
  (52 shorter events, 1.0 us)
Async XLA Ops:
  2.3 2.1 %collective-permute-start = (bf16[512,512]{1,0:T(8,128)(2,1)S(1)}, bf16[512,512]{1,0:T(8,128)(2,1)S(1)}, u32[]{:S(2)}, u32[]{:S(2)}) collective-permute-start(bf16[512,512]{1,0:T(8,128)(2,1)S(1)} %get-tuple-element.34), channel_id=1, source_target_pairs={{0,8},{8,0},{16,24},{24,16},{1,9},{9,1},{17,25},{25,17},{2,10},{10... | collective-permute-start | bytes 1572872 | tf_op jit(solution)/shard_map/first/ppermute | solution.py:342
  2.8 8.8 %collective-permute-start.5 = (bf16[512,512]{1,0:T(8,128)(2,1)S(1)}, bf16[512,512]{1,0:T(8,128)(2,1)S(1)}, u32[]{:S(2)}, u32[]{:S(2)}) collective-permute-start(bf16[512,512]{1,0:T(8,128)(2,1)S(1)} %get-tuple-element.39), channel_id=1, source_target_pairs={{8,16},{16,8},{9,17},{17,9},{10,18},{18,10},{11,19},{19,11},{12,20... | collective-permute-start | bytes 1572872 | tf_op jit(solution)/shard_map/first/ppermute | solution.py:342
  8.6 9.0 %collective-permute-start.1 = (bf16[4,64,512]{2,1,0:T(8,128)(2,1)S(1)}, bf16[4,64,512]{2,1,0:T(8,128)(2,1)S(1)}, u32[]{:S(2)}, u32[]{:S(2)}) collective-permute-start(bf16[4,64,512]{2,1,0:T(8,128)(2,1)S(1)} %get-tuple-element.37), channel_id=1, source_target_pairs={{0,1},{1,0},{2,3},{3,2},{4,5},{5,4},{6,7},{7,6},{8,9},{9,8},{10,11... | collective-permute-start | bytes 786440 | tf_op jit(solution)/shard_map/first/ppermute | solution.py:347
  14.7 8.4 %collective-permute-start.6 = (bf16[4,64,512]{2,1,0:T(8,128)(2,1)S(1)}, bf16[4,64,512]{2,1,0:T(8,128)(2,1)S(1)}, u32[]{:S(2)}, u32[]{:S(2)}) collective-permute-start(bf16[4,64,512]{2,1,0:T(8,128)(2,1)S(1)} %get-tuple-element.41), channel_id=1, source_target_pairs={{0,1},{1,0},{2,3},{3,2},{4,5},{5,4},{6,7},{7,6},{8,9},{9,8},{10,11... | collective-permute-start | bytes 786440 | tf_op jit(solution)/shard_map/first/ppermute | solution.py:347
  17.7 11.3 %copy-start.1 = (s32[2]{0:T(128)S(1)}, s32[2]{0:T(128)}, u32[]{:S(2)}) copy-start(s32[2]{0:T(128)} %size_ref.9) | copy-start | bytes 28
  17.7 11.3 %copy-start.2 = (f32[2,512]{1,0:T(2,128)S(1)}, f32[2,512]{1,0:T(2,128)}, u32[]{:S(2)}) copy-start(f32[2,512]{1,0:T(2,128)} %left_row.3) | copy-start | bytes 12292
  17.7 11.3 %copy-start.3 = (f32[2,512]{1,0:T(2,128)S(1)}, f32[2,512]{1,0:T(2,128)}, u32[]{:S(2)}) copy-start(f32[2,512]{1,0:T(2,128)} %right_row.3) | copy-start | bytes 12292
  17.8 9.3 %collective-permute-start.2 = (bf16[64,512]{1,0:T(8,128)(2,1)S(1)}, bf16[64,512]{1,0:T(8,128)(2,1)S(1)}, u32[]{:S(2)}, u32[]{:S(2)}) collective-permute-start(bf16[64,512]{1,0:T(8,128)(2,1)S(1)} %get-tuple-element.87), channel_id=1, source_target_pairs={{0,6},{1,7},{2,4},{3,5},{4,2},{5,3},{6,0},{7,1},{8,14},{9,15},{10,... | collective-permute-start | bytes 196616 | tf_op jit(solution)/shard_map/gather/ppermute | solution.py:353
  22.4 6.5 %collective-permute-start.3 = (bf16[64,512]{1,0:T(8,128)(2,1)S(1)}, bf16[64,512]{1,0:T(8,128)(2,1)S(1)}, u32[]{:S(2)}, u32[]{:S(2)}) collective-permute-start(bf16[64,512]{1,0:T(8,128)(2,1)S(1)} %get-tuple-element.86), channel_id=1, source_target_pairs={{0,4},{1,5},{2,6},{3,7},{4,0},{5,1},{6,2},{7,3},{8,12},{9,13},{10,... | collective-permute-start | bytes 196616 | tf_op jit(solution)/shard_map/gather/ppermute | solution.py:353
  22.4 6.5 %collective-permute-start.4 = (bf16[64,512]{1,0:T(8,128)(2,1)S(1)}, bf16[64,512]{1,0:T(8,128)(2,1)S(1)}, u32[]{:S(2)}, u32[]{:S(2)}) collective-permute-start(bf16[64,512]{1,0:T(8,128)(2,1)S(1)} %get-tuple-element.85), channel_id=1, source_target_pairs={{0,2},{1,3},{2,0},{3,1},{4,6},{5,7},{6,4},{7,5},{8,10},{9,11},{10,... | collective-permute-start | bytes 196616 | tf_op jit(solution)/shard_map/gather/ppermute | solution.py:353
  23.2 26.0 %copy-start.4 = (s32[4]{0:T(128)S(1)}, s32[4]{0:T(128)}, u32[]{:S(2)}) copy-start(s32[4]{0:T(128)} %shift_ref.5) | copy-start | bytes 52
  23.2 9.1 %collective-permute-start.7 = (bf16[64,512]{1,0:T(8,128)(2,1)S(1)}, bf16[64,512]{1,0:T(8,128)(2,1)S(1)}, u32[]{:S(2)}, u32[]{:S(2)}) collective-permute-start(bf16[64,512]{1,0:T(8,128)(2,1)S(1)} %get-tuple-element.84), channel_id=1, source_target_pairs={{0,6},{1,7},{2,4},{3,5},{4,2},{5,3},{6,0},{7,1},{8,14},{9,15},{10,... | collective-permute-start | bytes 196616 | tf_op jit(solution)/shard_map/gather/ppermute | solution.py:353
  27.0 7.5 %collective-permute-start.8 = (bf16[64,512]{1,0:T(8,128)(2,1)S(1)}, bf16[64,512]{1,0:T(8,128)(2,1)S(1)}, u32[]{:S(2)}, u32[]{:S(2)}) collective-permute-start(bf16[64,512]{1,0:T(8,128)(2,1)S(1)} %get-tuple-element.83), channel_id=1, source_target_pairs={{0,4},{1,5},{2,6},{3,7},{4,0},{5,1},{6,2},{7,3},{8,12},{9,13},{10,... | collective-permute-start | bytes 196616 | tf_op jit(solution)/shard_map/gather/ppermute | solution.py:353
  27.1 7.5 %collective-permute-start.9 = (bf16[64,512]{1,0:T(8,128)(2,1)S(1)}, bf16[64,512]{1,0:T(8,128)(2,1)S(1)}, u32[]{:S(2)}, u32[]{:S(2)}) collective-permute-start(bf16[64,512]{1,0:T(8,128)(2,1)S(1)} %get-tuple-element.82), channel_id=1, source_target_pairs={{0,2},{1,3},{2,0},{3,1},{4,6},{5,7},{6,4},{7,5},{8,10},{9,11},{10,... | collective-permute-start | bytes 196616 | tf_op jit(solution)/shard_map/gather/ppermute | solution.py:353
  29.7 7.9 %collective-permute-start.12 = (bf16[1,64,512]{2,1,0:T(8,128)(2,1)S(1)}, bf16[1,64,512]{2,1,0:T(8,128)(2,1)S(1)}, u32[]{:S(2)}, u32[]{:S(2)}) collective-permute-start(bf16[1,64,512]{2,1,0:T(8,128)(2,1)S(1)} %bitcast.42), channel_id=1, source_target_pairs={{0,6},{1,7},{2,4},{3,5},{4,2},{5,3},{6,0},{7,1},{8,14},{9,15},{10,... | collective-permute-start | bytes 196616 | tf_op jit(solution)/shard_map/gather/ppermute | solution.py:358
  32.3 7.9 %collective-permute-start.11 = (bf16[1,64,512]{2,1,0:T(8,128)(2,1)S(1)}, bf16[1,64,512]{2,1,0:T(8,128)(2,1)S(1)}, u32[]{:S(2)}, u32[]{:S(2)}) collective-permute-start(bf16[1,64,512]{2,1,0:T(8,128)(2,1)S(1)} %bitcast.43), channel_id=1, source_target_pairs={{0,4},{1,5},{2,6},{3,7},{4,0},{5,1},{6,2},{7,3},{8,12},{9,13},{10,... | collective-permute-start | bytes 196616 | tf_op jit(solution)/shard_map/gather/ppermute | solution.py:358
  32.3 7.9 %collective-permute-start.10 = (bf16[1,64,512]{2,1,0:T(8,128)(2,1)S(1)}, bf16[1,64,512]{2,1,0:T(8,128)(2,1)S(1)}, u32[]{:S(2)}, u32[]{:S(2)}) collective-permute-start(bf16[1,64,512]{2,1,0:T(8,128)(2,1)S(1)} %bitcast.44), channel_id=1, source_target_pairs={{0,2},{1,3},{2,0},{3,1},{4,6},{5,7},{6,4},{7,5},{8,10},{9,11},{10,... | collective-permute-start | bytes 196616 | tf_op jit(solution)/shard_map/gather/ppermute | solution.py:358
  35.3 6.7 %collective-permute-start.16 = (bf16[1,64,512]{2,1,0:T(8,128)(2,1)S(1)}, bf16[1,64,512]{2,1,0:T(8,128)(2,1)S(1)}, u32[]{:S(2)}, u32[]{:S(2)}) collective-permute-start(bf16[1,64,512]{2,1,0:T(8,128)(2,1)S(1)} %bitcast.46), channel_id=1, source_target_pairs={{0,6},{1,7},{2,4},{3,5},{4,2},{5,3},{6,0},{7,1},{8,14},{9,15},{10,... | collective-permute-start | bytes 196616 | tf_op jit(solution)/shard_map/gather/ppermute | solution.py:358
  37.6 8.3 %collective-permute-start.15 = (bf16[1,64,512]{2,1,0:T(8,128)(2,1)S(1)}, bf16[1,64,512]{2,1,0:T(8,128)(2,1)S(1)}, u32[]{:S(2)}, u32[]{:S(2)}) collective-permute-start(bf16[1,64,512]{2,1,0:T(8,128)(2,1)S(1)} %bitcast.47), channel_id=1, source_target_pairs={{0,4},{1,5},{2,6},{3,7},{4,0},{5,1},{6,2},{7,3},{8,12},{9,13},{10,... | collective-permute-start | bytes 196616 | tf_op jit(solution)/shard_map/gather/ppermute | solution.py:358
  37.6 8.3 %collective-permute-start.14 = (bf16[1,64,512]{2,1,0:T(8,128)(2,1)S(1)}, bf16[1,64,512]{2,1,0:T(8,128)(2,1)S(1)}, u32[]{:S(2)}, u32[]{:S(2)}) collective-permute-start(bf16[1,64,512]{2,1,0:T(8,128)(2,1)S(1)} %bitcast.48), channel_id=1, source_target_pairs={{0,2},{1,3},{2,0},{3,1},{4,6},{5,7},{6,4},{7,5},{8,10},{9,11},{10,... | collective-permute-start | bytes 196616 | tf_op jit(solution)/shard_map/gather/ppermute | solution.py:358
  40.2 8.9 %collective-permute-start.13 = (bf16[4,64,512]{2,1,0:T(8,128)(2,1)S(1)}, bf16[4,64,512]{2,1,0:T(8,128)(2,1)S(1)}, u32[]{:S(2)}, u32[]{:S(2)}) collective-permute-start(bf16[4,64,512]{2,1,0:T(8,128)(2,1)S(1)} %get-tuple-element.81.mine), channel_id=1, source_target_pairs={{0,1},{1,0},{2,3},{3,2},{4,5},{5,4},{6,7},{7,6},{8,9},{9,8},{10,11... | collective-permute-start | bytes 786440 | tf_op jit(solution)/shard_map/gather/ppermute | solution.py:412
  45.9 9.2 %collective-permute-start.17 = (bf16[4,64,512]{2,1,0:T(8,128)(2,1)S(1)}, bf16[4,64,512]{2,1,0:T(8,128)(2,1)S(1)}, u32[]{:S(2)}, u32[]{:S(2)}) collective-permute-start(bf16[4,64,512]{2,1,0:T(8,128)(2,1)S(1)} %get-tuple-element.76.refs_0_), channel_id=1, source_target_pairs={{0,1},{1,0},{2,3},{3,2},{4,5},{5,4},{6,7},{7,6},{8,9},{9,8},{10,11... | collective-permute-start | bytes 786440 | tf_op jit(solution)/shard_map/gather/ppermute | solution.py:412
  49.2 1.6 %copy-start = (f32[2,512,512]{2,1,0:T(8,128)S(1)}, f32[2,512,512]{2,1,0:T(8,128)}, u32[]{:S(2)}) copy-start(f32[2,512,512]{2,1,0:T(8,128)} %vector_ref.3) | copy-start | bytes 6291460
  55.1 1.9 %collective-permute-start.18 = (bf16[2,4,64,512]{3,2,1,0:T(8,128)(2,1)S(1)}, bf16[2,4,64,512]{3,2,1,0:T(8,128)(2,1)S(1)}, u32[]{:S(2)}, u32[]{:S(2)}) collective-permute-start(bf16[2,4,64,512]{3,2,1,0:T(8,128)(2,1)S(1)} %pad_maximum_fusion), channel_id=1, source_target_pairs={{0,8},{8,0},{16,24},{24,16},{1,9},{9,1},{17,25},{25,17},{2,10},{10... | collective-permute-start | bytes 1572872 | tf_op jit(solution)/shard_map/second/ppermute | solution.py:342
  55.2 7.9 %collective-permute-start.23 = (bf16[2,4,64,512]{3,2,1,0:T(8,128)(2,1)S(1)}, bf16[2,4,64,512]{3,2,1,0:T(8,128)(2,1)S(1)}, u32[]{:S(2)}, u32[]{:S(2)}) collective-permute-start(bf16[2,4,64,512]{3,2,1,0:T(8,128)(2,1)S(1)} %pad_maximum_fusion.1), channel_id=1, source_target_pairs={{8,16},{16,8},{9,17},{17,9},{10,18},{18,10},{11,19},{19,11},{12,20... | collective-permute-start | bytes 1572872 | tf_op jit(solution)/shard_map/second/ppermute | solution.py:342
  60.0 9.2 %collective-permute-start.19 = (bf16[4,64,512]{2,1,0:T(8,128)(2,1)S(1)}, bf16[4,64,512]{2,1,0:T(8,128)(2,1)S(1)}, u32[]{:S(2)}, u32[]{:S(2)}) collective-permute-start(bf16[4,64,512]{2,1,0:T(8,128)(2,1)S(1)} %get-tuple-element.55), channel_id=1, source_target_pairs={{0,1},{1,0},{2,3},{3,2},{4,5},{5,4},{6,7},{7,6},{8,9},{9,8},{10,11... | collective-permute-start | bytes 786440 | tf_op jit(solution)/shard_map/second/ppermute | solution.py:347
  64.6 9.1 %collective-permute-start.24 = (bf16[4,64,512]{2,1,0:T(8,128)(2,1)S(1)}, bf16[4,64,512]{2,1,0:T(8,128)(2,1)S(1)}, u32[]{:S(2)}, u32[]{:S(2)}) collective-permute-start(bf16[4,64,512]{2,1,0:T(8,128)(2,1)S(1)} %get-tuple-element.62), channel_id=1, source_target_pairs={{0,1},{1,0},{2,3},{3,2},{4,5},{5,4},{6,7},{7,6},{8,9},{9,8},{10,11... | collective-permute-start | bytes 786440 | tf_op jit(solution)/shard_map/second/ppermute | solution.py:347
  69.3 9.4 %collective-permute-start.20 = (bf16[64,512]{1,0:T(8,128)(2,1)S(1)}, bf16[64,512]{1,0:T(8,128)(2,1)S(1)}, u32[]{:S(2)}, u32[]{:S(2)}) collective-permute-start(bf16[64,512]{1,0:T(8,128)(2,1)S(1)} %get-tuple-element.79), channel_id=1, source_target_pairs={{0,6},{1,7},{2,4},{3,5},{4,2},{5,3},{6,0},{7,1},{8,14},{9,15},{10,... | collective-permute-start | bytes 196616 | tf_op jit(solution)/shard_map/scalars/ppermute | solution.py:353
  71.5 8.0 %collective-permute-start.21 = (bf16[64,512]{1,0:T(8,128)(2,1)S(1)}, bf16[64,512]{1,0:T(8,128)(2,1)S(1)}, u32[]{:S(2)}, u32[]{:S(2)}) collective-permute-start(bf16[64,512]{1,0:T(8,128)(2,1)S(1)} %get-tuple-element.78), channel_id=1, source_target_pairs={{0,4},{1,5},{2,6},{3,7},{4,0},{5,1},{6,2},{7,3},{8,12},{9,13},{10,... | collective-permute-start | bytes 196616 | tf_op jit(solution)/shard_map/scalars/ppermute | solution.py:353
  71.5 5.6 %collective-permute-start.22 = (bf16[64,512]{1,0:T(8,128)(2,1)S(1)}, bf16[64,512]{1,0:T(8,128)(2,1)S(1)}, u32[]{:S(2)}, u32[]{:S(2)}) collective-permute-start(bf16[64,512]{1,0:T(8,128)(2,1)S(1)} %get-tuple-element.77), channel_id=1, source_target_pairs={{0,2},{1,3},{2,0},{3,1},{4,6},{5,7},{6,4},{7,5},{8,10},{9,11},{10,... | collective-permute-start | bytes 196616 | tf_op jit(solution)/shard_map/scalars/ppermute | solution.py:353
  73.9 6.9 %collective-permute-start.25 = (bf16[64,512]{1,0:T(8,128)(2,1)S(1)}, bf16[64,512]{1,0:T(8,128)(2,1)S(1)}, u32[]{:S(2)}, u32[]{:S(2)}) collective-permute-start(bf16[64,512]{1,0:T(8,128)(2,1)S(1)} %get-tuple-element.74), channel_id=1, source_target_pairs={{0,6},{1,7},{2,4},{3,5},{4,2},{5,3},{6,0},{7,1},{8,14},{9,15},{10,... | collective-permute-start | bytes 196616 | tf_op jit(solution)/shard_map/scalars/ppermute | solution.py:353
  76.1 8.4 %collective-permute-start.26 = (bf16[64,512]{1,0:T(8,128)(2,1)S(1)}, bf16[64,512]{1,0:T(8,128)(2,1)S(1)}, u32[]{:S(2)}, u32[]{:S(2)}) collective-permute-start(bf16[64,512]{1,0:T(8,128)(2,1)S(1)} %get-tuple-element.73), channel_id=1, source_target_pairs={{0,4},{1,5},{2,6},{3,7},{4,0},{5,1},{6,2},{7,3},{8,12},{9,13},{10,... | collective-permute-start | bytes 196616 | tf_op jit(solution)/shard_map/scalars/ppermute | solution.py:353
  77.1 7.4 %collective-permute-start.27 = (bf16[64,512]{1,0:T(8,128)(2,1)S(1)}, bf16[64,512]{1,0:T(8,128)(2,1)S(1)}, u32[]{:S(2)}, u32[]{:S(2)}) collective-permute-start(bf16[64,512]{1,0:T(8,128)(2,1)S(1)} %get-tuple-element.72), channel_id=1, source_target_pairs={{0,2},{1,3},{2,0},{3,1},{4,6},{5,7},{6,4},{7,5},{8,10},{9,11},{10,... | collective-permute-start | bytes 196616 | tf_op jit(solution)/shard_map/scalars/ppermute | solution.py:353
  78.7 5.8 %collective-permute-start.28 = (f32[8,512]{1,0:T(8,128)S(1)}, f32[8,512]{1,0:T(8,128)S(1)}, u32[]{:S(2)}, u32[]{:S(2)}) collective-permute-start(f32[8,512]{1,0:T(8,128)S(1)} %add.19.refs_14_), channel_id=1, source_target_pairs={{0,8},{8,0},{16,24},{24,16},{1,9},{9,1},{17,25},{25,17},{2,10},{10... | collective-permute-start | bytes 49160 | tf_op jit(solution)/shard_map/scalars/ppermute | solution.py:476
  79.5 5.0 %collective-permute-start.29 = (f32[8,512]{1,0:T(8,128)S(1)}, f32[8,512]{1,0:T(8,128)S(1)}, u32[]{:S(2)}, u32[]{:S(2)}) collective-permute-start(f32[8,512]{1,0:T(8,128)S(1)} %add.19.refs_14_), channel_id=1, source_target_pairs={{0,16},{8,24},{16,0},{24,8},{1,17},{9,25},{17,1},{25,9},{2,18},{10... | collective-permute-start | bytes 49160 | tf_op jit(solution)/shard_map/scalars/ppermute | solution.py:476
  80.8 3.6 %collective-permute-start.30 = (f32[8,512]{1,0:T(8,128)S(1)}, f32[8,512]{1,0:T(8,128)S(1)}, u32[]{:S(2)}, u32[]{:S(2)}) collective-permute-start(f32[8,512]{1,0:T(8,128)S(1)} %add.19.refs_14_), channel_id=1, source_target_pairs={{0,24},{8,16},{16,8},{24,0},{1,25},{9,17},{17,9},{25,1},{2,26},{10... | collective-permute-start | bytes 49160 | tf_op jit(solution)/shard_map/scalars/ppermute | solution.py:476

commit v4 on v3

--- a/solution.py
+++ b/solution.py
@@ -346,7 +346,7 @@
             return keep
         return keep + lax.ppermute(send, "term", pairs_low(ranks)).astype(jnp.float32)
 
-    hops = range(count - 1, 0, -1)
+    hops = range(1, count)
 
     def high_parts(total):
         return [total[0]] + [
@@ -465,7 +465,7 @@
 
     with jax.named_scope("scalars"):
         parts = [high_parts(total) for total in totals]
-        sums = after_all(sum(sums), totals[-1], parts[0][-1])
+        sums = after_all(sum(sums), totals[-1], parts[0][min(1, count - 1)])
         tables, reach = [sums], 1
         while reach < groups:
             if groups & (groups - 1):

time: 86.1 us -> 88.7 us (1.030)
  starting transfers between devices: 41.6 us -> 43.5 us
    ppermute x12, waiting for transfers between devices: 6.15 us -> 4.95 us  [high_parts(): lax.ppermute(total[k].astype(jnp.bfloat16), 'term', pairs_high(ranks, low...]
    ppermute x2, starting transfers between devices: 2.81 us -> 3.77 us  [on_device(): theirs = lax.ppermute(mine, 'term', pairs_low(ranks)) if low > 1 else mine]
where the time goes in v4:
time: 88.7 us; the launch traced here: 88.2 us
  starting transfers between devices  43.5 us (49%)
  waiting for transfers between devices  22.6 us (25%)
  Pallas kernels  20.2 us (23%)
  between operations  0.9 us (1%)
    pallas_call x11, Pallas kernels, call(): pl.pallas_call(kernel, out_shape=out_shape, in_specs=[SMEM] * len(scalars...  20.2 us
    ppermute x12, starting transfers between devices, high_parts(): lax.ppermute(total[k].astype(jnp.bfloat16), 'term', pairs_high(ranks, low...  18.7 us
    ppermute x6, starting transfers between devices, gather_high(): lax.ppermute(held, 'term', pairs_high(ranks, low, k))  9.7 us
    ppermute x4, starting transfers between devices, low_sum(): lax.ppermute(send, 'term', pairs_low(ranks)).astype(jnp.float32)  6.64 us
    ppermute x2, waiting for transfers between devices, on_device(): theirs = lax.ppermute(mine, 'term', pairs_low(ranks)) if low > 1 else mine  5.59 us
    ppermute x4, waiting for transfers between devices, low_sum(): lax.ppermute(send, 'term', pairs_low(ranks)).astype(jnp.float32)  5.46 us
    ppermute x12, waiting for transfers between devices, high_parts(): lax.ppermute(total[k].astype(jnp.bfloat16), 'term', pairs_high(ranks, low...  4.95 us
    ppermute x6, waiting for transfers between devices, gather_high(): lax.ppermute(held, 'term', pairs_high(ranks, low, k))  4.48 us
  transfers between devices with their start and end apart: 31, of which 13 were waited for; matrix products, arithmetic and copies ran while one was open for 1% of the time, Pallas kernels for 19%

profile of v4, /device:TPU:0, one launch (start us, length us, event | category | flops | bytes accessed | tf_op | source)
XLA Modules:
  0.0 88.2 jit_solution(11039926946009283885)
XLA Ops:
  0.6 1.6 %first.3 = (bf16[2,512,512]{2,1,0:T(8,128)(2,1)S(1)}, bf16[512,512]{1,0:T(8,128)(2,1)S(1)}, bf16[512,512]{1,0:T(8,128)(2,1)S(1)}) custom-call(s32[2]{0:T(128)} %size_ref.9, f32[2,512,512]{2,1,0:T(8,128)} %vector_ref.3), custom_call_target="tpu_custom_call" | custom-call | flops 1048576 | bytes 4096 | tf_op jit(solution)/shard_map/first/pallas_call | solution.py:303
  2.3 0.5 collective-permute-start
  2.8 0.7 collective-permute-start.5
  3.5 0.8 collective-permute-done.refs_0_
  4.3 4.3 %first.4 = (bf16[4,64,512]{2,1,0:T(8,128)(2,1)S(1)}, f32[4,64,512]{2,1,0:T(8,128)S(1)}, bf16[4,512,512]{2,1,0:T(8,128)(2,1)S(1)}, bf16[4,512,512]{2,1,0:T(8,128)(2,1)S(1)}, f32[2,64,512]{2,1,0:T(8,128)S(1)}) custom-call(bf16[2,512,512]{2,1,0:T(8,128)(2,1)S(1)} %get-tuple-element.33.own, bf16[512,512]{1,0:T(8,128)(2,1)S(1)} %collective-permute-done.refs_0_, ...), custom_call_target="tpu_custom_call" | custom-call | flops 2147483648 | bytes 8388608 | tf_op jit(solution)/shard_map/first/pallas_call | solution.py:303
  8.6 2.9 %collective-permute-start.1 = (bf16[4,64,512]{2,1,0:T(8,128)(2,1)S(1)}, bf16[4,64,512]{2,1,0:T(8,128)(2,1)S(1)}, u32[]{:S(2)}, u32[]{:S(2)}) collective-permute-start(bf16[4,64,512]{2,1,0:T(8,128)(2,1)S(1)} %get-tuple-element.37), channel_id=1, source_target_pairs={{0,1},{1,0},{2,3},{3,2},{4,5},{5,4},{6,7},{7,6},{8,9},{9,8},{10,11... | collective-permute-start | bytes 786440 | tf_op jit(solution)/shard_map/first/ppermute | solution.py:347
  11.6 2.9 %first.5 = (bf16[4,64,512]{2,1,0:T(8,128)(2,1)S(1)}, f32[4,64,512]{2,1,0:T(8,128)S(1)}, bf16[4,512,512]{2,1,0:T(8,128)(2,1)S(1)}, bf16[4,512,512]{2,1,0:T(8,128)(2,1)S(1)}) custom-call(bf16[2,512,512]{2,1,0:T(8,128)(2,1)S(1)} %get-tuple-element.33.own, bf16[512,512]{1,0:T(8,128)(2,1)S(1)} %collective-permute-done.5.refs_0_, s32[4]{0:T(128)} %shift_ref.5, ...), custom_call_target="tpu_custom_call" | custom-call | flops 2147483648 | bytes 8388608 | tf_op jit(solution)/shard_map/first/pallas_call | solution.py:303
  14.5 0.8 collective-permute-start.6
  15.3 2.4 %collective-permute-done.1 = bf16[4,64,512]{2,1,0:T(8,128)(2,1)S(1)} collective-permute-done((bf16[4,64,512]{2,1,0:T(8,128)(2,1)S(1)}, bf16[4,64,512]{2,1,0:T(8,128)(2,1)S(1)}, u32[]{:S(2)}, u32[]{:S(2)}) %collective-permute-start.1) | collective-permute-done | bytes 262176 | tf_op jit(solution)/shard_map/first/ppermute | solution.py:347
  17.8 2.6 %collective-permute-start.2 = (bf16[64,512]{1,0:T(8,128)(2,1)S(1)}, bf16[64,512]{1,0:T(8,128)(2,1)S(1)}, u32[]{:S(2)}, u32[]{:S(2)}) collective-permute-start(bf16[64,512]{1,0:T(8,128)(2,1)S(1)} %get-tuple-element.87), channel_id=1, source_target_pairs={{0,2},{1,3},{2,0},{3,1},{4,6},{5,7},{6,4},{7,5},{8,10},{9,11},{10,... | collective-permute-start | bytes 196616 | tf_op jit(solution)/shard_map/gather/ppermute | solution.py:353
  20.4 2.6 %collective-permute-start.3 = (bf16[64,512]{1,0:T(8,128)(2,1)S(1)}, bf16[64,512]{1,0:T(8,128)(2,1)S(1)}, u32[]{:S(2)}, u32[]{:S(2)}) collective-permute-start(bf16[64,512]{1,0:T(8,128)(2,1)S(1)} %get-tuple-element.86), channel_id=1, source_target_pairs={{0,4},{1,5},{2,6},{3,7},{4,0},{5,1},{6,2},{7,3},{8,12},{9,13},{10,... | collective-permute-start | bytes 196616 | tf_op jit(solution)/shard_map/gather/ppermute | solution.py:353
  23.1 0.9 %collective-permute-start.7 = (bf16[64,512]{1,0:T(8,128)(2,1)S(1)}, bf16[64,512]{1,0:T(8,128)(2,1)S(1)}, u32[]{:S(2)}, u32[]{:S(2)}) collective-permute-start(bf16[64,512]{1,0:T(8,128)(2,1)S(1)} %get-tuple-element.84), channel_id=1, source_target_pairs={{0,2},{1,3},{2,0},{3,1},{4,6},{5,7},{6,4},{7,5},{8,10},{9,11},{10,... | collective-permute-start | bytes 196616 | tf_op jit(solution)/shard_map/gather/ppermute | solution.py:353
  24.1 3.6 %collective-permute-start.8 = (bf16[64,512]{1,0:T(8,128)(2,1)S(1)}, bf16[64,512]{1,0:T(8,128)(2,1)S(1)}, u32[]{:S(2)}, u32[]{:S(2)}) collective-permute-start(bf16[64,512]{1,0:T(8,128)(2,1)S(1)} %get-tuple-element.83), channel_id=1, source_target_pairs={{0,4},{1,5},{2,6},{3,7},{4,0},{5,1},{6,2},{7,3},{8,12},{9,13},{10,... | collective-permute-start | bytes 196616 | tf_op jit(solution)/shard_map/gather/ppermute | solution.py:353
  27.7 1.8 %collective-permute-done.4.refs_3_ = bf16[64,512]{1,0:T(8,128)(2,1)S(1)} collective-permute-done((bf16[64,512]{1,0:T(8,128)(2,1)S(1)}, bf16[64,512]{1,0:T(8,128)(2,1)S(1)}, u32[]{:S(2)}, u32[]{:S(2)}) %collective-permute-start.4) | collective-permute-done | bytes 65568 | tf_op jit(solution)/shard_map/gather/ppermute | solution.py:353
  29.5 0.7 gather.2
  30.2 2.1 %collective-permute-start.12 = (bf16[1,64,512]{2,1,0:T(8,128)(2,1)S(1)}, bf16[1,64,512]{2,1,0:T(8,128)(2,1)S(1)}, u32[]{:S(2)}, u32[]{:S(2)}) collective-permute-start(bf16[1,64,512]{2,1,0:T(8,128)(2,1)S(1)} %bitcast.42), channel_id=1, source_target_pairs={{0,6},{1,7},{2,4},{3,5},{4,2},{5,3},{6,0},{7,1},{8,14},{9,15},{10,... | collective-permute-start | bytes 196616 | tf_op jit(solution)/shard_map/gather/ppermute | solution.py:358
  32.3 0.5 collective-permute-start.11
  32.8 1.9 %collective-permute-start.10 = (bf16[1,64,512]{2,1,0:T(8,128)(2,1)S(1)}, bf16[1,64,512]{2,1,0:T(8,128)(2,1)S(1)}, u32[]{:S(2)}, u32[]{:S(2)}) collective-permute-start(bf16[1,64,512]{2,1,0:T(8,128)(2,1)S(1)} %bitcast.44), channel_id=1, source_target_pairs={{0,2},{1,3},{2,0},{3,1},{4,6},{5,7},{6,4},{7,5},{8,10},{9,11},{10,... | collective-permute-start | bytes 196616 | tf_op jit(solution)/shard_map/gather/ppermute | solution.py:358
  34.7 0.7 gather.3
  35.4 2.1 %collective-permute-start.16 = (bf16[1,64,512]{2,1,0:T(8,128)(2,1)S(1)}, bf16[1,64,512]{2,1,0:T(8,128)(2,1)S(1)}, u32[]{:S(2)}, u32[]{:S(2)}) collective-permute-start(bf16[1,64,512]{2,1,0:T(8,128)(2,1)S(1)} %bitcast.46), channel_id=1, source_target_pairs={{0,6},{1,7},{2,4},{3,5},{4,2},{5,3},{6,0},{7,1},{8,14},{9,15},{10,... | collective-permute-start | bytes 196616 | tf_op jit(solution)/shard_map/gather/ppermute | solution.py:358
  37.5 3.2 %collective-permute-start.15 = (bf16[1,64,512]{2,1,0:T(8,128)(2,1)S(1)}, bf16[1,64,512]{2,1,0:T(8,128)(2,1)S(1)}, u32[]{:S(2)}, u32[]{:S(2)}) collective-permute-start(bf16[1,64,512]{2,1,0:T(8,128)(2,1)S(1)} %bitcast.47), channel_id=1, source_target_pairs={{0,4},{1,5},{2,6},{3,7},{4,0},{5,1},{6,2},{7,3},{8,12},{9,13},{10,... | collective-permute-start | bytes 196616 | tf_op jit(solution)/shard_map/gather/ppermute | solution.py:358
  40.6 2.1 %collective-permute-done.11 = bf16[1,64,512]{2,1,0:T(8,128)(2,1)S(1)} collective-permute-done((bf16[1,64,512]{2,1,0:T(8,128)(2,1)S(1)}, bf16[1,64,512]{2,1,0:T(8,128)(2,1)S(1)}, u32[]{:S(2)}, u32[]{:S(2)}) %collective-permute-start.11) | collective-permute-done | bytes 65568 | tf_op jit(solution)/shard_map/gather/ppermute | solution.py:358
  42.8 1.8 %collective-permute-start.13 = (bf16[4,64,512]{2,1,0:T(8,128)(2,1)S(1)}, bf16[4,64,512]{2,1,0:T(8,128)(2,1)S(1)}, u32[]{:S(2)}, u32[]{:S(2)}) collective-permute-start(bf16[4,64,512]{2,1,0:T(8,128)(2,1)S(1)} %get-tuple-element.81.mine), channel_id=1, source_target_pairs={{0,1},{1,0},{2,3},{3,2},{4,5},{5,4},{6,7},{7,6},{8,9},{9,8},{10,11... | collective-permute-start | bytes 786440 | tf_op jit(solution)/shard_map/gather/ppermute | solution.py:412
  44.6 2.3 %collective-permute-done.15 = bf16[1,64,512]{2,1,0:T(8,128)(2,1)S(1)} collective-permute-done((bf16[1,64,512]{2,1,0:T(8,128)(2,1)S(1)}, bf16[1,64,512]{2,1,0:T(8,128)(2,1)S(1)}, u32[]{:S(2)}, u32[]{:S(2)}) %collective-permute-start.15) | collective-permute-done | bytes 65568 | tf_op jit(solution)/shard_map/gather/ppermute | solution.py:358
  47.0 1.9 %collective-permute-start.17 = (bf16[4,64,512]{2,1,0:T(8,128)(2,1)S(1)}, bf16[4,64,512]{2,1,0:T(8,128)(2,1)S(1)}, u32[]{:S(2)}, u32[]{:S(2)}) collective-permute-start(bf16[4,64,512]{2,1,0:T(8,128)(2,1)S(1)} %get-tuple-element.76.refs_0_), channel_id=1, source_target_pairs={{0,1},{1,0},{2,3},{3,2},{4,5},{5,4},{6,7},{7,6},{8,9},{9,8},{10,11... | collective-permute-start | bytes 786440 | tf_op jit(solution)/shard_map/gather/ppermute | solution.py:412
  49.0 3.0 %collective-permute-done.13.theirs = bf16[4,64,512]{2,1,0:T(8,128)(2,1)S(1)} collective-permute-done((bf16[4,64,512]{2,1,0:T(8,128)(2,1)S(1)}, bf16[4,64,512]{2,1,0:T(8,128)(2,1)S(1)}, u32[]{:S(2)}, u32[]{:S(2)}) %collective-permute-start.13) | collective-permute-done | bytes 262176 | tf_op jit(solution)/shard_map/gather/ppermute | solution.py:412
  52.0 1.4 %second.5 = (f32[512,512]{1,0:T(8,128)S(1)}, bf16[512,512]{1,0:T(8,128)(2,1)S(1)}) custom-call(s32[4]{0:T(128)S(1)} %copy-done.4, bf16[4,512,512]{2,1,0:T(8,128)(2,1)S(1)} %get-tuple-element.47.left, bf16[4,512,512]{2,1,0:T(8,128)(2,1)S(1)} %get-tuple-element.48.right, bf16[4,64,512]{2,1,0:T(8,128)(2,1)S(1)} %get-tuple-element.81.mine, ...), custom_call_target="tpu_custom_call" | custom-call | flops 1 | tf_op jit(solution)/shard_map/second/pallas_call | solution.py:303
  53.6 1.0 %second.6 = f32[8,512]{1,0:T(8,128)S(1)} custom-call(s32[2]{0:T(128)S(1)} %copy-done.1, f32[2,512,512]{2,1,0:T(8,128)S(1)} %copy-done, bf16[512,512]{1,0:T(8,128)(2,1)S(1)} %get-tuple-element.51.block.first_block), custom_call_target="tpu_custom_call" | custom-call | flops 1 | tf_op jit(solution)/shard_map/second/pallas_call | solution.py:303
  54.6 2.6 %collective-permute-done.17.refs_1_ = bf16[4,64,512]{2,1,0:T(8,128)(2,1)S(1)} collective-permute-done((bf16[4,64,512]{2,1,0:T(8,128)(2,1)S(1)}, bf16[4,64,512]{2,1,0:T(8,128)(2,1)S(1)}, u32[]{:S(2)}, u32[]{:S(2)}) %collective-permute-start.17) | collective-permute-done | bytes 262176 | tf_op jit(solution)/shard_map/gather/ppermute | solution.py:412
  57.3 0.9 collective-permute-start.23
  58.2 1.0 %collective-permute-done.18.refs_2_ = bf16[2,4,64,512]{3,2,1,0:T(8,128)(2,1)S(1)} collective-permute-done((bf16[2,4,64,512]{3,2,1,0:T(8,128)(2,1)S(1)}, bf16[2,4,64,512]{3,2,1,0:T(8,128)(2,1)S(1)}, u32[]{:S(2)}, u32[]{:S(2)}) %collective-permute-start.18) | collective-permute-done | bytes 524320 | tf_op jit(solution)/shard_map/second/ppermute | solution.py:342
  59.1 3.0 %second.7 = (bf16[4,64,512]{2,1,0:T(8,128)(2,1)S(1)}, f32[4,64,512]{2,1,0:T(8,128)S(1)}, bf16[2,512,512]{2,1,0:T(8,128)(2,1)S(1)}) custom-call(s32[4]{0:T(128)S(1)} %copy-done.4, f32[512,512]{1,0:T(8,128)S(1)} %get-tuple-element.50.acc_ref, bf16[512,512]{1,0:T(8,128)(2,1)S(1)} %get-tuple-element.51.block.first_block, ...), custom_call_target="tpu_custom_call" | custom-call | flops 1073741824 | bytes 4194304 | tf_op jit(solution)/shard_map/second/pallas_call | solution.py:303
  62.1 2.1 %collective-permute-start.19 = (bf16[4,64,512]{2,1,0:T(8,128)(2,1)S(1)}, bf16[4,64,512]{2,1,0:T(8,128)(2,1)S(1)}, u32[]{:S(2)}, u32[]{:S(2)}) collective-permute-start(bf16[4,64,512]{2,1,0:T(8,128)(2,1)S(1)} %get-tuple-element.55), channel_id=1, source_target_pairs={{0,1},{1,0},{2,3},{3,2},{4,5},{5,4},{6,7},{7,6},{8,9},{9,8},{10,11... | collective-permute-start | bytes 786440 | tf_op jit(solution)/shard_map/second/ppermute | solution.py:347
  64.2 1.0 %second.8 = f32[8,512]{1,0:T(8,128)S(1)} custom-call(s32[2]{0:T(128)S(1)} %copy-done.1, f32[2,512,512]{2,1,0:T(8,128)S(1)} %copy-done, bf16[2,512,512]{2,1,0:T(8,128)(2,1)S(1)} %get-tuple-element.58.block.own), custom_call_target="tpu_custom_call" | custom-call | flops 1 | tf_op jit(solution)/shard_map/second/pallas_call | solution.py:303
  65.3 2.2 %second.9 = (bf16[4,64,512]{2,1,0:T(8,128)(2,1)S(1)}, f32[4,64,512]{2,1,0:T(8,128)S(1)}) custom-call(s32[4]{0:T(128)S(1)} %copy-done.4, bf16[2,512,512]{2,1,0:T(8,128)(2,1)S(1)} %get-tuple-element.58.block.own, bf16[4,512,512]{2,1,0:T(8,128)(2,1)S(1)} %get-tuple-element.59.left, bf16[4,512,512]{2,1,0:T(8,128)(2,1)S(1)} %get-tuple-element.60.right, ...), custom_call_target="tpu_custom_call" | custom-call | flops 2147483648 | bytes 8388608 | tf_op jit(solution)/shard_map/second/pallas_call | solution.py:303
  67.4 0.8 collective-permute-start.24
  68.2 3.1 %collective-permute-done.19 = bf16[4,64,512]{2,1,0:T(8,128)(2,1)S(1)} collective-permute-done((bf16[4,64,512]{2,1,0:T(8,128)(2,1)S(1)}, bf16[4,64,512]{2,1,0:T(8,128)(2,1)S(1)}, u32[]{:S(2)}, u32[]{:S(2)}) %collective-permute-start.19) | collective-permute-done | bytes 262176 | tf_op jit(solution)/shard_map/second/ppermute | solution.py:347
  71.4 0.2 collective-permute-start.20
  71.7 3.3 %collective-permute-start.21 = (bf16[64,512]{1,0:T(8,128)(2,1)S(1)}, bf16[64,512]{1,0:T(8,128)(2,1)S(1)}, u32[]{:S(2)}, u32[]{:S(2)}) collective-permute-start(bf16[64,512]{1,0:T(8,128)(2,1)S(1)} %get-tuple-element.78), channel_id=1, source_target_pairs={{0,4},{1,5},{2,6},{3,7},{4,0},{5,1},{6,2},{7,3},{8,12},{9,13},{10,... | collective-permute-start | bytes 196616 | tf_op jit(solution)/shard_map/scalars/ppermute | solution.py:353
  74.9 0.9 %collective-permute-start.22 = (bf16[64,512]{1,0:T(8,128)(2,1)S(1)}, bf16[64,512]{1,0:T(8,128)(2,1)S(1)}, u32[]{:S(2)}, u32[]{:S(2)}) collective-permute-start(bf16[64,512]{1,0:T(8,128)(2,1)S(1)} %get-tuple-element.77), channel_id=1, source_target_pairs={{0,6},{1,7},{2,4},{3,5},{4,2},{5,3},{6,0},{7,1},{8,14},{9,15},{10,... | collective-permute-start | bytes 196616 | tf_op jit(solution)/shard_map/scalars/ppermute | solution.py:353
  76.1 3.5 %collective-permute-start.26 = (bf16[64,512]{1,0:T(8,128)(2,1)S(1)}, bf16[64,512]{1,0:T(8,128)(2,1)S(1)}, u32[]{:S(2)}, u32[]{:S(2)}) collective-permute-start(bf16[64,512]{1,0:T(8,128)(2,1)S(1)} %get-tuple-element.73), channel_id=1, source_target_pairs={{0,4},{1,5},{2,6},{3,7},{4,0},{5,1},{6,2},{7,3},{8,12},{9,13},{10,... | collective-permute-start | bytes 196616 | tf_op jit(solution)/shard_map/scalars/ppermute | solution.py:353
  79.6 0.9 %collective-permute-start.27 = (bf16[64,512]{1,0:T(8,128)(2,1)S(1)}, bf16[64,512]{1,0:T(8,128)(2,1)S(1)}, u32[]{:S(2)}, u32[]{:S(2)}) collective-permute-start(bf16[64,512]{1,0:T(8,128)(2,1)S(1)} %get-tuple-element.72), channel_id=1, source_target_pairs={{0,6},{1,7},{2,4},{3,5},{4,2},{5,3},{6,0},{7,1},{8,14},{9,15},{10,... | collective-permute-start | bytes 196616 | tf_op jit(solution)/shard_map/scalars/ppermute | solution.py:353
  80.5 0.7 collective-permute-start.28
  81.5 1.9 %collective-permute-start.29 = (f32[8,512]{1,0:T(8,128)S(1)}, f32[8,512]{1,0:T(8,128)S(1)}, u32[]{:S(2)}, u32[]{:S(2)}) collective-permute-start(f32[8,512]{1,0:T(8,128)S(1)} %add.19.refs_14_), channel_id=1, source_target_pairs={{0,16},{8,24},{16,0},{24,8},{1,17},{9,25},{17,1},{25,9},{2,18},{10... | collective-permute-start | bytes 49160 | tf_op jit(solution)/shard_map/scalars/ppermute | solution.py:476
  83.4 1.6 %collective-permute-done.26.refs_12_ = bf16[64,512]{1,0:T(8,128)(2,1)S(1)} collective-permute-done((bf16[64,512]{1,0:T(8,128)(2,1)S(1)}, bf16[64,512]{1,0:T(8,128)(2,1)S(1)}, u32[]{:S(2)}, u32[]{:S(2)}) %collective-permute-start.26) | collective-permute-done | bytes 65568 | tf_op jit(solution)/shard_map/scalars/ppermute | solution.py:353
  85.0 1.4 %collective-permute-done.27.refs_13_ = bf16[64,512]{1,0:T(8,128)(2,1)S(1)} collective-permute-done((bf16[64,512]{1,0:T(8,128)(2,1)S(1)}, bf16[64,512]{1,0:T(8,128)(2,1)S(1)}, u32[]{:S(2)}, u32[]{:S(2)}) %collective-permute-start.27) | collective-permute-done | bytes 65568 | tf_op jit(solution)/shard_map/scalars/ppermute | solution.py:353
  86.3 0.3 collective-permute-done.30.refs_17_
  86.7 1.5 %scalars.1 = (f32[2,64,512]{2,1,0:T(8,128)}, f32[2,64,512]{2,1,0:T(8,128)}) custom-call(s32[2]{0:T(128)S(1)} %copy-done.1, f32[2,64,512]{2,1,0:T(8,128)S(1)} %get-tuple-element.35.start, f32[64,512]{1,0:T(8,128)S(1)} %get-tuple-element.38.refs_0_, f32[64,512]{1,0:T(8,128)S(1)} %get-tuple-element.42.refs_1_, f32[64,512]{1,0:T(8,128)S(1)} %get-tuple-element.43.refs_2_, ...), custom_call_target="tpu_custom_call" | custom-call | flops 1048576 | bytes 4096 | tf_op jit(solution)/shard_map/scalars/pallas_call | solution.py:303
  (52 shorter events, 1.2 us)
Async XLA Ops:
  2.3 2.1 %collective-permute-start = (bf16[512,512]{1,0:T(8,128)(2,1)S(1)}, bf16[512,512]{1,0:T(8,128)(2,1)S(1)}, u32[]{:S(2)}, u32[]{:S(2)}) collective-permute-start(bf16[512,512]{1,0:T(8,128)(2,1)S(1)} %get-tuple-element.34), channel_id=1, source_target_pairs={{0,8},{8,0},{16,24},{24,16},{1,9},{9,1},{17,25},{25,17},{2,10},{10... | collective-permute-start | bytes 1572872 | tf_op jit(solution)/shard_map/first/ppermute | solution.py:342
  2.8 8.8 %collective-permute-start.5 = (bf16[512,512]{1,0:T(8,128)(2,1)S(1)}, bf16[512,512]{1,0:T(8,128)(2,1)S(1)}, u32[]{:S(2)}, u32[]{:S(2)}) collective-permute-start(bf16[512,512]{1,0:T(8,128)(2,1)S(1)} %get-tuple-element.39), channel_id=1, source_target_pairs={{8,16},{16,8},{9,17},{17,9},{10,18},{18,10},{11,19},{19,11},{12,20... | collective-permute-start | bytes 1572872 | tf_op jit(solution)/shard_map/first/ppermute | solution.py:342
  8.6 9.0 %collective-permute-start.1 = (bf16[4,64,512]{2,1,0:T(8,128)(2,1)S(1)}, bf16[4,64,512]{2,1,0:T(8,128)(2,1)S(1)}, u32[]{:S(2)}, u32[]{:S(2)}) collective-permute-start(bf16[4,64,512]{2,1,0:T(8,128)(2,1)S(1)} %get-tuple-element.37), channel_id=1, source_target_pairs={{0,1},{1,0},{2,3},{3,2},{4,5},{5,4},{6,7},{7,6},{8,9},{9,8},{10,11... | collective-permute-start | bytes 786440 | tf_op jit(solution)/shard_map/first/ppermute | solution.py:347
  14.5 8.5 %collective-permute-start.6 = (bf16[4,64,512]{2,1,0:T(8,128)(2,1)S(1)}, bf16[4,64,512]{2,1,0:T(8,128)(2,1)S(1)}, u32[]{:S(2)}, u32[]{:S(2)}) collective-permute-start(bf16[4,64,512]{2,1,0:T(8,128)(2,1)S(1)} %get-tuple-element.41), channel_id=1, source_target_pairs={{0,1},{1,0},{2,3},{3,2},{4,5},{5,4},{6,7},{7,6},{8,9},{9,8},{10,11... | collective-permute-start | bytes 786440 | tf_op jit(solution)/shard_map/first/ppermute | solution.py:347
  17.7 11.8 %copy-start.1 = (s32[2]{0:T(128)S(1)}, s32[2]{0:T(128)}, u32[]{:S(2)}) copy-start(s32[2]{0:T(128)} %size_ref.9) | copy-start | bytes 28
  17.7 11.8 %copy-start.2 = (f32[2,512]{1,0:T(2,128)S(1)}, f32[2,512]{1,0:T(2,128)}, u32[]{:S(2)}) copy-start(f32[2,512]{1,0:T(2,128)} %left_row.3) | copy-start | bytes 12292
  17.7 11.8 %copy-start.3 = (f32[2,512]{1,0:T(2,128)S(1)}, f32[2,512]{1,0:T(2,128)}, u32[]{:S(2)}) copy-start(f32[2,512]{1,0:T(2,128)} %right_row.3) | copy-start | bytes 12292
  17.8 9.9 %collective-permute-start.2 = (bf16[64,512]{1,0:T(8,128)(2,1)S(1)}, bf16[64,512]{1,0:T(8,128)(2,1)S(1)}, u32[]{:S(2)}, u32[]{:S(2)}) collective-permute-start(bf16[64,512]{1,0:T(8,128)(2,1)S(1)} %get-tuple-element.87), channel_id=1, source_target_pairs={{0,2},{1,3},{2,0},{3,1},{4,6},{5,7},{6,4},{7,5},{8,10},{9,11},{10,... | collective-permute-start | bytes 196616 | tf_op jit(solution)/shard_map/gather/ppermute | solution.py:353
  20.4 7.3 %collective-permute-start.3 = (bf16[64,512]{1,0:T(8,128)(2,1)S(1)}, bf16[64,512]{1,0:T(8,128)(2,1)S(1)}, u32[]{:S(2)}, u32[]{:S(2)}) collective-permute-start(bf16[64,512]{1,0:T(8,128)(2,1)S(1)} %get-tuple-element.86), channel_id=1, source_target_pairs={{0,4},{1,5},{2,6},{3,7},{4,0},{5,1},{6,2},{7,3},{8,12},{9,13},{10,... | collective-permute-start | bytes 196616 | tf_op jit(solution)/shard_map/gather/ppermute | solution.py:353
  23.0 6.5 %collective-permute-start.4 = (bf16[64,512]{1,0:T(8,128)(2,1)S(1)}, bf16[64,512]{1,0:T(8,128)(2,1)S(1)}, u32[]{:S(2)}, u32[]{:S(2)}) collective-permute-start(bf16[64,512]{1,0:T(8,128)(2,1)S(1)} %get-tuple-element.85), channel_id=1, source_target_pairs={{0,6},{1,7},{2,4},{3,5},{4,2},{5,3},{6,0},{7,1},{8,14},{9,15},{10,... | collective-permute-start | bytes 196616 | tf_op jit(solution)/shard_map/gather/ppermute | solution.py:353
  23.1 28.9 %copy-start.4 = (s32[4]{0:T(128)S(1)}, s32[4]{0:T(128)}, u32[]{:S(2)}) copy-start(s32[4]{0:T(128)} %shift_ref.5) | copy-start | bytes 52
  23.1 9.6 %collective-permute-start.7 = (bf16[64,512]{1,0:T(8,128)(2,1)S(1)}, bf16[64,512]{1,0:T(8,128)(2,1)S(1)}, u32[]{:S(2)}, u32[]{:S(2)}) collective-permute-start(bf16[64,512]{1,0:T(8,128)(2,1)S(1)} %get-tuple-element.84), channel_id=1, source_target_pairs={{0,2},{1,3},{2,0},{3,1},{4,6},{5,7},{6,4},{7,5},{8,10},{9,11},{10,... | collective-permute-start | bytes 196616 | tf_op jit(solution)/shard_map/gather/ppermute | solution.py:353
  24.1 10.6 %collective-permute-start.8 = (bf16[64,512]{1,0:T(8,128)(2,1)S(1)}, bf16[64,512]{1,0:T(8,128)(2,1)S(1)}, u32[]{:S(2)}, u32[]{:S(2)}) collective-permute-start(bf16[64,512]{1,0:T(8,128)(2,1)S(1)} %get-tuple-element.83), channel_id=1, source_target_pairs={{0,4},{1,5},{2,6},{3,7},{4,0},{5,1},{6,2},{7,3},{8,12},{9,13},{10,... | collective-permute-start | bytes 196616 | tf_op jit(solution)/shard_map/gather/ppermute | solution.py:353
  27.7 7.0 %collective-permute-start.9 = (bf16[64,512]{1,0:T(8,128)(2,1)S(1)}, bf16[64,512]{1,0:T(8,128)(2,1)S(1)}, u32[]{:S(2)}, u32[]{:S(2)}) collective-permute-start(bf16[64,512]{1,0:T(8,128)(2,1)S(1)} %get-tuple-element.82), channel_id=1, source_target_pairs={{0,6},{1,7},{2,4},{3,5},{4,2},{5,3},{6,0},{7,1},{8,14},{9,15},{10,... | collective-permute-start | bytes 196616 | tf_op jit(solution)/shard_map/gather/ppermute | solution.py:353
  30.2 10.4 %collective-permute-start.12 = (bf16[1,64,512]{2,1,0:T(8,128)(2,1)S(1)}, bf16[1,64,512]{2,1,0:T(8,128)(2,1)S(1)}, u32[]{:S(2)}, u32[]{:S(2)}) collective-permute-start(bf16[1,64,512]{2,1,0:T(8,128)(2,1)S(1)} %bitcast.42), channel_id=1, source_target_pairs={{0,6},{1,7},{2,4},{3,5},{4,2},{5,3},{6,0},{7,1},{8,14},{9,15},{10,... | collective-permute-start | bytes 196616 | tf_op jit(solution)/shard_map/gather/ppermute | solution.py:358
  32.3 10.5 %collective-permute-start.11 = (bf16[1,64,512]{2,1,0:T(8,128)(2,1)S(1)}, bf16[1,64,512]{2,1,0:T(8,128)(2,1)S(1)}, u32[]{:S(2)}, u32[]{:S(2)}) collective-permute-start(bf16[1,64,512]{2,1,0:T(8,128)(2,1)S(1)} %bitcast.43), channel_id=1, source_target_pairs={{0,4},{1,5},{2,6},{3,7},{4,0},{5,1},{6,2},{7,3},{8,12},{9,13},{10,... | collective-permute-start | bytes 196616 | tf_op jit(solution)/shard_map/gather/ppermute | solution.py:358
  32.8 10.0 %collective-permute-start.10 = (bf16[1,64,512]{2,1,0:T(8,128)(2,1)S(1)}, bf16[1,64,512]{2,1,0:T(8,128)(2,1)S(1)}, u32[]{:S(2)}, u32[]{:S(2)}) collective-permute-start(bf16[1,64,512]{2,1,0:T(8,128)(2,1)S(1)} %bitcast.44), channel_id=1, source_target_pairs={{0,2},{1,3},{2,0},{3,1},{4,6},{5,7},{6,4},{7,5},{8,10},{9,11},{10,... | collective-permute-start | bytes 196616 | tf_op jit(solution)/shard_map/gather/ppermute | solution.py:358
  35.4 9.3 %collective-permute-start.16 = (bf16[1,64,512]{2,1,0:T(8,128)(2,1)S(1)}, bf16[1,64,512]{2,1,0:T(8,128)(2,1)S(1)}, u32[]{:S(2)}, u32[]{:S(2)}) collective-permute-start(bf16[1,64,512]{2,1,0:T(8,128)(2,1)S(1)} %bitcast.46), channel_id=1, source_target_pairs={{0,6},{1,7},{2,4},{3,5},{4,2},{5,3},{6,0},{7,1},{8,14},{9,15},{10,... | collective-permute-start | bytes 196616 | tf_op jit(solution)/shard_map/gather/ppermute | solution.py:358
  37.5 9.5 %collective-permute-start.15 = (bf16[1,64,512]{2,1,0:T(8,128)(2,1)S(1)}, bf16[1,64,512]{2,1,0:T(8,128)(2,1)S(1)}, u32[]{:S(2)}, u32[]{:S(2)}) collective-permute-start(bf16[1,64,512]{2,1,0:T(8,128)(2,1)S(1)} %bitcast.47), channel_id=1, source_target_pairs={{0,4},{1,5},{2,6},{3,7},{4,0},{5,1},{6,2},{7,3},{8,12},{9,13},{10,... | collective-permute-start | bytes 196616 | tf_op jit(solution)/shard_map/gather/ppermute | solution.py:358
  40.6 6.4 %collective-permute-start.14 = (bf16[1,64,512]{2,1,0:T(8,128)(2,1)S(1)}, bf16[1,64,512]{2,1,0:T(8,128)(2,1)S(1)}, u32[]{:S(2)}, u32[]{:S(2)}) collective-permute-start(bf16[1,64,512]{2,1,0:T(8,128)(2,1)S(1)} %bitcast.48), channel_id=1, source_target_pairs={{0,2},{1,3},{2,0},{3,1},{4,6},{5,7},{6,4},{7,5},{8,10},{9,11},{10,... | collective-permute-start | bytes 196616 | tf_op jit(solution)/shard_map/gather/ppermute | solution.py:358
  42.8 9.2 %collective-permute-start.13 = (bf16[4,64,512]{2,1,0:T(8,128)(2,1)S(1)}, bf16[4,64,512]{2,1,0:T(8,128)(2,1)S(1)}, u32[]{:S(2)}, u32[]{:S(2)}) collective-permute-start(bf16[4,64,512]{2,1,0:T(8,128)(2,1)S(1)} %get-tuple-element.81.mine), channel_id=1, source_target_pairs={{0,1},{1,0},{2,3},{3,2},{4,5},{5,4},{6,7},{7,6},{8,9},{9,8},{10,11... | collective-permute-start | bytes 786440 | tf_op jit(solution)/shard_map/gather/ppermute | solution.py:412
  47.0 10.2 %collective-permute-start.17 = (bf16[4,64,512]{2,1,0:T(8,128)(2,1)S(1)}, bf16[4,64,512]{2,1,0:T(8,128)(2,1)S(1)}, u32[]{:S(2)}, u32[]{:S(2)}) collective-permute-start(bf16[4,64,512]{2,1,0:T(8,128)(2,1)S(1)} %get-tuple-element.76.refs_0_), channel_id=1, source_target_pairs={{0,1},{1,0},{2,3},{3,2},{4,5},{5,4},{6,7},{7,6},{8,9},{9,8},{10,11... | collective-permute-start | bytes 786440 | tf_op jit(solution)/shard_map/gather/ppermute | solution.py:412
  52.0 1.6 %copy-start = (f32[2,512,512]{2,1,0:T(8,128)S(1)}, f32[2,512,512]{2,1,0:T(8,128)}, u32[]{:S(2)}) copy-start(f32[2,512,512]{2,1,0:T(8,128)} %vector_ref.3) | copy-start | bytes 6291460
  57.2 1.9 %collective-permute-start.18 = (bf16[2,4,64,512]{3,2,1,0:T(8,128)(2,1)S(1)}, bf16[2,4,64,512]{3,2,1,0:T(8,128)(2,1)S(1)}, u32[]{:S(2)}, u32[]{:S(2)}) collective-permute-start(bf16[2,4,64,512]{3,2,1,0:T(8,128)(2,1)S(1)} %pad_maximum_fusion), channel_id=1, source_target_pairs={{0,8},{8,0},{16,24},{24,16},{1,9},{9,1},{17,25},{25,17},{2,10},{10... | collective-permute-start | bytes 1572872 | tf_op jit(solution)/shard_map/second/ppermute | solution.py:342
  57.3 8.0 %collective-permute-start.23 = (bf16[2,4,64,512]{3,2,1,0:T(8,128)(2,1)S(1)}, bf16[2,4,64,512]{3,2,1,0:T(8,128)(2,1)S(1)}, u32[]{:S(2)}, u32[]{:S(2)}) collective-permute-start(bf16[2,4,64,512]{3,2,1,0:T(8,128)(2,1)S(1)} %pad_maximum_fusion.1), channel_id=1, source_target_pairs={{8,16},{16,8},{9,17},{17,9},{10,18},{18,10},{11,19},{19,11},{12,20... | collective-permute-start | bytes 1572872 | tf_op jit(solution)/shard_map/second/ppermute | solution.py:342
  62.1 9.2 %collective-permute-start.19 = (bf16[4,64,512]{2,1,0:T(8,128)(2,1)S(1)}, bf16[4,64,512]{2,1,0:T(8,128)(2,1)S(1)}, u32[]{:S(2)}, u32[]{:S(2)}) collective-permute-start(bf16[4,64,512]{2,1,0:T(8,128)(2,1)S(1)} %get-tuple-element.55), channel_id=1, source_target_pairs={{0,1},{1,0},{2,3},{3,2},{4,5},{5,4},{6,7},{7,6},{8,9},{9,8},{10,11... | collective-permute-start | bytes 786440 | tf_op jit(solution)/shard_map/second/ppermute | solution.py:347
  67.4 8.4 %collective-permute-start.24 = (bf16[4,64,512]{2,1,0:T(8,128)(2,1)S(1)}, bf16[4,64,512]{2,1,0:T(8,128)(2,1)S(1)}, u32[]{:S(2)}, u32[]{:S(2)}) collective-permute-start(bf16[4,64,512]{2,1,0:T(8,128)(2,1)S(1)} %get-tuple-element.62), channel_id=1, source_target_pairs={{0,1},{1,0},{2,3},{3,2},{4,5},{5,4},{6,7},{7,6},{8,9},{9,8},{10,11... | collective-permute-start | bytes 786440 | tf_op jit(solution)/shard_map/second/ppermute | solution.py:347
  71.4 8.2 %collective-permute-start.20 = (bf16[64,512]{1,0:T(8,128)(2,1)S(1)}, bf16[64,512]{1,0:T(8,128)(2,1)S(1)}, u32[]{:S(2)}, u32[]{:S(2)}) collective-permute-start(bf16[64,512]{1,0:T(8,128)(2,1)S(1)} %get-tuple-element.79), channel_id=1, source_target_pairs={{0,2},{1,3},{2,0},{3,1},{4,6},{5,7},{6,4},{7,5},{8,10},{9,11},{10,... | collective-permute-start | bytes 196616 | tf_op jit(solution)/shard_map/scalars/ppermute | solution.py:353
  71.7 8.9 %collective-permute-start.21 = (bf16[64,512]{1,0:T(8,128)(2,1)S(1)}, bf16[64,512]{1,0:T(8,128)(2,1)S(1)}, u32[]{:S(2)}, u32[]{:S(2)}) collective-permute-start(bf16[64,512]{1,0:T(8,128)(2,1)S(1)} %get-tuple-element.78), channel_id=1, source_target_pairs={{0,4},{1,5},{2,6},{3,7},{4,0},{5,1},{6,2},{7,3},{8,12},{9,13},{10,... | collective-permute-start | bytes 196616 | tf_op jit(solution)/shard_map/scalars/ppermute | solution.py:353
  74.9 6.5 %collective-permute-start.22 = (bf16[64,512]{1,0:T(8,128)(2,1)S(1)}, bf16[64,512]{1,0:T(8,128)(2,1)S(1)}, u32[]{:S(2)}, u32[]{:S(2)}) collective-permute-start(bf16[64,512]{1,0:T(8,128)(2,1)S(1)} %get-tuple-element.77), channel_id=1, source_target_pairs={{0,6},{1,7},{2,4},{3,5},{4,2},{5,3},{6,0},{7,1},{8,14},{9,15},{10,... | collective-permute-start | bytes 196616 | tf_op jit(solution)/shard_map/scalars/ppermute | solution.py:353
  76.0 7.3 %collective-permute-start.25 = (bf16[64,512]{1,0:T(8,128)(2,1)S(1)}, bf16[64,512]{1,0:T(8,128)(2,1)S(1)}, u32[]{:S(2)}, u32[]{:S(2)}) collective-permute-start(bf16[64,512]{1,0:T(8,128)(2,1)S(1)} %get-tuple-element.74), channel_id=1, source_target_pairs={{0,2},{1,3},{2,0},{3,1},{4,6},{5,7},{6,4},{7,5},{8,10},{9,11},{10,... | collective-permute-start | bytes 196616 | tf_op jit(solution)/shard_map/scalars/ppermute | solution.py:353
  76.1 8.9 %collective-permute-start.26 = (bf16[64,512]{1,0:T(8,128)(2,1)S(1)}, bf16[64,512]{1,0:T(8,128)(2,1)S(1)}, u32[]{:S(2)}, u32[]{:S(2)}) collective-permute-start(bf16[64,512]{1,0:T(8,128)(2,1)S(1)} %get-tuple-element.73), channel_id=1, source_target_pairs={{0,4},{1,5},{2,6},{3,7},{4,0},{5,1},{6,2},{7,3},{8,12},{9,13},{10,... | collective-permute-start | bytes 196616 | tf_op jit(solution)/shard_map/scalars/ppermute | solution.py:353
  79.6 6.7 %collective-permute-start.27 = (bf16[64,512]{1,0:T(8,128)(2,1)S(1)}, bf16[64,512]{1,0:T(8,128)(2,1)S(1)}, u32[]{:S(2)}, u32[]{:S(2)}) collective-permute-start(bf16[64,512]{1,0:T(8,128)(2,1)S(1)} %get-tuple-element.72), channel_id=1, source_target_pairs={{0,6},{1,7},{2,4},{3,5},{4,2},{5,3},{6,0},{7,1},{8,14},{9,15},{10,... | collective-permute-start | bytes 196616 | tf_op jit(solution)/shard_map/scalars/ppermute | solution.py:353
  80.5 5.8 %collective-permute-start.28 = (f32[8,512]{1,0:T(8,128)S(1)}, f32[8,512]{1,0:T(8,128)S(1)}, u32[]{:S(2)}, u32[]{:S(2)}) collective-permute-start(f32[8,512]{1,0:T(8,128)S(1)} %add.19.refs_14_), channel_id=1, source_target_pairs={{0,8},{8,0},{16,24},{24,16},{1,9},{9,1},{17,25},{25,17},{2,10},{10... | collective-permute-start | bytes 49160 | tf_op jit(solution)/shard_map/scalars/ppermute | solution.py:476
  81.5 4.9 %collective-permute-start.29 = (f32[8,512]{1,0:T(8,128)S(1)}, f32[8,512]{1,0:T(8,128)S(1)}, u32[]{:S(2)}, u32[]{:S(2)}) collective-permute-start(f32[8,512]{1,0:T(8,128)S(1)} %add.19.refs_14_), channel_id=1, source_target_pairs={{0,16},{8,24},{16,0},{24,8},{1,17},{9,25},{17,1},{25,9},{2,18},{10... | collective-permute-start | bytes 49160 | tf_op jit(solution)/shard_map/scalars/ppermute | solution.py:476
  83.3 3.3 %collective-permute-start.30 = (f32[8,512]{1,0:T(8,128)S(1)}, f32[8,512]{1,0:T(8,128)S(1)}, u32[]{:S(2)}, u32[]{:S(2)}) collective-permute-start(f32[8,512]{1,0:T(8,128)S(1)} %add.19.refs_14_), channel_id=1, source_target_pairs={{0,24},{8,16},{16,8},{24,0},{1,25},{9,17},{17,9},{25,1},{2,26},{10... | collective-permute-start | bytes 49160 | tf_op jit(solution)/shard_map/scalars/ppermute | solution.py:476

commit v5 on v3

--- a/solution.py
+++ b/solution.py
@@ -39,8 +39,11 @@
     return row_of
 
 
-def add_pair(acc, left, right, block):
-    mixed = jnp.dot(left[...], block[...], preferred_element_type=jnp.float32)
+def add_pair(dims, far, acc, left, right, block):
+    count, low, span = dims[3:]
+    row_of = row_finder(count, low, span)
+    rows = [left[pl.ds(row_of(step, far), span), :] for step in range(count)]
+    mixed = jnp.dot(jnp.concatenate(rows), block[...], preferred_element_type=jnp.float32)
     acc[...] += lax.dot_general(
         mixed.astype(jnp.bfloat16), right[...], NT, preferred_element_type=jnp.float32
     )
@@ -61,7 +64,9 @@
     return side, (here + side >= 0) & (here + side < groups)
 
 
-def add_pairs(dims, turn, shift_ref, acc, left, right, own, halos, arrived=None, skip_own=False):
+def add_pairs(
+    dims, turn, far, shift_ref, acc, left, right, own, halos, arrived=None, skip_own=False
+):
     sectors, terms = dims[:2]
     s = sector_at(turn, sectors)
     for t in range(terms):
@@ -74,14 +79,14 @@
 
         @pl.when(inside)
         def _():
-            add_pair(acc, left.at[t], right.at[t], own.at[partner])
+            add_pair(dims, far, acc, left.at[t], right.at[t], own.at[partner])
 
         for block, halo in zip(halos, halos_at(turn, sectors)):
             side, there = halo_side(halo)
 
             @pl.when((shift_ref[t] == side) & there)
             def _():
-                add_pair(acc, left.at[t], right.at[t], block)
+                add_pair(dims, far, acc, left.at[t], right.at[t], block)
 
 
 def place_rows(dims, wb, pieces):
@@ -90,15 +95,6 @@
     for far in range(low):
         for step in range(count):
             wb[pl.ds(row_of(step, far), span), :] = pieces[far][step]
-
-
-def cut(dims, acc, send_ref, keep_ref):
-    sectors, terms, size, count, low, span = dims
-    row_of = row_finder(count, low, span)
-    for step in range(count):
-        if low > 1:
-            send_ref[step] = acc[pl.ds(row_of(step, 1), span), :].astype(jnp.bfloat16)
-        keep_ref[step] = acc[pl.ds(row_of(step, 0), span), :]
 
 
 def live_tile(shape, first_row, limit):
@@ -154,7 +150,7 @@
 def load_kernel(dims, turn, own, *refs):
     sectors, terms, size, count, low, span = dims
     blocks, refs = refs[: len(halos_at(turn, sectors))], refs[len(halos_at(turn, sectors)) :]
-    shift_hbm, size_hbm, left_hbm, right_hbm, vector_hbm, send_ref, keep_ref, left, right, *refs = refs
+    shift_hbm, size_hbm, left_hbm, right_hbm, vector_hbm, send_ref, left, right, *refs = refs
     start, refs = (refs[0], refs[1:]) if turn == 0 else (None, refs)
     acc, shift_ref, size_ref, sems, row_sems, scalar_sems = refs
     s = sector_at(turn, sectors)
@@ -176,11 +172,9 @@
     ]
     for copy in scalars:
         copy.start()
-    for pair in copies:
+    for pair in copies[:2]:
         for copy in pair:
             copy.start()
-    for copy in rows:
-        copy.start()
     acc[...] = jnp.zeros_like(acc)
     for copy in scalars:
         copy.wait()
@@ -188,48 +182,57 @@
     def arrived(t):
         for copy in copies[t]:
             copy.wait()
-
-    add_pairs(dims, turn, shift_ref, acc, left, right, own, blocks, arrived)
-    cut(dims, acc, send_ref, keep_ref)
+        for pair in copies[t + 2 : t + 3]:
+            for copy in pair:
+                copy.start()
+        if t == terms - 1:
+            for copy in rows:
+                copy.start()
+
+    add_pairs(dims, turn, low - 1, shift_ref, acc, left, right, own, blocks, arrived)
+    send_ref[...] = acc[...].astype(send_ref.dtype)
     for e, copy in enumerate(rows):
         copy.wait()
         live = live_tile((span, size), first, size_ref[e])
         start[e] = jnp.where(live, start[e], 0.0)
 
 
-def self_kernel(dims, shift_ref, left, right, mine, theirs, acc, own):
-    acc[...] = jnp.zeros_like(acc)
+def keep_kernel(dims, turn, began, shift_ref, own, left, right, *refs):
+    blocks, keep_ref = refs[: len(halos_at(turn, dims[0]))], refs[-1]
+    keep_ref[...] = refs[-2][...] if began else jnp.zeros_like(keep_ref)
+    add_pairs(dims, turn, 0, shift_ref, keep_ref, left, right, own, blocks, skip_own=began)
+
+
+def self_kernel(dims, shift_ref, left, right, mine, theirs, own, *accs):
     place_rows(dims, own, [mine, theirs])
-    for t in range(dims[1]):
-
-        @pl.when(shift_ref[t] == 0)
-        def _():
-            add_pair(acc, left.at[t], right.at[t], own)
-
-
-def rest_kernel(dims, shift_ref, acc_ref, first_block, left, right, *refs):
-    sectors = dims[0]
-    pieces, refs = refs[: 2 * sectors - 2], refs[2 * sectors - 2 :]
-    halos, (send_ref, keep_ref, own, acc, wb) = refs[:-5], refs[-5:]
-    acc[...] = acc_ref[...]
-    own[sector_at(0, sectors)] = first_block[...]
-    for turn in range(1, sectors):
-        place_rows(dims, own.at[sector_at(turn, sectors)], pieces[2 * turn - 2 : 2 * turn])
+    for far, acc in enumerate(accs):
+        acc[...] = jnp.zeros_like(acc)
+        for t in range(dims[1]):
+
+            @pl.when(shift_ref[t] == 0)
+            def _():
+                add_pair(dims, far, acc, left.at[t], right.at[t], own)
+
+
+def send_kernel(dims, turn, shift_ref, left, right, *refs):
+    sectors, low = dims[0], dims[4]
+    refs, (acc,) = refs[:-1], refs[-1:]
+    halos, refs = refs[: len(halos_at(turn, sectors))], refs[len(halos_at(turn, sectors)) :]
+    if turn == 0:
+        began, first_block, *pieces = refs[: 2 * sectors]
+        send_ref, blocks, own = refs[2 * sectors :]
+        acc[...] = began[...]
+        own[sector_at(0, sectors)] = first_block[...]
+        for n in range(1, sectors):
+            place_rows(dims, own.at[sector_at(n, sectors)], pieces[2 * n - 2 : 2 * n])
+    else:
+        own, send_ref, blocks = refs
+        acc[...] = jnp.zeros_like(acc)
     for n, halo in enumerate(halos):
-        place_rows(dims, wb.at[n], [halo.at[0], halo.at[1]])
-    blocks = [wb.at[n] for n in range(len(halos))]
-    add_pairs(dims, 0, shift_ref, acc, left, right, own, blocks, skip_own=True)
-    cut(dims, acc, send_ref, keep_ref)
-
-
-def full_kernel(dims, turn, shift_ref, own, left, right, *refs):
-    halos, (send_ref, keep_ref, acc, wb) = refs[:-4], refs[-4:]
-    acc[...] = jnp.zeros_like(acc)
-    for n, halo in enumerate(halos):
-        place_rows(dims, wb.at[n], [halo.at[0], halo.at[1]])
-    blocks = [wb.at[n] for n in range(len(halos))]
-    add_pairs(dims, turn, shift_ref, acc, left, right, own, blocks)
-    cut(dims, acc, send_ref, keep_ref)
+        place_rows(dims, blocks.at[n], [halo.at[0], halo.at[1]])
+    held = [blocks.at[n] for n in range(len(halos))]
+    add_pairs(dims, turn, low - 1, shift_ref, acc, left, right, own, held, skip_own=turn == 0)
+    send_ref[...] = acc[...].astype(send_ref.dtype)
 
 
 def sums_kernel(dims, turn, size_ref, vector_ref, block, sums):
@@ -332,7 +335,9 @@
     rows = pltpu.VMEM((sectors, span, size), jnp.float32)
     square = pltpu.VMEM((size, size), jnp.float32)
     square_low = pltpu.VMEM((size, size), jnp.bfloat16)
-    cut_shapes = [jax.ShapeDtypeStruct((count, span, size), d) for d in (jnp.bfloat16, jnp.float32)]
+    part = pltpu.VMEM((count * span, size), jnp.float32)
+    kept = jax.ShapeDtypeStruct((count * span, size), jnp.float32)
+    sent = jax.ShapeDtypeStruct(kept.shape, jnp.bfloat16 if low > 1 else jnp.float32)
     pairs = [
         [p for i in range(start, groups - 1, 2) for p in ((i, i + 1), (i + 1, i))]
         for start in range(2)
@@ -342,9 +347,25 @@
         return lax.ppermute(edge, "sector", pairs[which]) if pairs[which] else edge
 
     def low_sum(send, keep):
+        total = send
+        if low > 1:
+            got = lax.ppermute(send, "term", pairs_low(ranks))
+            arrived.append(got)
+            total = keep + got.astype(jnp.float32)
+        return total.reshape(count, span, size)
+
+    arrived = []
+
+    def keep_rows(turn, own, blocks, began=()):
         if low == 1:
-            return keep
-        return keep + lax.ppermute(send, "term", pairs_low(ranks)).astype(jnp.float32)
+            return None
+        return call(
+            functools.partial(keep_kernel, dims, turn, bool(began)),
+            [kept],
+            (sector_shifts,),
+            (own, left[turn], right[turn], *blocks, *began),
+            flops=terms * pair_flops // 2,
+        )[0]
 
     hops = range(count - 1, 0, -1)
 
@@ -375,27 +396,29 @@
         )
         halos = [halo(edge, which) for which, edge in enumerate(edges)]
         matrices = pltpu.VMEM((terms, size, size), jnp.bfloat16)
-        cuts, left, right = [], [None] * sectors, [None] * sectors
+        cuts, totals, left, right = [], [], [None] * sectors, [None] * sectors
         for turn in turns:
-            send, keep, left[turn], right[turn], *more = call(
+            blocks = [halos[h] for h in halos_at(turn, sectors)]
+            ahead = [c for c in cuts[-1:] if low > 1]
+            send, left[turn], right[turn], *more = call(
                 functools.partial(load_kernel, dims, turn),
-                [*cut_shapes, matrices, matrices] + ([rows] if turn == 0 else []),
+                [sent, matrices, matrices] + ([rows] if turn == 0 else []),
                 (),
-                (rounded, *[halos[h] for h in halos_at(turn, sectors)]),
+                (after_all(rounded, *[keep for _, keep in ahead]), *blocks),
                 (sector_shifts, sector_sizes, left_block, right_block, lanczos_vector),
                 [
-                    square,
+                    part,
                     pltpu.SMEM((terms,), jnp.int32),
                     pltpu.SMEM((sectors,), jnp.int32),
                     pltpu.SemaphoreType.DMA((2, terms)),
                     pltpu.SemaphoreType.DMA((sectors,)),
                     pltpu.SemaphoreType.DMA((2,)),
                 ],
-                terms * pair_flops,
+                terms * pair_flops // 2,
             )
-            cuts.append((send, keep))
+            cuts.append((send, keep_rows(turn, after_all(rounded, *arrived[-1:]), blocks)))
+            totals.append(low_sum(*cuts[-1]))
             start = more[0] if turn == 0 else start
-        totals = [low_sum(*c) for c in cuts]
 
     with jax.named_scope("gather"):
         shifted, plus, minus, pieces = [[None] * sectors for _ in range(4)]
@@ -421,47 +444,52 @@
         )[0]
 
     with jax.named_scope("second"):
-        acc, block = call(
+        block, *began = call(
             functools.partial(self_kernel, dims),
-            [square, square_low],
+            [square_low] + [part] * low,
             (sector_shifts,),
             (left[0], right[0], *pieces[0]),
             flops=1,
         )
         sums = [sector_sums(0, block)]
-        whole = after_all(jnp.stack(pieces[0]), pieces[-1][1], acc, sums[0])
+        whole = after_all(jnp.stack(pieces[0]), pieces[-1][1], *began, sums[0])
         halos = [halo(edge, n) for n, edge in enumerate((whole, jnp.stack(pieces[-1])))]
-        *first_cut, own = call(
-            functools.partial(rest_kernel, dims),
-            [*cut_shapes, pltpu.VMEM((sectors, size, size), jnp.bfloat16)],
+        blocks = [halos[h] for h in halos_at(0, sectors)]
+        placed = pltpu.VMEM((2, size, size), jnp.bfloat16)
+        send, beside, own = call(
+            functools.partial(send_kernel, dims, 0),
+            [sent, placed, pltpu.VMEM((sectors, size, size), jnp.bfloat16)],
             (sector_shifts,),
             (
-                acc,
-                block,
                 left[0],
                 right[0],
+                *blocks,
+                began[-1],
+                block,
                 *[piece for both in pieces[1:] for piece in both],
-                *[halos[h] for h in halos_at(0, sectors)],
             ),
-            scratch=[square, pltpu.VMEM((2, size, size), jnp.bfloat16)],
-            flops=terms * pair_flops // 2,
+            scratch=[part],
+            flops=terms * pair_flops // 4,
         )
-        cuts = [first_cut]
+        cuts = [(send, keep_rows(0, own, [beside[n] for n in range(len(blocks))], began[:1]))]
         for turn in turns[1:]:
-            sums.append(sector_sums(turn, after_all(own, *first_cut)))
-        own = after_all(own, *sums)
+            sums.append(sector_sums(turn, after_all(own, send)))
+        totals = [low_sum(*cuts[0])]
         for turn in turns[1:]:
-            cuts.append(
-                call(
-                    functools.partial(full_kernel, dims, turn),
-                    cut_shapes,
-                    (sector_shifts,),
-                    (own, left[turn], right[turn], *[halos[h] for h in halos_at(turn, sectors)]),
-                    scratch=[square, pltpu.VMEM((2, size, size), jnp.bfloat16)],
-                    flops=terms * pair_flops,
-                )
+            if low > 1:
+                own = after_all(own, *sums, cuts[-1][1])
+            blocks = [halos[h] for h in halos_at(turn, sectors)]
+            send, beside = call(
+                functools.partial(send_kernel, dims, turn),
+                [sent, placed],
+                (sector_shifts,),
+                (left[turn], right[turn], *blocks, own),
+                scratch=[part],
+                flops=terms * pair_flops // 2,
             )
-        totals = [low_sum(*c) for c in cuts]
+            blocks = [beside[n] for n in range(len(blocks))]
+            cuts.append((send, keep_rows(turn, after_all(own, *arrived[-1:]), blocks)))
+            totals.append(low_sum(*cuts[-1]))
 
     with jax.named_scope("scalars"):
         parts = [high_parts(total) for total in totals]

time: 86.1 us -> 89.7 us (1.042)
  Pallas kernels: 19.7 us -> 28.4 us
  starting transfers between devices: 41.6 us -> 38.6 us
  waiting for transfers between devices: 22.9 us -> 20.5 us
    pallas_call x11 -> x15, Pallas kernels: 19.7 us -> 28.4 us  [call(): pl.pallas_call(kernel, out_shape=out_shape, in_specs=[SMEM] * len(scalars...]
    ppermute x2, starting transfers between devices: 2.81 us -> 0.34 us  [on_device(): theirs = lax.ppermute(mine, 'term', pairs_low(ranks)) if low > 1 else mine]
    ppermute x12, waiting for transfers between devices: 6.15 us -> 3.72 us  [high_parts(): lax.ppermute(total[k].astype(jnp.bfloat16), 'term', pairs_high(ranks, low...]
    ppermute x4, waiting for transfers between devices: 5.19 us -> 3.34 us  [low_sum(): got = lax.ppermute(send, 'term', pairs_low(ranks))]
    ppermute x4, starting transfers between devices: 7.47 us -> 5.71 us  [low_sum(): got = lax.ppermute(send, 'term', pairs_low(ranks))]
    ppermute x2, waiting for transfers between devices: 5.17 us -> 6.1 us  [on_device(): theirs = lax.ppermute(mine, 'term', pairs_low(ranks)) if low > 1 else mine]
  transfers between devices with their start and end apart: 31 -> 31, of which waited for: 13 -> 12; matrix products, arithmetic and copies ran while one was open for 1% -> 1% of each run, Pallas kernels for 19% -> 28%
where the time goes in v5:
time: 89.7 us; the launch traced here: 89.3 us
  starting transfers between devices  38.6 us (43%)
  Pallas kernels  28.4 us (32%)
  waiting for transfers between devices  20.5 us (23%)
  between operations  1 us (1%)
    pallas_call x15, Pallas kernels, call(): pl.pallas_call(kernel, out_shape=out_shape, in_specs=[SMEM] * len(scalars...  28.4 us
    ppermute x12, starting transfers between devices, high_parts(): lax.ppermute(total[k].astype(jnp.bfloat16), 'term', pairs_high(ranks, low...  18.7 us
    ppermute x6, starting transfers between devices, gather_high(): lax.ppermute(held, 'term', pairs_high(ranks, low, k))  8.91 us
    ppermute x2, waiting for transfers between devices, on_device(): theirs = lax.ppermute(mine, 'term', pairs_low(ranks)) if low > 1 else mine  6.1 us
    ppermute x4, starting transfers between devices, low_sum(): got = lax.ppermute(send, 'term', pairs_low(ranks))  5.71 us
    ppermute x6, waiting for transfers between devices, gather_high(): lax.ppermute(held, 'term', pairs_high(ranks, low, k))  4.67 us
    ppermute x12, waiting for transfers between devices, high_parts(): lax.ppermute(total[k].astype(jnp.bfloat16), 'term', pairs_high(ranks, low...  3.72 us
    ppermute x4, waiting for transfers between devices, low_sum(): got = lax.ppermute(send, 'term', pairs_low(ranks))  3.34 us
  transfers between devices with their start and end apart: 31, of which 12 were waited for; matrix products, arithmetic and copies ran while one was open for 1% of the time, Pallas kernels for 28%

profile of v5, /device:TPU:0, one launch (start us, length us, event | category | flops | bytes accessed | tf_op | source)
XLA Modules:
  0.0 89.3 jit_solution(3263067542183641139)
XLA Ops:
  0.6 1.6 %first.5 = (bf16[2,512,512]{2,1,0:T(8,128)(2,1)S(1)}, bf16[512,512]{1,0:T(8,128)(2,1)S(1)}, bf16[512,512]{1,0:T(8,128)(2,1)S(1)}) custom-call(s32[2]{0:T(128)} %size_ref.9, f32[2,512,512]{2,1,0:T(8,128)} %vector_ref.3), custom_call_target="tpu_custom_call" | custom-call | flops 1048576 | bytes 4096 | tf_op jit(solution)/shard_map/first/pallas_call | solution.py:306
  2.3 0.5 collective-permute-start
  2.8 0.7 collective-permute-start.5
  3.5 0.8 collective-permute-done.refs_0_
  4.3 4.1 %first.6 = (bf16[256,512]{1,0:T(8,128)(2,1)S(1)}, bf16[4,512,512]{2,1,0:T(8,128)(2,1)S(1)}, bf16[4,512,512]{2,1,0:T(8,128)(2,1)S(1)}, f32[2,64,512]{2,1,0:T(8,128)S(1)}) custom-call(bf16[2,512,512]{2,1,0:T(8,128)(2,1)S(1)} %get-tuple-element.43.own, bf16[512,512]{1,0:T(8,128)(2,1)S(1)} %collective-permute-done.refs_0_, s32[4]{0:T(128)} %shift_ref.13, ...), custom_call_target="tpu_custom_call" | custom-call | flops 1073741824 | bytes 4194304 | tf_op jit(solution)/shard_map/first/pallas_call | solution.py:306
  8.4 3.0 %collective-permute-start.1 = (bf16[256,512]{1,0:T(8,128)(2,1)S(1)}, bf16[256,512]{1,0:T(8,128)(2,1)S(1)}, u32[]{:S(2)}, u32[]{:S(2)}) collective-permute-start(bf16[256,512]{1,0:T(8,128)(2,1)S(1)} %get-tuple-element.40), channel_id=1, source_target_pairs={{0,1},{1,0},{2,3},{3,2},{4,5},{5,4},{6,7},{7,6},{8,9},{9,8},{10,11... | collective-permute-start | bytes 786440 | tf_op jit(solution)/shard_map/first/ppermute | solution.py:352
  11.4 2.7 %first.7 = f32[256,512]{1,0:T(8,128)S(1)} custom-call(s32[4]{0:T(128)S(1)} %copy-done.1, bf16[2,512,512]{2,1,0:T(8,128)(2,1)S(1)} %get-tuple-element.43.own, bf16[4,512,512]{2,1,0:T(8,128)(2,1)S(1)} %get-tuple-element.38.left, bf16[4,512,512]{2,1,0:T(8,128)(2,1)S(1)} %get-tuple-element.39.right, bf16[512,512]{1,0:T(8,128)(2,1)S(1)} %collective-permute-done.refs_0_), custom_call_target="tpu_custom_call" | custom-call | flops 1073741824 | bytes 4194304 | tf_op jit(solution)/shard_map/first/pallas_call | solution.py:306
  14.1 3.7 %first.8 = (bf16[256,512]{1,0:T(8,128)(2,1)S(1)}, bf16[4,512,512]{2,1,0:T(8,128)(2,1)S(1)}, bf16[4,512,512]{2,1,0:T(8,128)(2,1)S(1)}) custom-call(bf16[2,512,512]{2,1,0:T(8,128)(2,1)S(1)} %get-tuple-element.43.own, bf16[512,512]{1,0:T(8,128)(2,1)S(1)} %collective-permute-done.5.refs_0_, s32[4]{0:T(128)} %shift_ref.13, s32[2]{0:T(128)} %size_ref.9, ...), custom_call_target="tpu_custom_call" | custom-call | flops 1073741824 | bytes 4194304 | tf_op jit(solution)/shard_map/first/pallas_call | solution.py:306
  18.0 4.2 %collective-permute-start.2 = (bf16[64,512]{1,0:T(8,128)(2,1)S(1)}, bf16[64,512]{1,0:T(8,128)(2,1)S(1)}, u32[]{:S(2)}, u32[]{:S(2)}) collective-permute-start(bf16[64,512]{1,0:T(8,128)(2,1)S(1)} %get-tuple-element.91), channel_id=1, source_target_pairs={{0,6},{1,7},{2,4},{3,5},{4,2},{5,3},{6,0},{7,1},{8,14},{9,15},{10,... | collective-permute-start | bytes 196616 | tf_op jit(solution)/shard_map/gather/ppermute | solution.py:374
  22.2 0.6 collective-permute-start.4
  22.9 1.7 %first.9 = f32[256,512]{1,0:T(8,128)S(1)} custom-call(s32[4]{0:T(128)S(1)} %copy-done.2, bf16[2,512,512]{2,1,0:T(8,128)(2,1)S(1)} %get-tuple-element.43.own, bf16[4,512,512]{2,1,0:T(8,128)(2,1)S(1)} %get-tuple-element.45.left, bf16[4,512,512]{2,1,0:T(8,128)(2,1)S(1)} %get-tuple-element.46.right, bf16[512,512]{1,0:T(8,128)(2,1)S(1)} %collective-permute-done.5.refs_0_), custom_call_target="tpu_custom_call" | custom-call | flops 1073741824 | bytes 4194304 | tf_op jit(solution)/shard_map/first/pallas_call | solution.py:306
  24.6 2.1 %collective-permute-done.6 = bf16[256,512]{1,0:T(8,128)(2,1)S(1)} collective-permute-done((bf16[256,512]{1,0:T(8,128)(2,1)S(1)}, bf16[256,512]{1,0:T(8,128)(2,1)S(1)}, u32[]{:S(2)}, u32[]{:S(2)}) %collective-permute-start.6) | collective-permute-done | bytes 262176 | tf_op jit(solution)/shard_map/first/ppermute | solution.py:352
  26.8 3.7 %collective-permute-start.7 = (bf16[64,512]{1,0:T(8,128)(2,1)S(1)}, bf16[64,512]{1,0:T(8,128)(2,1)S(1)}, u32[]{:S(2)}, u32[]{:S(2)}) collective-permute-start(bf16[64,512]{1,0:T(8,128)(2,1)S(1)} %get-tuple-element.88), channel_id=1, source_target_pairs={{0,6},{1,7},{2,4},{3,5},{4,2},{5,3},{6,0},{7,1},{8,14},{9,15},{10,... | collective-permute-start | bytes 196616 | tf_op jit(solution)/shard_map/gather/ppermute | solution.py:374
  30.6 0.7 collective-permute-start.9
  31.4 0.7 gather.2
  32.1 3.7 %collective-permute-start.12 = (bf16[1,64,512]{2,1,0:T(8,128)(2,1)S(1)}, bf16[1,64,512]{2,1,0:T(8,128)(2,1)S(1)}, u32[]{:S(2)}, u32[]{:S(2)}) collective-permute-start(bf16[1,64,512]{2,1,0:T(8,128)(2,1)S(1)} %bitcast.14), channel_id=1, source_target_pairs={{0,6},{1,7},{2,4},{3,5},{4,2},{5,3},{6,0},{7,1},{8,14},{9,15},{10,... | collective-permute-start | bytes 196616 | tf_op jit(solution)/shard_map/gather/ppermute | solution.py:379
  35.8 0.8 collective-permute-start.10
  36.5 1.3 %collective-permute-done.8.refs_2_ = bf16[64,512]{1,0:T(8,128)(2,1)S(1)} collective-permute-done((bf16[64,512]{1,0:T(8,128)(2,1)S(1)}, bf16[64,512]{1,0:T(8,128)(2,1)S(1)}, u32[]{:S(2)}, u32[]{:S(2)}) %collective-permute-start.8) | collective-permute-done | bytes 65568 | tf_op jit(solution)/shard_map/gather/ppermute | solution.py:374
  37.8 0.7 gather.3
  38.5 2.4 %collective-permute-start.16 = (bf16[1,64,512]{2,1,0:T(8,128)(2,1)S(1)}, bf16[1,64,512]{2,1,0:T(8,128)(2,1)S(1)}, u32[]{:S(2)}, u32[]{:S(2)}) collective-permute-start(bf16[1,64,512]{2,1,0:T(8,128)(2,1)S(1)} %bitcast.18), channel_id=1, source_target_pairs={{0,6},{1,7},{2,4},{3,5},{4,2},{5,3},{6,0},{7,1},{8,14},{9,15},{10,... | collective-permute-start | bytes 196616 | tf_op jit(solution)/shard_map/gather/ppermute | solution.py:379
  40.9 2.1 %collective-permute-start.14 = (bf16[1,64,512]{2,1,0:T(8,128)(2,1)S(1)}, bf16[1,64,512]{2,1,0:T(8,128)(2,1)S(1)}, u32[]{:S(2)}, u32[]{:S(2)}) collective-permute-start(bf16[1,64,512]{2,1,0:T(8,128)(2,1)S(1)} %bitcast.20), channel_id=1, source_target_pairs={{0,2},{1,3},{2,0},{3,1},{4,6},{5,7},{6,4},{7,5},{8,10},{9,11},{10,... | collective-permute-start | bytes 196616 | tf_op jit(solution)/shard_map/gather/ppermute | solution.py:379
  43.0 0.9 %collective-permute-done.11 = bf16[1,64,512]{2,1,0:T(8,128)(2,1)S(1)} collective-permute-done((bf16[1,64,512]{2,1,0:T(8,128)(2,1)S(1)}, bf16[1,64,512]{2,1,0:T(8,128)(2,1)S(1)}, u32[]{:S(2)}, u32[]{:S(2)}) %collective-permute-start.11) | collective-permute-done | bytes 65568 | tf_op jit(solution)/shard_map/gather/ppermute | solution.py:379
  44.1 1.2 %collective-permute-done.16 = bf16[1,64,512]{2,1,0:T(8,128)(2,1)S(1)} collective-permute-done((bf16[1,64,512]{2,1,0:T(8,128)(2,1)S(1)}, bf16[1,64,512]{2,1,0:T(8,128)(2,1)S(1)}, u32[]{:S(2)}, u32[]{:S(2)}) %collective-permute-start.16) | collective-permute-done | bytes 65568 | tf_op jit(solution)/shard_map/gather/ppermute | solution.py:379
  45.2 2.5 %collective-permute-done.15 = bf16[1,64,512]{2,1,0:T(8,128)(2,1)S(1)} collective-permute-done((bf16[1,64,512]{2,1,0:T(8,128)(2,1)S(1)}, bf16[1,64,512]{2,1,0:T(8,128)(2,1)S(1)}, u32[]{:S(2)}, u32[]{:S(2)}) %collective-permute-start.15) | collective-permute-done | bytes 65568 | tf_op jit(solution)/shard_map/gather/ppermute | solution.py:379
  47.8 0.3 collective-permute-start.17
  48.1 4.7 %collective-permute-done.13.theirs = bf16[4,64,512]{2,1,0:T(8,128)(2,1)S(1)} collective-permute-done((bf16[4,64,512]{2,1,0:T(8,128)(2,1)S(1)}, bf16[4,64,512]{2,1,0:T(8,128)(2,1)S(1)}, u32[]{:S(2)}, u32[]{:S(2)}) %collective-permute-start.13) | collective-permute-done | bytes 262176 | tf_op jit(solution)/shard_map/gather/ppermute | solution.py:435
  52.9 1.9 %second.7 = (bf16[512,512]{1,0:T(8,128)(2,1)S(1)}, f32[256,512]{1,0:T(8,128)S(1)}, f32[256,512]{1,0:T(8,128)S(1)}) custom-call(s32[4]{0:T(128)S(1)} %copy-done.2, bf16[4,512,512]{2,1,0:T(8,128)(2,1)S(1)} %get-tuple-element.38.left, bf16[4,512,512]{2,1,0:T(8,128)(2,1)S(1)} %get-tuple-element.39.right, bf16[4,64,512]{2,1,0:T(8,128)(2,1)S(1)} %get-tuple-element.85.mine, ...), custom_call_target="tpu_custom_call" | custom-call | flops 1 | tf_op jit(solution)/shard_map/second/pallas_call | solution.py:306
  54.8 1.0 %second.8 = f32[8,512]{1,0:T(8,128)S(1)} custom-call(s32[2]{0:T(128)S(1)} %copy-done.3, f32[2,512,512]{2,1,0:T(8,128)S(1)} %copy-done, bf16[512,512]{1,0:T(8,128)(2,1)S(1)} %get-tuple-element.57.block.refs_2_), custom_call_target="tpu_custom_call" | custom-call | flops 1 | tf_op jit(solution)/shard_map/second/pallas_call | solution.py:306
  55.9 1.4 %collective-permute-done.17.refs_4_ = bf16[4,64,512]{2,1,0:T(8,128)(2,1)S(1)} collective-permute-done((bf16[4,64,512]{2,1,0:T(8,128)(2,1)S(1)}, bf16[4,64,512]{2,1,0:T(8,128)(2,1)S(1)}, u32[]{:S(2)}, u32[]{:S(2)}) %collective-permute-start.17) | collective-permute-done | bytes 262176 | tf_op jit(solution)/shard_map/gather/ppermute | solution.py:435
  57.3 0.7 collective-permute-start.23
  58.0 1.2 %collective-permute-done.18.refs_0_ = bf16[2,4,64,512]{3,2,1,0:T(8,128)(2,1)S(1)} collective-permute-done((bf16[2,4,64,512]{3,2,1,0:T(8,128)(2,1)S(1)}, bf16[2,4,64,512]{3,2,1,0:T(8,128)(2,1)S(1)}, u32[]{:S(2)}, u32[]{:S(2)}) %collective-permute-start.18) | collective-permute-done | bytes 524320 | tf_op jit(solution)/shard_map/second/ppermute | solution.py:347
  59.1 2.3 %second.9 = (bf16[256,512]{1,0:T(8,128)(2,1)S(1)}, bf16[2,512,512]{2,1,0:T(8,128)(2,1)S(1)}, bf16[2,512,512]{2,1,0:T(8,128)(2,1)S(1)}) custom-call(s32[4]{0:T(128)S(1)} %copy-done.2, bf16[4,512,512]{2,1,0:T(8,128)(2,1)S(1)} %get-tuple-element.38.left, bf16[4,512,512]{2,1,0:T(8,128)(2,1)S(1)} %get-tuple-element.39.right, ...), custom_call_target="tpu_custom_call" | custom-call | flops 536870912 | bytes 2097152 | tf_op jit(solution)/shard_map/second/pallas_call | solution.py:306
  61.4 1.1 %collective-permute-start.19 = (bf16[256,512]{1,0:T(8,128)(2,1)S(1)}, bf16[256,512]{1,0:T(8,128)(2,1)S(1)}, u32[]{:S(2)}, u32[]{:S(2)}) collective-permute-start(bf16[256,512]{1,0:T(8,128)(2,1)S(1)} %get-tuple-element.61), channel_id=1, source_target_pairs={{0,1},{1,0},{2,3},{3,2},{4,5},{5,4},{6,7},{7,6},{8,9},{9,8},{10,11... | collective-permute-start | bytes 786440 | tf_op jit(solution)/shard_map/second/ppermute | solution.py:352
  62.6 1.0 %second.11 = f32[8,512]{1,0:T(8,128)S(1)} custom-call(s32[2]{0:T(128)S(1)} %copy-done.3, f32[2,512,512]{2,1,0:T(8,128)S(1)} %copy-done, bf16[2,512,512]{2,1,0:T(8,128)(2,1)S(1)} %get-tuple-element.64.own.block.refs_1_), custom_call_target="tpu_custom_call" | custom-call | flops 1 | tf_op jit(solution)/shard_map/second/pallas_call | solution.py:306
  63.6 2.2 %second.10 = f32[256,512]{1,0:T(8,128)S(1)} custom-call(s32[4]{0:T(128)S(1)} %copy-done.2, bf16[2,512,512]{2,1,0:T(8,128)(2,1)S(1)} %get-tuple-element.64.own.block.refs_1_, bf16[4,512,512]{2,1,0:T(8,128)(2,1)S(1)} %get-tuple-element.38.left, bf16[4,512,512]{2,1,0:T(8,128)(2,1)S(1)} %get-tuple-element.39.right, ...), custom_call_target="tpu_custom_call" | custom-call | flops 1073741824 | bytes 4194304 | tf_op jit(solution)/shard_map/second/pallas_call | solution.py:306
  65.8 1.7 %second.12 = (bf16[256,512]{1,0:T(8,128)(2,1)S(1)}, bf16[2,512,512]{2,1,0:T(8,128)(2,1)S(1)}) custom-call(s32[4]{0:T(128)S(1)} %copy-done.2, bf16[4,512,512]{2,1,0:T(8,128)(2,1)S(1)} %get-tuple-element.45.left, bf16[4,512,512]{2,1,0:T(8,128)(2,1)S(1)} %get-tuple-element.46.right, bf16[2,4,64,512]{3,2,1,0:T(8,128)(2,1)S(1)} %collective-permute-done.23.refs_0_, ...), custom_call_target="tpu_custom_call" | custom-call | flops 1073741824 | bytes 4194304 | tf_op jit(solution)/shard_map/second/pallas_call | solution.py:306
  67.5 1.5 %collective-permute-start.24 = (bf16[256,512]{1,0:T(8,128)(2,1)S(1)}, bf16[256,512]{1,0:T(8,128)(2,1)S(1)}, u32[]{:S(2)}, u32[]{:S(2)}) collective-permute-start(bf16[256,512]{1,0:T(8,128)(2,1)S(1)} %get-tuple-element.66), channel_id=1, source_target_pairs={{0,1},{1,0},{2,3},{3,2},{4,5},{5,4},{6,7},{7,6},{8,9},{9,8},{10,11... | collective-permute-start | bytes 786440 | tf_op jit(solution)/shard_map/second/ppermute | solution.py:352
  69.1 1.2 %collective-permute-done.19 = bf16[256,512]{1,0:T(8,128)(2,1)S(1)} collective-permute-done((bf16[256,512]{1,0:T(8,128)(2,1)S(1)}, bf16[256,512]{1,0:T(8,128)(2,1)S(1)}, u32[]{:S(2)}, u32[]{:S(2)}) %collective-permute-start.19) | collective-permute-done | bytes 262176 | tf_op jit(solution)/shard_map/second/ppermute | solution.py:352
  70.4 3.3 %collective-permute-start.20 = (bf16[64,512]{1,0:T(8,128)(2,1)S(1)}, bf16[64,512]{1,0:T(8,128)(2,1)S(1)}, u32[]{:S(2)}, u32[]{:S(2)}) collective-permute-start(bf16[64,512]{1,0:T(8,128)(2,1)S(1)} %get-tuple-element.83), channel_id=1, source_target_pairs={{0,6},{1,7},{2,4},{3,5},{4,2},{5,3},{6,0},{7,1},{8,14},{9,15},{10,... | collective-permute-start | bytes 196616 | tf_op jit(solution)/shard_map/scalars/ppermute | solution.py:374
  73.7 1.2 %collective-permute-start.22 = (bf16[64,512]{1,0:T(8,128)(2,1)S(1)}, bf16[64,512]{1,0:T(8,128)(2,1)S(1)}, u32[]{:S(2)}, u32[]{:S(2)}) collective-permute-start(bf16[64,512]{1,0:T(8,128)(2,1)S(1)} %get-tuple-element.81), channel_id=1, source_target_pairs={{0,2},{1,3},{2,0},{3,1},{4,6},{5,7},{6,4},{7,5},{8,10},{9,11},{10,... | collective-permute-start | bytes 196616 | tf_op jit(solution)/shard_map/scalars/ppermute | solution.py:374
  74.9 1.7 %second.13 = f32[256,512]{1,0:T(8,128)S(1)} custom-call(s32[4]{0:T(128)S(1)} %copy-done.2, bf16[2,512,512]{2,1,0:T(8,128)(2,1)S(1)} %get-tuple-element.64.own.block.refs_1_, bf16[4,512,512]{2,1,0:T(8,128)(2,1)S(1)} %get-tuple-element.45.left, bf16[4,512,512]{2,1,0:T(8,128)(2,1)S(1)} %get-tuple-element.46.right, bf16[512,512]{1,0:T(8,128)(2,1)S(1)} %slice_bitcast_fusion.refs_0_), custom_call_target="tpu_custom_call" | custom-call | flops 1073741824 | bytes 4194304 | tf_op jit(solution)/shard_map/second/pallas_call | solution.py:306
  76.7 4.3 %collective-permute-start.25 = (bf16[64,512]{1,0:T(8,128)(2,1)S(1)}, bf16[64,512]{1,0:T(8,128)(2,1)S(1)}, u32[]{:S(2)}, u32[]{:S(2)}) collective-permute-start(bf16[64,512]{1,0:T(8,128)(2,1)S(1)} %get-tuple-element.78), channel_id=1, source_target_pairs={{0,6},{1,7},{2,4},{3,5},{4,2},{5,3},{6,0},{7,1},{8,14},{9,15},{10,... | collective-permute-start | bytes 196616 | tf_op jit(solution)/shard_map/scalars/ppermute | solution.py:374
  81.0 0.6 collective-permute-start.27
  81.6 1.3 %collective-permute-start.28 = (f32[8,512]{1,0:T(8,128)S(1)}, f32[8,512]{1,0:T(8,128)S(1)}, u32[]{:S(2)}, u32[]{:S(2)}) collective-permute-start(f32[8,512]{1,0:T(8,128)S(1)} %add.19.refs_14_), channel_id=1, source_target_pairs={{0,8},{8,0},{16,24},{24,16},{1,9},{9,1},{17,25},{25,17},{2,10},{10... | collective-permute-start | bytes 49160 | tf_op jit(solution)/shard_map/scalars/ppermute | solution.py:504
  82.9 1.6 %collective-permute-start.29 = (f32[8,512]{1,0:T(8,128)S(1)}, f32[8,512]{1,0:T(8,128)S(1)}, u32[]{:S(2)}, u32[]{:S(2)}) collective-permute-start(f32[8,512]{1,0:T(8,128)S(1)} %add.19.refs_14_), channel_id=1, source_target_pairs={{0,16},{8,24},{16,0},{24,8},{1,17},{9,25},{17,1},{25,9},{2,18},{10... | collective-permute-start | bytes 49160 | tf_op jit(solution)/shard_map/scalars/ppermute | solution.py:504
  84.7 2.4 %collective-permute-done.26.refs_12_ = bf16[64,512]{1,0:T(8,128)(2,1)S(1)} collective-permute-done((bf16[64,512]{1,0:T(8,128)(2,1)S(1)}, bf16[64,512]{1,0:T(8,128)(2,1)S(1)}, u32[]{:S(2)}, u32[]{:S(2)}) %collective-permute-start.26) | collective-permute-done | bytes 65568 | tf_op jit(solution)/shard_map/scalars/ppermute | solution.py:374
  87.1 0.6 collective-permute-done.30.refs_17_
  87.7 1.5 %scalars.1 = (f32[2,64,512]{2,1,0:T(8,128)}, f32[2,64,512]{2,1,0:T(8,128)}) custom-call(s32[2]{0:T(128)S(1)} %copy-done.3, f32[2,64,512]{2,1,0:T(8,128)S(1)} %get-tuple-element.37.start, f32[64,512]{1,0:T(8,128)S(1)} %get-tuple-element.41.refs_0_, f32[64,512]{1,0:T(8,128)S(1)} %get-tuple-element.48.refs_1_, f32[64,512]{1,0:T(8,128)S(1)} %get-tuple-element.49.refs_2_, ...), custom_call_target="tpu_custom_call" | custom-call | flops 1048576 | bytes 4096 | tf_op jit(solution)/shard_map/scalars/pallas_call | solution.py:306
  (60 shorter events, 1.2 us)
Async XLA Ops:
  2.3 2.1 %collective-permute-start = (bf16[512,512]{1,0:T(8,128)(2,1)S(1)}, bf16[512,512]{1,0:T(8,128)(2,1)S(1)}, u32[]{:S(2)}, u32[]{:S(2)}) collective-permute-start(bf16[512,512]{1,0:T(8,128)(2,1)S(1)} %get-tuple-element.36), channel_id=1, source_target_pairs={{0,8},{8,0},{16,24},{24,16},{1,9},{9,1},{17,25},{25,17},{2,10},{10... | collective-permute-start | bytes 1572872 | tf_op jit(solution)/shard_map/first/ppermute | solution.py:347
  2.8 11.3 %collective-permute-start.5 = (bf16[512,512]{1,0:T(8,128)(2,1)S(1)}, bf16[512,512]{1,0:T(8,128)(2,1)S(1)}, u32[]{:S(2)}, u32[]{:S(2)}) collective-permute-start(bf16[512,512]{1,0:T(8,128)(2,1)S(1)} %get-tuple-element.44), channel_id=1, source_target_pairs={{8,16},{16,8},{9,17},{17,9},{10,18},{18,10},{11,19},{19,11},{12,20... | collective-permute-start | bytes 1572872 | tf_op jit(solution)/shard_map/first/ppermute | solution.py:347
  3.5 7.9 %copy-start.1 = (s32[4]{0:T(128)S(1)}, s32[4]{0:T(128)}, u32[]{:S(2)}) copy-start(s32[4]{0:T(128)} %shift_ref.13) | copy-start | bytes 52
  8.4 9.4 %collective-permute-start.1 = (bf16[256,512]{1,0:T(8,128)(2,1)S(1)}, bf16[256,512]{1,0:T(8,128)(2,1)S(1)}, u32[]{:S(2)}, u32[]{:S(2)}) collective-permute-start(bf16[256,512]{1,0:T(8,128)(2,1)S(1)} %get-tuple-element.40), channel_id=1, source_target_pairs={{0,1},{1,0},{2,3},{3,2},{4,5},{5,4},{6,7},{7,6},{8,9},{9,8},{10,11... | collective-permute-start | bytes 786440 | tf_op jit(solution)/shard_map/first/ppermute | solution.py:352
  14.1 8.8 %copy-start.2 = (s32[4]{0:T(128)S(1)}, s32[4]{0:T(128)}, u32[]{:S(2)}) copy-start(s32[4]{0:T(128)} %shift_ref.13) | copy-start | bytes 52
  17.8 8.9 %collective-permute-start.6 = (bf16[256,512]{1,0:T(8,128)(2,1)S(1)}, bf16[256,512]{1,0:T(8,128)(2,1)S(1)}, u32[]{:S(2)}, u32[]{:S(2)}) collective-permute-start(bf16[256,512]{1,0:T(8,128)(2,1)S(1)} %get-tuple-element.47), channel_id=1, source_target_pairs={{0,1},{1,0},{2,3},{3,2},{4,5},{5,4},{6,7},{7,6},{8,9},{9,8},{10,11... | collective-permute-start | bytes 786440 | tf_op jit(solution)/shard_map/first/ppermute | solution.py:352
  18.0 12.6 %collective-permute-start.2 = (bf16[64,512]{1,0:T(8,128)(2,1)S(1)}, bf16[64,512]{1,0:T(8,128)(2,1)S(1)}, u32[]{:S(2)}, u32[]{:S(2)}) collective-permute-start(bf16[64,512]{1,0:T(8,128)(2,1)S(1)} %get-tuple-element.91), channel_id=1, source_target_pairs={{0,6},{1,7},{2,4},{3,5},{4,2},{5,3},{6,0},{7,1},{8,14},{9,15},{10,... | collective-permute-start | bytes 196616 | tf_op jit(solution)/shard_map/gather/ppermute | solution.py:374
  22.2 9.1 %collective-permute-start.3 = (bf16[64,512]{1,0:T(8,128)(2,1)S(1)}, bf16[64,512]{1,0:T(8,128)(2,1)S(1)}, u32[]{:S(2)}, u32[]{:S(2)}) collective-permute-start(bf16[64,512]{1,0:T(8,128)(2,1)S(1)} %get-tuple-element.90), channel_id=1, source_target_pairs={{0,4},{1,5},{2,6},{3,7},{4,0},{5,1},{6,2},{7,3},{8,12},{9,13},{10,... | collective-permute-start | bytes 196616 | tf_op jit(solution)/shard_map/gather/ppermute | solution.py:374
  22.2 9.1 %collective-permute-start.4 = (bf16[64,512]{1,0:T(8,128)(2,1)S(1)}, bf16[64,512]{1,0:T(8,128)(2,1)S(1)}, u32[]{:S(2)}, u32[]{:S(2)}) collective-permute-start(bf16[64,512]{1,0:T(8,128)(2,1)S(1)} %get-tuple-element.89), channel_id=1, source_target_pairs={{0,2},{1,3},{2,0},{3,1},{4,6},{5,7},{6,4},{7,5},{8,10},{9,11},{10,... | collective-permute-start | bytes 196616 | tf_op jit(solution)/shard_map/gather/ppermute | solution.py:374
  24.5 6.8 %copy-start.3 = (s32[2]{0:T(128)S(1)}, s32[2]{0:T(128)}, u32[]{:S(2)}) copy-start(s32[2]{0:T(128)} %size_ref.9) | copy-start | bytes 28
  24.5 6.8 %copy-start.4 = (f32[2,512]{1,0:T(2,128)S(1)}, f32[2,512]{1,0:T(2,128)}, u32[]{:S(2)}) copy-start(f32[2,512]{1,0:T(2,128)} %left_row.3) | copy-start | bytes 12292
  24.6 6.8 %copy-start.5 = (f32[2,512]{1,0:T(2,128)S(1)}, f32[2,512]{1,0:T(2,128)}, u32[]{:S(2)}) copy-start(f32[2,512]{1,0:T(2,128)} %right_row.3) | copy-start | bytes 12292
  26.8 8.9 %collective-permute-start.7 = (bf16[64,512]{1,0:T(8,128)(2,1)S(1)}, bf16[64,512]{1,0:T(8,128)(2,1)S(1)}, u32[]{:S(2)}, u32[]{:S(2)}) collective-permute-start(bf16[64,512]{1,0:T(8,128)(2,1)S(1)} %get-tuple-element.88), channel_id=1, source_target_pairs={{0,6},{1,7},{2,4},{3,5},{4,2},{5,3},{6,0},{7,1},{8,14},{9,15},{10,... | collective-permute-start | bytes 196616 | tf_op jit(solution)/shard_map/gather/ppermute | solution.py:374
  30.5 7.3 %collective-permute-start.8 = (bf16[64,512]{1,0:T(8,128)(2,1)S(1)}, bf16[64,512]{1,0:T(8,128)(2,1)S(1)}, u32[]{:S(2)}, u32[]{:S(2)}) collective-permute-start(bf16[64,512]{1,0:T(8,128)(2,1)S(1)} %get-tuple-element.87), channel_id=1, source_target_pairs={{0,4},{1,5},{2,6},{3,7},{4,0},{5,1},{6,2},{7,3},{8,12},{9,13},{10,... | collective-permute-start | bytes 196616 | tf_op jit(solution)/shard_map/gather/ppermute | solution.py:374
  30.6 7.2 %collective-permute-start.9 = (bf16[64,512]{1,0:T(8,128)(2,1)S(1)}, bf16[64,512]{1,0:T(8,128)(2,1)S(1)}, u32[]{:S(2)}, u32[]{:S(2)}) collective-permute-start(bf16[64,512]{1,0:T(8,128)(2,1)S(1)} %get-tuple-element.86), channel_id=1, source_target_pairs={{0,2},{1,3},{2,0},{3,1},{4,6},{5,7},{6,4},{7,5},{8,10},{9,11},{10,... | collective-permute-start | bytes 196616 | tf_op jit(solution)/shard_map/gather/ppermute | solution.py:374
  32.1 8.9 %collective-permute-start.12 = (bf16[1,64,512]{2,1,0:T(8,128)(2,1)S(1)}, bf16[1,64,512]{2,1,0:T(8,128)(2,1)S(1)}, u32[]{:S(2)}, u32[]{:S(2)}) collective-permute-start(bf16[1,64,512]{2,1,0:T(8,128)(2,1)S(1)} %bitcast.14), channel_id=1, source_target_pairs={{0,6},{1,7},{2,4},{3,5},{4,2},{5,3},{6,0},{7,1},{8,14},{9,15},{10,... | collective-permute-start | bytes 196616 | tf_op jit(solution)/shard_map/gather/ppermute | solution.py:379
  35.8 8.2 %collective-permute-start.11 = (bf16[1,64,512]{2,1,0:T(8,128)(2,1)S(1)}, bf16[1,64,512]{2,1,0:T(8,128)(2,1)S(1)}, u32[]{:S(2)}, u32[]{:S(2)}) collective-permute-start(bf16[1,64,512]{2,1,0:T(8,128)(2,1)S(1)} %bitcast.15), channel_id=1, source_target_pairs={{0,4},{1,5},{2,6},{3,7},{4,0},{5,1},{6,2},{7,3},{8,12},{9,13},{10,... | collective-permute-start | bytes 196616 | tf_op jit(solution)/shard_map/gather/ppermute | solution.py:379
  35.8 8.2 %collective-permute-start.10 = (bf16[1,64,512]{2,1,0:T(8,128)(2,1)S(1)}, bf16[1,64,512]{2,1,0:T(8,128)(2,1)S(1)}, u32[]{:S(2)}, u32[]{:S(2)}) collective-permute-start(bf16[1,64,512]{2,1,0:T(8,128)(2,1)S(1)} %bitcast.16), channel_id=1, source_target_pairs={{0,2},{1,3},{2,0},{3,1},{4,6},{5,7},{6,4},{7,5},{8,10},{9,11},{10,... | collective-permute-start | bytes 196616 | tf_op jit(solution)/shard_map/gather/ppermute | solution.py:379
  38.5 6.7 %collective-permute-start.16 = (bf16[1,64,512]{2,1,0:T(8,128)(2,1)S(1)}, bf16[1,64,512]{2,1,0:T(8,128)(2,1)S(1)}, u32[]{:S(2)}, u32[]{:S(2)}) collective-permute-start(bf16[1,64,512]{2,1,0:T(8,128)(2,1)S(1)} %bitcast.18), channel_id=1, source_target_pairs={{0,6},{1,7},{2,4},{3,5},{4,2},{5,3},{6,0},{7,1},{8,14},{9,15},{10,... | collective-permute-start | bytes 196616 | tf_op jit(solution)/shard_map/gather/ppermute | solution.py:379
  40.9 6.9 %collective-permute-start.15 = (bf16[1,64,512]{2,1,0:T(8,128)(2,1)S(1)}, bf16[1,64,512]{2,1,0:T(8,128)(2,1)S(1)}, u32[]{:S(2)}, u32[]{:S(2)}) collective-permute-start(bf16[1,64,512]{2,1,0:T(8,128)(2,1)S(1)} %bitcast.19), channel_id=1, source_target_pairs={{0,4},{1,5},{2,6},{3,7},{4,0},{5,1},{6,2},{7,3},{8,12},{9,13},{10,... | collective-permute-start | bytes 196616 | tf_op jit(solution)/shard_map/gather/ppermute | solution.py:379
  40.9 6.9 %collective-permute-start.14 = (bf16[1,64,512]{2,1,0:T(8,128)(2,1)S(1)}, bf16[1,64,512]{2,1,0:T(8,128)(2,1)S(1)}, u32[]{:S(2)}, u32[]{:S(2)}) collective-permute-start(bf16[1,64,512]{2,1,0:T(8,128)(2,1)S(1)} %bitcast.20), channel_id=1, source_target_pairs={{0,2},{1,3},{2,0},{3,1},{4,6},{5,7},{6,4},{7,5},{8,10},{9,11},{10,... | collective-permute-start | bytes 196616 | tf_op jit(solution)/shard_map/gather/ppermute | solution.py:379
  44.0 8.9 %collective-permute-start.13 = (bf16[4,64,512]{2,1,0:T(8,128)(2,1)S(1)}, bf16[4,64,512]{2,1,0:T(8,128)(2,1)S(1)}, u32[]{:S(2)}, u32[]{:S(2)}) collective-permute-start(bf16[4,64,512]{2,1,0:T(8,128)(2,1)S(1)} %get-tuple-element.85.mine), channel_id=1, source_target_pairs={{0,1},{1,0},{2,3},{3,2},{4,5},{5,4},{6,7},{7,6},{8,9},{9,8},{10,11... | collective-permute-start | bytes 786440 | tf_op jit(solution)/shard_map/gather/ppermute | solution.py:435
  47.8 6.9 %copy-start = (f32[2,512,512]{2,1,0:T(8,128)S(1)}, f32[2,512,512]{2,1,0:T(8,128)}, u32[]{:S(2)}) copy-start(f32[2,512,512]{2,1,0:T(8,128)} %vector_ref.3) | copy-start | bytes 6291460
  47.8 9.4 %collective-permute-start.17 = (bf16[4,64,512]{2,1,0:T(8,128)(2,1)S(1)}, bf16[4,64,512]{2,1,0:T(8,128)(2,1)S(1)}, u32[]{:S(2)}, u32[]{:S(2)}) collective-permute-start(bf16[4,64,512]{2,1,0:T(8,128)(2,1)S(1)} %get-tuple-element.80.refs_3_), channel_id=1, source_target_pairs={{0,1},{1,0},{2,3},{3,2},{4,5},{5,4},{6,7},{7,6},{8,9},{9,8},{10,11... | collective-permute-start | bytes 786440 | tf_op jit(solution)/shard_map/gather/ppermute | solution.py:435
  57.2 1.9 %collective-permute-start.18 = (bf16[2,4,64,512]{3,2,1,0:T(8,128)(2,1)S(1)}, bf16[2,4,64,512]{3,2,1,0:T(8,128)(2,1)S(1)}, u32[]{:S(2)}, u32[]{:S(2)}) collective-permute-start(bf16[2,4,64,512]{3,2,1,0:T(8,128)(2,1)S(1)} %pad_maximum_fusion), channel_id=1, source_target_pairs={{0,8},{8,0},{16,24},{24,16},{1,9},{9,1},{17,25},{25,17},{2,10},{10... | collective-permute-start | bytes 1572872 | tf_op jit(solution)/shard_map/second/ppermute | solution.py:347
  57.3 8.5 %collective-permute-start.23 = (bf16[2,4,64,512]{3,2,1,0:T(8,128)(2,1)S(1)}, bf16[2,4,64,512]{3,2,1,0:T(8,128)(2,1)S(1)}, u32[]{:S(2)}, u32[]{:S(2)}) collective-permute-start(bf16[2,4,64,512]{3,2,1,0:T(8,128)(2,1)S(1)} %pad_maximum_fusion.1), channel_id=1, source_target_pairs={{8,16},{16,8},{9,17},{17,9},{10,18},{18,10},{11,19},{19,11},{12,20... | collective-permute-start | bytes 1572872 | tf_op jit(solution)/shard_map/second/ppermute | solution.py:347
  61.4 8.9 %collective-permute-start.19 = (bf16[256,512]{1,0:T(8,128)(2,1)S(1)}, bf16[256,512]{1,0:T(8,128)(2,1)S(1)}, u32[]{:S(2)}, u32[]{:S(2)}) collective-permute-start(bf16[256,512]{1,0:T(8,128)(2,1)S(1)} %get-tuple-element.61), channel_id=1, source_target_pairs={{0,1},{1,0},{2,3},{3,2},{4,5},{5,4},{6,7},{7,6},{8,9},{9,8},{10,11... | collective-permute-start | bytes 786440 | tf_op jit(solution)/shard_map/second/ppermute | solution.py:352
  67.5 9.0 %collective-permute-start.24 = (bf16[256,512]{1,0:T(8,128)(2,1)S(1)}, bf16[256,512]{1,0:T(8,128)(2,1)S(1)}, u32[]{:S(2)}, u32[]{:S(2)}) collective-permute-start(bf16[256,512]{1,0:T(8,128)(2,1)S(1)} %get-tuple-element.66), channel_id=1, source_target_pairs={{0,1},{1,0},{2,3},{3,2},{4,5},{5,4},{6,7},{7,6},{8,9},{9,8},{10,11... | collective-permute-start | bytes 786440 | tf_op jit(solution)/shard_map/second/ppermute | solution.py:352
  70.4 11.2 %collective-permute-start.20 = (bf16[64,512]{1,0:T(8,128)(2,1)S(1)}, bf16[64,512]{1,0:T(8,128)(2,1)S(1)}, u32[]{:S(2)}, u32[]{:S(2)}) collective-permute-start(bf16[64,512]{1,0:T(8,128)(2,1)S(1)} %get-tuple-element.83), channel_id=1, source_target_pairs={{0,6},{1,7},{2,4},{3,5},{4,2},{5,3},{6,0},{7,1},{8,14},{9,15},{10,... | collective-permute-start | bytes 196616 | tf_op jit(solution)/shard_map/scalars/ppermute | solution.py:374
  73.7 9.2 %collective-permute-start.21 = (bf16[64,512]{1,0:T(8,128)(2,1)S(1)}, bf16[64,512]{1,0:T(8,128)(2,1)S(1)}, u32[]{:S(2)}, u32[]{:S(2)}) collective-permute-start(bf16[64,512]{1,0:T(8,128)(2,1)S(1)} %get-tuple-element.82), channel_id=1, source_target_pairs={{0,4},{1,5},{2,6},{3,7},{4,0},{5,1},{6,2},{7,3},{8,12},{9,13},{10,... | collective-permute-start | bytes 196616 | tf_op jit(solution)/shard_map/scalars/ppermute | solution.py:374
  73.7 7.3 %collective-permute-start.22 = (bf16[64,512]{1,0:T(8,128)(2,1)S(1)}, bf16[64,512]{1,0:T(8,128)(2,1)S(1)}, u32[]{:S(2)}, u32[]{:S(2)}) collective-permute-start(bf16[64,512]{1,0:T(8,128)(2,1)S(1)} %get-tuple-element.81), channel_id=1, source_target_pairs={{0,2},{1,3},{2,0},{3,1},{4,6},{5,7},{6,4},{7,5},{8,10},{9,11},{10,... | collective-permute-start | bytes 196616 | tf_op jit(solution)/shard_map/scalars/ppermute | solution.py:374
  76.7 7.9 %collective-permute-start.25 = (bf16[64,512]{1,0:T(8,128)(2,1)S(1)}, bf16[64,512]{1,0:T(8,128)(2,1)S(1)}, u32[]{:S(2)}, u32[]{:S(2)}) collective-permute-start(bf16[64,512]{1,0:T(8,128)(2,1)S(1)} %get-tuple-element.78), channel_id=1, source_target_pairs={{0,6},{1,7},{2,4},{3,5},{4,2},{5,3},{6,0},{7,1},{8,14},{9,15},{10,... | collective-permute-start | bytes 196616 | tf_op jit(solution)/shard_map/scalars/ppermute | solution.py:374
  81.0 6.1 %collective-permute-start.26 = (bf16[64,512]{1,0:T(8,128)(2,1)S(1)}, bf16[64,512]{1,0:T(8,128)(2,1)S(1)}, u32[]{:S(2)}, u32[]{:S(2)}) collective-permute-start(bf16[64,512]{1,0:T(8,128)(2,1)S(1)} %get-tuple-element.77), channel_id=1, source_target_pairs={{0,4},{1,5},{2,6},{3,7},{4,0},{5,1},{6,2},{7,3},{8,12},{9,13},{10,... | collective-permute-start | bytes 196616 | tf_op jit(solution)/shard_map/scalars/ppermute | solution.py:374
  81.0 6.1 %collective-permute-start.27 = (bf16[64,512]{1,0:T(8,128)(2,1)S(1)}, bf16[64,512]{1,0:T(8,128)(2,1)S(1)}, u32[]{:S(2)}, u32[]{:S(2)}) collective-permute-start(bf16[64,512]{1,0:T(8,128)(2,1)S(1)} %get-tuple-element.76), channel_id=1, source_target_pairs={{0,2},{1,3},{2,0},{3,1},{4,6},{5,7},{6,4},{7,5},{8,10},{9,11},{10,... | collective-permute-start | bytes 196616 | tf_op jit(solution)/shard_map/scalars/ppermute | solution.py:374
  81.6 5.5 %collective-permute-start.28 = (f32[8,512]{1,0:T(8,128)S(1)}, f32[8,512]{1,0:T(8,128)S(1)}, u32[]{:S(2)}, u32[]{:S(2)}) collective-permute-start(f32[8,512]{1,0:T(8,128)S(1)} %add.19.refs_14_), channel_id=1, source_target_pairs={{0,8},{8,0},{16,24},{24,16},{1,9},{9,1},{17,25},{25,17},{2,10},{10... | collective-permute-start | bytes 49160 | tf_op jit(solution)/shard_map/scalars/ppermute | solution.py:504
  82.9 4.1 %collective-permute-start.29 = (f32[8,512]{1,0:T(8,128)S(1)}, f32[8,512]{1,0:T(8,128)S(1)}, u32[]{:S(2)}, u32[]{:S(2)}) collective-permute-start(f32[8,512]{1,0:T(8,128)S(1)} %add.19.refs_14_), channel_id=1, source_target_pairs={{0,16},{8,24},{16,0},{24,8},{1,17},{9,25},{17,1},{25,9},{2,18},{10... | collective-permute-start | bytes 49160 | tf_op jit(solution)/shard_map/scalars/ppermute | solution.py:504
  84.6 3.2 %collective-permute-start.30 = (f32[8,512]{1,0:T(8,128)S(1)}, f32[8,512]{1,0:T(8,128)S(1)}, u32[]{:S(2)}, u32[]{:S(2)}) collective-permute-start(f32[8,512]{1,0:T(8,128)S(1)} %add.19.refs_14_), channel_id=1, source_target_pairs={{0,24},{8,16},{16,8},{24,0},{1,25},{9,17},{17,9},{25,1},{2,26},{10... | collective-permute-start | bytes 49160 | tf_op jit(solution)/shard_map/scalars/ppermute | solution.py:504

commit v6 on v3

--- a/solution.py
+++ b/solution.py
@@ -270,7 +270,7 @@
 def finish_kernel(dims, cells, scale, size_ref, start, *refs):
     sectors, terms, size, count, low, span = dims
     shifted, plus, minus = [refs[k * sectors : (k + 1) * sectors] for k in range(3)]
-    parts, refs = refs[3 * sectors : 3 * sectors + count * sectors], refs[3 * sectors + count * sectors :]
+    totals, refs = refs[3 * sectors : 4 * sectors], refs[4 * sectors :]
     tables, (next_ref, sigma_ref) = refs[:-2], refs[-2:]
     first = row_finder(count, low, span)(0, 0)
     sums = sum(table[...] for table in tables)
@@ -285,10 +285,7 @@
     for turn in range(sectors):
         s = sector_at(turn, sectors)
         next_ref[s] = (shifted[turn][...] - delta * start[s]) * inverse
-        total = parts[turn * count][...]
-        for part in parts[turn * count + 1 : (turn + 1) * count]:
-            total += part[...].astype(jnp.float32)
-        mixed = jnp.where(live_tile((span, size), first, size_ref[s]), scale * total, 0.0)
+        mixed = jnp.where(live_tile((span, size), first, size_ref[s]), scale * totals[turn][...], 0.0)
         sigma_ref[s] = (plus[turn][...] - delta * minus[turn][...] + mixed) * inverse
 
 
@@ -341,10 +338,14 @@
     def halo(edge, which):
         return lax.ppermute(edge, "sector", pairs[which]) if pairs[which] else edge
 
+    received = []
+
     def low_sum(send, keep):
+        received.append(send)
         if low == 1:
             return keep
-        return keep + lax.ppermute(send, "term", pairs_low(ranks)).astype(jnp.float32)
+        received.append(lax.ppermute(send, "term", pairs_low(ranks)))
+        return keep + received[-1].astype(jnp.float32)
 
     hops = range(count - 1, 0, -1)
 
@@ -381,7 +382,10 @@
                 functools.partial(load_kernel, dims, turn),
                 [*cut_shapes, matrices, matrices] + ([rows] if turn == 0 else []),
                 (),
-                (rounded, *[halos[h] for h in halos_at(turn, sectors)]),
+                (
+                    after_all(rounded, *[send for send, _ in cuts[-1:]]),
+                    *[halos[h] for h in halos_at(turn, sectors)],
+                ),
                 (sector_shifts, sector_sizes, left_block, right_block, lanczos_vector),
                 [
                     square,
@@ -408,8 +412,12 @@
                 (sector_sizes,),
                 (start, left_energy, right_energy, *parts[turn]),
             )
-            mine = gather_high(held[None])
-            theirs = lax.ppermute(mine, "term", pairs_low(ranks)) if low > 1 else mine
+            mine = theirs = gather_high(held[None])
+            if low > 1:
+                theirs = lax.ppermute(held, "term", pairs_low(ranks))[None]
+                if count > 1:
+                    late = lax.ppermute(mine[1:], "term", pairs_low(ranks))
+                    theirs = jnp.concatenate([theirs, late])
             pieces[turn] = [mine, theirs]
     def sector_sums(turn, block):
         return call(
@@ -461,7 +469,9 @@
                     flops=terms * pair_flops,
                 )
             )
-        totals = [low_sum(*c) for c in cuts]
+        totals = [low_sum(*cuts[0])]
+        for send, *kept_rows in cuts[1:]:
+            totals.append(low_sum(after_all(send, received[-1]), *kept_rows))
 
     with jax.named_scope("scalars"):
         parts = [high_parts(total) for total in totals]
@@ -478,7 +488,7 @@
                 ]
                 reach *= width
         out = jax.ShapeDtypeStruct((sectors, span, size), jnp.float32)
-        flat = [part for each in parts for part in each]
+        flat = [sum(part.astype(jnp.float32) for part in each) for each in parts]
         return call(
             functools.partial(finish_kernel, dims, cells, scale),
             [out, out],

time: 86.1 us -> 90.4 us (1.050)
  starting transfers between devices: 41.6 us -> 44.8 us
  waiting for transfers between devices: 22.9 us -> 24.1 us
    ppermute x6 -> x8, starting transfers between devices: 10.3 us -> 14.3 us  [the longest x4 7.27 us: low_sum(): received.append(lax.ppermute(send, 'term', pairs_low(ranks)))]
    ppermute x6 -> x8, waiting for transfers between devices: 10.4 us -> 13 us  [the longest x4 10 us: low_sum(): received.append(lax.ppermute(send, 'term', pairs_low(ranks)))]
    ppermute x6, waiting for transfers between devices: 4.64 us -> 3.13 us  [gather_high(): lax.ppermute(held, 'term', pairs_high(ranks, low, k))]
    ppermute x3, starting transfers between devices: 2.24 us -> 1.28 us  [on_device(): lax.ppermute(sums, 'sector', [(i, i ^ reach * k) for i in range(groups)])]
  transfers between devices with their start and end apart: 31 -> 33, of which waited for: 13 -> 14; matrix products, arithmetic and copies ran while one was open for 1% -> 1% of each run, Pallas kernels for 19% -> 18%
where the time goes in v6:
time: 90.4 us; the launch traced here: 90.1 us
  starting transfers between devices  44.8 us (50%)
  waiting for transfers between devices  24.1 us (27%)
  Pallas kernels  19.3 us (21%)
  between operations  0.98 us (1%)
    pallas_call x11, Pallas kernels, call(): pl.pallas_call(kernel, out_shape=out_shape, in_specs=[SMEM] * len(scalars...  19.3 us
    ppermute x12, starting transfers between devices, high_parts(): lax.ppermute(total[k].astype(jnp.bfloat16), 'term', pairs_high(ranks, low...  18.6 us
    ppermute x4, waiting for transfers between devices, low_sum(): received.append(lax.ppermute(send, 'term', pairs_low(ranks)))  10 us
    ppermute x6, starting transfers between devices, gather_high(): lax.ppermute(held, 'term', pairs_high(ranks, low, k))  8.67 us
    ppermute x4, starting transfers between devices, low_sum(): received.append(lax.ppermute(send, 'term', pairs_low(ranks)))  7.27 us
    ppermute x12, waiting for transfers between devices, high_parts(): lax.ppermute(total[k].astype(jnp.bfloat16), 'term', pairs_high(ranks, low...  6.11 us
    ppermute x2, starting transfers between devices, on_device(): theirs = lax.ppermute(held, 'term', pairs_low(ranks))[None]  4.75 us
    ppermute x6, waiting for transfers between devices, gather_high(): lax.ppermute(held, 'term', pairs_high(ranks, low, k))  3.13 us
  transfers between devices with their start and end apart: 33, of which 14 were waited for; matrix products, arithmetic and copies ran while one was open for 1% of the time, Pallas kernels for 18%

profile of v6, /device:TPU:0, one launch (start us, length us, event | category | flops | bytes accessed | tf_op | source)
XLA Modules:
  0.0 90.1 jit_solution(3531106855457281438)
XLA Ops:
  0.6 1.6 %first.3 = (bf16[2,512,512]{2,1,0:T(8,128)(2,1)S(1)}, bf16[512,512]{1,0:T(8,128)(2,1)S(1)}, bf16[512,512]{1,0:T(8,128)(2,1)S(1)}) custom-call(s32[2]{0:T(128)} %size_ref.9, f32[2,512,512]{2,1,0:T(8,128)} %vector_ref.3), custom_call_target="tpu_custom_call" | custom-call | flops 1048576 | bytes 4096 | tf_op jit(solution)/shard_map/first/pallas_call | solution.py:300
  2.3 0.5 collective-permute-start
  2.8 0.7 collective-permute-start.5
  3.5 0.8 collective-permute-done.refs_0_
  4.3 4.3 %first.4 = (bf16[4,64,512]{2,1,0:T(8,128)(2,1)S(1)}, f32[4,64,512]{2,1,0:T(8,128)S(1)}, bf16[4,512,512]{2,1,0:T(8,128)(2,1)S(1)}, bf16[4,512,512]{2,1,0:T(8,128)(2,1)S(1)}, f32[2,64,512]{2,1,0:T(8,128)S(1)}) custom-call(bf16[2,512,512]{2,1,0:T(8,128)(2,1)S(1)} %get-tuple-element.41.own, bf16[512,512]{1,0:T(8,128)(2,1)S(1)} %collective-permute-done.refs_0_, ...), custom_call_target="tpu_custom_call" | custom-call | flops 2147483648 | bytes 8388608 | tf_op jit(solution)/shard_map/first/pallas_call | solution.py:300
  8.6 3.0 %collective-permute-start.1 = (bf16[4,64,512]{2,1,0:T(8,128)(2,1)S(1)}, bf16[4,64,512]{2,1,0:T(8,128)(2,1)S(1)}, u32[]{:S(2)}, u32[]{:S(2)}) collective-permute-start(bf16[4,64,512]{2,1,0:T(8,128)(2,1)S(1)} %get-tuple-element.39), channel_id=1, source_target_pairs={{0,1},{1,0},{2,3},{3,2},{4,5},{5,4},{6,7},{7,6},{8,9},{9,8},{10,11... | collective-permute-start | bytes 786440 | tf_op jit(solution)/shard_map/first/ppermute | solution.py:347
  11.6 2.5 %first.5 = (bf16[4,64,512]{2,1,0:T(8,128)(2,1)S(1)}, f32[4,64,512]{2,1,0:T(8,128)S(1)}, bf16[4,512,512]{2,1,0:T(8,128)(2,1)S(1)}, bf16[4,512,512]{2,1,0:T(8,128)(2,1)S(1)}) custom-call(bf16[2,512,512]{2,1,0:T(8,128)(2,1)S(1)} %get-tuple-element.41.own, bf16[512,512]{1,0:T(8,128)(2,1)S(1)} %collective-permute-done.5.refs_0_, s32[4]{0:T(128)} %shift_ref.5, ...), custom_call_target="tpu_custom_call" | custom-call | flops 2147483648 | bytes 8388608 | tf_op jit(solution)/shard_map/first/pallas_call | solution.py:300
  14.1 1.1 %collective-permute-start.6 = (bf16[4,64,512]{2,1,0:T(8,128)(2,1)S(1)}, bf16[4,64,512]{2,1,0:T(8,128)(2,1)S(1)}, u32[]{:S(2)}, u32[]{:S(2)}) collective-permute-start(bf16[4,64,512]{2,1,0:T(8,128)(2,1)S(1)} %get-tuple-element.44), channel_id=1, source_target_pairs={{0,1},{1,0},{2,3},{3,2},{4,5},{5,4},{6,7},{7,6},{8,9},{9,8},{10,11... | collective-permute-start | bytes 786440 | tf_op jit(solution)/shard_map/first/ppermute | solution.py:347
  15.2 2.5 %collective-permute-done.1 = bf16[4,64,512]{2,1,0:T(8,128)(2,1)S(1)} collective-permute-done((bf16[4,64,512]{2,1,0:T(8,128)(2,1)S(1)}, bf16[4,64,512]{2,1,0:T(8,128)(2,1)S(1)}, u32[]{:S(2)}, u32[]{:S(2)}) %collective-permute-start.1) | collective-permute-done | bytes 262176 | tf_op jit(solution)/shard_map/first/ppermute | solution.py:347
  17.8 2.6 %collective-permute-start.4 = (bf16[64,512]{1,0:T(8,128)(2,1)S(1)}, bf16[64,512]{1,0:T(8,128)(2,1)S(1)}, u32[]{:S(2)}, u32[]{:S(2)}) collective-permute-start(bf16[64,512]{1,0:T(8,128)(2,1)S(1)} %get-tuple-element.93), channel_id=1, source_target_pairs={{0,2},{1,3},{2,0},{3,1},{4,6},{5,7},{6,4},{7,5},{8,10},{9,11},{10,... | collective-permute-start | bytes 196616 | tf_op jit(solution)/shard_map/gather/ppermute | solution.py:354
  20.4 2.6 %collective-permute-start.3 = (bf16[64,512]{1,0:T(8,128)(2,1)S(1)}, bf16[64,512]{1,0:T(8,128)(2,1)S(1)}, u32[]{:S(2)}, u32[]{:S(2)}) collective-permute-start(bf16[64,512]{1,0:T(8,128)(2,1)S(1)} %get-tuple-element.94), channel_id=1, source_target_pairs={{0,4},{1,5},{2,6},{3,7},{4,0},{5,1},{6,2},{7,3},{8,12},{9,13},{10,... | collective-permute-start | bytes 196616 | tf_op jit(solution)/shard_map/gather/ppermute | solution.py:354
  23.1 0.9 %collective-permute-start.9 = (bf16[64,512]{1,0:T(8,128)(2,1)S(1)}, bf16[64,512]{1,0:T(8,128)(2,1)S(1)}, u32[]{:S(2)}, u32[]{:S(2)}) collective-permute-start(bf16[64,512]{1,0:T(8,128)(2,1)S(1)} %get-tuple-element.90), channel_id=1, source_target_pairs={{0,2},{1,3},{2,0},{3,1},{4,6},{5,7},{6,4},{7,5},{8,10},{9,11},{10,... | collective-permute-start | bytes 196616 | tf_op jit(solution)/shard_map/gather/ppermute | solution.py:354
  24.1 3.6 %collective-permute-start.8 = (bf16[64,512]{1,0:T(8,128)(2,1)S(1)}, bf16[64,512]{1,0:T(8,128)(2,1)S(1)}, u32[]{:S(2)}, u32[]{:S(2)}) collective-permute-start(bf16[64,512]{1,0:T(8,128)(2,1)S(1)} %get-tuple-element.91), channel_id=1, source_target_pairs={{0,4},{1,5},{2,6},{3,7},{4,0},{5,1},{6,2},{7,3},{8,12},{9,13},{10,... | collective-permute-start | bytes 196616 | tf_op jit(solution)/shard_map/gather/ppermute | solution.py:354
  27.7 1.8 %collective-permute-done.2.refs_1_ = bf16[64,512]{1,0:T(8,128)(2,1)S(1)} collective-permute-done((bf16[64,512]{1,0:T(8,128)(2,1)S(1)}, bf16[64,512]{1,0:T(8,128)(2,1)S(1)}, u32[]{:S(2)}, u32[]{:S(2)}) %collective-permute-start.2) | collective-permute-done | bytes 65568 | tf_op jit(solution)/shard_map/gather/ppermute | solution.py:354
  29.5 0.7 gather.2
  30.2 2.1 %collective-permute-start.12 = (bf16[1,64,512]{2,1,0:T(8,128)(2,1)S(1)}, bf16[1,64,512]{2,1,0:T(8,128)(2,1)S(1)}, u32[]{:S(2)}, u32[]{:S(2)}) collective-permute-start(bf16[1,64,512]{2,1,0:T(8,128)(2,1)S(1)} %bitcast.60), channel_id=1, source_target_pairs={{0,6},{1,7},{2,4},{3,5},{4,2},{5,3},{6,0},{7,1},{8,14},{9,15},{10,... | collective-permute-start | bytes 196616 | tf_op jit(solution)/shard_map/gather/ppermute | solution.py:359
  32.3 0.5 collective-permute-start.11
  32.8 1.8 %collective-permute-start.10 = (bf16[1,64,512]{2,1,0:T(8,128)(2,1)S(1)}, bf16[1,64,512]{2,1,0:T(8,128)(2,1)S(1)}, u32[]{:S(2)}, u32[]{:S(2)}) collective-permute-start(bf16[1,64,512]{2,1,0:T(8,128)(2,1)S(1)} %bitcast.62), channel_id=1, source_target_pairs={{0,2},{1,3},{2,0},{3,1},{4,6},{5,7},{6,4},{7,5},{8,10},{9,11},{10,... | collective-permute-start | bytes 196616 | tf_op jit(solution)/shard_map/gather/ppermute | solution.py:359
  34.6 1.9 %collective-permute-start.13 = (bf16[64,512]{1,0:T(8,128)(2,1)S(1)}, bf16[64,512]{1,0:T(8,128)(2,1)S(1)}, u32[]{:S(2)}, u32[]{:S(2)}) collective-permute-start(bf16[64,512]{1,0:T(8,128)(2,1)S(1)} %get-tuple-element.52), channel_id=1, source_target_pairs={{0,1},{1,0},{2,3},{3,2},{4,5},{5,4},{6,7},{7,6},{8,9},{9,8},{10,11... | collective-permute-start | bytes 196616 | tf_op jit(solution)/shard_map/gather/ppermute | solution.py:417
  36.5 0.7 gather.3
  37.2 2.1 %collective-permute-start.17 = (bf16[1,64,512]{2,1,0:T(8,128)(2,1)S(1)}, bf16[1,64,512]{2,1,0:T(8,128)(2,1)S(1)}, u32[]{:S(2)}, u32[]{:S(2)}) collective-permute-start(bf16[1,64,512]{2,1,0:T(8,128)(2,1)S(1)} %bitcast.56), channel_id=1, source_target_pairs={{0,6},{1,7},{2,4},{3,5},{4,2},{5,3},{6,0},{7,1},{8,14},{9,15},{10,... | collective-permute-start | bytes 196616 | tf_op jit(solution)/shard_map/gather/ppermute | solution.py:359
  39.3 1.8 %collective-permute-start.16 = (bf16[1,64,512]{2,1,0:T(8,128)(2,1)S(1)}, bf16[1,64,512]{2,1,0:T(8,128)(2,1)S(1)}, u32[]{:S(2)}, u32[]{:S(2)}) collective-permute-start(bf16[1,64,512]{2,1,0:T(8,128)(2,1)S(1)} %bitcast.57), channel_id=1, source_target_pairs={{0,4},{1,5},{2,6},{3,7},{4,0},{5,1},{6,2},{7,3},{8,12},{9,13},{10,... | collective-permute-start | bytes 196616 | tf_op jit(solution)/shard_map/gather/ppermute | solution.py:359
  41.7 2.9 %collective-permute-start.18 = (bf16[64,512]{1,0:T(8,128)(2,1)S(1)}, bf16[64,512]{1,0:T(8,128)(2,1)S(1)}, u32[]{:S(2)}, u32[]{:S(2)}) collective-permute-start(bf16[64,512]{1,0:T(8,128)(2,1)S(1)} %get-tuple-element.55), channel_id=1, source_target_pairs={{0,1},{1,0},{2,3},{3,2},{4,5},{5,4},{6,7},{7,6},{8,9},{9,8},{10,11... | collective-permute-start | bytes 196616 | tf_op jit(solution)/shard_map/gather/ppermute | solution.py:417
  44.7 2.7 %collective-permute-done.16 = bf16[1,64,512]{2,1,0:T(8,128)(2,1)S(1)} collective-permute-done((bf16[1,64,512]{2,1,0:T(8,128)(2,1)S(1)}, bf16[1,64,512]{2,1,0:T(8,128)(2,1)S(1)}, u32[]{:S(2)}, u32[]{:S(2)}) %collective-permute-start.16) | collective-permute-done | bytes 65568 | tf_op jit(solution)/shard_map/gather/ppermute | solution.py:359
  47.6 2.2 %collective-permute-start.19 = (bf16[3,64,512]{2,1,0:T(8,128)(2,1)S(1)}, bf16[3,64,512]{2,1,0:T(8,128)(2,1)S(1)}, u32[]{:S(2)}, u32[]{:S(2)}) collective-permute-start(bf16[3,64,512]{2,1,0:T(8,128)(2,1)S(1)} %pad_maximum_fusion.7), channel_id=1, source_target_pairs={{0,1},{1,0},{2,3},{3,2},{4,5},{5,4},{6,7},{7,6},{8,9},{9,8},{10,11... | collective-permute-start | bytes 589832 | tf_op jit(solution)/shard_map/gather/ppermute | solution.py:419
  49.8 2.3 %collective-permute-done.14 = bf16[3,64,512]{2,1,0:T(8,128)(2,1)S(1)} collective-permute-done((bf16[3,64,512]{2,1,0:T(8,128)(2,1)S(1)}, bf16[3,64,512]{2,1,0:T(8,128)(2,1)S(1)}, u32[]{:S(2)}, u32[]{:S(2)}) %collective-permute-start.14) | collective-permute-done | bytes 196640 | tf_op jit(solution)/shard_map/gather/ppermute | solution.py:419
  52.2 1.6 %second.5 = (f32[512,512]{1,0:T(8,128)S(1)}, bf16[512,512]{1,0:T(8,128)(2,1)S(1)}) custom-call(s32[4]{0:T(128)S(1)} %copy-done.4, bf16[4,512,512]{2,1,0:T(8,128)(2,1)S(1)} %get-tuple-element.50.left, bf16[4,512,512]{2,1,0:T(8,128)(2,1)S(1)} %get-tuple-element.51.right, bf16[4,64,512]{2,1,0:T(8,128)(2,1)S(1)} %get-tuple-element.87.mine, ...), custom_call_target="tpu_custom_call" | custom-call | flops 1 | tf_op jit(solution)/shard_map/second/pallas_call | solution.py:300
  53.8 1.0 %second.6 = f32[8,512]{1,0:T(8,128)S(1)} custom-call(s32[2]{0:T(128)S(1)} %copy-done.1, f32[2,512,512]{2,1,0:T(8,128)S(1)} %copy-done, bf16[512,512]{1,0:T(8,128)(2,1)S(1)} %get-tuple-element.54.block.first_block), custom_call_target="tpu_custom_call" | custom-call | flops 1 | tf_op jit(solution)/shard_map/second/pallas_call | solution.py:300
  54.9 0.6 collective-permute-done.19
  55.7 0.7 collective-permute-start.25
  56.4 1.1 %collective-permute-done.20.refs_2_ = bf16[2,4,64,512]{3,2,1,0:T(8,128)(2,1)S(1)} collective-permute-done((bf16[2,4,64,512]{3,2,1,0:T(8,128)(2,1)S(1)}, bf16[2,4,64,512]{3,2,1,0:T(8,128)(2,1)S(1)}, u32[]{:S(2)}, u32[]{:S(2)}) %collective-permute-start.20) | collective-permute-done | bytes 524320 | tf_op jit(solution)/shard_map/second/ppermute | solution.py:339
  57.5 3.0 %second.7 = (bf16[4,64,512]{2,1,0:T(8,128)(2,1)S(1)}, f32[4,64,512]{2,1,0:T(8,128)S(1)}, bf16[2,512,512]{2,1,0:T(8,128)(2,1)S(1)}) custom-call(s32[4]{0:T(128)S(1)} %copy-done.4, f32[512,512]{1,0:T(8,128)S(1)} %get-tuple-element.53.acc_ref, bf16[512,512]{1,0:T(8,128)(2,1)S(1)} %get-tuple-element.54.block.first_block, ...), custom_call_target="tpu_custom_call" | custom-call | flops 1073741824 | bytes 4194304 | tf_op jit(solution)/shard_map/second/pallas_call | solution.py:300
  60.5 1.6 %collective-permute-start.21 = (bf16[4,64,512]{2,1,0:T(8,128)(2,1)S(1)}, bf16[4,64,512]{2,1,0:T(8,128)(2,1)S(1)}, u32[]{:S(2)}, u32[]{:S(2)}) collective-permute-start(bf16[4,64,512]{2,1,0:T(8,128)(2,1)S(1)} %get-tuple-element.58), channel_id=1, source_target_pairs={{0,1},{1,0},{2,3},{3,2},{4,5},{5,4},{6,7},{7,6},{8,9},{9,8},{10,11... | collective-permute-start | bytes 786440 | tf_op jit(solution)/shard_map/second/ppermute | solution.py:347
  62.1 1.0 %second.8 = f32[8,512]{1,0:T(8,128)S(1)} custom-call(s32[2]{0:T(128)S(1)} %copy-done.1, f32[2,512,512]{2,1,0:T(8,128)S(1)} %copy-done, bf16[2,512,512]{2,1,0:T(8,128)(2,1)S(1)} %get-tuple-element.61.block.own), custom_call_target="tpu_custom_call" | custom-call | flops 1 | tf_op jit(solution)/shard_map/second/pallas_call | solution.py:300
  63.2 1.5 %second.9 = (bf16[4,64,512]{2,1,0:T(8,128)(2,1)S(1)}, f32[4,64,512]{2,1,0:T(8,128)S(1)}) custom-call(s32[4]{0:T(128)S(1)} %copy-done.4, bf16[2,512,512]{2,1,0:T(8,128)(2,1)S(1)} %get-tuple-element.61.block.own, bf16[4,512,512]{2,1,0:T(8,128)(2,1)S(1)} %get-tuple-element.62.left, bf16[4,512,512]{2,1,0:T(8,128)(2,1)S(1)} %get-tuple-element.63.right, ...), custom_call_target="tpu_custom_call" | custom-call | flops 2147483648 | bytes 8388608 | tf_op jit(solution)/shard_map/second/pallas_call | solution.py:300
  64.7 4.8 %collective-permute-done.21 = bf16[4,64,512]{2,1,0:T(8,128)(2,1)S(1)} collective-permute-done((bf16[4,64,512]{2,1,0:T(8,128)(2,1)S(1)}, bf16[4,64,512]{2,1,0:T(8,128)(2,1)S(1)}, u32[]{:S(2)}, u32[]{:S(2)}) %collective-permute-start.21) | collective-permute-done | bytes 262176 | tf_op jit(solution)/shard_map/second/ppermute | solution.py:347
  69.4 1.6 %collective-permute-start.26 = (bf16[4,64,512]{2,1,0:T(8,128)(2,1)S(1)}, bf16[4,64,512]{2,1,0:T(8,128)(2,1)S(1)}, u32[]{:S(2)}, u32[]{:S(2)}) collective-permute-start(bf16[4,64,512]{2,1,0:T(8,128)(2,1)S(1)} %get-tuple-element.66), channel_id=1, source_target_pairs={{0,1},{1,0},{2,3},{3,2},{4,5},{5,4},{6,7},{7,6},{8,9},{9,8},{10,11... | collective-permute-start | bytes 786440 | tf_op jit(solution)/shard_map/second/ppermute | solution.py:347
  71.1 2.7 %collective-permute-start.22 = (bf16[64,512]{1,0:T(8,128)(2,1)S(1)}, bf16[64,512]{1,0:T(8,128)(2,1)S(1)}, u32[]{:S(2)}, u32[]{:S(2)}) collective-permute-start(bf16[64,512]{1,0:T(8,128)(2,1)S(1)} %get-tuple-element.83), channel_id=1, source_target_pairs={{0,6},{1,7},{2,4},{3,5},{4,2},{5,3},{6,0},{7,1},{8,14},{9,15},{10,... | collective-permute-start | bytes 196616 | tf_op jit(solution)/shard_map/scalars/ppermute | solution.py:354
  73.8 0.9 collective-permute-start.24
  74.7 0.9 collective-permute-start.23
  75.6 2.7 %collective-permute-done.26 = bf16[4,64,512]{2,1,0:T(8,128)(2,1)S(1)} collective-permute-done((bf16[4,64,512]{2,1,0:T(8,128)(2,1)S(1)}, bf16[4,64,512]{2,1,0:T(8,128)(2,1)S(1)}, u32[]{:S(2)}, u32[]{:S(2)}) %collective-permute-start.26) | collective-permute-done | bytes 262176 | tf_op jit(solution)/shard_map/second/ppermute | solution.py:347
  78.4 2.4 %collective-permute-start.27 = (bf16[64,512]{1,0:T(8,128)(2,1)S(1)}, bf16[64,512]{1,0:T(8,128)(2,1)S(1)}, u32[]{:S(2)}, u32[]{:S(2)}) collective-permute-start(bf16[64,512]{1,0:T(8,128)(2,1)S(1)} %get-tuple-element.76), channel_id=1, source_target_pairs={{0,6},{1,7},{2,4},{3,5},{4,2},{5,3},{6,0},{7,1},{8,14},{9,15},{10,... | collective-permute-start | bytes 196616 | tf_op jit(solution)/shard_map/scalars/ppermute | solution.py:354
  81.2 1.7 %collective-permute-start.28 = (bf16[64,512]{1,0:T(8,128)(2,1)S(1)}, bf16[64,512]{1,0:T(8,128)(2,1)S(1)}, u32[]{:S(2)}, u32[]{:S(2)}) collective-permute-start(bf16[64,512]{1,0:T(8,128)(2,1)S(1)} %get-tuple-element.78), channel_id=1, source_target_pairs={{0,4},{1,5},{2,6},{3,7},{4,0},{5,1},{6,2},{7,3},{8,12},{9,13},{10,... | collective-permute-start | bytes 196616 | tf_op jit(solution)/shard_map/scalars/ppermute | solution.py:354
  83.0 1.2 %collective-permute-start.31 = (f32[8,512]{1,0:T(8,128)S(1)}, f32[8,512]{1,0:T(8,128)S(1)}, u32[]{:S(2)}, u32[]{:S(2)}) collective-permute-start(f32[8,512]{1,0:T(8,128)S(1)} %add.43.refs_8_), channel_id=1, source_target_pairs={{0,16},{8,24},{16,0},{24,8},{1,17},{9,25},{17,1},{25,9},{2,18},{10... | collective-permute-start | bytes 49160 | tf_op jit(solution)/shard_map/scalars/ppermute | solution.py:486
  84.2 1.0 %collective-permute-done.27 = bf16[64,512]{1,0:T(8,128)(2,1)S(1)} collective-permute-done((bf16[64,512]{1,0:T(8,128)(2,1)S(1)}, bf16[64,512]{1,0:T(8,128)(2,1)S(1)}, u32[]{:S(2)}, u32[]{:S(2)}) %collective-permute-start.27) | collective-permute-done | bytes 65568 | tf_op jit(solution)/shard_map/scalars/ppermute | solution.py:354
  85.2 0.9 collective-permute-done.29
  86.1 2.4 %collective-permute-done.28 = bf16[64,512]{1,0:T(8,128)(2,1)S(1)} collective-permute-done((bf16[64,512]{1,0:T(8,128)(2,1)S(1)}, bf16[64,512]{1,0:T(8,128)(2,1)S(1)}, u32[]{:S(2)}, u32[]{:S(2)}) %collective-permute-start.28) | collective-permute-done | bytes 65568 | tf_op jit(solution)/shard_map/scalars/ppermute | solution.py:354
  88.6 1.5 %scalars.1 = (f32[2,64,512]{2,1,0:T(8,128)}, f32[2,64,512]{2,1,0:T(8,128)}) custom-call(s32[2]{0:T(128)S(1)} %copy-done.1, f32[2,64,512]{2,1,0:T(8,128)S(1)} %get-tuple-element.37.start, f32[64,512]{1,0:T(8,128)S(1)} %get-tuple-element.40.refs_0_, f32[64,512]{1,0:T(8,128)S(1)} %get-tuple-element.45.refs_1_, f32[64,512]{1,0:T(8,128)S(1)} %get-tuple-element.46.refs_2_, ...), custom_call_target="tpu_custom_call" | custom-call | flops 1048576 | bytes 4096 | tf_op jit(solution)/shard_map/scalars/pallas_call | solution.py:300
  (60 shorter events, 2.2 us)
Async XLA Ops:
  2.3 2.1 %collective-permute-start = (bf16[512,512]{1,0:T(8,128)(2,1)S(1)}, bf16[512,512]{1,0:T(8,128)(2,1)S(1)}, u32[]{:S(2)}, u32[]{:S(2)}) collective-permute-start(bf16[512,512]{1,0:T(8,128)(2,1)S(1)} %get-tuple-element.36), channel_id=1, source_target_pairs={{0,8},{8,0},{16,24},{24,16},{1,9},{9,1},{17,25},{25,17},{2,10},{10... | collective-permute-start | bytes 1572872 | tf_op jit(solution)/shard_map/first/ppermute | solution.py:339
  2.8 8.8 %collective-permute-start.5 = (bf16[512,512]{1,0:T(8,128)(2,1)S(1)}, bf16[512,512]{1,0:T(8,128)(2,1)S(1)}, u32[]{:S(2)}, u32[]{:S(2)}) collective-permute-start(bf16[512,512]{1,0:T(8,128)(2,1)S(1)} %get-tuple-element.42), channel_id=1, source_target_pairs={{8,16},{16,8},{9,17},{17,9},{10,18},{18,10},{11,19},{19,11},{12,20... | collective-permute-start | bytes 1572872 | tf_op jit(solution)/shard_map/first/ppermute | solution.py:339
  8.6 9.0 %collective-permute-start.1 = (bf16[4,64,512]{2,1,0:T(8,128)(2,1)S(1)}, bf16[4,64,512]{2,1,0:T(8,128)(2,1)S(1)}, u32[]{:S(2)}, u32[]{:S(2)}) collective-permute-start(bf16[4,64,512]{2,1,0:T(8,128)(2,1)S(1)} %get-tuple-element.39), channel_id=1, source_target_pairs={{0,1},{1,0},{2,3},{3,2},{4,5},{5,4},{6,7},{7,6},{8,9},{9,8},{10,11... | collective-permute-start | bytes 786440 | tf_op jit(solution)/shard_map/first/ppermute | solution.py:347
  14.1 8.9 %collective-permute-start.6 = (bf16[4,64,512]{2,1,0:T(8,128)(2,1)S(1)}, bf16[4,64,512]{2,1,0:T(8,128)(2,1)S(1)}, u32[]{:S(2)}, u32[]{:S(2)}) collective-permute-start(bf16[4,64,512]{2,1,0:T(8,128)(2,1)S(1)} %get-tuple-element.44), channel_id=1, source_target_pairs={{0,1},{1,0},{2,3},{3,2},{4,5},{5,4},{6,7},{7,6},{8,9},{9,8},{10,11... | collective-permute-start | bytes 786440 | tf_op jit(solution)/shard_map/first/ppermute | solution.py:347
  17.7 11.8 %copy-start.1 = (s32[2]{0:T(128)S(1)}, s32[2]{0:T(128)}, u32[]{:S(2)}) copy-start(s32[2]{0:T(128)} %size_ref.9) | copy-start | bytes 28
  17.7 11.8 %copy-start.2 = (f32[2,512]{1,0:T(2,128)S(1)}, f32[2,512]{1,0:T(2,128)}, u32[]{:S(2)}) copy-start(f32[2,512]{1,0:T(2,128)} %left_row.3) | copy-start | bytes 12292
  17.7 11.8 %copy-start.3 = (f32[2,512]{1,0:T(2,128)S(1)}, f32[2,512]{1,0:T(2,128)}, u32[]{:S(2)}) copy-start(f32[2,512]{1,0:T(2,128)} %right_row.3) | copy-start | bytes 12292
  17.8 9.8 %collective-permute-start.4 = (bf16[64,512]{1,0:T(8,128)(2,1)S(1)}, bf16[64,512]{1,0:T(8,128)(2,1)S(1)}, u32[]{:S(2)}, u32[]{:S(2)}) collective-permute-start(bf16[64,512]{1,0:T(8,128)(2,1)S(1)} %get-tuple-element.93), channel_id=1, source_target_pairs={{0,2},{1,3},{2,0},{3,1},{4,6},{5,7},{6,4},{7,5},{8,10},{9,11},{10,... | collective-permute-start | bytes 196616 | tf_op jit(solution)/shard_map/gather/ppermute | solution.py:354
  20.4 7.3 %collective-permute-start.3 = (bf16[64,512]{1,0:T(8,128)(2,1)S(1)}, bf16[64,512]{1,0:T(8,128)(2,1)S(1)}, u32[]{:S(2)}, u32[]{:S(2)}) collective-permute-start(bf16[64,512]{1,0:T(8,128)(2,1)S(1)} %get-tuple-element.94), channel_id=1, source_target_pairs={{0,4},{1,5},{2,6},{3,7},{4,0},{5,1},{6,2},{7,3},{8,12},{9,13},{10,... | collective-permute-start | bytes 196616 | tf_op jit(solution)/shard_map/gather/ppermute | solution.py:354
  23.0 6.5 %collective-permute-start.2 = (bf16[64,512]{1,0:T(8,128)(2,1)S(1)}, bf16[64,512]{1,0:T(8,128)(2,1)S(1)}, u32[]{:S(2)}, u32[]{:S(2)}) collective-permute-start(bf16[64,512]{1,0:T(8,128)(2,1)S(1)} %get-tuple-element.95), channel_id=1, source_target_pairs={{0,6},{1,7},{2,4},{3,5},{4,2},{5,3},{6,0},{7,1},{8,14},{9,15},{10,... | collective-permute-start | bytes 196616 | tf_op jit(solution)/shard_map/gather/ppermute | solution.py:354
  23.1 29.1 %copy-start.4 = (s32[4]{0:T(128)S(1)}, s32[4]{0:T(128)}, u32[]{:S(2)}) copy-start(s32[4]{0:T(128)} %shift_ref.5) | copy-start | bytes 52
  23.1 9.7 %collective-permute-start.9 = (bf16[64,512]{1,0:T(8,128)(2,1)S(1)}, bf16[64,512]{1,0:T(8,128)(2,1)S(1)}, u32[]{:S(2)}, u32[]{:S(2)}) collective-permute-start(bf16[64,512]{1,0:T(8,128)(2,1)S(1)} %get-tuple-element.90), channel_id=1, source_target_pairs={{0,2},{1,3},{2,0},{3,1},{4,6},{5,7},{6,4},{7,5},{8,10},{9,11},{10,... | collective-permute-start | bytes 196616 | tf_op jit(solution)/shard_map/gather/ppermute | solution.py:354
  24.1 10.5 %collective-permute-start.8 = (bf16[64,512]{1,0:T(8,128)(2,1)S(1)}, bf16[64,512]{1,0:T(8,128)(2,1)S(1)}, u32[]{:S(2)}, u32[]{:S(2)}) collective-permute-start(bf16[64,512]{1,0:T(8,128)(2,1)S(1)} %get-tuple-element.91), channel_id=1, source_target_pairs={{0,4},{1,5},{2,6},{3,7},{4,0},{5,1},{6,2},{7,3},{8,12},{9,13},{10,... | collective-permute-start | bytes 196616 | tf_op jit(solution)/shard_map/gather/ppermute | solution.py:354
  27.7 8.8 %collective-permute-start.7 = (bf16[64,512]{1,0:T(8,128)(2,1)S(1)}, bf16[64,512]{1,0:T(8,128)(2,1)S(1)}, u32[]{:S(2)}, u32[]{:S(2)}) collective-permute-start(bf16[64,512]{1,0:T(8,128)(2,1)S(1)} %get-tuple-element.92), channel_id=1, source_target_pairs={{0,6},{1,7},{2,4},{3,5},{4,2},{5,3},{6,0},{7,1},{8,14},{9,15},{10,... | collective-permute-start | bytes 196616 | tf_op jit(solution)/shard_map/gather/ppermute | solution.py:354
  30.2 9.2 %collective-permute-start.12 = (bf16[1,64,512]{2,1,0:T(8,128)(2,1)S(1)}, bf16[1,64,512]{2,1,0:T(8,128)(2,1)S(1)}, u32[]{:S(2)}, u32[]{:S(2)}) collective-permute-start(bf16[1,64,512]{2,1,0:T(8,128)(2,1)S(1)} %bitcast.60), channel_id=1, source_target_pairs={{0,6},{1,7},{2,4},{3,5},{4,2},{5,3},{6,0},{7,1},{8,14},{9,15},{10,... | collective-permute-start | bytes 196616 | tf_op jit(solution)/shard_map/gather/ppermute | solution.py:359
  32.3 9.1 %collective-permute-start.11 = (bf16[1,64,512]{2,1,0:T(8,128)(2,1)S(1)}, bf16[1,64,512]{2,1,0:T(8,128)(2,1)S(1)}, u32[]{:S(2)}, u32[]{:S(2)}) collective-permute-start(bf16[1,64,512]{2,1,0:T(8,128)(2,1)S(1)} %bitcast.61), channel_id=1, source_target_pairs={{0,4},{1,5},{2,6},{3,7},{4,0},{5,1},{6,2},{7,3},{8,12},{9,13},{10,... | collective-permute-start | bytes 196616 | tf_op jit(solution)/shard_map/gather/ppermute | solution.py:359
  32.8 8.9 %collective-permute-start.10 = (bf16[1,64,512]{2,1,0:T(8,128)(2,1)S(1)}, bf16[1,64,512]{2,1,0:T(8,128)(2,1)S(1)}, u32[]{:S(2)}, u32[]{:S(2)}) collective-permute-start(bf16[1,64,512]{2,1,0:T(8,128)(2,1)S(1)} %bitcast.62), channel_id=1, source_target_pairs={{0,2},{1,3},{2,0},{3,1},{4,6},{5,7},{6,4},{7,5},{8,10},{9,11},{10,... | collective-permute-start | bytes 196616 | tf_op jit(solution)/shard_map/gather/ppermute | solution.py:359
  34.6 15.2 %collective-permute-start.13 = (bf16[64,512]{1,0:T(8,128)(2,1)S(1)}, bf16[64,512]{1,0:T(8,128)(2,1)S(1)}, u32[]{:S(2)}, u32[]{:S(2)}) collective-permute-start(bf16[64,512]{1,0:T(8,128)(2,1)S(1)} %get-tuple-element.52), channel_id=1, source_target_pairs={{0,1},{1,0},{2,3},{3,2},{4,5},{5,4},{6,7},{7,6},{8,9},{9,8},{10,11... | collective-permute-start | bytes 196616 | tf_op jit(solution)/shard_map/gather/ppermute | solution.py:417
  37.2 7.4 %collective-permute-start.17 = (bf16[1,64,512]{2,1,0:T(8,128)(2,1)S(1)}, bf16[1,64,512]{2,1,0:T(8,128)(2,1)S(1)}, u32[]{:S(2)}, u32[]{:S(2)}) collective-permute-start(bf16[1,64,512]{2,1,0:T(8,128)(2,1)S(1)} %bitcast.56), channel_id=1, source_target_pairs={{0,6},{1,7},{2,4},{3,5},{4,2},{5,3},{6,0},{7,1},{8,14},{9,15},{10,... | collective-permute-start | bytes 196616 | tf_op jit(solution)/shard_map/gather/ppermute | solution.py:359
  39.3 8.0 %collective-permute-start.16 = (bf16[1,64,512]{2,1,0:T(8,128)(2,1)S(1)}, bf16[1,64,512]{2,1,0:T(8,128)(2,1)S(1)}, u32[]{:S(2)}, u32[]{:S(2)}) collective-permute-start(bf16[1,64,512]{2,1,0:T(8,128)(2,1)S(1)} %bitcast.57), channel_id=1, source_target_pairs={{0,4},{1,5},{2,6},{3,7},{4,0},{5,1},{6,2},{7,3},{8,12},{9,13},{10,... | collective-permute-start | bytes 196616 | tf_op jit(solution)/shard_map/gather/ppermute | solution.py:359
  41.4 6.2 %collective-permute-start.15 = (bf16[1,64,512]{2,1,0:T(8,128)(2,1)S(1)}, bf16[1,64,512]{2,1,0:T(8,128)(2,1)S(1)}, u32[]{:S(2)}, u32[]{:S(2)}) collective-permute-start(bf16[1,64,512]{2,1,0:T(8,128)(2,1)S(1)} %bitcast.58), channel_id=1, source_target_pairs={{0,2},{1,3},{2,0},{3,1},{4,6},{5,7},{6,4},{7,5},{8,10},{9,11},{10,... | collective-permute-start | bytes 196616 | tf_op jit(solution)/shard_map/gather/ppermute | solution.py:359
  41.7 13.2 %collective-permute-start.18 = (bf16[64,512]{1,0:T(8,128)(2,1)S(1)}, bf16[64,512]{1,0:T(8,128)(2,1)S(1)}, u32[]{:S(2)}, u32[]{:S(2)}) collective-permute-start(bf16[64,512]{1,0:T(8,128)(2,1)S(1)} %get-tuple-element.55), channel_id=1, source_target_pairs={{0,1},{1,0},{2,3},{3,2},{4,5},{5,4},{6,7},{7,6},{8,9},{9,8},{10,11... | collective-permute-start | bytes 196616 | tf_op jit(solution)/shard_map/gather/ppermute | solution.py:417
  44.6 7.6 %collective-permute-start.14 = (bf16[3,64,512]{2,1,0:T(8,128)(2,1)S(1)}, bf16[3,64,512]{2,1,0:T(8,128)(2,1)S(1)}, u32[]{:S(2)}, u32[]{:S(2)}) collective-permute-start(bf16[3,64,512]{2,1,0:T(8,128)(2,1)S(1)} %pad_maximum_fusion.6), channel_id=1, source_target_pairs={{0,1},{1,0},{2,3},{3,2},{4,5},{5,4},{6,7},{7,6},{8,9},{9,8},{10,11... | collective-permute-start | bytes 589832 | tf_op jit(solution)/shard_map/gather/ppermute | solution.py:419
  47.6 7.9 %collective-permute-start.19 = (bf16[3,64,512]{2,1,0:T(8,128)(2,1)S(1)}, bf16[3,64,512]{2,1,0:T(8,128)(2,1)S(1)}, u32[]{:S(2)}, u32[]{:S(2)}) collective-permute-start(bf16[3,64,512]{2,1,0:T(8,128)(2,1)S(1)} %pad_maximum_fusion.7), channel_id=1, source_target_pairs={{0,1},{1,0},{2,3},{3,2},{4,5},{5,4},{6,7},{7,6},{8,9},{9,8},{10,11... | collective-permute-start | bytes 589832 | tf_op jit(solution)/shard_map/gather/ppermute | solution.py:419
  52.2 1.6 %copy-start = (f32[2,512,512]{2,1,0:T(8,128)S(1)}, f32[2,512,512]{2,1,0:T(8,128)}, u32[]{:S(2)}) copy-start(f32[2,512,512]{2,1,0:T(8,128)} %vector_ref.3) | copy-start | bytes 6291460
  55.5 2.0 %collective-permute-start.20 = (bf16[2,4,64,512]{3,2,1,0:T(8,128)(2,1)S(1)}, bf16[2,4,64,512]{3,2,1,0:T(8,128)(2,1)S(1)}, u32[]{:S(2)}, u32[]{:S(2)}) collective-permute-start(bf16[2,4,64,512]{3,2,1,0:T(8,128)(2,1)S(1)} %pad_maximum_fusion), channel_id=1, source_target_pairs={{0,8},{8,0},{16,24},{24,16},{1,9},{9,1},{17,25},{25,17},{2,10},{10... | collective-permute-start | bytes 1572872 | tf_op jit(solution)/shard_map/second/ppermute | solution.py:339
  55.7 7.4 %collective-permute-start.25 = (bf16[2,4,64,512]{3,2,1,0:T(8,128)(2,1)S(1)}, bf16[2,4,64,512]{3,2,1,0:T(8,128)(2,1)S(1)}, u32[]{:S(2)}, u32[]{:S(2)}) collective-permute-start(bf16[2,4,64,512]{3,2,1,0:T(8,128)(2,1)S(1)} %pad_maximum_fusion.1), channel_id=1, source_target_pairs={{8,16},{16,8},{9,17},{17,9},{10,18},{18,10},{11,19},{19,11},{12,20... | collective-permute-start | bytes 1572872 | tf_op jit(solution)/shard_map/second/ppermute | solution.py:339
  60.5 8.9 %collective-permute-start.21 = (bf16[4,64,512]{2,1,0:T(8,128)(2,1)S(1)}, bf16[4,64,512]{2,1,0:T(8,128)(2,1)S(1)}, u32[]{:S(2)}, u32[]{:S(2)}) collective-permute-start(bf16[4,64,512]{2,1,0:T(8,128)(2,1)S(1)} %get-tuple-element.58), channel_id=1, source_target_pairs={{0,1},{1,0},{2,3},{3,2},{4,5},{5,4},{6,7},{7,6},{8,9},{9,8},{10,11... | collective-permute-start | bytes 786440 | tf_op jit(solution)/shard_map/second/ppermute | solution.py:347
  69.4 8.9 %collective-permute-start.26 = (bf16[4,64,512]{2,1,0:T(8,128)(2,1)S(1)}, bf16[4,64,512]{2,1,0:T(8,128)(2,1)S(1)}, u32[]{:S(2)}, u32[]{:S(2)}) collective-permute-start(bf16[4,64,512]{2,1,0:T(8,128)(2,1)S(1)} %get-tuple-element.66), channel_id=1, source_target_pairs={{0,1},{1,0},{2,3},{3,2},{4,5},{5,4},{6,7},{7,6},{8,9},{9,8},{10,11... | collective-permute-start | bytes 786440 | tf_op jit(solution)/shard_map/second/ppermute | solution.py:347
  71.1 10.0 %collective-permute-start.22 = (bf16[64,512]{1,0:T(8,128)(2,1)S(1)}, bf16[64,512]{1,0:T(8,128)(2,1)S(1)}, u32[]{:S(2)}, u32[]{:S(2)}) collective-permute-start(bf16[64,512]{1,0:T(8,128)(2,1)S(1)} %get-tuple-element.83), channel_id=1, source_target_pairs={{0,6},{1,7},{2,4},{3,5},{4,2},{5,3},{6,0},{7,1},{8,14},{9,15},{10,... | collective-permute-start | bytes 196616 | tf_op jit(solution)/shard_map/scalars/ppermute | solution.py:354
  73.8 9.1 %collective-permute-start.24 = (bf16[64,512]{1,0:T(8,128)(2,1)S(1)}, bf16[64,512]{1,0:T(8,128)(2,1)S(1)}, u32[]{:S(2)}, u32[]{:S(2)}) collective-permute-start(bf16[64,512]{1,0:T(8,128)(2,1)S(1)} %get-tuple-element.84), channel_id=1, source_target_pairs={{0,2},{1,3},{2,0},{3,1},{4,6},{5,7},{6,4},{7,5},{8,10},{9,11},{10,... | collective-permute-start | bytes 196616 | tf_op jit(solution)/shard_map/scalars/ppermute | solution.py:354
  74.7 8.2 %collective-permute-start.23 = (bf16[64,512]{1,0:T(8,128)(2,1)S(1)}, bf16[64,512]{1,0:T(8,128)(2,1)S(1)}, u32[]{:S(2)}, u32[]{:S(2)}) collective-permute-start(bf16[64,512]{1,0:T(8,128)(2,1)S(1)} %get-tuple-element.85), channel_id=1, source_target_pairs={{0,4},{1,5},{2,6},{3,7},{4,0},{5,1},{6,2},{7,3},{8,12},{9,13},{10,... | collective-permute-start | bytes 196616 | tf_op jit(solution)/shard_map/scalars/ppermute | solution.py:354
  78.4 6.8 %collective-permute-start.27 = (bf16[64,512]{1,0:T(8,128)(2,1)S(1)}, bf16[64,512]{1,0:T(8,128)(2,1)S(1)}, u32[]{:S(2)}, u32[]{:S(2)}) collective-permute-start(bf16[64,512]{1,0:T(8,128)(2,1)S(1)} %get-tuple-element.76), channel_id=1, source_target_pairs={{0,6},{1,7},{2,4},{3,5},{4,2},{5,3},{6,0},{7,1},{8,14},{9,15},{10,... | collective-permute-start | bytes 196616 | tf_op jit(solution)/shard_map/scalars/ppermute | solution.py:354
  80.9 5.2 %collective-permute-start.29 = (bf16[64,512]{1,0:T(8,128)(2,1)S(1)}, bf16[64,512]{1,0:T(8,128)(2,1)S(1)}, u32[]{:S(2)}, u32[]{:S(2)}) collective-permute-start(bf16[64,512]{1,0:T(8,128)(2,1)S(1)} %get-tuple-element.77), channel_id=1, source_target_pairs={{0,2},{1,3},{2,0},{3,1},{4,6},{5,7},{6,4},{7,5},{8,10},{9,11},{10,... | collective-permute-start | bytes 196616 | tf_op jit(solution)/shard_map/scalars/ppermute | solution.py:354
  81.2 7.4 %collective-permute-start.28 = (bf16[64,512]{1,0:T(8,128)(2,1)S(1)}, bf16[64,512]{1,0:T(8,128)(2,1)S(1)}, u32[]{:S(2)}, u32[]{:S(2)}) collective-permute-start(bf16[64,512]{1,0:T(8,128)(2,1)S(1)} %get-tuple-element.78), channel_id=1, source_target_pairs={{0,4},{1,5},{2,6},{3,7},{4,0},{5,1},{6,2},{7,3},{8,12},{9,13},{10,... | collective-permute-start | bytes 196616 | tf_op jit(solution)/shard_map/scalars/ppermute | solution.py:354
  82.9 5.6 %collective-permute-start.32 = (f32[8,512]{1,0:T(8,128)S(1)}, f32[8,512]{1,0:T(8,128)S(1)}, u32[]{:S(2)}, u32[]{:S(2)}) collective-permute-start(f32[8,512]{1,0:T(8,128)S(1)} %add.43.refs_8_), channel_id=1, source_target_pairs={{0,24},{8,16},{16,8},{24,0},{1,25},{9,17},{17,9},{25,1},{2,26},{10... | collective-permute-start | bytes 49160 | tf_op jit(solution)/shard_map/scalars/ppermute | solution.py:486
  83.0 5.6 %collective-permute-start.31 = (f32[8,512]{1,0:T(8,128)S(1)}, f32[8,512]{1,0:T(8,128)S(1)}, u32[]{:S(2)}, u32[]{:S(2)}) collective-permute-start(f32[8,512]{1,0:T(8,128)S(1)} %add.43.refs_8_), channel_id=1, source_target_pairs={{0,16},{8,24},{16,0},{24,8},{1,17},{9,25},{17,1},{25,9},{2,18},{10... | collective-permute-start | bytes 49160 | tf_op jit(solution)/shard_map/scalars/ppermute | solution.py:486
  85.2 3.4 %collective-permute-start.30 = (f32[8,512]{1,0:T(8,128)S(1)}, f32[8,512]{1,0:T(8,128)S(1)}, u32[]{:S(2)}, u32[]{:S(2)}) collective-permute-start(f32[8,512]{1,0:T(8,128)S(1)} %add.43.refs_8_), channel_id=1, source_target_pairs={{0,8},{8,0},{16,24},{24,16},{1,9},{9,1},{17,25},{25,17},{2,10},{10... | collective-permute-start | bytes 49160 | tf_op jit(solution)/shard_map/scalars/ppermute | solution.py:486

commit v7 on v6

--- a/solution.py
+++ b/solution.py
@@ -101,6 +101,15 @@
         keep_ref[step] = acc[pl.ds(row_of(step, 0), span), :]
 
 
+def place_halos(dims, turn, wb, refs):
+    refs, blocks = list(refs), []
+    for n, halo in enumerate(halos_at(turn, dims[0])):
+        pieces = [refs.pop(0) for _ in range(halo + 1)]
+        place_rows(dims, wb.at[n], pieces if halo else [pieces[0].at[0], pieces[0].at[1]])
+        blocks.append(wb.at[n])
+    return blocks
+
+
 def live_tile(shape, first_row, limit):
     row = first_row + lax.broadcasted_iota(jnp.int32, shape, 0)
     return (row < limit) & (lax.broadcasted_iota(jnp.int32, shape, 1) < limit)
@@ -114,7 +123,7 @@
     return left + right_row[pl.ds(s, 1), :]
 
 
-def round_kernel(size_hbm, vector_hbm, rounded, edge, other_edge, vector, sizes, sems):
+def round_kernel(size_hbm, vector_hbm, rounded, edge, upper, lower, vector, sizes, sems):
     sectors, size = vector.shape[:2]
     parts = sems.shape[0] // sectors
     rows = size // parts
@@ -148,15 +157,19 @@
                 if turn == 0:
                     edge[part, :] = value
                 if turn == sectors - 1:
-                    other_edge[part, :] = value
+                    if n < parts // 2:
+                        upper[part, :] = value
+                    else:
+                        lower[pl.ds(first - size // 2, tile), :] = value
 
 
 def load_kernel(dims, turn, own, *refs):
     sectors, terms, size, count, low, span = dims
-    blocks, refs = refs[: len(halos_at(turn, sectors))], refs[len(halos_at(turn, sectors)) :]
+    pieces = {h: h + 1 for h in halos_at(turn, sectors)}
+    blocks, refs = refs[: sum(pieces.values())], refs[sum(pieces.values()) :]
     shift_hbm, size_hbm, left_hbm, right_hbm, vector_hbm, send_ref, keep_ref, left, right, *refs = refs
     start, refs = (refs[0], refs[1:]) if turn == 0 else (None, refs)
-    acc, shift_ref, size_ref, sems, row_sems, scalar_sems = refs
+    acc, wb, shift_ref, size_ref, sems, row_sems, scalar_sems = refs
     s = sector_at(turn, sectors)
     scalars = [
         pltpu.make_async_copy(shift_hbm, shift_ref, scalar_sems.at[0]),
@@ -182,6 +195,10 @@
     for copy in rows:
         copy.start()
     acc[...] = jnp.zeros_like(acc)
+    if 1 in pieces:
+        for n, half in enumerate(blocks[-2:]):
+            wb[pl.ds(n * (size // 2), size // 2), :] = half[...]
+        blocks = [*blocks[:-2], wb]
     for copy in scalars:
         copy.wait()
 
@@ -215,9 +232,7 @@
     own[sector_at(0, sectors)] = first_block[...]
     for turn in range(1, sectors):
         place_rows(dims, own.at[sector_at(turn, sectors)], pieces[2 * turn - 2 : 2 * turn])
-    for n, halo in enumerate(halos):
-        place_rows(dims, wb.at[n], [halo.at[0], halo.at[1]])
-    blocks = [wb.at[n] for n in range(len(halos))]
+    blocks = place_halos(dims, 0, wb, halos)
     add_pairs(dims, 0, shift_ref, acc, left, right, own, blocks, skip_own=True)
     cut(dims, acc, send_ref, keep_ref)
 
@@ -225,9 +240,7 @@
 def full_kernel(dims, turn, shift_ref, own, left, right, *refs):
     halos, (send_ref, keep_ref, acc, wb) = refs[:-4], refs[-4:]
     acc[...] = jnp.zeros_like(acc)
-    for n, halo in enumerate(halos):
-        place_rows(dims, wb.at[n], [halo.at[0], halo.at[1]])
-    blocks = [wb.at[n] for n in range(len(halos))]
+    blocks = place_halos(dims, turn, wb, halos)
     add_pairs(dims, turn, shift_ref, acc, left, right, own, blocks)
     cut(dims, acc, send_ref, keep_ref)
 
@@ -360,11 +373,12 @@
         return jnp.concatenate([held] + [got[k] for k in range(1, count)])
 
     with jax.named_scope("first"):
-        parts = 2 if size % 256 == 0 else 1
+        parts = 2
         block = jax.ShapeDtypeStruct((size, size), jnp.bfloat16)
-        rounded, *edges = call(
+        half = jax.ShapeDtypeStruct((size // 2, size), jnp.bfloat16)
+        rounded, edge, *halves = call(
             round_kernel,
-            [pltpu.VMEM(lanczos_vector.shape, jnp.bfloat16), block, block],
+            [pltpu.VMEM(lanczos_vector.shape, jnp.bfloat16), block, half, half],
             (),
             (),
             (sector_sizes, lanczos_vector),
@@ -374,7 +388,7 @@
                 pltpu.SemaphoreType.DMA((sectors * parts + 1,)),
             ],
         )
-        halos = [halo(edge, which) for which, edge in enumerate(edges)]
+        halos = [[halo(edge, 0)], [halo(edge, 1) for edge in halves]]
         matrices = pltpu.VMEM((terms, size, size), jnp.bfloat16)
         cuts, left, right = [], [None] * sectors, [None] * sectors
         for turn in turns:
@@ -384,11 +398,12 @@
                 (),
                 (
                     after_all(rounded, *[send for send, _ in cuts[-1:]]),
-                    *[halos[h] for h in halos_at(turn, sectors)],
+                    *[piece for h in halos_at(turn, sectors) for piece in halos[h]],
                 ),
                 (sector_shifts, sector_sizes, left_block, right_block, lanczos_vector),
                 [
                     square,
+                    square_low,
                     pltpu.SMEM((terms,), jnp.int32),
                     pltpu.SMEM((sectors,), jnp.int32),
                     pltpu.SemaphoreType.DMA((2, terms)),
@@ -412,12 +427,8 @@
                 (sector_sizes,),
                 (start, left_energy, right_energy, *parts[turn]),
             )
-            mine = theirs = gather_high(held[None])
-            if low > 1:
-                theirs = lax.ppermute(held, "term", pairs_low(ranks))[None]
-                if count > 1:
-                    late = lax.ppermute(mine[1:], "term", pairs_low(ranks))
-                    theirs = jnp.concatenate([theirs, late])
+            mine = gather_high(held[None])
+            theirs = lax.ppermute(mine, "term", pairs_low(ranks)) if low > 1 else mine
             pieces[turn] = [mine, theirs]
     def sector_sums(turn, block):
         return call(
@@ -438,7 +449,7 @@
         )
         sums = [sector_sums(0, block)]
         whole = after_all(jnp.stack(pieces[0]), pieces[-1][1], acc, sums[0])
-        halos = [halo(edge, n) for n, edge in enumerate((whole, jnp.stack(pieces[-1])))]
+        halos = [[halo(whole, 0)], [halo(piece, 1) for piece in pieces[-1]]]
         *first_cut, own = call(
             functools.partial(rest_kernel, dims),
             [*cut_shapes, pltpu.VMEM((sectors, size, size), jnp.bfloat16)],
@@ -449,7 +460,7 @@
                 left[0],
                 right[0],
                 *[piece for both in pieces[1:] for piece in both],
-                *[halos[h] for h in halos_at(0, sectors)],
+                *[piece for h in halos_at(0, sectors) for piece in halos[h]],
             ),
             scratch=[square, pltpu.VMEM((2, size, size), jnp.bfloat16)],
             flops=terms * pair_flops // 2,
@@ -464,7 +475,12 @@
                     functools.partial(full_kernel, dims, turn),
                     cut_shapes,
                     (sector_shifts,),
-                    (own, left[turn], right[turn], *[halos[h] for h in halos_at(turn, sectors)]),
+                    (
+                        own,
+                        left[turn],
+                        right[turn],
+                        *[piece for h in halos_at(turn, sectors) for piece in halos[h]],
+                    ),
                     scratch=[square, pltpu.VMEM((2, size, size), jnp.bfloat16)],
                     flops=terms * pair_flops,
                 )

time: 90.4 us -> 91.6 us (1.013)
  starting transfers between devices: 44.8 us -> 50.6 us
  waiting for transfers between devices: 24.1 us -> 19.4 us
    ppermute x3, starting transfers between devices: 1.28 us -> 8.68 us  [on_device(): lax.ppermute(sums, 'sector', [(i, i ^ reach * k) for i in range(groups)])]
    ppermute x12, waiting for transfers between devices: 6.11 us -> 2.02 us  [high_parts(): lax.ppermute(total[k].astype(jnp.bfloat16), 'term', pairs_high(ranks, low...]
    ppermute x4, waiting for transfers between devices: 10 us -> 6.2 us  [low_sum(): received.append(lax.ppermute(send, 'term', pairs_low(ranks)))]
    ppermute x3, waiting for transfers between devices: 0.01 us -> 3.05 us  [on_device(): lax.ppermute(sums, 'sector', [(i, i ^ reach * k) for i in range(groups)])]
    ppermute x4 -> x2, starting transfers between devices: 7.05 us -> 4.37 us  [on_device(): theirs = lax.ppermute(mine, 'term', pairs_low(ranks)) if low > 1 else mine]
    ppermute x4 -> x2, waiting for transfers between devices: 2.92 us -> 4.53 us  [on_device(): theirs = lax.ppermute(mine, 'term', pairs_low(ranks)) if low > 1 else mine]
    ppermute x4 -> x6, starting transfers between devices: 1.97 us -> 3.5 us  [halo(): return lax.ppermute(edge, 'sector', pairs[which]) if pairs[which] else edge]
    ppermute x4 -> x6, waiting for transfers between devices: 1.93 us -> 0.44 us  [halo(): return lax.ppermute(edge, 'sector', pairs[which]) if pairs[which] else edge]
  transfers between devices with their start and end apart: 33 -> 33, of which waited for: 14 -> 12; matrix products, arithmetic and copies ran while one was open for 1% -> 1% of each run, Pallas kernels for 18% -> 17%
where the time goes in v7:
time: 91.6 us
  starting transfers between devices  50.6 us (55%)
  waiting for transfers between devices  19.4 us (21%)
  Pallas kernels  19.1 us (21%)
  local copies, waits for them, and re-layouts  1.02 us (1%)
  between operations  0.93 us (1%)
    pallas_call x11, Pallas kernels, call(): pl.pallas_call(kernel, out_shape=out_shape, in_specs=[SMEM] * len(scalars...  19.1 us
    ppermute x12, starting transfers between devices, high_parts(): lax.ppermute(total[k].astype(jnp.bfloat16), 'term', pairs_high(ranks, low...  18.2 us
    ppermute x6, starting transfers between devices, gather_high(): lax.ppermute(held, 'term', pairs_high(ranks, low, k))  8.97 us
    ppermute x3, starting transfers between devices, on_device(): lax.ppermute(sums, 'sector', [(i, i ^ reach * k) for i in range(groups)])  8.68 us
    ppermute x4, starting transfers between devices, low_sum(): received.append(lax.ppermute(send, 'term', pairs_low(ranks)))  6.9 us
    ppermute x4, waiting for transfers between devices, low_sum(): received.append(lax.ppermute(send, 'term', pairs_low(ranks)))  6.2 us
    ppermute x2, waiting for transfers between devices, on_device(): theirs = lax.ppermute(mine, 'term', pairs_low(ranks)) if low > 1 else mine  4.53 us
    ppermute x2, starting transfers between devices, on_device(): theirs = lax.ppermute(mine, 'term', pairs_low(ranks)) if low > 1 else mine  4.37 us
  transfers between devices with their start and end apart: 33, of which 12 were waited for; matrix products, arithmetic and copies ran while one was open for 1% of the time, Pallas kernels for 17%

profile of v7, /device:TPU:0, one launch (start us, length us, event | category | flops | bytes accessed | tf_op | source)
XLA Modules:
  0.0 91.6 jit_solution(7685123412795240705)
XLA Ops:
  0.6 1.6 %first.3 = (bf16[2,512,512]{2,1,0:T(8,128)(2,1)S(1)}, bf16[512,512]{1,0:T(8,128)(2,1)S(1)}, bf16[256,512]{1,0:T(8,128)(2,1)S(1)}, bf16[256,512]{1,0:T(8,128)(2,1)S(1)}) custom-call(s32[2]{0:T(128)} %size_ref.9, f32[2,512,512]{2,1,0:T(8,128)} %vector_ref.3), custom_call_target="tpu_custom_call" | custom-call | flops 1048576 | bytes 4096 | tf_op jit(solution)/shard_map/first/pallas_call | solution.py:313
  2.3 0.5 collective-permute-start
  2.8 0.7 collective-permute-start.5
  3.5 0.7 collective-permute-start.6
  4.3 4.3 %first.4 = (bf16[4,64,512]{2,1,0:T(8,128)(2,1)S(1)}, f32[4,64,512]{2,1,0:T(8,128)S(1)}, bf16[4,512,512]{2,1,0:T(8,128)(2,1)S(1)}, bf16[4,512,512]{2,1,0:T(8,128)(2,1)S(1)}, f32[2,64,512]{2,1,0:T(8,128)S(1)}) custom-call(bf16[2,512,512]{2,1,0:T(8,128)(2,1)S(1)} %get-tuple-element.42.own, bf16[512,512]{1,0:T(8,128)(2,1)S(1)} %collective-permute-done.refs_0_, ...), custom_call_target="tpu_custom_call" | custom-call | flops 2147483648 | bytes 8388608 | tf_op jit(solution)/shard_map/first/pallas_call | solution.py:313
  8.6 3.0 %collective-permute-start.1 = (bf16[4,64,512]{2,1,0:T(8,128)(2,1)S(1)}, bf16[4,64,512]{2,1,0:T(8,128)(2,1)S(1)}, u32[]{:S(2)}, u32[]{:S(2)}) collective-permute-start(bf16[4,64,512]{2,1,0:T(8,128)(2,1)S(1)} %get-tuple-element.40), channel_id=1, source_target_pairs={{0,1},{1,0},{2,3},{3,2},{4,5},{5,4},{6,7},{7,6},{8,9},{9,8},{10,11... | collective-permute-start | bytes 786440 | tf_op jit(solution)/shard_map/first/ppermute | solution.py:360
  11.6 2.5 %first.5 = (bf16[4,64,512]{2,1,0:T(8,128)(2,1)S(1)}, f32[4,64,512]{2,1,0:T(8,128)S(1)}, bf16[4,512,512]{2,1,0:T(8,128)(2,1)S(1)}, bf16[4,512,512]{2,1,0:T(8,128)(2,1)S(1)}) custom-call(bf16[2,512,512]{2,1,0:T(8,128)(2,1)S(1)} %get-tuple-element.42.own, bf16[256,512]{1,0:T(8,128)(2,1)S(1)} %collective-permute-done.5.refs_0_, ...), custom_call_target="tpu_custom_call" | custom-call | flops 2147483648 | bytes 8388608 | tf_op jit(solution)/shard_map/first/pallas_call | solution.py:313
  14.1 1.2 %collective-permute-start.7 = (bf16[4,64,512]{2,1,0:T(8,128)(2,1)S(1)}, bf16[4,64,512]{2,1,0:T(8,128)(2,1)S(1)}, u32[]{:S(2)}, u32[]{:S(2)}) collective-permute-start(bf16[4,64,512]{2,1,0:T(8,128)(2,1)S(1)} %get-tuple-element.46), channel_id=1, source_target_pairs={{0,1},{1,0},{2,3},{3,2},{4,5},{5,4},{6,7},{7,6},{8,9},{9,8},{10,11... | collective-permute-start | bytes 786440 | tf_op jit(solution)/shard_map/first/ppermute | solution.py:360
  15.3 0.7 collective-permute-done.1
  16.1 4.2 %collective-permute-start.2 = (bf16[64,512]{1,0:T(8,128)(2,1)S(1)}, bf16[64,512]{1,0:T(8,128)(2,1)S(1)}, u32[]{:S(2)}, u32[]{:S(2)}) collective-permute-start(bf16[64,512]{1,0:T(8,128)(2,1)S(1)} %get-tuple-element.91), channel_id=1, source_target_pairs={{0,6},{1,7},{2,4},{3,5},{4,2},{5,3},{6,0},{7,1},{8,14},{9,15},{10,... | collective-permute-start | bytes 196616 | tf_op jit(solution)/shard_map/gather/ppermute | solution.py:367
  20.2 0.6 collective-permute-start.4
  20.9 1.4 %collective-permute-done.7 = bf16[4,64,512]{2,1,0:T(8,128)(2,1)S(1)} collective-permute-done((bf16[4,64,512]{2,1,0:T(8,128)(2,1)S(1)}, bf16[4,64,512]{2,1,0:T(8,128)(2,1)S(1)}, u32[]{:S(2)}, u32[]{:S(2)}) %collective-permute-start.7) | collective-permute-done | bytes 262176 | tf_op jit(solution)/shard_map/first/ppermute | solution.py:360
  22.4 3.9 %collective-permute-start.8 = (bf16[64,512]{1,0:T(8,128)(2,1)S(1)}, bf16[64,512]{1,0:T(8,128)(2,1)S(1)}, u32[]{:S(2)}, u32[]{:S(2)}) collective-permute-start(bf16[64,512]{1,0:T(8,128)(2,1)S(1)} %get-tuple-element.88), channel_id=1, source_target_pairs={{0,6},{1,7},{2,4},{3,5},{4,2},{5,3},{6,0},{7,1},{8,14},{9,15},{10,... | collective-permute-start | bytes 196616 | tf_op jit(solution)/shard_map/gather/ppermute | solution.py:367
  26.4 0.6 collective-permute-start.10
  27.0 0.7 gather.2
  27.6 3.9 %collective-permute-start.13 = (bf16[1,64,512]{2,1,0:T(8,128)(2,1)S(1)}, bf16[1,64,512]{2,1,0:T(8,128)(2,1)S(1)}, u32[]{:S(2)}, u32[]{:S(2)}) collective-permute-start(bf16[1,64,512]{2,1,0:T(8,128)(2,1)S(1)} %bitcast.50), channel_id=1, source_target_pairs={{0,6},{1,7},{2,4},{3,5},{4,2},{5,3},{6,0},{7,1},{8,14},{9,15},{10,... | collective-permute-start | bytes 196616 | tf_op jit(solution)/shard_map/gather/ppermute | solution.py:372
  31.5 0.6 collective-permute-start.11
  32.2 2.0 %collective-permute-done.9.refs_2_ = bf16[64,512]{1,0:T(8,128)(2,1)S(1)} collective-permute-done((bf16[64,512]{1,0:T(8,128)(2,1)S(1)}, bf16[64,512]{1,0:T(8,128)(2,1)S(1)}, u32[]{:S(2)}, u32[]{:S(2)}) %collective-permute-start.9) | collective-permute-done | bytes 65568 | tf_op jit(solution)/shard_map/gather/ppermute | solution.py:367
  34.2 0.7 gather.3
  34.8 1.8 %collective-permute-start.17 = (bf16[1,64,512]{2,1,0:T(8,128)(2,1)S(1)}, bf16[1,64,512]{2,1,0:T(8,128)(2,1)S(1)}, u32[]{:S(2)}, u32[]{:S(2)}) collective-permute-start(bf16[1,64,512]{2,1,0:T(8,128)(2,1)S(1)} %bitcast.54), channel_id=1, source_target_pairs={{0,6},{1,7},{2,4},{3,5},{4,2},{5,3},{6,0},{7,1},{8,14},{9,15},{10,... | collective-permute-start | bytes 196616 | tf_op jit(solution)/shard_map/gather/ppermute | solution.py:372
  36.7 2.6 %collective-permute-start.15 = (bf16[1,64,512]{2,1,0:T(8,128)(2,1)S(1)}, bf16[1,64,512]{2,1,0:T(8,128)(2,1)S(1)}, u32[]{:S(2)}, u32[]{:S(2)}) collective-permute-start(bf16[1,64,512]{2,1,0:T(8,128)(2,1)S(1)} %bitcast.56), channel_id=1, source_target_pairs={{0,2},{1,3},{2,0},{3,1},{4,6},{5,7},{6,4},{7,5},{8,10},{9,11},{10,... | collective-permute-start | bytes 196616 | tf_op jit(solution)/shard_map/gather/ppermute | solution.py:372
  39.4 2.2 %collective-permute-start.14 = (bf16[4,64,512]{2,1,0:T(8,128)(2,1)S(1)}, bf16[4,64,512]{2,1,0:T(8,128)(2,1)S(1)}, u32[]{:S(2)}, u32[]{:S(2)}) collective-permute-start(bf16[4,64,512]{2,1,0:T(8,128)(2,1)S(1)} %get-tuple-element.85.mine), channel_id=1, source_target_pairs={{0,1},{1,0},{2,3},{3,2},{4,5},{5,4},{6,7},{7,6},{8,9},{9,8},{10,11... | collective-permute-start | bytes 786440 | tf_op jit(solution)/shard_map/gather/ppermute | solution.py:431
  41.6 3.1 %collective-permute-done.16 = bf16[1,64,512]{2,1,0:T(8,128)(2,1)S(1)} collective-permute-done((bf16[1,64,512]{2,1,0:T(8,128)(2,1)S(1)}, bf16[1,64,512]{2,1,0:T(8,128)(2,1)S(1)}, u32[]{:S(2)}, u32[]{:S(2)}) %collective-permute-start.16) | collective-permute-done | bytes 65568 | tf_op jit(solution)/shard_map/gather/ppermute | solution.py:372
  44.7 2.2 %collective-permute-start.18 = (bf16[4,64,512]{2,1,0:T(8,128)(2,1)S(1)}, bf16[4,64,512]{2,1,0:T(8,128)(2,1)S(1)}, u32[]{:S(2)}, u32[]{:S(2)}) collective-permute-start(bf16[4,64,512]{2,1,0:T(8,128)(2,1)S(1)} %pad_maximum_fusion.2.refs_0_), channel_id=1, source_target_pairs={{0,1},{1,0},{2,3},{3,2},{4,5},{5,4},{6,7},{7,6},{8,9},{9,8},{10,11... | collective-permute-start | bytes 786440 | tf_op jit(solution)/shard_map/gather/ppermute | solution.py:431
  47.0 0.7 second.5
  47.7 0.9 copy-done
  48.6 1.0 %second.6 = f32[8,512]{1,0:T(8,128)S(1)} custom-call(s32[2]{0:T(128)S(1)} %copy-done.1, f32[2,512,512]{2,1,0:T(8,128)S(1)} %copy-done, bf16[512,512]{1,0:T(8,128)(2,1)S(1)} %get-tuple-element.56.block.first_block), custom_call_target="tpu_custom_call" | custom-call | flops 1 | tf_op jit(solution)/shard_map/second/pallas_call | solution.py:313
  49.7 4.4 %collective-permute-done.18.refs_1_ = bf16[4,64,512]{2,1,0:T(8,128)(2,1)S(1)} collective-permute-done((bf16[4,64,512]{2,1,0:T(8,128)(2,1)S(1)}, bf16[4,64,512]{2,1,0:T(8,128)(2,1)S(1)}, u32[]{:S(2)}, u32[]{:S(2)}) %collective-permute-start.18) | collective-permute-done | bytes 262176 | tf_op jit(solution)/shard_map/gather/ppermute | solution.py:431
  54.2 0.7 collective-permute-start.24
  54.9 0.9 collective-permute-start.25
  56.0 3.7 %second.7 = (bf16[4,64,512]{2,1,0:T(8,128)(2,1)S(1)}, f32[4,64,512]{2,1,0:T(8,128)S(1)}, bf16[2,512,512]{2,1,0:T(8,128)(2,1)S(1)}) custom-call(s32[4]{0:T(128)S(1)} %copy-done.4, f32[512,512]{1,0:T(8,128)S(1)} %get-tuple-element.55.acc_ref, bf16[512,512]{1,0:T(8,128)(2,1)S(1)} %get-tuple-element.56.block.first_block, ...), custom_call_target="tpu_custom_call" | custom-call | flops 1073741824 | bytes 4194304 | tf_op jit(solution)/shard_map/second/pallas_call | solution.py:313
  59.7 1.4 %collective-permute-start.20 = (bf16[4,64,512]{2,1,0:T(8,128)(2,1)S(1)}, bf16[4,64,512]{2,1,0:T(8,128)(2,1)S(1)}, u32[]{:S(2)}, u32[]{:S(2)}) collective-permute-start(bf16[4,64,512]{2,1,0:T(8,128)(2,1)S(1)} %get-tuple-element.60), channel_id=1, source_target_pairs={{0,1},{1,0},{2,3},{3,2},{4,5},{5,4},{6,7},{7,6},{8,9},{9,8},{10,11... | collective-permute-start | bytes 786440 | tf_op jit(solution)/shard_map/second/ppermute | solution.py:360
  61.1 1.0 %second.8 = f32[8,512]{1,0:T(8,128)S(1)} custom-call(s32[2]{0:T(128)S(1)} %copy-done.1, f32[2,512,512]{2,1,0:T(8,128)S(1)} %copy-done, bf16[2,512,512]{2,1,0:T(8,128)(2,1)S(1)} %get-tuple-element.63.block.own), custom_call_target="tpu_custom_call" | custom-call | flops 1 | tf_op jit(solution)/shard_map/second/pallas_call | solution.py:313
  62.2 1.5 %second.9 = (bf16[4,64,512]{2,1,0:T(8,128)(2,1)S(1)}, f32[4,64,512]{2,1,0:T(8,128)S(1)}) custom-call(s32[4]{0:T(128)S(1)} %copy-done.4, bf16[2,512,512]{2,1,0:T(8,128)(2,1)S(1)} %get-tuple-element.63.block.own, bf16[4,512,512]{2,1,0:T(8,128)(2,1)S(1)} %get-tuple-element.64.left, bf16[4,512,512]{2,1,0:T(8,128)(2,1)S(1)} %get-tuple-element.65.right, ...), custom_call_target="tpu_custom_call" | custom-call | flops 2147483648 | bytes 8388608 | tf_op jit(solution)/shard_map/second/pallas_call | solution.py:313
  63.6 2.5 %collective-permute-done.20 = bf16[4,64,512]{2,1,0:T(8,128)(2,1)S(1)} collective-permute-done((bf16[4,64,512]{2,1,0:T(8,128)(2,1)S(1)}, bf16[4,64,512]{2,1,0:T(8,128)(2,1)S(1)}, u32[]{:S(2)}, u32[]{:S(2)}) %collective-permute-start.20) | collective-permute-done | bytes 262176 | tf_op jit(solution)/shard_map/second/ppermute | solution.py:360
  66.1 1.3 %collective-permute-start.26 = (bf16[4,64,512]{2,1,0:T(8,128)(2,1)S(1)}, bf16[4,64,512]{2,1,0:T(8,128)(2,1)S(1)}, u32[]{:S(2)}, u32[]{:S(2)}) collective-permute-start(bf16[4,64,512]{2,1,0:T(8,128)(2,1)S(1)} %get-tuple-element.68), channel_id=1, source_target_pairs={{0,1},{1,0},{2,3},{3,2},{4,5},{5,4},{6,7},{7,6},{8,9},{9,8},{10,11... | collective-permute-start | bytes 786440 | tf_op jit(solution)/shard_map/second/ppermute | solution.py:360
  67.6 0.7 collective-permute-start.23
  68.3 1.3 %collective-permute-start.22 = (bf16[64,512]{1,0:T(8,128)(2,1)S(1)}, bf16[64,512]{1,0:T(8,128)(2,1)S(1)}, u32[]{:S(2)}, u32[]{:S(2)}) collective-permute-start(bf16[64,512]{1,0:T(8,128)(2,1)S(1)} %get-tuple-element.83), channel_id=1, source_target_pairs={{0,4},{1,5},{2,6},{3,7},{4,0},{5,1},{6,2},{7,3},{8,12},{9,13},{10,... | collective-permute-start | bytes 196616 | tf_op jit(solution)/shard_map/scalars/ppermute | solution.py:367
  69.6 2.4 %collective-permute-start.21 = (bf16[64,512]{1,0:T(8,128)(2,1)S(1)}, bf16[64,512]{1,0:T(8,128)(2,1)S(1)}, u32[]{:S(2)}, u32[]{:S(2)}) collective-permute-start(bf16[64,512]{1,0:T(8,128)(2,1)S(1)} %get-tuple-element.81), channel_id=1, source_target_pairs={{0,6},{1,7},{2,4},{3,5},{4,2},{5,3},{6,0},{7,1},{8,14},{9,15},{10,... | collective-permute-start | bytes 196616 | tf_op jit(solution)/shard_map/scalars/ppermute | solution.py:367
  72.1 1.7 %collective-permute-done.26 = bf16[4,64,512]{2,1,0:T(8,128)(2,1)S(1)} collective-permute-done((bf16[4,64,512]{2,1,0:T(8,128)(2,1)S(1)}, bf16[4,64,512]{2,1,0:T(8,128)(2,1)S(1)}, u32[]{:S(2)}, u32[]{:S(2)}) %collective-permute-start.26) | collective-permute-done | bytes 262176 | tf_op jit(solution)/shard_map/second/ppermute | solution.py:360
  73.8 0.5 collective-permute-start.29
  74.3 2.4 %collective-permute-start.28 = (bf16[64,512]{1,0:T(8,128)(2,1)S(1)}, bf16[64,512]{1,0:T(8,128)(2,1)S(1)}, u32[]{:S(2)}, u32[]{:S(2)}) collective-permute-start(bf16[64,512]{1,0:T(8,128)(2,1)S(1)} %get-tuple-element.80), channel_id=1, source_target_pairs={{0,4},{1,5},{2,6},{3,7},{4,0},{5,1},{6,2},{7,3},{8,12},{9,13},{10,... | collective-permute-start | bytes 196616 | tf_op jit(solution)/shard_map/scalars/ppermute | solution.py:367
  76.8 1.5 %collective-permute-start.27 = (bf16[64,512]{1,0:T(8,128)(2,1)S(1)}, bf16[64,512]{1,0:T(8,128)(2,1)S(1)}, u32[]{:S(2)}, u32[]{:S(2)}) collective-permute-start(bf16[64,512]{1,0:T(8,128)(2,1)S(1)} %get-tuple-element.78), channel_id=1, source_target_pairs={{0,6},{1,7},{2,4},{3,5},{4,2},{5,3},{6,0},{7,1},{8,14},{9,15},{10,... | collective-permute-start | bytes 196616 | tf_op jit(solution)/shard_map/scalars/ppermute | solution.py:367
  78.3 4.2 %collective-permute-start.30 = (f32[8,512]{1,0:T(8,128)S(1)}, f32[8,512]{1,0:T(8,128)S(1)}, u32[]{:S(2)}, u32[]{:S(2)}) collective-permute-start(f32[8,512]{1,0:T(8,128)S(1)} %add.43.refs_8_), channel_id=1, source_target_pairs={{0,8},{8,0},{16,24},{24,16},{1,9},{9,1},{17,25},{25,17},{2,10},{10... | collective-permute-start | bytes 49160 | tf_op jit(solution)/shard_map/scalars/ppermute | solution.py:502
  82.5 4.4 %collective-permute-start.31 = (f32[8,512]{1,0:T(8,128)S(1)}, f32[8,512]{1,0:T(8,128)S(1)}, u32[]{:S(2)}, u32[]{:S(2)}) collective-permute-start(f32[8,512]{1,0:T(8,128)S(1)} %add.43.refs_8_), channel_id=1, source_target_pairs={{0,16},{8,24},{16,0},{24,8},{1,17},{9,25},{17,1},{25,9},{2,18},{10... | collective-permute-start | bytes 49160 | tf_op jit(solution)/shard_map/scalars/ppermute | solution.py:502
  87.1 1.6 %collective-permute-done.31.refs_10_ = f32[8,512]{1,0:T(8,128)S(1)} collective-permute-done((f32[8,512]{1,0:T(8,128)S(1)}, f32[8,512]{1,0:T(8,128)S(1)}, u32[]{:S(2)}, u32[]{:S(2)}) %collective-permute-start.31) | collective-permute-done | bytes 16416 | tf_op jit(solution)/shard_map/scalars/ppermute | solution.py:502
  88.7 1.4 %collective-permute-done.32.refs_11_ = f32[8,512]{1,0:T(8,128)S(1)} collective-permute-done((f32[8,512]{1,0:T(8,128)S(1)}, f32[8,512]{1,0:T(8,128)S(1)}, u32[]{:S(2)}, u32[]{:S(2)}) %collective-permute-start.32) | collective-permute-done | bytes 16416 | tf_op jit(solution)/shard_map/scalars/ppermute | solution.py:502
  90.1 1.5 %scalars.1 = (f32[2,64,512]{2,1,0:T(8,128)}, f32[2,64,512]{2,1,0:T(8,128)}) custom-call(s32[2]{0:T(128)S(1)} %copy-done.1, f32[2,64,512]{2,1,0:T(8,128)S(1)} %get-tuple-element.38.start, f32[64,512]{1,0:T(8,128)S(1)} %get-tuple-element.41.refs_0_, f32[64,512]{1,0:T(8,128)S(1)} %get-tuple-element.47.refs_1_, f32[64,512]{1,0:T(8,128)S(1)} %get-tuple-element.48.refs_2_, ...), custom_call_target="tpu_custom_call" | custom-call | flops 1048576 | bytes 4096 | tf_op jit(solution)/shard_map/scalars/pallas_call | solution.py:313
  (55 shorter events, 1.5 us)
Async XLA Ops:
  2.3 2.1 %collective-permute-start = (bf16[512,512]{1,0:T(8,128)(2,1)S(1)}, bf16[512,512]{1,0:T(8,128)(2,1)S(1)}, u32[]{:S(2)}, u32[]{:S(2)}) collective-permute-start(bf16[512,512]{1,0:T(8,128)(2,1)S(1)} %get-tuple-element.37), channel_id=1, source_target_pairs={{0,8},{8,0},{16,24},{24,16},{1,9},{9,1},{17,25},{25,17},{2,10},{10... | collective-permute-start | bytes 1572872 | tf_op jit(solution)/shard_map/first/ppermute | solution.py:352
  2.8 8.8 %collective-permute-start.5 = (bf16[256,512]{1,0:T(8,128)(2,1)S(1)}, bf16[256,512]{1,0:T(8,128)(2,1)S(1)}, u32[]{:S(2)}, u32[]{:S(2)}) collective-permute-start(bf16[256,512]{1,0:T(8,128)(2,1)S(1)} %get-tuple-element.43), channel_id=1, source_target_pairs={{8,16},{16,8},{9,17},{17,9},{10,18},{18,10},{11,19},{19,11},{12,20... | collective-permute-start | bytes 786440 | tf_op jit(solution)/shard_map/first/ppermute | solution.py:352
  3.5 8.1 %collective-permute-start.6 = (bf16[256,512]{1,0:T(8,128)(2,1)S(1)}, bf16[256,512]{1,0:T(8,128)(2,1)S(1)}, u32[]{:S(2)}, u32[]{:S(2)}) collective-permute-start(bf16[256,512]{1,0:T(8,128)(2,1)S(1)} %get-tuple-element.44), channel_id=1, source_target_pairs={{8,16},{16,8},{9,17},{17,9},{10,18},{18,10},{11,19},{19,11},{12,20... | collective-permute-start | bytes 786440 | tf_op jit(solution)/shard_map/first/ppermute | solution.py:352
  8.6 7.3 %collective-permute-start.1 = (bf16[4,64,512]{2,1,0:T(8,128)(2,1)S(1)}, bf16[4,64,512]{2,1,0:T(8,128)(2,1)S(1)}, u32[]{:S(2)}, u32[]{:S(2)}) collective-permute-start(bf16[4,64,512]{2,1,0:T(8,128)(2,1)S(1)} %get-tuple-element.40), channel_id=1, source_target_pairs={{0,1},{1,0},{2,3},{3,2},{4,5},{5,4},{6,7},{7,6},{8,9},{9,8},{10,11... | collective-permute-start | bytes 786440 | tf_op jit(solution)/shard_map/first/ppermute | solution.py:360
  14.1 8.2 %collective-permute-start.7 = (bf16[4,64,512]{2,1,0:T(8,128)(2,1)S(1)}, bf16[4,64,512]{2,1,0:T(8,128)(2,1)S(1)}, u32[]{:S(2)}, u32[]{:S(2)}) collective-permute-start(bf16[4,64,512]{2,1,0:T(8,128)(2,1)S(1)} %get-tuple-element.46), channel_id=1, source_target_pairs={{0,1},{1,0},{2,3},{3,2},{4,5},{5,4},{6,7},{7,6},{8,9},{9,8},{10,11... | collective-permute-start | bytes 786440 | tf_op jit(solution)/shard_map/first/ppermute | solution.py:360
  16.0 11.0 %copy-start.1 = (s32[2]{0:T(128)S(1)}, s32[2]{0:T(128)}, u32[]{:S(2)}) copy-start(s32[2]{0:T(128)} %size_ref.9) | copy-start | bytes 28
  16.0 11.0 %copy-start.2 = (f32[2,512]{1,0:T(2,128)S(1)}, f32[2,512]{1,0:T(2,128)}, u32[]{:S(2)}) copy-start(f32[2,512]{1,0:T(2,128)} %left_row.3) | copy-start | bytes 12292
  16.0 11.0 %copy-start.3 = (f32[2,512]{1,0:T(2,128)S(1)}, f32[2,512]{1,0:T(2,128)}, u32[]{:S(2)}) copy-start(f32[2,512]{1,0:T(2,128)} %right_row.3) | copy-start | bytes 12292
  16.1 10.3 %collective-permute-start.2 = (bf16[64,512]{1,0:T(8,128)(2,1)S(1)}, bf16[64,512]{1,0:T(8,128)(2,1)S(1)}, u32[]{:S(2)}, u32[]{:S(2)}) collective-permute-start(bf16[64,512]{1,0:T(8,128)(2,1)S(1)} %get-tuple-element.91), channel_id=1, source_target_pairs={{0,6},{1,7},{2,4},{3,5},{4,2},{5,3},{6,0},{7,1},{8,14},{9,15},{10,... | collective-permute-start | bytes 196616 | tf_op jit(solution)/shard_map/gather/ppermute | solution.py:367
  20.2 6.7 %collective-permute-start.3 = (bf16[64,512]{1,0:T(8,128)(2,1)S(1)}, bf16[64,512]{1,0:T(8,128)(2,1)S(1)}, u32[]{:S(2)}, u32[]{:S(2)}) collective-permute-start(bf16[64,512]{1,0:T(8,128)(2,1)S(1)} %get-tuple-element.90), channel_id=1, source_target_pairs={{0,4},{1,5},{2,6},{3,7},{4,0},{5,1},{6,2},{7,3},{8,12},{9,13},{10,... | collective-permute-start | bytes 196616 | tf_op jit(solution)/shard_map/gather/ppermute | solution.py:367
  20.2 6.7 %collective-permute-start.4 = (bf16[64,512]{1,0:T(8,128)(2,1)S(1)}, bf16[64,512]{1,0:T(8,128)(2,1)S(1)}, u32[]{:S(2)}, u32[]{:S(2)}) collective-permute-start(bf16[64,512]{1,0:T(8,128)(2,1)S(1)} %get-tuple-element.89), channel_id=1, source_target_pairs={{0,2},{1,3},{2,0},{3,1},{4,6},{5,7},{6,4},{7,5},{8,10},{9,11},{10,... | collective-permute-start | bytes 196616 | tf_op jit(solution)/shard_map/gather/ppermute | solution.py:367
  22.4 24.7 %copy-start.4 = (s32[4]{0:T(128)S(1)}, s32[4]{0:T(128)}, u32[]{:S(2)}) copy-start(s32[4]{0:T(128)} %shift_ref.5) | copy-start | bytes 52
  22.4 9.1 %collective-permute-start.8 = (bf16[64,512]{1,0:T(8,128)(2,1)S(1)}, bf16[64,512]{1,0:T(8,128)(2,1)S(1)}, u32[]{:S(2)}, u32[]{:S(2)}) collective-permute-start(bf16[64,512]{1,0:T(8,128)(2,1)S(1)} %get-tuple-element.88), channel_id=1, source_target_pairs={{0,6},{1,7},{2,4},{3,5},{4,2},{5,3},{6,0},{7,1},{8,14},{9,15},{10,... | collective-permute-start | bytes 196616 | tf_op jit(solution)/shard_map/gather/ppermute | solution.py:367
  26.3 7.9 %collective-permute-start.9 = (bf16[64,512]{1,0:T(8,128)(2,1)S(1)}, bf16[64,512]{1,0:T(8,128)(2,1)S(1)}, u32[]{:S(2)}, u32[]{:S(2)}) collective-permute-start(bf16[64,512]{1,0:T(8,128)(2,1)S(1)} %get-tuple-element.87), channel_id=1, source_target_pairs={{0,4},{1,5},{2,6},{3,7},{4,0},{5,1},{6,2},{7,3},{8,12},{9,13},{10,... | collective-permute-start | bytes 196616 | tf_op jit(solution)/shard_map/gather/ppermute | solution.py:367
  26.4 7.8 %collective-permute-start.10 = (bf16[64,512]{1,0:T(8,128)(2,1)S(1)}, bf16[64,512]{1,0:T(8,128)(2,1)S(1)}, u32[]{:S(2)}, u32[]{:S(2)}) collective-permute-start(bf16[64,512]{1,0:T(8,128)(2,1)S(1)} %get-tuple-element.86), channel_id=1, source_target_pairs={{0,2},{1,3},{2,0},{3,1},{4,6},{5,7},{6,4},{7,5},{8,10},{9,11},{10,... | collective-permute-start | bytes 196616 | tf_op jit(solution)/shard_map/gather/ppermute | solution.py:367
  27.6 9.1 %collective-permute-start.13 = (bf16[1,64,512]{2,1,0:T(8,128)(2,1)S(1)}, bf16[1,64,512]{2,1,0:T(8,128)(2,1)S(1)}, u32[]{:S(2)}, u32[]{:S(2)}) collective-permute-start(bf16[1,64,512]{2,1,0:T(8,128)(2,1)S(1)} %bitcast.50), channel_id=1, source_target_pairs={{0,6},{1,7},{2,4},{3,5},{4,2},{5,3},{6,0},{7,1},{8,14},{9,15},{10,... | collective-permute-start | bytes 196616 | tf_op jit(solution)/shard_map/gather/ppermute | solution.py:372
  31.5 7.8 %collective-permute-start.12 = (bf16[1,64,512]{2,1,0:T(8,128)(2,1)S(1)}, bf16[1,64,512]{2,1,0:T(8,128)(2,1)S(1)}, u32[]{:S(2)}, u32[]{:S(2)}) collective-permute-start(bf16[1,64,512]{2,1,0:T(8,128)(2,1)S(1)} %bitcast.51), channel_id=1, source_target_pairs={{0,4},{1,5},{2,6},{3,7},{4,0},{5,1},{6,2},{7,3},{8,12},{9,13},{10,... | collective-permute-start | bytes 196616 | tf_op jit(solution)/shard_map/gather/ppermute | solution.py:372
  31.5 7.8 %collective-permute-start.11 = (bf16[1,64,512]{2,1,0:T(8,128)(2,1)S(1)}, bf16[1,64,512]{2,1,0:T(8,128)(2,1)S(1)}, u32[]{:S(2)}, u32[]{:S(2)}) collective-permute-start(bf16[1,64,512]{2,1,0:T(8,128)(2,1)S(1)} %bitcast.52), channel_id=1, source_target_pairs={{0,2},{1,3},{2,0},{3,1},{4,6},{5,7},{6,4},{7,5},{8,10},{9,11},{10,... | collective-permute-start | bytes 196616 | tf_op jit(solution)/shard_map/gather/ppermute | solution.py:372
  34.8 6.7 %collective-permute-start.17 = (bf16[1,64,512]{2,1,0:T(8,128)(2,1)S(1)}, bf16[1,64,512]{2,1,0:T(8,128)(2,1)S(1)}, u32[]{:S(2)}, u32[]{:S(2)}) collective-permute-start(bf16[1,64,512]{2,1,0:T(8,128)(2,1)S(1)} %bitcast.54), channel_id=1, source_target_pairs={{0,6},{1,7},{2,4},{3,5},{4,2},{5,3},{6,0},{7,1},{8,14},{9,15},{10,... | collective-permute-start | bytes 196616 | tf_op jit(solution)/shard_map/gather/ppermute | solution.py:372
  36.7 8.0 %collective-permute-start.16 = (bf16[1,64,512]{2,1,0:T(8,128)(2,1)S(1)}, bf16[1,64,512]{2,1,0:T(8,128)(2,1)S(1)}, u32[]{:S(2)}, u32[]{:S(2)}) collective-permute-start(bf16[1,64,512]{2,1,0:T(8,128)(2,1)S(1)} %bitcast.55), channel_id=1, source_target_pairs={{0,4},{1,5},{2,6},{3,7},{4,0},{5,1},{6,2},{7,3},{8,12},{9,13},{10,... | collective-permute-start | bytes 196616 | tf_op jit(solution)/shard_map/gather/ppermute | solution.py:372
  36.7 8.0 %collective-permute-start.15 = (bf16[1,64,512]{2,1,0:T(8,128)(2,1)S(1)}, bf16[1,64,512]{2,1,0:T(8,128)(2,1)S(1)}, u32[]{:S(2)}, u32[]{:S(2)}) collective-permute-start(bf16[1,64,512]{2,1,0:T(8,128)(2,1)S(1)} %bitcast.56), channel_id=1, source_target_pairs={{0,2},{1,3},{2,0},{3,1},{4,6},{5,7},{6,4},{7,5},{8,10},{9,11},{10,... | collective-permute-start | bytes 196616 | tf_op jit(solution)/shard_map/gather/ppermute | solution.py:372
  39.4 7.7 %collective-permute-start.14 = (bf16[4,64,512]{2,1,0:T(8,128)(2,1)S(1)}, bf16[4,64,512]{2,1,0:T(8,128)(2,1)S(1)}, u32[]{:S(2)}, u32[]{:S(2)}) collective-permute-start(bf16[4,64,512]{2,1,0:T(8,128)(2,1)S(1)} %get-tuple-element.85.mine), channel_id=1, source_target_pairs={{0,1},{1,0},{2,3},{3,2},{4,5},{5,4},{6,7},{7,6},{8,9},{9,8},{10,11... | collective-permute-start | bytes 786440 | tf_op jit(solution)/shard_map/gather/ppermute | solution.py:431
  44.7 9.4 %collective-permute-start.18 = (bf16[4,64,512]{2,1,0:T(8,128)(2,1)S(1)}, bf16[4,64,512]{2,1,0:T(8,128)(2,1)S(1)}, u32[]{:S(2)}, u32[]{:S(2)}) collective-permute-start(bf16[4,64,512]{2,1,0:T(8,128)(2,1)S(1)} %pad_maximum_fusion.2.refs_0_), channel_id=1, source_target_pairs={{0,1},{1,0},{2,3},{3,2},{4,5},{5,4},{6,7},{7,6},{8,9},{9,8},{10,11... | collective-permute-start | bytes 786440 | tf_op jit(solution)/shard_map/gather/ppermute | solution.py:431
  47.0 1.6 %copy-start = (f32[2,512,512]{2,1,0:T(8,128)S(1)}, f32[2,512,512]{2,1,0:T(8,128)}, u32[]{:S(2)}) copy-start(f32[2,512,512]{2,1,0:T(8,128)} %vector_ref.3) | copy-start | bytes 6291460
  54.1 1.9 %collective-permute-start.19 = (bf16[2,4,64,512]{3,2,1,0:T(8,128)(2,1)S(1)}, bf16[2,4,64,512]{3,2,1,0:T(8,128)(2,1)S(1)}, u32[]{:S(2)}, u32[]{:S(2)}) collective-permute-start(bf16[2,4,64,512]{3,2,1,0:T(8,128)(2,1)S(1)} %pad_maximum_fusion), channel_id=1, source_target_pairs={{0,8},{8,0},{16,24},{24,16},{1,9},{9,1},{17,25},{25,17},{2,10},{10... | collective-permute-start | bytes 1572872 | tf_op jit(solution)/shard_map/second/ppermute | solution.py:352
  54.2 7.9 %collective-permute-start.24 = (bf16[4,64,512]{2,1,0:T(8,128)(2,1)S(1)}, bf16[4,64,512]{2,1,0:T(8,128)(2,1)S(1)}, u32[]{:S(2)}, u32[]{:S(2)}) collective-permute-start(bf16[4,64,512]{2,1,0:T(8,128)(2,1)S(1)} %pad_maximum_fusion.2.refs_0_), channel_id=1, source_target_pairs={{8,16},{16,8},{9,17},{17,9},{10,18},{18,10},{11,19},{19,11},{12,20... | collective-permute-start | bytes 786440 | tf_op jit(solution)/shard_map/second/ppermute | solution.py:352
  54.9 7.2 %collective-permute-start.25 = (bf16[4,64,512]{2,1,0:T(8,128)(2,1)S(1)}, bf16[4,64,512]{2,1,0:T(8,128)(2,1)S(1)}, u32[]{:S(2)}, u32[]{:S(2)}) collective-permute-start(bf16[4,64,512]{2,1,0:T(8,128)(2,1)S(1)} %collective-permute-done.18.refs_1_), channel_id=1, source_target_pairs={{8,16},{16,8},{9,17},{17,9},{10,18},{18,10},{11,19},{19,11},{12,20... | collective-permute-start | bytes 786440 | tf_op jit(solution)/shard_map/second/ppermute | solution.py:352
  59.7 6.4 %collective-permute-start.20 = (bf16[4,64,512]{2,1,0:T(8,128)(2,1)S(1)}, bf16[4,64,512]{2,1,0:T(8,128)(2,1)S(1)}, u32[]{:S(2)}, u32[]{:S(2)}) collective-permute-start(bf16[4,64,512]{2,1,0:T(8,128)(2,1)S(1)} %get-tuple-element.60), channel_id=1, source_target_pairs={{0,1},{1,0},{2,3},{3,2},{4,5},{5,4},{6,7},{7,6},{8,9},{9,8},{10,11... | collective-permute-start | bytes 786440 | tf_op jit(solution)/shard_map/second/ppermute | solution.py:360
  66.1 7.6 %collective-permute-start.26 = (bf16[4,64,512]{2,1,0:T(8,128)(2,1)S(1)}, bf16[4,64,512]{2,1,0:T(8,128)(2,1)S(1)}, u32[]{:S(2)}, u32[]{:S(2)}) collective-permute-start(bf16[4,64,512]{2,1,0:T(8,128)(2,1)S(1)} %get-tuple-element.68), channel_id=1, source_target_pairs={{0,1},{1,0},{2,3},{3,2},{4,5},{5,4},{6,7},{7,6},{8,9},{9,8},{10,11... | collective-permute-start | bytes 786440 | tf_op jit(solution)/shard_map/second/ppermute | solution.py:360
  67.6 9.2 %collective-permute-start.23 = (bf16[64,512]{1,0:T(8,128)(2,1)S(1)}, bf16[64,512]{1,0:T(8,128)(2,1)S(1)}, u32[]{:S(2)}, u32[]{:S(2)}) collective-permute-start(bf16[64,512]{1,0:T(8,128)(2,1)S(1)} %get-tuple-element.82), channel_id=1, source_target_pairs={{0,2},{1,3},{2,0},{3,1},{4,6},{5,7},{6,4},{7,5},{8,10},{9,11},{10,... | collective-permute-start | bytes 196616 | tf_op jit(solution)/shard_map/scalars/ppermute | solution.py:367
  68.3 10.0 %collective-permute-start.22 = (bf16[64,512]{1,0:T(8,128)(2,1)S(1)}, bf16[64,512]{1,0:T(8,128)(2,1)S(1)}, u32[]{:S(2)}, u32[]{:S(2)}) collective-permute-start(bf16[64,512]{1,0:T(8,128)(2,1)S(1)} %get-tuple-element.83), channel_id=1, source_target_pairs={{0,4},{1,5},{2,6},{3,7},{4,0},{5,1},{6,2},{7,3},{8,12},{9,13},{10,... | collective-permute-start | bytes 196616 | tf_op jit(solution)/shard_map/scalars/ppermute | solution.py:367
  69.6 8.7 %collective-permute-start.21 = (bf16[64,512]{1,0:T(8,128)(2,1)S(1)}, bf16[64,512]{1,0:T(8,128)(2,1)S(1)}, u32[]{:S(2)}, u32[]{:S(2)}) collective-permute-start(bf16[64,512]{1,0:T(8,128)(2,1)S(1)} %get-tuple-element.81), channel_id=1, source_target_pairs={{0,6},{1,7},{2,4},{3,5},{4,2},{5,3},{6,0},{7,1},{8,14},{9,15},{10,... | collective-permute-start | bytes 196616 | tf_op jit(solution)/shard_map/scalars/ppermute | solution.py:367
  73.8 13.1 %collective-permute-start.29 = (bf16[64,512]{1,0:T(8,128)(2,1)S(1)}, bf16[64,512]{1,0:T(8,128)(2,1)S(1)}, u32[]{:S(2)}, u32[]{:S(2)}) collective-permute-start(bf16[64,512]{1,0:T(8,128)(2,1)S(1)} %get-tuple-element.79), channel_id=1, source_target_pairs={{0,2},{1,3},{2,0},{3,1},{4,6},{5,7},{6,4},{7,5},{8,10},{9,11},{10,... | collective-permute-start | bytes 196616 | tf_op jit(solution)/shard_map/scalars/ppermute | solution.py:367
  74.3 12.7 %collective-permute-start.28 = (bf16[64,512]{1,0:T(8,128)(2,1)S(1)}, bf16[64,512]{1,0:T(8,128)(2,1)S(1)}, u32[]{:S(2)}, u32[]{:S(2)}) collective-permute-start(bf16[64,512]{1,0:T(8,128)(2,1)S(1)} %get-tuple-element.80), channel_id=1, source_target_pairs={{0,4},{1,5},{2,6},{3,7},{4,0},{5,1},{6,2},{7,3},{8,12},{9,13},{10,... | collective-permute-start | bytes 196616 | tf_op jit(solution)/shard_map/scalars/ppermute | solution.py:367
  76.8 10.3 %collective-permute-start.27 = (bf16[64,512]{1,0:T(8,128)(2,1)S(1)}, bf16[64,512]{1,0:T(8,128)(2,1)S(1)}, u32[]{:S(2)}, u32[]{:S(2)}) collective-permute-start(bf16[64,512]{1,0:T(8,128)(2,1)S(1)} %get-tuple-element.78), channel_id=1, source_target_pairs={{0,6},{1,7},{2,4},{3,5},{4,2},{5,3},{6,0},{7,1},{8,14},{9,15},{10,... | collective-permute-start | bytes 196616 | tf_op jit(solution)/shard_map/scalars/ppermute | solution.py:367
  78.3 8.7 %collective-permute-start.30 = (f32[8,512]{1,0:T(8,128)S(1)}, f32[8,512]{1,0:T(8,128)S(1)}, u32[]{:S(2)}, u32[]{:S(2)}) collective-permute-start(f32[8,512]{1,0:T(8,128)S(1)} %add.43.refs_8_), channel_id=1, source_target_pairs={{0,8},{8,0},{16,24},{24,16},{1,9},{9,1},{17,25},{25,17},{2,10},{10... | collective-permute-start | bytes 49160 | tf_op jit(solution)/shard_map/scalars/ppermute | solution.py:502
  82.5 6.1 %collective-permute-start.31 = (f32[8,512]{1,0:T(8,128)S(1)}, f32[8,512]{1,0:T(8,128)S(1)}, u32[]{:S(2)}, u32[]{:S(2)}) collective-permute-start(f32[8,512]{1,0:T(8,128)S(1)} %add.43.refs_8_), channel_id=1, source_target_pairs={{0,16},{8,24},{16,0},{24,8},{1,17},{9,25},{17,1},{25,9},{2,18},{10... | collective-permute-start | bytes 49160 | tf_op jit(solution)/shard_map/scalars/ppermute | solution.py:502
  86.9 3.2 %collective-permute-start.32 = (f32[8,512]{1,0:T(8,128)S(1)}, f32[8,512]{1,0:T(8,128)S(1)}, u32[]{:S(2)}, u32[]{:S(2)}) collective-permute-start(f32[8,512]{1,0:T(8,128)S(1)} %add.43.refs_8_), channel_id=1, source_target_pairs={{0,24},{8,16},{16,8},{24,0},{1,25},{9,17},{17,9},{25,1},{2,26},{10... | collective-permute-start | bytes 49160 | tf_op jit(solution)/shard_map/scalars/ppermute | solution.py:502

commit v8 on v3

--- a/solution.py
+++ b/solution.py
@@ -164,8 +164,9 @@
     ]
     copies = [
         [
-            pltpu.make_async_copy(hbm.at[s, t], vmem.at[t], sems.at[k, t])
+            pltpu.make_async_copy(hbm.at[s, t, part, :], vmem.at[t, part, :], sems.at[k, t, n])
             for k, (hbm, vmem) in enumerate(((left_hbm, left), (right_hbm, right)))
+            for n, part in enumerate((pl.ds(0, size // 2), pl.ds(size // 2, size // 2)))
         ]
         for t in range(terms)
     ]
@@ -387,7 +388,7 @@
                     square,
                     pltpu.SMEM((terms,), jnp.int32),
                     pltpu.SMEM((sectors,), jnp.int32),
-                    pltpu.SemaphoreType.DMA((2, terms)),
+                    pltpu.SemaphoreType.DMA((2, terms, 2)),
                     pltpu.SemaphoreType.DMA((sectors,)),
                     pltpu.SemaphoreType.DMA((2,)),
                 ],

time: 86.1 us -> 86.7 us (level)
  starting transfers between devices: 41.6 us -> 36.9 us
  waiting for transfers between devices: 22.9 us -> 25.5 us
  Pallas kernels: 19.7 us -> 21.8 us
    ppermute x4, starting transfers between devices: 7.47 us -> 4.49 us  [low_sum(): lax.ppermute(send, 'term', pairs_low(ranks)).astype(jnp.float32)]
    pallas_call x11, Pallas kernels: 19.7 us -> 21.8 us  [call(): pl.pallas_call(kernel, out_shape=out_shape, in_specs=[SMEM] * len(scalars...]
    ppermute x12, waiting for transfers between devices: 6.15 us -> 7.87 us  [high_parts(): lax.ppermute(total[k].astype(jnp.bfloat16), 'term', pairs_high(ranks, low...]
    ppermute x12, starting transfers between devices: 18 us -> 16.7 us  [high_parts(): lax.ppermute(total[k].astype(jnp.bfloat16), 'term', pairs_high(ranks, low...]
  transfers between devices with their start and end apart: 31 -> 31, of which waited for: 13 -> 13; matrix products, arithmetic and copies ran while one was open for 1% -> 1% of each run, Pallas kernels for 19% -> 21%
where the time goes in v8:
time: 86.7 us
  starting transfers between devices  36.9 us (43%)
  waiting for transfers between devices  25.5 us (29%)
  Pallas kernels  21.8 us (25%)
  local copies, waits for them, and re-layouts  1.03 us (1%)
  between operations  0.91 us (1%)
    pallas_call x11, Pallas kernels, call(): pl.pallas_call(kernel, out_shape=out_shape, in_specs=[SMEM] * len(scalars...  21.8 us
    ppermute x12, starting transfers between devices, high_parts(): lax.ppermute(total[k].astype(jnp.bfloat16), 'term', pairs_high(ranks, low...  16.7 us
    ppermute x6, starting transfers between devices, gather_high(): lax.ppermute(held, 'term', pairs_high(ranks, low, k))  8.91 us
    ppermute x12, waiting for transfers between devices, high_parts(): lax.ppermute(total[k].astype(jnp.bfloat16), 'term', pairs_high(ranks, low...  7.87 us
    ppermute x4, waiting for transfers between devices, low_sum(): lax.ppermute(send, 'term', pairs_low(ranks)).astype(jnp.float32)  6.03 us
    ppermute x2, waiting for transfers between devices, on_device(): theirs = lax.ppermute(mine, 'term', pairs_low(ranks)) if low > 1 else mine  5.17 us
    ppermute x6, waiting for transfers between devices, gather_high(): lax.ppermute(held, 'term', pairs_high(ranks, low, k))  4.65 us
    ppermute x4, starting transfers between devices, low_sum(): lax.ppermute(send, 'term', pairs_low(ranks)).astype(jnp.float32)  4.49 us
  transfers between devices with their start and end apart: 31, of which 13 were waited for; matrix products, arithmetic and copies ran while one was open for 1% of the time, Pallas kernels for 21%

profile of v8, /device:TPU:0, one launch (start us, length us, event | category | flops | bytes accessed | tf_op | source)
XLA Modules:
  0.0 86.7 jit_solution(16255307978383418142)
XLA Ops:
  0.6 1.6 %first.3 = (bf16[2,512,512]{2,1,0:T(8,128)(2,1)S(1)}, bf16[512,512]{1,0:T(8,128)(2,1)S(1)}, bf16[512,512]{1,0:T(8,128)(2,1)S(1)}) custom-call(s32[2]{0:T(128)} %size_ref.9, f32[2,512,512]{2,1,0:T(8,128)} %vector_ref.3), custom_call_target="tpu_custom_call" | custom-call | flops 1048576 | bytes 4096 | tf_op jit(solution)/shard_map/first/pallas_call | solution.py:304
  2.3 0.5 collective-permute-start
  2.8 0.7 collective-permute-start.5
  3.5 0.8 collective-permute-done.refs_0_
  4.3 4.4 %first.4 = (bf16[4,64,512]{2,1,0:T(8,128)(2,1)S(1)}, f32[4,64,512]{2,1,0:T(8,128)S(1)}, bf16[4,512,512]{2,1,0:T(8,128)(2,1)S(1)}, bf16[4,512,512]{2,1,0:T(8,128)(2,1)S(1)}, f32[2,64,512]{2,1,0:T(8,128)S(1)}) custom-call(bf16[2,512,512]{2,1,0:T(8,128)(2,1)S(1)} %get-tuple-element.33.own, bf16[512,512]{1,0:T(8,128)(2,1)S(1)} %collective-permute-done.refs_0_, ...), custom_call_target="tpu_custom_call" | custom-call | flops 2147483648 | bytes 8388608 | tf_op jit(solution)/shard_map/first/pallas_call | solution.py:304
  8.7 3.0 %collective-permute-start.1 = (bf16[4,64,512]{2,1,0:T(8,128)(2,1)S(1)}, bf16[4,64,512]{2,1,0:T(8,128)(2,1)S(1)}, u32[]{:S(2)}, u32[]{:S(2)}) collective-permute-start(bf16[4,64,512]{2,1,0:T(8,128)(2,1)S(1)} %get-tuple-element.37), channel_id=1, source_target_pairs={{0,1},{1,0},{2,3},{3,2},{4,5},{5,4},{6,7},{7,6},{8,9},{9,8},{10,11... | collective-permute-start | bytes 786440 | tf_op jit(solution)/shard_map/first/ppermute | solution.py:348
  11.7 3.6 %first.5 = (bf16[4,64,512]{2,1,0:T(8,128)(2,1)S(1)}, f32[4,64,512]{2,1,0:T(8,128)S(1)}, bf16[4,512,512]{2,1,0:T(8,128)(2,1)S(1)}, bf16[4,512,512]{2,1,0:T(8,128)(2,1)S(1)}) custom-call(bf16[2,512,512]{2,1,0:T(8,128)(2,1)S(1)} %get-tuple-element.33.own, bf16[512,512]{1,0:T(8,128)(2,1)S(1)} %collective-permute-done.5.refs_0_, s32[4]{0:T(128)} %shift_ref.5, ...), custom_call_target="tpu_custom_call" | custom-call | flops 2147483648 | bytes 8388608 | tf_op jit(solution)/shard_map/first/pallas_call | solution.py:304
  15.4 2.3 %collective-permute-done.1 = bf16[4,64,512]{2,1,0:T(8,128)(2,1)S(1)} collective-permute-done((bf16[4,64,512]{2,1,0:T(8,128)(2,1)S(1)}, bf16[4,64,512]{2,1,0:T(8,128)(2,1)S(1)}, u32[]{:S(2)}, u32[]{:S(2)}) %collective-permute-start.1) | collective-permute-done | bytes 262176 | tf_op jit(solution)/shard_map/first/ppermute | solution.py:348
  17.9 4.6 %collective-permute-start.2 = (bf16[64,512]{1,0:T(8,128)(2,1)S(1)}, bf16[64,512]{1,0:T(8,128)(2,1)S(1)}, u32[]{:S(2)}, u32[]{:S(2)}) collective-permute-start(bf16[64,512]{1,0:T(8,128)(2,1)S(1)} %get-tuple-element.87), channel_id=1, source_target_pairs={{0,6},{1,7},{2,4},{3,5},{4,2},{5,3},{6,0},{7,1},{8,14},{9,15},{10,... | collective-permute-start | bytes 196616 | tf_op jit(solution)/shard_map/gather/ppermute | solution.py:354
  22.5 0.6 collective-permute-start.4
  23.3 3.8 %collective-permute-start.7 = (bf16[64,512]{1,0:T(8,128)(2,1)S(1)}, bf16[64,512]{1,0:T(8,128)(2,1)S(1)}, u32[]{:S(2)}, u32[]{:S(2)}) collective-permute-start(bf16[64,512]{1,0:T(8,128)(2,1)S(1)} %get-tuple-element.84), channel_id=1, source_target_pairs={{0,6},{1,7},{2,4},{3,5},{4,2},{5,3},{6,0},{7,1},{8,14},{9,15},{10,... | collective-permute-start | bytes 196616 | tf_op jit(solution)/shard_map/gather/ppermute | solution.py:354
  27.2 0.6 collective-permute-start.9
  27.8 1.2 %collective-permute-done.3.refs_2_ = bf16[64,512]{1,0:T(8,128)(2,1)S(1)} collective-permute-done((bf16[64,512]{1,0:T(8,128)(2,1)S(1)}, bf16[64,512]{1,0:T(8,128)(2,1)S(1)}, u32[]{:S(2)}, u32[]{:S(2)}) %collective-permute-start.3) | collective-permute-done | bytes 65568 | tf_op jit(solution)/shard_map/gather/ppermute | solution.py:354
  29.1 0.7 gather.2
  29.8 2.6 %collective-permute-start.12 = (bf16[1,64,512]{2,1,0:T(8,128)(2,1)S(1)}, bf16[1,64,512]{2,1,0:T(8,128)(2,1)S(1)}, u32[]{:S(2)}, u32[]{:S(2)}) collective-permute-start(bf16[1,64,512]{2,1,0:T(8,128)(2,1)S(1)} %bitcast.42), channel_id=1, source_target_pairs={{0,6},{1,7},{2,4},{3,5},{4,2},{5,3},{6,0},{7,1},{8,14},{9,15},{10,... | collective-permute-start | bytes 196616 | tf_op jit(solution)/shard_map/gather/ppermute | solution.py:359
  32.4 1.9 %collective-permute-start.10 = (bf16[1,64,512]{2,1,0:T(8,128)(2,1)S(1)}, bf16[1,64,512]{2,1,0:T(8,128)(2,1)S(1)}, u32[]{:S(2)}, u32[]{:S(2)}) collective-permute-start(bf16[1,64,512]{2,1,0:T(8,128)(2,1)S(1)} %bitcast.44), channel_id=1, source_target_pairs={{0,2},{1,3},{2,0},{3,1},{4,6},{5,7},{6,4},{7,5},{8,10},{9,11},{10,... | collective-permute-start | bytes 196616 | tf_op jit(solution)/shard_map/gather/ppermute | solution.py:359
  34.2 0.4 collective-permute-done.8.refs_2_
  34.7 0.7 gather.3
  35.4 2.3 %collective-permute-start.16 = (bf16[1,64,512]{2,1,0:T(8,128)(2,1)S(1)}, bf16[1,64,512]{2,1,0:T(8,128)(2,1)S(1)}, u32[]{:S(2)}, u32[]{:S(2)}) collective-permute-start(bf16[1,64,512]{2,1,0:T(8,128)(2,1)S(1)} %bitcast.46), channel_id=1, source_target_pairs={{0,6},{1,7},{2,4},{3,5},{4,2},{5,3},{6,0},{7,1},{8,14},{9,15},{10,... | collective-permute-start | bytes 196616 | tf_op jit(solution)/shard_map/gather/ppermute | solution.py:359
  37.7 2.2 %collective-permute-start.14 = (bf16[1,64,512]{2,1,0:T(8,128)(2,1)S(1)}, bf16[1,64,512]{2,1,0:T(8,128)(2,1)S(1)}, u32[]{:S(2)}, u32[]{:S(2)}) collective-permute-start(bf16[1,64,512]{2,1,0:T(8,128)(2,1)S(1)} %bitcast.48), channel_id=1, source_target_pairs={{0,2},{1,3},{2,0},{3,1},{4,6},{5,7},{6,4},{7,5},{8,10},{9,11},{10,... | collective-permute-start | bytes 196616 | tf_op jit(solution)/shard_map/gather/ppermute | solution.py:359
  39.8 0.5 collective-permute-done.11
  40.3 1.4 %collective-permute-start.13 = (bf16[4,64,512]{2,1,0:T(8,128)(2,1)S(1)}, bf16[4,64,512]{2,1,0:T(8,128)(2,1)S(1)}, u32[]{:S(2)}, u32[]{:S(2)}) collective-permute-start(bf16[4,64,512]{2,1,0:T(8,128)(2,1)S(1)} %get-tuple-element.81.mine), channel_id=1, source_target_pairs={{0,1},{1,0},{2,3},{3,2},{4,5},{5,4},{6,7},{7,6},{8,9},{9,8},{10,11... | collective-permute-start | bytes 786440 | tf_op jit(solution)/shard_map/gather/ppermute | solution.py:413
  41.7 0.3 collective-permute-done.16
  42.1 3.8 %collective-permute-done.15 = bf16[1,64,512]{2,1,0:T(8,128)(2,1)S(1)} collective-permute-done((bf16[1,64,512]{2,1,0:T(8,128)(2,1)S(1)}, bf16[1,64,512]{2,1,0:T(8,128)(2,1)S(1)}, u32[]{:S(2)}, u32[]{:S(2)}) %collective-permute-start.15) | collective-permute-done | bytes 65568 | tf_op jit(solution)/shard_map/gather/ppermute | solution.py:359
  46.0 1.4 %collective-permute-start.17 = (bf16[4,64,512]{2,1,0:T(8,128)(2,1)S(1)}, bf16[4,64,512]{2,1,0:T(8,128)(2,1)S(1)}, u32[]{:S(2)}, u32[]{:S(2)}) collective-permute-start(bf16[4,64,512]{2,1,0:T(8,128)(2,1)S(1)} %get-tuple-element.76.refs_0_), channel_id=1, source_target_pairs={{0,1},{1,0},{2,3},{3,2},{4,5},{5,4},{6,7},{7,6},{8,9},{9,8},{10,11... | collective-permute-start | bytes 786440 | tf_op jit(solution)/shard_map/gather/ppermute | solution.py:413
  47.4 1.9 %collective-permute-done.13.theirs = bf16[4,64,512]{2,1,0:T(8,128)(2,1)S(1)} collective-permute-done((bf16[4,64,512]{2,1,0:T(8,128)(2,1)S(1)}, bf16[4,64,512]{2,1,0:T(8,128)(2,1)S(1)}, u32[]{:S(2)}, u32[]{:S(2)}) %collective-permute-start.13) | collective-permute-done | bytes 262176 | tf_op jit(solution)/shard_map/gather/ppermute | solution.py:413
  49.3 0.7 second.5
  50.0 0.9 %copy-done = f32[2,512,512]{2,1,0:T(8,128)S(1)} copy-done((f32[2,512,512]{2,1,0:T(8,128)S(1)}, f32[2,512,512]{2,1,0:T(8,128)}, u32[]{:S(2)}) %copy-start) | copy-done | bytes 2097176
  50.9 1.0 %second.6 = f32[8,512]{1,0:T(8,128)S(1)} custom-call(s32[2]{0:T(128)S(1)} %copy-done.1, f32[2,512,512]{2,1,0:T(8,128)S(1)} %copy-done, bf16[512,512]{1,0:T(8,128)(2,1)S(1)} %get-tuple-element.51.block.first_block), custom_call_target="tpu_custom_call" | custom-call | flops 1 | tf_op jit(solution)/shard_map/second/pallas_call | solution.py:304
  52.0 3.3 %collective-permute-done.17.refs_1_ = bf16[4,64,512]{2,1,0:T(8,128)(2,1)S(1)} collective-permute-done((bf16[4,64,512]{2,1,0:T(8,128)(2,1)S(1)}, bf16[4,64,512]{2,1,0:T(8,128)(2,1)S(1)}, u32[]{:S(2)}, u32[]{:S(2)}) %collective-permute-start.17) | collective-permute-done | bytes 262176 | tf_op jit(solution)/shard_map/gather/ppermute | solution.py:413
  55.3 0.9 %collective-permute-start.23 = (bf16[2,4,64,512]{3,2,1,0:T(8,128)(2,1)S(1)}, bf16[2,4,64,512]{3,2,1,0:T(8,128)(2,1)S(1)}, u32[]{:S(2)}, u32[]{:S(2)}) collective-permute-start(bf16[2,4,64,512]{3,2,1,0:T(8,128)(2,1)S(1)} %pad_maximum_fusion.1), channel_id=1, source_target_pairs={{8,16},{16,8},{9,17},{17,9},{10,18},{18,10},{11,19},{19,11},{12,20... | collective-permute-start | bytes 1572872 | tf_op jit(solution)/shard_map/second/ppermute | solution.py:343
  56.2 0.9 %collective-permute-done.18.refs_2_ = bf16[2,4,64,512]{3,2,1,0:T(8,128)(2,1)S(1)} collective-permute-done((bf16[2,4,64,512]{3,2,1,0:T(8,128)(2,1)S(1)}, bf16[2,4,64,512]{3,2,1,0:T(8,128)(2,1)S(1)}, u32[]{:S(2)}, u32[]{:S(2)}) %collective-permute-start.18) | collective-permute-done | bytes 524320 | tf_op jit(solution)/shard_map/second/ppermute | solution.py:343
  57.1 3.7 %second.7 = (bf16[4,64,512]{2,1,0:T(8,128)(2,1)S(1)}, f32[4,64,512]{2,1,0:T(8,128)S(1)}, bf16[2,512,512]{2,1,0:T(8,128)(2,1)S(1)}) custom-call(s32[4]{0:T(128)S(1)} %copy-done.4, f32[512,512]{1,0:T(8,128)S(1)} %get-tuple-element.50.acc_ref, bf16[512,512]{1,0:T(8,128)(2,1)S(1)} %get-tuple-element.51.block.first_block, ...), custom_call_target="tpu_custom_call" | custom-call | flops 1073741824 | bytes 4194304 | tf_op jit(solution)/shard_map/second/pallas_call | solution.py:304
  60.8 0.7 collective-permute-start.19
  61.5 1.0 %second.8 = f32[8,512]{1,0:T(8,128)S(1)} custom-call(s32[2]{0:T(128)S(1)} %copy-done.1, f32[2,512,512]{2,1,0:T(8,128)S(1)} %copy-done, bf16[2,512,512]{2,1,0:T(8,128)(2,1)S(1)} %get-tuple-element.58.block.own), custom_call_target="tpu_custom_call" | custom-call | flops 1 | tf_op jit(solution)/shard_map/second/pallas_call | solution.py:304
  62.5 2.9 %second.9 = (bf16[4,64,512]{2,1,0:T(8,128)(2,1)S(1)}, f32[4,64,512]{2,1,0:T(8,128)S(1)}) custom-call(s32[4]{0:T(128)S(1)} %copy-done.4, bf16[2,512,512]{2,1,0:T(8,128)(2,1)S(1)} %get-tuple-element.58.block.own, bf16[4,512,512]{2,1,0:T(8,128)(2,1)S(1)} %get-tuple-element.59.left, bf16[4,512,512]{2,1,0:T(8,128)(2,1)S(1)} %get-tuple-element.60.right, ...), custom_call_target="tpu_custom_call" | custom-call | flops 2147483648 | bytes 8388608 | tf_op jit(solution)/shard_map/second/pallas_call | solution.py:304
  65.4 0.8 collective-permute-start.24
  66.2 3.7 %collective-permute-done.19 = bf16[4,64,512]{2,1,0:T(8,128)(2,1)S(1)} collective-permute-done((bf16[4,64,512]{2,1,0:T(8,128)(2,1)S(1)}, bf16[4,64,512]{2,1,0:T(8,128)(2,1)S(1)}, u32[]{:S(2)}, u32[]{:S(2)}) %collective-permute-start.19) | collective-permute-done | bytes 262176 | tf_op jit(solution)/shard_map/second/ppermute | solution.py:348
  70.0 1.6 %collective-permute-start.20 = (bf16[64,512]{1,0:T(8,128)(2,1)S(1)}, bf16[64,512]{1,0:T(8,128)(2,1)S(1)}, u32[]{:S(2)}, u32[]{:S(2)}) collective-permute-start(bf16[64,512]{1,0:T(8,128)(2,1)S(1)} %get-tuple-element.79), channel_id=1, source_target_pairs={{0,6},{1,7},{2,4},{3,5},{4,2},{5,3},{6,0},{7,1},{8,14},{9,15},{10,... | collective-permute-start | bytes 196616 | tf_op jit(solution)/shard_map/scalars/ppermute | solution.py:354
  71.6 2.9 %collective-permute-start.22 = (bf16[64,512]{1,0:T(8,128)(2,1)S(1)}, bf16[64,512]{1,0:T(8,128)(2,1)S(1)}, u32[]{:S(2)}, u32[]{:S(2)}) collective-permute-start(bf16[64,512]{1,0:T(8,128)(2,1)S(1)} %get-tuple-element.77), channel_id=1, source_target_pairs={{0,2},{1,3},{2,0},{3,1},{4,6},{5,7},{6,4},{7,5},{8,10},{9,11},{10,... | collective-permute-start | bytes 196616 | tf_op jit(solution)/shard_map/scalars/ppermute | solution.py:354
  74.6 1.6 %collective-permute-start.25 = (bf16[64,512]{1,0:T(8,128)(2,1)S(1)}, bf16[64,512]{1,0:T(8,128)(2,1)S(1)}, u32[]{:S(2)}, u32[]{:S(2)}) collective-permute-start(bf16[64,512]{1,0:T(8,128)(2,1)S(1)} %get-tuple-element.74), channel_id=1, source_target_pairs={{0,6},{1,7},{2,4},{3,5},{4,2},{5,3},{6,0},{7,1},{8,14},{9,15},{10,... | collective-permute-start | bytes 196616 | tf_op jit(solution)/shard_map/scalars/ppermute | solution.py:354
  76.2 2.4 %collective-permute-done.22.refs_9_ = bf16[64,512]{1,0:T(8,128)(2,1)S(1)} collective-permute-done((bf16[64,512]{1,0:T(8,128)(2,1)S(1)}, bf16[64,512]{1,0:T(8,128)(2,1)S(1)}, u32[]{:S(2)}, u32[]{:S(2)}) %collective-permute-start.22) | collective-permute-done | bytes 65568 | tf_op jit(solution)/shard_map/scalars/ppermute | solution.py:354
  78.6 0.8 collective-permute-start.27
  79.4 0.1 collective-permute-start.28
  79.6 1.6 %collective-permute-start.29 = (f32[8,512]{1,0:T(8,128)S(1)}, f32[8,512]{1,0:T(8,128)S(1)}, u32[]{:S(2)}, u32[]{:S(2)}) collective-permute-start(f32[8,512]{1,0:T(8,128)S(1)} %add.19.refs_14_), channel_id=1, source_target_pairs={{0,16},{8,24},{16,0},{24,8},{1,17},{9,25},{17,1},{25,9},{2,18},{10... | collective-permute-start | bytes 49160 | tf_op jit(solution)/shard_map/scalars/ppermute | solution.py:477
  81.2 0.1 collective-permute-start.30
  81.3 3.8 %collective-permute-done.26.refs_12_ = bf16[64,512]{1,0:T(8,128)(2,1)S(1)} collective-permute-done((bf16[64,512]{1,0:T(8,128)(2,1)S(1)}, bf16[64,512]{1,0:T(8,128)(2,1)S(1)}, u32[]{:S(2)}, u32[]{:S(2)}) %collective-permute-start.26) | collective-permute-done | bytes 65568 | tf_op jit(solution)/shard_map/scalars/ppermute | solution.py:354
  85.2 1.5 %scalars.1 = (f32[2,64,512]{2,1,0:T(8,128)}, f32[2,64,512]{2,1,0:T(8,128)}) custom-call(s32[2]{0:T(128)S(1)} %copy-done.1, f32[2,64,512]{2,1,0:T(8,128)S(1)} %get-tuple-element.35.start, f32[64,512]{1,0:T(8,128)S(1)} %get-tuple-element.38.refs_0_, f32[64,512]{1,0:T(8,128)S(1)} %get-tuple-element.42.refs_1_, f32[64,512]{1,0:T(8,128)S(1)} %get-tuple-element.43.refs_2_, ...), custom_call_target="tpu_custom_call" | custom-call | flops 1048576 | bytes 4096 | tf_op jit(solution)/shard_map/scalars/pallas_call | solution.py:304
  (52 shorter events, 1.0 us)
Async XLA Ops:
  2.3 2.1 %collective-permute-start = (bf16[512,512]{1,0:T(8,128)(2,1)S(1)}, bf16[512,512]{1,0:T(8,128)(2,1)S(1)}, u32[]{:S(2)}, u32[]{:S(2)}) collective-permute-start(bf16[512,512]{1,0:T(8,128)(2,1)S(1)} %get-tuple-element.34), channel_id=1, source_target_pairs={{0,8},{8,0},{16,24},{24,16},{1,9},{9,1},{17,25},{25,17},{2,10},{10... | collective-permute-start | bytes 1572872 | tf_op jit(solution)/shard_map/first/ppermute | solution.py:343
  2.8 8.9 %collective-permute-start.5 = (bf16[512,512]{1,0:T(8,128)(2,1)S(1)}, bf16[512,512]{1,0:T(8,128)(2,1)S(1)}, u32[]{:S(2)}, u32[]{:S(2)}) collective-permute-start(bf16[512,512]{1,0:T(8,128)(2,1)S(1)} %get-tuple-element.39), channel_id=1, source_target_pairs={{8,16},{16,8},{9,17},{17,9},{10,18},{18,10},{11,19},{19,11},{12,20... | collective-permute-start | bytes 1572872 | tf_op jit(solution)/shard_map/first/ppermute | solution.py:343
  8.7 9.0 %collective-permute-start.1 = (bf16[4,64,512]{2,1,0:T(8,128)(2,1)S(1)}, bf16[4,64,512]{2,1,0:T(8,128)(2,1)S(1)}, u32[]{:S(2)}, u32[]{:S(2)}) collective-permute-start(bf16[4,64,512]{2,1,0:T(8,128)(2,1)S(1)} %get-tuple-element.37), channel_id=1, source_target_pairs={{0,1},{1,0},{2,3},{3,2},{4,5},{5,4},{6,7},{7,6},{8,9},{9,8},{10,11... | collective-permute-start | bytes 786440 | tf_op jit(solution)/shard_map/first/ppermute | solution.py:348
  15.3 7.8 %collective-permute-start.6 = (bf16[4,64,512]{2,1,0:T(8,128)(2,1)S(1)}, bf16[4,64,512]{2,1,0:T(8,128)(2,1)S(1)}, u32[]{:S(2)}, u32[]{:S(2)}) collective-permute-start(bf16[4,64,512]{2,1,0:T(8,128)(2,1)S(1)} %get-tuple-element.41), channel_id=1, source_target_pairs={{0,1},{1,0},{2,3},{3,2},{4,5},{5,4},{6,7},{7,6},{8,9},{9,8},{10,11... | collective-permute-start | bytes 786440 | tf_op jit(solution)/shard_map/first/ppermute | solution.py:348
  17.8 11.3 %copy-start.1 = (s32[2]{0:T(128)S(1)}, s32[2]{0:T(128)}, u32[]{:S(2)}) copy-start(s32[2]{0:T(128)} %size_ref.9) | copy-start | bytes 28
  17.8 11.3 %copy-start.2 = (f32[2,512]{1,0:T(2,128)S(1)}, f32[2,512]{1,0:T(2,128)}, u32[]{:S(2)}) copy-start(f32[2,512]{1,0:T(2,128)} %left_row.3) | copy-start | bytes 12292
  17.8 11.3 %copy-start.3 = (f32[2,512]{1,0:T(2,128)S(1)}, f32[2,512]{1,0:T(2,128)}, u32[]{:S(2)}) copy-start(f32[2,512]{1,0:T(2,128)} %right_row.3) | copy-start | bytes 12292
  17.9 9.3 %collective-permute-start.2 = (bf16[64,512]{1,0:T(8,128)(2,1)S(1)}, bf16[64,512]{1,0:T(8,128)(2,1)S(1)}, u32[]{:S(2)}, u32[]{:S(2)}) collective-permute-start(bf16[64,512]{1,0:T(8,128)(2,1)S(1)} %get-tuple-element.87), channel_id=1, source_target_pairs={{0,6},{1,7},{2,4},{3,5},{4,2},{5,3},{6,0},{7,1},{8,14},{9,15},{10,... | collective-permute-start | bytes 196616 | tf_op jit(solution)/shard_map/gather/ppermute | solution.py:354
  22.5 6.5 %collective-permute-start.3 = (bf16[64,512]{1,0:T(8,128)(2,1)S(1)}, bf16[64,512]{1,0:T(8,128)(2,1)S(1)}, u32[]{:S(2)}, u32[]{:S(2)}) collective-permute-start(bf16[64,512]{1,0:T(8,128)(2,1)S(1)} %get-tuple-element.86), channel_id=1, source_target_pairs={{0,4},{1,5},{2,6},{3,7},{4,0},{5,1},{6,2},{7,3},{8,12},{9,13},{10,... | collective-permute-start | bytes 196616 | tf_op jit(solution)/shard_map/gather/ppermute | solution.py:354
  22.5 6.5 %collective-permute-start.4 = (bf16[64,512]{1,0:T(8,128)(2,1)S(1)}, bf16[64,512]{1,0:T(8,128)(2,1)S(1)}, u32[]{:S(2)}, u32[]{:S(2)}) collective-permute-start(bf16[64,512]{1,0:T(8,128)(2,1)S(1)} %get-tuple-element.85), channel_id=1, source_target_pairs={{0,2},{1,3},{2,0},{3,1},{4,6},{5,7},{6,4},{7,5},{8,10},{9,11},{10,... | collective-permute-start | bytes 196616 | tf_op jit(solution)/shard_map/gather/ppermute | solution.py:354
  23.3 26.0 %copy-start.4 = (s32[4]{0:T(128)S(1)}, s32[4]{0:T(128)}, u32[]{:S(2)}) copy-start(s32[4]{0:T(128)} %shift_ref.5) | copy-start | bytes 52
  23.3 9.1 %collective-permute-start.7 = (bf16[64,512]{1,0:T(8,128)(2,1)S(1)}, bf16[64,512]{1,0:T(8,128)(2,1)S(1)}, u32[]{:S(2)}, u32[]{:S(2)}) collective-permute-start(bf16[64,512]{1,0:T(8,128)(2,1)S(1)} %get-tuple-element.84), channel_id=1, source_target_pairs={{0,6},{1,7},{2,4},{3,5},{4,2},{5,3},{6,0},{7,1},{8,14},{9,15},{10,... | collective-permute-start | bytes 196616 | tf_op jit(solution)/shard_map/gather/ppermute | solution.py:354
  27.1 7.6 %collective-permute-start.8 = (bf16[64,512]{1,0:T(8,128)(2,1)S(1)}, bf16[64,512]{1,0:T(8,128)(2,1)S(1)}, u32[]{:S(2)}, u32[]{:S(2)}) collective-permute-start(bf16[64,512]{1,0:T(8,128)(2,1)S(1)} %get-tuple-element.83), channel_id=1, source_target_pairs={{0,4},{1,5},{2,6},{3,7},{4,0},{5,1},{6,2},{7,3},{8,12},{9,13},{10,... | collective-permute-start | bytes 196616 | tf_op jit(solution)/shard_map/gather/ppermute | solution.py:354
  27.2 7.5 %collective-permute-start.9 = (bf16[64,512]{1,0:T(8,128)(2,1)S(1)}, bf16[64,512]{1,0:T(8,128)(2,1)S(1)}, u32[]{:S(2)}, u32[]{:S(2)}) collective-permute-start(bf16[64,512]{1,0:T(8,128)(2,1)S(1)} %get-tuple-element.82), channel_id=1, source_target_pairs={{0,2},{1,3},{2,0},{3,1},{4,6},{5,7},{6,4},{7,5},{8,10},{9,11},{10,... | collective-permute-start | bytes 196616 | tf_op jit(solution)/shard_map/gather/ppermute | solution.py:354
  29.8 7.9 %collective-permute-start.12 = (bf16[1,64,512]{2,1,0:T(8,128)(2,1)S(1)}, bf16[1,64,512]{2,1,0:T(8,128)(2,1)S(1)}, u32[]{:S(2)}, u32[]{:S(2)}) collective-permute-start(bf16[1,64,512]{2,1,0:T(8,128)(2,1)S(1)} %bitcast.42), channel_id=1, source_target_pairs={{0,6},{1,7},{2,4},{3,5},{4,2},{5,3},{6,0},{7,1},{8,14},{9,15},{10,... | collective-permute-start | bytes 196616 | tf_op jit(solution)/shard_map/gather/ppermute | solution.py:359
  32.4 7.9 %collective-permute-start.11 = (bf16[1,64,512]{2,1,0:T(8,128)(2,1)S(1)}, bf16[1,64,512]{2,1,0:T(8,128)(2,1)S(1)}, u32[]{:S(2)}, u32[]{:S(2)}) collective-permute-start(bf16[1,64,512]{2,1,0:T(8,128)(2,1)S(1)} %bitcast.43), channel_id=1, source_target_pairs={{0,4},{1,5},{2,6},{3,7},{4,0},{5,1},{6,2},{7,3},{8,12},{9,13},{10,... | collective-permute-start | bytes 196616 | tf_op jit(solution)/shard_map/gather/ppermute | solution.py:359
  32.4 7.9 %collective-permute-start.10 = (bf16[1,64,512]{2,1,0:T(8,128)(2,1)S(1)}, bf16[1,64,512]{2,1,0:T(8,128)(2,1)S(1)}, u32[]{:S(2)}, u32[]{:S(2)}) collective-permute-start(bf16[1,64,512]{2,1,0:T(8,128)(2,1)S(1)} %bitcast.44), channel_id=1, source_target_pairs={{0,2},{1,3},{2,0},{3,1},{4,6},{5,7},{6,4},{7,5},{8,10},{9,11},{10,... | collective-permute-start | bytes 196616 | tf_op jit(solution)/shard_map/gather/ppermute | solution.py:359
  35.4 6.7 %collective-permute-start.16 = (bf16[1,64,512]{2,1,0:T(8,128)(2,1)S(1)}, bf16[1,64,512]{2,1,0:T(8,128)(2,1)S(1)}, u32[]{:S(2)}, u32[]{:S(2)}) collective-permute-start(bf16[1,64,512]{2,1,0:T(8,128)(2,1)S(1)} %bitcast.46), channel_id=1, source_target_pairs={{0,6},{1,7},{2,4},{3,5},{4,2},{5,3},{6,0},{7,1},{8,14},{9,15},{10,... | collective-permute-start | bytes 196616 | tf_op jit(solution)/shard_map/gather/ppermute | solution.py:359
  37.6 8.3 %collective-permute-start.15 = (bf16[1,64,512]{2,1,0:T(8,128)(2,1)S(1)}, bf16[1,64,512]{2,1,0:T(8,128)(2,1)S(1)}, u32[]{:S(2)}, u32[]{:S(2)}) collective-permute-start(bf16[1,64,512]{2,1,0:T(8,128)(2,1)S(1)} %bitcast.47), channel_id=1, source_target_pairs={{0,4},{1,5},{2,6},{3,7},{4,0},{5,1},{6,2},{7,3},{8,12},{9,13},{10,... | collective-permute-start | bytes 196616 | tf_op jit(solution)/shard_map/gather/ppermute | solution.py:359
  37.7 8.3 %collective-permute-start.14 = (bf16[1,64,512]{2,1,0:T(8,128)(2,1)S(1)}, bf16[1,64,512]{2,1,0:T(8,128)(2,1)S(1)}, u32[]{:S(2)}, u32[]{:S(2)}) collective-permute-start(bf16[1,64,512]{2,1,0:T(8,128)(2,1)S(1)} %bitcast.48), channel_id=1, source_target_pairs={{0,2},{1,3},{2,0},{3,1},{4,6},{5,7},{6,4},{7,5},{8,10},{9,11},{10,... | collective-permute-start | bytes 196616 | tf_op jit(solution)/shard_map/gather/ppermute | solution.py:359
  40.3 8.9 %collective-permute-start.13 = (bf16[4,64,512]{2,1,0:T(8,128)(2,1)S(1)}, bf16[4,64,512]{2,1,0:T(8,128)(2,1)S(1)}, u32[]{:S(2)}, u32[]{:S(2)}) collective-permute-start(bf16[4,64,512]{2,1,0:T(8,128)(2,1)S(1)} %get-tuple-element.81.mine), channel_id=1, source_target_pairs={{0,1},{1,0},{2,3},{3,2},{4,5},{5,4},{6,7},{7,6},{8,9},{9,8},{10,11... | collective-permute-start | bytes 786440 | tf_op jit(solution)/shard_map/gather/ppermute | solution.py:413
  46.0 9.2 %collective-permute-start.17 = (bf16[4,64,512]{2,1,0:T(8,128)(2,1)S(1)}, bf16[4,64,512]{2,1,0:T(8,128)(2,1)S(1)}, u32[]{:S(2)}, u32[]{:S(2)}) collective-permute-start(bf16[4,64,512]{2,1,0:T(8,128)(2,1)S(1)} %get-tuple-element.76.refs_0_), channel_id=1, source_target_pairs={{0,1},{1,0},{2,3},{3,2},{4,5},{5,4},{6,7},{7,6},{8,9},{9,8},{10,11... | collective-permute-start | bytes 786440 | tf_op jit(solution)/shard_map/gather/ppermute | solution.py:413
  49.3 1.6 %copy-start = (f32[2,512,512]{2,1,0:T(8,128)S(1)}, f32[2,512,512]{2,1,0:T(8,128)}, u32[]{:S(2)}) copy-start(f32[2,512,512]{2,1,0:T(8,128)} %vector_ref.3) | copy-start | bytes 6291460
  55.2 1.9 %collective-permute-start.18 = (bf16[2,4,64,512]{3,2,1,0:T(8,128)(2,1)S(1)}, bf16[2,4,64,512]{3,2,1,0:T(8,128)(2,1)S(1)}, u32[]{:S(2)}, u32[]{:S(2)}) collective-permute-start(bf16[2,4,64,512]{3,2,1,0:T(8,128)(2,1)S(1)} %pad_maximum_fusion), channel_id=1, source_target_pairs={{0,8},{8,0},{16,24},{24,16},{1,9},{9,1},{17,25},{25,17},{2,10},{10... | collective-permute-start | bytes 1572872 | tf_op jit(solution)/shard_map/second/ppermute | solution.py:343
  55.3 7.2 %collective-permute-start.23 = (bf16[2,4,64,512]{3,2,1,0:T(8,128)(2,1)S(1)}, bf16[2,4,64,512]{3,2,1,0:T(8,128)(2,1)S(1)}, u32[]{:S(2)}, u32[]{:S(2)}) collective-permute-start(bf16[2,4,64,512]{3,2,1,0:T(8,128)(2,1)S(1)} %pad_maximum_fusion.1), channel_id=1, source_target_pairs={{8,16},{16,8},{9,17},{17,9},{10,18},{18,10},{11,19},{19,11},{12,20... | collective-permute-start | bytes 1572872 | tf_op jit(solution)/shard_map/second/ppermute | solution.py:343
  60.8 9.1 %collective-permute-start.19 = (bf16[4,64,512]{2,1,0:T(8,128)(2,1)S(1)}, bf16[4,64,512]{2,1,0:T(8,128)(2,1)S(1)}, u32[]{:S(2)}, u32[]{:S(2)}) collective-permute-start(bf16[4,64,512]{2,1,0:T(8,128)(2,1)S(1)} %get-tuple-element.55), channel_id=1, source_target_pairs={{0,1},{1,0},{2,3},{3,2},{4,5},{5,4},{6,7},{7,6},{8,9},{9,8},{10,11... | collective-permute-start | bytes 786440 | tf_op jit(solution)/shard_map/second/ppermute | solution.py:348
  65.4 9.0 %collective-permute-start.24 = (bf16[4,64,512]{2,1,0:T(8,128)(2,1)S(1)}, bf16[4,64,512]{2,1,0:T(8,128)(2,1)S(1)}, u32[]{:S(2)}, u32[]{:S(2)}) collective-permute-start(bf16[4,64,512]{2,1,0:T(8,128)(2,1)S(1)} %get-tuple-element.62), channel_id=1, source_target_pairs={{0,1},{1,0},{2,3},{3,2},{4,5},{5,4},{6,7},{7,6},{8,9},{9,8},{10,11... | collective-permute-start | bytes 786440 | tf_op jit(solution)/shard_map/second/ppermute | solution.py:348
  70.0 9.4 %collective-permute-start.20 = (bf16[64,512]{1,0:T(8,128)(2,1)S(1)}, bf16[64,512]{1,0:T(8,128)(2,1)S(1)}, u32[]{:S(2)}, u32[]{:S(2)}) collective-permute-start(bf16[64,512]{1,0:T(8,128)(2,1)S(1)} %get-tuple-element.79), channel_id=1, source_target_pairs={{0,6},{1,7},{2,4},{3,5},{4,2},{5,3},{6,0},{7,1},{8,14},{9,15},{10,... | collective-permute-start | bytes 196616 | tf_op jit(solution)/shard_map/scalars/ppermute | solution.py:354
  71.6 8.0 %collective-permute-start.21 = (bf16[64,512]{1,0:T(8,128)(2,1)S(1)}, bf16[64,512]{1,0:T(8,128)(2,1)S(1)}, u32[]{:S(2)}, u32[]{:S(2)}) collective-permute-start(bf16[64,512]{1,0:T(8,128)(2,1)S(1)} %get-tuple-element.78), channel_id=1, source_target_pairs={{0,4},{1,5},{2,6},{3,7},{4,0},{5,1},{6,2},{7,3},{8,12},{9,13},{10,... | collective-permute-start | bytes 196616 | tf_op jit(solution)/shard_map/scalars/ppermute | solution.py:354
  71.6 7.0 %collective-permute-start.22 = (bf16[64,512]{1,0:T(8,128)(2,1)S(1)}, bf16[64,512]{1,0:T(8,128)(2,1)S(1)}, u32[]{:S(2)}, u32[]{:S(2)}) collective-permute-start(bf16[64,512]{1,0:T(8,128)(2,1)S(1)} %get-tuple-element.77), channel_id=1, source_target_pairs={{0,2},{1,3},{2,0},{3,1},{4,6},{5,7},{6,4},{7,5},{8,10},{9,11},{10,... | collective-permute-start | bytes 196616 | tf_op jit(solution)/shard_map/scalars/ppermute | solution.py:354
  74.6 6.6 %collective-permute-start.25 = (bf16[64,512]{1,0:T(8,128)(2,1)S(1)}, bf16[64,512]{1,0:T(8,128)(2,1)S(1)}, u32[]{:S(2)}, u32[]{:S(2)}) collective-permute-start(bf16[64,512]{1,0:T(8,128)(2,1)S(1)} %get-tuple-element.74), channel_id=1, source_target_pairs={{0,6},{1,7},{2,4},{3,5},{4,2},{5,3},{6,0},{7,1},{8,14},{9,15},{10,... | collective-permute-start | bytes 196616 | tf_op jit(solution)/shard_map/scalars/ppermute | solution.py:354
  76.2 9.0 %collective-permute-start.26 = (bf16[64,512]{1,0:T(8,128)(2,1)S(1)}, bf16[64,512]{1,0:T(8,128)(2,1)S(1)}, u32[]{:S(2)}, u32[]{:S(2)}) collective-permute-start(bf16[64,512]{1,0:T(8,128)(2,1)S(1)} %get-tuple-element.73), channel_id=1, source_target_pairs={{0,4},{1,5},{2,6},{3,7},{4,0},{5,1},{6,2},{7,3},{8,12},{9,13},{10,... | collective-permute-start | bytes 196616 | tf_op jit(solution)/shard_map/scalars/ppermute | solution.py:354
  78.6 6.6 %collective-permute-start.27 = (bf16[64,512]{1,0:T(8,128)(2,1)S(1)}, bf16[64,512]{1,0:T(8,128)(2,1)S(1)}, u32[]{:S(2)}, u32[]{:S(2)}) collective-permute-start(bf16[64,512]{1,0:T(8,128)(2,1)S(1)} %get-tuple-element.72), channel_id=1, source_target_pairs={{0,2},{1,3},{2,0},{3,1},{4,6},{5,7},{6,4},{7,5},{8,10},{9,11},{10,... | collective-permute-start | bytes 196616 | tf_op jit(solution)/shard_map/scalars/ppermute | solution.py:354
  79.4 5.7 %collective-permute-start.28 = (f32[8,512]{1,0:T(8,128)S(1)}, f32[8,512]{1,0:T(8,128)S(1)}, u32[]{:S(2)}, u32[]{:S(2)}) collective-permute-start(f32[8,512]{1,0:T(8,128)S(1)} %add.19.refs_14_), channel_id=1, source_target_pairs={{0,8},{8,0},{16,24},{24,16},{1,9},{9,1},{17,25},{25,17},{2,10},{10... | collective-permute-start | bytes 49160 | tf_op jit(solution)/shard_map/scalars/ppermute | solution.py:477
  79.6 5.6 %collective-permute-start.29 = (f32[8,512]{1,0:T(8,128)S(1)}, f32[8,512]{1,0:T(8,128)S(1)}, u32[]{:S(2)}, u32[]{:S(2)}) collective-permute-start(f32[8,512]{1,0:T(8,128)S(1)} %add.19.refs_14_), channel_id=1, source_target_pairs={{0,16},{8,24},{16,0},{24,8},{1,17},{9,25},{17,1},{25,9},{2,18},{10... | collective-permute-start | bytes 49160 | tf_op jit(solution)/shard_map/scalars/ppermute | solution.py:477
  81.2 4.0 %collective-permute-start.30 = (f32[8,512]{1,0:T(8,128)S(1)}, f32[8,512]{1,0:T(8,128)S(1)}, u32[]{:S(2)}, u32[]{:S(2)}) collective-permute-start(f32[8,512]{1,0:T(8,128)S(1)} %add.19.refs_14_), channel_id=1, source_target_pairs={{0,24},{8,16},{16,8},{24,0},{1,25},{9,17},{17,9},{25,1},{2,26},{10... | collective-permute-start | bytes 49160 | tf_op jit(solution)/shard_map/scalars/ppermute | solution.py:477

commit v9 on v8

--- a/solution.py
+++ b/solution.py
@@ -46,6 +46,14 @@
     )
 
 
+def add_small_pair(acc, left, right, block):
+    half = block.shape[0] // 2
+    mixed = jnp.dot(left[:, :half], block[:half, :half], preferred_element_type=jnp.float32)
+    acc[...] += lax.dot_general(
+        mixed.astype(jnp.bfloat16), right[:, :half], NT, preferred_element_type=jnp.float32
+    )
+
+
 def sector_at(turn, sectors):
     odd = lax.rem(lax.axis_index("sector"), 2)
     return odd * turn + (1 - odd) * (sectors - 1 - turn)
@@ -61,7 +69,9 @@
     return side, (here + side >= 0) & (here + side < groups)
 
 
-def add_pairs(dims, turn, shift_ref, acc, left, right, own, halos, arrived=None, skip_own=False):
+def add_pairs(
+    dims, turn, shift_ref, size_ref, acc, left, right, own, halos, arrived=None, skip_own=False
+):
     sectors, terms = dims[:2]
     s = sector_at(turn, sectors)
     for t in range(terms):
@@ -72,7 +82,13 @@
         if skip_own:
             inside &= shift_ref[t] != 0
 
-        @pl.when(inside)
+        small = size_ref[jnp.clip(partner, 0, sectors - 1)] <= dims[2] // 2
+
+        @pl.when(inside & small)
+        def _():
+            add_small_pair(acc, left.at[t], right.at[t], own.at[partner])
+
+        @pl.when(inside & jnp.logical_not(small))
         def _():
             add_pair(acc, left.at[t], right.at[t], own.at[partner])
 
@@ -190,7 +206,7 @@
         for copy in copies[t]:
             copy.wait()
 
-    add_pairs(dims, turn, shift_ref, acc, left, right, own, blocks, arrived)
+    add_pairs(dims, turn, shift_ref, size_ref, acc, left, right, own, blocks, arrived)
     cut(dims, acc, send_ref, keep_ref)
     for e, copy in enumerate(rows):
         copy.wait()
@@ -208,7 +224,7 @@
             add_pair(acc, left.at[t], right.at[t], own)
 
 
-def rest_kernel(dims, shift_ref, acc_ref, first_block, left, right, *refs):
+def rest_kernel(dims, shift_ref, size_ref, acc_ref, first_block, left, right, *refs):
     sectors = dims[0]
     pieces, refs = refs[: 2 * sectors - 2], refs[2 * sectors - 2 :]
     halos, (send_ref, keep_ref, own, acc, wb) = refs[:-5], refs[-5:]
@@ -219,17 +235,17 @@
     for n, halo in enumerate(halos):
         place_rows(dims, wb.at[n], [halo.at[0], halo.at[1]])
     blocks = [wb.at[n] for n in range(len(halos))]
-    add_pairs(dims, 0, shift_ref, acc, left, right, own, blocks, skip_own=True)
+    add_pairs(dims, 0, shift_ref, size_ref, acc, left, right, own, blocks, skip_own=True)
     cut(dims, acc, send_ref, keep_ref)
 
 
-def full_kernel(dims, turn, shift_ref, own, left, right, *refs):
+def full_kernel(dims, turn, shift_ref, size_ref, own, left, right, *refs):
     halos, (send_ref, keep_ref, acc, wb) = refs[:-4], refs[-4:]
     acc[...] = jnp.zeros_like(acc)
     for n, halo in enumerate(halos):
         place_rows(dims, wb.at[n], [halo.at[0], halo.at[1]])
     blocks = [wb.at[n] for n in range(len(halos))]
-    add_pairs(dims, turn, shift_ref, acc, left, right, own, blocks)
+    add_pairs(dims, turn, shift_ref, size_ref, acc, left, right, own, blocks)
     cut(dims, acc, send_ref, keep_ref)
 
 
@@ -435,7 +451,7 @@
         *first_cut, own = call(
             functools.partial(rest_kernel, dims),
             [*cut_shapes, pltpu.VMEM((sectors, size, size), jnp.bfloat16)],
-            (sector_shifts,),
+            (sector_shifts, sector_sizes),
             (
                 acc,
                 block,
@@ -456,7 +472,7 @@
                 call(
                     functools.partial(full_kernel, dims, turn),
                     cut_shapes,
-                    (sector_shifts,),
+                    (sector_shifts, sector_sizes),
                     (own, left[turn], right[turn], *[halos[h] for h in halos_at(turn, sectors)]),
                     scratch=[square, pltpu.VMEM((2, size, size), jnp.bfloat16)],
                     flops=terms * pair_flops,

time: 86.7 us -> 86.1 us (level)
  starting transfers between devices: 36.9 us -> 40.8 us
  waiting for transfers between devices: 25.5 us -> 22 us
  local copies, waits for them, and re-layouts: 1.03 us -> 0.12 us
    ppermute x12, waiting for transfers between devices: 7.87 us -> 3.46 us  [high_parts(): lax.ppermute(total[k].astype(jnp.bfloat16), 'term', pairs_high(ranks, low...]
    ppermute x12, starting transfers between devices: 16.7 us -> 19.6 us  [high_parts(): lax.ppermute(total[k].astype(jnp.bfloat16), 'term', pairs_high(ranks, low...]
    ppermute x3, starting transfers between devices: 1.86 us -> 3.6 us  [on_device(): lax.ppermute(sums, 'sector', [(i, i ^ reach * k) for i in range(groups)])]
    ppermute x3, waiting for transfers between devices: 0.01 us -> 1.3 us  [on_device(): lax.ppermute(sums, 'sector', [(i, i ^ reach * k) for i in range(groups)])]
    unnamed x10, local copies, waits for them, and re-layouts: 0.94 us -> 0.02 us
where the time goes in v9:
time: 86.1 us; the launch traced here: 85.4 us
  starting transfers between devices  40.8 us (47%)
  waiting for transfers between devices  22 us (26%)
  Pallas kernels  21 us (24%)
  between operations  0.91 us (1%)
    pallas_call x11, Pallas kernels, call(): pl.pallas_call(kernel, out_shape=out_shape, in_specs=[SMEM] * len(scalars...  21 us
    ppermute x12, starting transfers between devices, high_parts(): lax.ppermute(total[k].astype(jnp.bfloat16), 'term', pairs_high(ranks, low...  19.6 us
    ppermute x6, starting transfers between devices, gather_high(): lax.ppermute(held, 'term', pairs_high(ranks, low, k))  8.91 us
    ppermute x4, waiting for transfers between devices, low_sum(): lax.ppermute(send, 'term', pairs_low(ranks)).astype(jnp.float32)  5.47 us
    ppermute x2, waiting for transfers between devices, on_device(): theirs = lax.ppermute(mine, 'term', pairs_low(ranks)) if low > 1 else mine  4.92 us
    ppermute x6, waiting for transfers between devices, gather_high(): lax.ppermute(held, 'term', pairs_high(ranks, low, k))  4.9 us
    ppermute x4, starting transfers between devices, low_sum(): lax.ppermute(send, 'term', pairs_low(ranks)).astype(jnp.float32)  4.48 us
    ppermute x3, starting transfers between devices, on_device(): lax.ppermute(sums, 'sector', [(i, i ^ reach * k) for i in range(groups)])  3.6 us
  transfers between devices with their start and end apart: 31, of which 13 were waited for; matrix products, arithmetic and copies ran while one was open for 1% of the time, Pallas kernels for 21%

profile of v9, /device:TPU:0, one launch (start us, length us, event | category | flops | bytes accessed | tf_op | source)
XLA Modules:
  0.0 85.4 jit_solution(2852539817447235919)
XLA Ops:
  0.6 1.6 %first.3 = (bf16[2,512,512]{2,1,0:T(8,128)(2,1)S(1)}, bf16[512,512]{1,0:T(8,128)(2,1)S(1)}, bf16[512,512]{1,0:T(8,128)(2,1)S(1)}) custom-call(s32[2]{0:T(128)} %size_ref.13, f32[2,512,512]{2,1,0:T(8,128)} %vector_ref.3), custom_call_target="tpu_custom_call" | custom-call | flops 1048576 | bytes 4096 | tf_op jit(solution)/shard_map/first/pallas_call | solution.py:320
  2.3 0.5 collective-permute-start
  2.8 0.7 collective-permute-start.5
  3.5 0.8 collective-permute-done.refs_0_
  4.3 4.1 %first.4 = (bf16[4,64,512]{2,1,0:T(8,128)(2,1)S(1)}, f32[4,64,512]{2,1,0:T(8,128)S(1)}, bf16[4,512,512]{2,1,0:T(8,128)(2,1)S(1)}, bf16[4,512,512]{2,1,0:T(8,128)(2,1)S(1)}, f32[2,64,512]{2,1,0:T(8,128)S(1)}) custom-call(bf16[2,512,512]{2,1,0:T(8,128)(2,1)S(1)} %get-tuple-element.33.own, bf16[512,512]{1,0:T(8,128)(2,1)S(1)} %collective-permute-done.refs_0_, ...), custom_call_target="tpu_custom_call" | custom-call | flops 2147483648 | bytes 8388608 | tf_op jit(solution)/shard_map/first/pallas_call | solution.py:320
  8.5 2.7 %collective-permute-start.1 = (bf16[4,64,512]{2,1,0:T(8,128)(2,1)S(1)}, bf16[4,64,512]{2,1,0:T(8,128)(2,1)S(1)}, u32[]{:S(2)}, u32[]{:S(2)}) collective-permute-start(bf16[4,64,512]{2,1,0:T(8,128)(2,1)S(1)} %get-tuple-element.37), channel_id=1, source_target_pairs={{0,1},{1,0},{2,3},{3,2},{4,5},{5,4},{6,7},{7,6},{8,9},{9,8},{10,11... | collective-permute-start | bytes 786440 | tf_op jit(solution)/shard_map/first/ppermute | solution.py:364
  11.2 3.6 %first.5 = (bf16[4,64,512]{2,1,0:T(8,128)(2,1)S(1)}, f32[4,64,512]{2,1,0:T(8,128)S(1)}, bf16[4,512,512]{2,1,0:T(8,128)(2,1)S(1)}, bf16[4,512,512]{2,1,0:T(8,128)(2,1)S(1)}) custom-call(bf16[2,512,512]{2,1,0:T(8,128)(2,1)S(1)} %get-tuple-element.33.own, bf16[512,512]{1,0:T(8,128)(2,1)S(1)} %collective-permute-done.5.refs_0_, s32[4]{0:T(128)} %shift_ref.5, ...), custom_call_target="tpu_custom_call" | custom-call | flops 2147483648 | bytes 8388608 | tf_op jit(solution)/shard_map/first/pallas_call | solution.py:320
  14.8 1.8 %collective-permute-done.1 = bf16[4,64,512]{2,1,0:T(8,128)(2,1)S(1)} collective-permute-done((bf16[4,64,512]{2,1,0:T(8,128)(2,1)S(1)}, bf16[4,64,512]{2,1,0:T(8,128)(2,1)S(1)}, u32[]{:S(2)}, u32[]{:S(2)}) %collective-permute-start.1) | collective-permute-done | bytes 262176 | tf_op jit(solution)/shard_map/first/ppermute | solution.py:364
  16.7 5.2 %collective-permute-start.2 = (bf16[64,512]{1,0:T(8,128)(2,1)S(1)}, bf16[64,512]{1,0:T(8,128)(2,1)S(1)}, u32[]{:S(2)}, u32[]{:S(2)}) collective-permute-start(bf16[64,512]{1,0:T(8,128)(2,1)S(1)} %get-tuple-element.87), channel_id=1, source_target_pairs={{0,6},{1,7},{2,4},{3,5},{4,2},{5,3},{6,0},{7,1},{8,14},{9,15},{10,... | collective-permute-start | bytes 196616 | tf_op jit(solution)/shard_map/gather/ppermute | solution.py:370
  21.9 0.6 collective-permute-start.4
  22.6 0.1 fusion.4
  22.7 3.8 %collective-permute-start.7 = (bf16[64,512]{1,0:T(8,128)(2,1)S(1)}, bf16[64,512]{1,0:T(8,128)(2,1)S(1)}, u32[]{:S(2)}, u32[]{:S(2)}) collective-permute-start(bf16[64,512]{1,0:T(8,128)(2,1)S(1)} %get-tuple-element.84), channel_id=1, source_target_pairs={{0,6},{1,7},{2,4},{3,5},{4,2},{5,3},{6,0},{7,1},{8,14},{9,15},{10,... | collective-permute-start | bytes 196616 | tf_op jit(solution)/shard_map/gather/ppermute | solution.py:370
  26.6 0.6 collective-permute-start.9
  27.3 1.4 %collective-permute-done.3.refs_2_ = bf16[64,512]{1,0:T(8,128)(2,1)S(1)} collective-permute-done((bf16[64,512]{1,0:T(8,128)(2,1)S(1)}, bf16[64,512]{1,0:T(8,128)(2,1)S(1)}, u32[]{:S(2)}, u32[]{:S(2)}) %collective-permute-start.3) | collective-permute-done | bytes 65568 | tf_op jit(solution)/shard_map/gather/ppermute | solution.py:370
  28.6 0.7 gather.2
  29.3 2.5 %collective-permute-start.12 = (bf16[1,64,512]{2,1,0:T(8,128)(2,1)S(1)}, bf16[1,64,512]{2,1,0:T(8,128)(2,1)S(1)}, u32[]{:S(2)}, u32[]{:S(2)}) collective-permute-start(bf16[1,64,512]{2,1,0:T(8,128)(2,1)S(1)} %bitcast.42), channel_id=1, source_target_pairs={{0,6},{1,7},{2,4},{3,5},{4,2},{5,3},{6,0},{7,1},{8,14},{9,15},{10,... | collective-permute-start | bytes 196616 | tf_op jit(solution)/shard_map/gather/ppermute | solution.py:375
  31.8 2.0 %collective-permute-start.10 = (bf16[1,64,512]{2,1,0:T(8,128)(2,1)S(1)}, bf16[1,64,512]{2,1,0:T(8,128)(2,1)S(1)}, u32[]{:S(2)}, u32[]{:S(2)}) collective-permute-start(bf16[1,64,512]{2,1,0:T(8,128)(2,1)S(1)} %bitcast.44), channel_id=1, source_target_pairs={{0,2},{1,3},{2,0},{3,1},{4,6},{5,7},{6,4},{7,5},{8,10},{9,11},{10,... | collective-permute-start | bytes 196616 | tf_op jit(solution)/shard_map/gather/ppermute | solution.py:375
  33.8 0.3 collective-permute-done.8.refs_2_
  34.1 0.7 gather.3
  34.8 2.4 %collective-permute-start.16 = (bf16[1,64,512]{2,1,0:T(8,128)(2,1)S(1)}, bf16[1,64,512]{2,1,0:T(8,128)(2,1)S(1)}, u32[]{:S(2)}, u32[]{:S(2)}) collective-permute-start(bf16[1,64,512]{2,1,0:T(8,128)(2,1)S(1)} %bitcast.46), channel_id=1, source_target_pairs={{0,6},{1,7},{2,4},{3,5},{4,2},{5,3},{6,0},{7,1},{8,14},{9,15},{10,... | collective-permute-start | bytes 196616 | tf_op jit(solution)/shard_map/gather/ppermute | solution.py:375
  37.2 2.0 %collective-permute-start.14 = (bf16[1,64,512]{2,1,0:T(8,128)(2,1)S(1)}, bf16[1,64,512]{2,1,0:T(8,128)(2,1)S(1)}, u32[]{:S(2)}, u32[]{:S(2)}) collective-permute-start(bf16[1,64,512]{2,1,0:T(8,128)(2,1)S(1)} %bitcast.48), channel_id=1, source_target_pairs={{0,2},{1,3},{2,0},{3,1},{4,6},{5,7},{6,4},{7,5},{8,10},{9,11},{10,... | collective-permute-start | bytes 196616 | tf_op jit(solution)/shard_map/gather/ppermute | solution.py:375
  39.3 0.5 collective-permute-done.11
  39.8 1.1 %collective-permute-start.13 = (bf16[4,64,512]{2,1,0:T(8,128)(2,1)S(1)}, bf16[4,64,512]{2,1,0:T(8,128)(2,1)S(1)}, u32[]{:S(2)}, u32[]{:S(2)}) collective-permute-start(bf16[4,64,512]{2,1,0:T(8,128)(2,1)S(1)} %get-tuple-element.81.mine), channel_id=1, source_target_pairs={{0,1},{1,0},{2,3},{3,2},{4,5},{5,4},{6,7},{7,6},{8,9},{9,8},{10,11... | collective-permute-start | bytes 786440 | tf_op jit(solution)/shard_map/gather/ppermute | solution.py:429
  40.9 0.1 collective-permute-done.16
  41.1 4.3 %collective-permute-done.15 = bf16[1,64,512]{2,1,0:T(8,128)(2,1)S(1)} collective-permute-done((bf16[1,64,512]{2,1,0:T(8,128)(2,1)S(1)}, bf16[1,64,512]{2,1,0:T(8,128)(2,1)S(1)}, u32[]{:S(2)}, u32[]{:S(2)}) %collective-permute-start.15) | collective-permute-done | bytes 65568 | tf_op jit(solution)/shard_map/gather/ppermute | solution.py:375
  45.4 1.1 %collective-permute-start.17 = (bf16[4,64,512]{2,1,0:T(8,128)(2,1)S(1)}, bf16[4,64,512]{2,1,0:T(8,128)(2,1)S(1)}, u32[]{:S(2)}, u32[]{:S(2)}) collective-permute-start(bf16[4,64,512]{2,1,0:T(8,128)(2,1)S(1)} %get-tuple-element.76.refs_0_), channel_id=1, source_target_pairs={{0,1},{1,0},{2,3},{3,2},{4,5},{5,4},{6,7},{7,6},{8,9},{9,8},{10,11... | collective-permute-start | bytes 786440 | tf_op jit(solution)/shard_map/gather/ppermute | solution.py:429
  46.6 2.1 %second.5 = (f32[512,512]{1,0:T(8,128)S(1)}, bf16[512,512]{1,0:T(8,128)(2,1)S(1)}) custom-call(s32[4]{0:T(128)S(1)} %copy-done.4, bf16[4,512,512]{2,1,0:T(8,128)(2,1)S(1)} %get-tuple-element.47.left, bf16[4,512,512]{2,1,0:T(8,128)(2,1)S(1)} %get-tuple-element.48.right, bf16[4,64,512]{2,1,0:T(8,128)(2,1)S(1)} %get-tuple-element.81.mine, ...), custom_call_target="tpu_custom_call" | custom-call | flops 1 | tf_op jit(solution)/shard_map/second/pallas_call | solution.py:320
  48.7 1.0 %second.6 = f32[8,512]{1,0:T(8,128)S(1)} custom-call(s32[2]{0:T(128)S(1)} %copy-done.1, f32[2,512,512]{2,1,0:T(8,128)S(1)} %copy-done, bf16[512,512]{1,0:T(8,128)(2,1)S(1)} %get-tuple-element.51.block.first_block), custom_call_target="tpu_custom_call" | custom-call | flops 1 | tf_op jit(solution)/shard_map/second/pallas_call | solution.py:320
  49.7 4.9 %collective-permute-done.17.refs_1_ = bf16[4,64,512]{2,1,0:T(8,128)(2,1)S(1)} collective-permute-done((bf16[4,64,512]{2,1,0:T(8,128)(2,1)S(1)}, bf16[4,64,512]{2,1,0:T(8,128)(2,1)S(1)}, u32[]{:S(2)}, u32[]{:S(2)}) %collective-permute-start.17) | collective-permute-done | bytes 262176 | tf_op jit(solution)/shard_map/gather/ppermute | solution.py:429
  54.8 0.7 collective-permute-start.23
  55.5 1.1 %collective-permute-done.18.refs_2_ = bf16[2,4,64,512]{3,2,1,0:T(8,128)(2,1)S(1)} collective-permute-done((bf16[2,4,64,512]{3,2,1,0:T(8,128)(2,1)S(1)}, bf16[2,4,64,512]{3,2,1,0:T(8,128)(2,1)S(1)}, u32[]{:S(2)}, u32[]{:S(2)}) %collective-permute-start.18) | collective-permute-done | bytes 524320 | tf_op jit(solution)/shard_map/second/ppermute | solution.py:359
  56.6 2.0 %second.7 = (bf16[4,64,512]{2,1,0:T(8,128)(2,1)S(1)}, f32[4,64,512]{2,1,0:T(8,128)S(1)}, bf16[2,512,512]{2,1,0:T(8,128)(2,1)S(1)}) custom-call(s32[4]{0:T(128)S(1)} %copy-done.4, s32[2]{0:T(128)S(1)} %copy-done.1, f32[512,512]{1,0:T(8,128)S(1)} %get-tuple-element.50.acc_ref, bf16[512,512]{1,0:T(8,128)(2,1)S(1)} %get-tuple-element.51.block.first_block, ...), custom_call_target="tpu_custom_call" | custom-call | flops 1073741824 | bytes 4194304 | tf_op jit(solution)/shard_map/second/pallas_call | solution.py:320
  58.6 1.6 %collective-permute-start.19 = (bf16[4,64,512]{2,1,0:T(8,128)(2,1)S(1)}, bf16[4,64,512]{2,1,0:T(8,128)(2,1)S(1)}, u32[]{:S(2)}, u32[]{:S(2)}) collective-permute-start(bf16[4,64,512]{2,1,0:T(8,128)(2,1)S(1)} %get-tuple-element.55), channel_id=1, source_target_pairs={{0,1},{1,0},{2,3},{3,2},{4,5},{5,4},{6,7},{7,6},{8,9},{9,8},{10,11... | collective-permute-start | bytes 786440 | tf_op jit(solution)/shard_map/second/ppermute | solution.py:364
  60.2 1.0 %second.8 = f32[8,512]{1,0:T(8,128)S(1)} custom-call(s32[2]{0:T(128)S(1)} %copy-done.1, f32[2,512,512]{2,1,0:T(8,128)S(1)} %copy-done, bf16[2,512,512]{2,1,0:T(8,128)(2,1)S(1)} %get-tuple-element.58.block.own), custom_call_target="tpu_custom_call" | custom-call | flops 1 | tf_op jit(solution)/shard_map/second/pallas_call | solution.py:320
  61.2 2.6 %second.9 = (bf16[4,64,512]{2,1,0:T(8,128)(2,1)S(1)}, f32[4,64,512]{2,1,0:T(8,128)S(1)}) custom-call(s32[4]{0:T(128)S(1)} %copy-done.4, s32[2]{0:T(128)S(1)} %copy-done.1, bf16[2,512,512]{2,1,0:T(8,128)(2,1)S(1)} %get-tuple-element.58.block.own, bf16[4,512,512]{2,1,0:T(8,128)(2,1)S(1)} %get-tuple-element.59.left, ...), custom_call_target="tpu_custom_call" | custom-call | flops 2147483648 | bytes 8388608 | tf_op jit(solution)/shard_map/second/pallas_call | solution.py:320
  63.8 0.2 collective-permute-start.24
  64.0 3.7 %collective-permute-done.19 = bf16[4,64,512]{2,1,0:T(8,128)(2,1)S(1)} collective-permute-done((bf16[4,64,512]{2,1,0:T(8,128)(2,1)S(1)}, bf16[4,64,512]{2,1,0:T(8,128)(2,1)S(1)}, u32[]{:S(2)}, u32[]{:S(2)}) %collective-permute-start.19) | collective-permute-done | bytes 262176 | tf_op jit(solution)/shard_map/second/ppermute | solution.py:364
  67.8 2.3 %collective-permute-start.20 = (bf16[64,512]{1,0:T(8,128)(2,1)S(1)}, bf16[64,512]{1,0:T(8,128)(2,1)S(1)}, u32[]{:S(2)}, u32[]{:S(2)}) collective-permute-start(bf16[64,512]{1,0:T(8,128)(2,1)S(1)} %get-tuple-element.79), channel_id=1, source_target_pairs={{0,6},{1,7},{2,4},{3,5},{4,2},{5,3},{6,0},{7,1},{8,14},{9,15},{10,... | collective-permute-start | bytes 196616 | tf_op jit(solution)/shard_map/scalars/ppermute | solution.py:370
  70.0 2.2 %collective-permute-start.22 = (bf16[64,512]{1,0:T(8,128)(2,1)S(1)}, bf16[64,512]{1,0:T(8,128)(2,1)S(1)}, u32[]{:S(2)}, u32[]{:S(2)}) collective-permute-start(bf16[64,512]{1,0:T(8,128)(2,1)S(1)} %get-tuple-element.77), channel_id=1, source_target_pairs={{0,2},{1,3},{2,0},{3,1},{4,6},{5,7},{6,4},{7,5},{8,10},{9,11},{10,... | collective-permute-start | bytes 196616 | tf_op jit(solution)/shard_map/scalars/ppermute | solution.py:370
  72.3 2.3 %collective-permute-start.25 = (bf16[64,512]{1,0:T(8,128)(2,1)S(1)}, bf16[64,512]{1,0:T(8,128)(2,1)S(1)}, u32[]{:S(2)}, u32[]{:S(2)}) collective-permute-start(bf16[64,512]{1,0:T(8,128)(2,1)S(1)} %get-tuple-element.74), channel_id=1, source_target_pairs={{0,6},{1,7},{2,4},{3,5},{4,2},{5,3},{6,0},{7,1},{8,14},{9,15},{10,... | collective-permute-start | bytes 196616 | tf_op jit(solution)/shard_map/scalars/ppermute | solution.py:370
  74.7 2.5 %collective-permute-start.27 = (bf16[64,512]{1,0:T(8,128)(2,1)S(1)}, bf16[64,512]{1,0:T(8,128)(2,1)S(1)}, u32[]{:S(2)}, u32[]{:S(2)}) collective-permute-start(bf16[64,512]{1,0:T(8,128)(2,1)S(1)} %get-tuple-element.72), channel_id=1, source_target_pairs={{0,2},{1,3},{2,0},{3,1},{4,6},{5,7},{6,4},{7,5},{8,10},{9,11},{10,... | collective-permute-start | bytes 196616 | tf_op jit(solution)/shard_map/scalars/ppermute | solution.py:370
  77.2 2.0 %collective-permute-start.28 = (f32[8,512]{1,0:T(8,128)S(1)}, f32[8,512]{1,0:T(8,128)S(1)}, u32[]{:S(2)}, u32[]{:S(2)}) collective-permute-start(f32[8,512]{1,0:T(8,128)S(1)} %add.19.refs_14_), channel_id=1, source_target_pairs={{0,8},{8,0},{16,24},{24,16},{1,9},{9,1},{17,25},{25,17},{2,10},{10... | collective-permute-start | bytes 49160 | tf_op jit(solution)/shard_map/scalars/ppermute | solution.py:493
  79.2 1.4 %collective-permute-start.29 = (f32[8,512]{1,0:T(8,128)S(1)}, f32[8,512]{1,0:T(8,128)S(1)}, u32[]{:S(2)}, u32[]{:S(2)}) collective-permute-start(f32[8,512]{1,0:T(8,128)S(1)} %add.19.refs_14_), channel_id=1, source_target_pairs={{0,16},{8,24},{16,0},{24,8},{1,17},{9,25},{17,1},{25,9},{2,18},{10... | collective-permute-start | bytes 49160 | tf_op jit(solution)/shard_map/scalars/ppermute | solution.py:493
  80.7 0.1 collective-permute-start.30
  80.8 1.7 %collective-permute-done.26.refs_12_ = bf16[64,512]{1,0:T(8,128)(2,1)S(1)} collective-permute-done((bf16[64,512]{1,0:T(8,128)(2,1)S(1)}, bf16[64,512]{1,0:T(8,128)(2,1)S(1)}, u32[]{:S(2)}, u32[]{:S(2)}) %collective-permute-start.26) | collective-permute-done | bytes 65568 | tf_op jit(solution)/shard_map/scalars/ppermute | solution.py:370
  82.5 0.4 collective-permute-done.29.refs_16_
  83.0 0.9 %collective-permute-done.30.refs_17_ = f32[8,512]{1,0:T(8,128)S(1)} collective-permute-done((f32[8,512]{1,0:T(8,128)S(1)}, f32[8,512]{1,0:T(8,128)S(1)}, u32[]{:S(2)}, u32[]{:S(2)}) %collective-permute-start.30) | collective-permute-done | bytes 16416 | tf_op jit(solution)/shard_map/scalars/ppermute | solution.py:493
  83.8 1.5 %scalars.1 = (f32[2,64,512]{2,1,0:T(8,128)}, f32[2,64,512]{2,1,0:T(8,128)}) custom-call(s32[2]{0:T(128)S(1)} %copy-done.1, f32[2,64,512]{2,1,0:T(8,128)S(1)} %get-tuple-element.35.start, f32[64,512]{1,0:T(8,128)S(1)} %get-tuple-element.38.refs_0_, f32[64,512]{1,0:T(8,128)S(1)} %get-tuple-element.42.refs_1_, f32[64,512]{1,0:T(8,128)S(1)} %get-tuple-element.43.refs_2_, ...), custom_call_target="tpu_custom_call" | custom-call | flops 1048576 | bytes 4096 | tf_op jit(solution)/shard_map/scalars/pallas_call | solution.py:320
  (52 shorter events, 0.9 us)
Async XLA Ops:
  2.3 2.1 %collective-permute-start = (bf16[512,512]{1,0:T(8,128)(2,1)S(1)}, bf16[512,512]{1,0:T(8,128)(2,1)S(1)}, u32[]{:S(2)}, u32[]{:S(2)}) collective-permute-start(bf16[512,512]{1,0:T(8,128)(2,1)S(1)} %get-tuple-element.34), channel_id=1, source_target_pairs={{0,8},{8,0},{16,24},{24,16},{1,9},{9,1},{17,25},{25,17},{2,10},{10... | collective-permute-start | bytes 1572872 | tf_op jit(solution)/shard_map/first/ppermute | solution.py:359
  2.8 8.4 %collective-permute-start.5 = (bf16[512,512]{1,0:T(8,128)(2,1)S(1)}, bf16[512,512]{1,0:T(8,128)(2,1)S(1)}, u32[]{:S(2)}, u32[]{:S(2)}) collective-permute-start(bf16[512,512]{1,0:T(8,128)(2,1)S(1)} %get-tuple-element.39), channel_id=1, source_target_pairs={{8,16},{16,8},{9,17},{17,9},{10,18},{18,10},{11,19},{19,11},{12,20... | collective-permute-start | bytes 1572872 | tf_op jit(solution)/shard_map/first/ppermute | solution.py:359
  8.5 8.1 %collective-permute-start.1 = (bf16[4,64,512]{2,1,0:T(8,128)(2,1)S(1)}, bf16[4,64,512]{2,1,0:T(8,128)(2,1)S(1)}, u32[]{:S(2)}, u32[]{:S(2)}) collective-permute-start(bf16[4,64,512]{2,1,0:T(8,128)(2,1)S(1)} %get-tuple-element.37), channel_id=1, source_target_pairs={{0,1},{1,0},{2,3},{3,2},{4,5},{5,4},{6,7},{7,6},{8,9},{9,8},{10,11... | collective-permute-start | bytes 786440 | tf_op jit(solution)/shard_map/first/ppermute | solution.py:364
  14.7 7.8 %collective-permute-start.6 = (bf16[4,64,512]{2,1,0:T(8,128)(2,1)S(1)}, bf16[4,64,512]{2,1,0:T(8,128)(2,1)S(1)}, u32[]{:S(2)}, u32[]{:S(2)}) collective-permute-start(bf16[4,64,512]{2,1,0:T(8,128)(2,1)S(1)} %get-tuple-element.41), channel_id=1, source_target_pairs={{0,1},{1,0},{2,3},{3,2},{4,5},{5,4},{6,7},{7,6},{8,9},{9,8},{10,11... | collective-permute-start | bytes 786440 | tf_op jit(solution)/shard_map/first/ppermute | solution.py:364
  16.6 12.0 %copy-start.1 = (s32[2]{0:T(128)S(1)}, s32[2]{0:T(128)}, u32[]{:S(2)}) copy-start(s32[2]{0:T(128)} %size_ref.13) | copy-start | bytes 28
  16.6 12.0 %copy-start.2 = (f32[2,512]{1,0:T(2,128)S(1)}, f32[2,512]{1,0:T(2,128)}, u32[]{:S(2)}) copy-start(f32[2,512]{1,0:T(2,128)} %left_row.3) | copy-start | bytes 12292
  16.6 12.0 %copy-start.3 = (f32[2,512]{1,0:T(2,128)S(1)}, f32[2,512]{1,0:T(2,128)}, u32[]{:S(2)}) copy-start(f32[2,512]{1,0:T(2,128)} %right_row.3) | copy-start | bytes 12292
  16.7 9.9 %collective-permute-start.2 = (bf16[64,512]{1,0:T(8,128)(2,1)S(1)}, bf16[64,512]{1,0:T(8,128)(2,1)S(1)}, u32[]{:S(2)}, u32[]{:S(2)}) collective-permute-start(bf16[64,512]{1,0:T(8,128)(2,1)S(1)} %get-tuple-element.87), channel_id=1, source_target_pairs={{0,6},{1,7},{2,4},{3,5},{4,2},{5,3},{6,0},{7,1},{8,14},{9,15},{10,... | collective-permute-start | bytes 196616 | tf_op jit(solution)/shard_map/gather/ppermute | solution.py:370
  21.9 6.7 %collective-permute-start.3 = (bf16[64,512]{1,0:T(8,128)(2,1)S(1)}, bf16[64,512]{1,0:T(8,128)(2,1)S(1)}, u32[]{:S(2)}, u32[]{:S(2)}) collective-permute-start(bf16[64,512]{1,0:T(8,128)(2,1)S(1)} %get-tuple-element.86), channel_id=1, source_target_pairs={{0,4},{1,5},{2,6},{3,7},{4,0},{5,1},{6,2},{7,3},{8,12},{9,13},{10,... | collective-permute-start | bytes 196616 | tf_op jit(solution)/shard_map/gather/ppermute | solution.py:370
  21.9 6.7 %collective-permute-start.4 = (bf16[64,512]{1,0:T(8,128)(2,1)S(1)}, bf16[64,512]{1,0:T(8,128)(2,1)S(1)}, u32[]{:S(2)}, u32[]{:S(2)}) collective-permute-start(bf16[64,512]{1,0:T(8,128)(2,1)S(1)} %get-tuple-element.85), channel_id=1, source_target_pairs={{0,2},{1,3},{2,0},{3,1},{4,6},{5,7},{6,4},{7,5},{8,10},{9,11},{10,... | collective-permute-start | bytes 196616 | tf_op jit(solution)/shard_map/gather/ppermute | solution.py:370
  22.7 23.9 %copy-start.4 = (s32[4]{0:T(128)S(1)}, s32[4]{0:T(128)}, u32[]{:S(2)}) copy-start(s32[4]{0:T(128)} %shift_ref.5) | copy-start | bytes 52
  22.7 9.1 %collective-permute-start.7 = (bf16[64,512]{1,0:T(8,128)(2,1)S(1)}, bf16[64,512]{1,0:T(8,128)(2,1)S(1)}, u32[]{:S(2)}, u32[]{:S(2)}) collective-permute-start(bf16[64,512]{1,0:T(8,128)(2,1)S(1)} %get-tuple-element.84), channel_id=1, source_target_pairs={{0,6},{1,7},{2,4},{3,5},{4,2},{5,3},{6,0},{7,1},{8,14},{9,15},{10,... | collective-permute-start | bytes 196616 | tf_op jit(solution)/shard_map/gather/ppermute | solution.py:370
  26.5 7.6 %collective-permute-start.8 = (bf16[64,512]{1,0:T(8,128)(2,1)S(1)}, bf16[64,512]{1,0:T(8,128)(2,1)S(1)}, u32[]{:S(2)}, u32[]{:S(2)}) collective-permute-start(bf16[64,512]{1,0:T(8,128)(2,1)S(1)} %get-tuple-element.83), channel_id=1, source_target_pairs={{0,4},{1,5},{2,6},{3,7},{4,0},{5,1},{6,2},{7,3},{8,12},{9,13},{10,... | collective-permute-start | bytes 196616 | tf_op jit(solution)/shard_map/gather/ppermute | solution.py:370
  26.6 7.5 %collective-permute-start.9 = (bf16[64,512]{1,0:T(8,128)(2,1)S(1)}, bf16[64,512]{1,0:T(8,128)(2,1)S(1)}, u32[]{:S(2)}, u32[]{:S(2)}) collective-permute-start(bf16[64,512]{1,0:T(8,128)(2,1)S(1)} %get-tuple-element.82), channel_id=1, source_target_pairs={{0,2},{1,3},{2,0},{3,1},{4,6},{5,7},{6,4},{7,5},{8,10},{9,11},{10,... | collective-permute-start | bytes 196616 | tf_op jit(solution)/shard_map/gather/ppermute | solution.py:370
  29.3 7.9 %collective-permute-start.12 = (bf16[1,64,512]{2,1,0:T(8,128)(2,1)S(1)}, bf16[1,64,512]{2,1,0:T(8,128)(2,1)S(1)}, u32[]{:S(2)}, u32[]{:S(2)}) collective-permute-start(bf16[1,64,512]{2,1,0:T(8,128)(2,1)S(1)} %bitcast.42), channel_id=1, source_target_pairs={{0,6},{1,7},{2,4},{3,5},{4,2},{5,3},{6,0},{7,1},{8,14},{9,15},{10,... | collective-permute-start | bytes 196616 | tf_op jit(solution)/shard_map/gather/ppermute | solution.py:375
  31.8 8.0 %collective-permute-start.11 = (bf16[1,64,512]{2,1,0:T(8,128)(2,1)S(1)}, bf16[1,64,512]{2,1,0:T(8,128)(2,1)S(1)}, u32[]{:S(2)}, u32[]{:S(2)}) collective-permute-start(bf16[1,64,512]{2,1,0:T(8,128)(2,1)S(1)} %bitcast.43), channel_id=1, source_target_pairs={{0,4},{1,5},{2,6},{3,7},{4,0},{5,1},{6,2},{7,3},{8,12},{9,13},{10,... | collective-permute-start | bytes 196616 | tf_op jit(solution)/shard_map/gather/ppermute | solution.py:375
  31.8 8.0 %collective-permute-start.10 = (bf16[1,64,512]{2,1,0:T(8,128)(2,1)S(1)}, bf16[1,64,512]{2,1,0:T(8,128)(2,1)S(1)}, u32[]{:S(2)}, u32[]{:S(2)}) collective-permute-start(bf16[1,64,512]{2,1,0:T(8,128)(2,1)S(1)} %bitcast.44), channel_id=1, source_target_pairs={{0,2},{1,3},{2,0},{3,1},{4,6},{5,7},{6,4},{7,5},{8,10},{9,11},{10,... | collective-permute-start | bytes 196616 | tf_op jit(solution)/shard_map/gather/ppermute | solution.py:375
  34.8 6.2 %collective-permute-start.16 = (bf16[1,64,512]{2,1,0:T(8,128)(2,1)S(1)}, bf16[1,64,512]{2,1,0:T(8,128)(2,1)S(1)}, u32[]{:S(2)}, u32[]{:S(2)}) collective-permute-start(bf16[1,64,512]{2,1,0:T(8,128)(2,1)S(1)} %bitcast.46), channel_id=1, source_target_pairs={{0,6},{1,7},{2,4},{3,5},{4,2},{5,3},{6,0},{7,1},{8,14},{9,15},{10,... | collective-permute-start | bytes 196616 | tf_op jit(solution)/shard_map/gather/ppermute | solution.py:375
  37.2 8.1 %collective-permute-start.15 = (bf16[1,64,512]{2,1,0:T(8,128)(2,1)S(1)}, bf16[1,64,512]{2,1,0:T(8,128)(2,1)S(1)}, u32[]{:S(2)}, u32[]{:S(2)}) collective-permute-start(bf16[1,64,512]{2,1,0:T(8,128)(2,1)S(1)} %bitcast.47), channel_id=1, source_target_pairs={{0,4},{1,5},{2,6},{3,7},{4,0},{5,1},{6,2},{7,3},{8,12},{9,13},{10,... | collective-permute-start | bytes 196616 | tf_op jit(solution)/shard_map/gather/ppermute | solution.py:375
  37.2 8.1 %collective-permute-start.14 = (bf16[1,64,512]{2,1,0:T(8,128)(2,1)S(1)}, bf16[1,64,512]{2,1,0:T(8,128)(2,1)S(1)}, u32[]{:S(2)}, u32[]{:S(2)}) collective-permute-start(bf16[1,64,512]{2,1,0:T(8,128)(2,1)S(1)} %bitcast.48), channel_id=1, source_target_pairs={{0,2},{1,3},{2,0},{3,1},{4,6},{5,7},{6,4},{7,5},{8,10},{9,11},{10,... | collective-permute-start | bytes 196616 | tf_op jit(solution)/shard_map/gather/ppermute | solution.py:375
  39.8 6.8 %collective-permute-start.13 = (bf16[4,64,512]{2,1,0:T(8,128)(2,1)S(1)}, bf16[4,64,512]{2,1,0:T(8,128)(2,1)S(1)}, u32[]{:S(2)}, u32[]{:S(2)}) collective-permute-start(bf16[4,64,512]{2,1,0:T(8,128)(2,1)S(1)} %get-tuple-element.81.mine), channel_id=1, source_target_pairs={{0,1},{1,0},{2,3},{3,2},{4,5},{5,4},{6,7},{7,6},{8,9},{9,8},{10,11... | collective-permute-start | bytes 786440 | tf_op jit(solution)/shard_map/gather/ppermute | solution.py:429
  45.4 9.2 %collective-permute-start.17 = (bf16[4,64,512]{2,1,0:T(8,128)(2,1)S(1)}, bf16[4,64,512]{2,1,0:T(8,128)(2,1)S(1)}, u32[]{:S(2)}, u32[]{:S(2)}) collective-permute-start(bf16[4,64,512]{2,1,0:T(8,128)(2,1)S(1)} %get-tuple-element.76.refs_0_), channel_id=1, source_target_pairs={{0,1},{1,0},{2,3},{3,2},{4,5},{5,4},{6,7},{7,6},{8,9},{9,8},{10,11... | collective-permute-start | bytes 786440 | tf_op jit(solution)/shard_map/gather/ppermute | solution.py:429
  46.6 2.1 %copy-start = (f32[2,512,512]{2,1,0:T(8,128)S(1)}, f32[2,512,512]{2,1,0:T(8,128)}, u32[]{:S(2)}) copy-start(f32[2,512,512]{2,1,0:T(8,128)} %vector_ref.3) | copy-start | bytes 6291460
  54.7 1.9 %collective-permute-start.18 = (bf16[2,4,64,512]{3,2,1,0:T(8,128)(2,1)S(1)}, bf16[2,4,64,512]{3,2,1,0:T(8,128)(2,1)S(1)}, u32[]{:S(2)}, u32[]{:S(2)}) collective-permute-start(bf16[2,4,64,512]{3,2,1,0:T(8,128)(2,1)S(1)} %pad_maximum_fusion), channel_id=1, source_target_pairs={{0,8},{8,0},{16,24},{24,16},{1,9},{9,1},{17,25},{25,17},{2,10},{10... | collective-permute-start | bytes 1572872 | tf_op jit(solution)/shard_map/second/ppermute | solution.py:359
  54.8 6.4 %collective-permute-start.23 = (bf16[2,4,64,512]{3,2,1,0:T(8,128)(2,1)S(1)}, bf16[2,4,64,512]{3,2,1,0:T(8,128)(2,1)S(1)}, u32[]{:S(2)}, u32[]{:S(2)}) collective-permute-start(bf16[2,4,64,512]{3,2,1,0:T(8,128)(2,1)S(1)} %pad_maximum_fusion.1), channel_id=1, source_target_pairs={{8,16},{16,8},{9,17},{17,9},{10,18},{18,10},{11,19},{19,11},{12,20... | collective-permute-start | bytes 1572872 | tf_op jit(solution)/shard_map/second/ppermute | solution.py:359
  58.6 9.0 %collective-permute-start.19 = (bf16[4,64,512]{2,1,0:T(8,128)(2,1)S(1)}, bf16[4,64,512]{2,1,0:T(8,128)(2,1)S(1)}, u32[]{:S(2)}, u32[]{:S(2)}) collective-permute-start(bf16[4,64,512]{2,1,0:T(8,128)(2,1)S(1)} %get-tuple-element.55), channel_id=1, source_target_pairs={{0,1},{1,0},{2,3},{3,2},{4,5},{5,4},{6,7},{7,6},{8,9},{9,8},{10,11... | collective-permute-start | bytes 786440 | tf_op jit(solution)/shard_map/second/ppermute | solution.py:364
  63.8 8.4 %collective-permute-start.24 = (bf16[4,64,512]{2,1,0:T(8,128)(2,1)S(1)}, bf16[4,64,512]{2,1,0:T(8,128)(2,1)S(1)}, u32[]{:S(2)}, u32[]{:S(2)}) collective-permute-start(bf16[4,64,512]{2,1,0:T(8,128)(2,1)S(1)} %get-tuple-element.62), channel_id=1, source_target_pairs={{0,1},{1,0},{2,3},{3,2},{4,5},{5,4},{6,7},{7,6},{8,9},{9,8},{10,11... | collective-permute-start | bytes 786440 | tf_op jit(solution)/shard_map/second/ppermute | solution.py:364
  67.8 9.4 %collective-permute-start.20 = (bf16[64,512]{1,0:T(8,128)(2,1)S(1)}, bf16[64,512]{1,0:T(8,128)(2,1)S(1)}, u32[]{:S(2)}, u32[]{:S(2)}) collective-permute-start(bf16[64,512]{1,0:T(8,128)(2,1)S(1)} %get-tuple-element.79), channel_id=1, source_target_pairs={{0,6},{1,7},{2,4},{3,5},{4,2},{5,3},{6,0},{7,1},{8,14},{9,15},{10,... | collective-permute-start | bytes 196616 | tf_op jit(solution)/shard_map/scalars/ppermute | solution.py:370
  70.0 9.2 %collective-permute-start.21 = (bf16[64,512]{1,0:T(8,128)(2,1)S(1)}, bf16[64,512]{1,0:T(8,128)(2,1)S(1)}, u32[]{:S(2)}, u32[]{:S(2)}) collective-permute-start(bf16[64,512]{1,0:T(8,128)(2,1)S(1)} %get-tuple-element.78), channel_id=1, source_target_pairs={{0,4},{1,5},{2,6},{3,7},{4,0},{5,1},{6,2},{7,3},{8,12},{9,13},{10,... | collective-permute-start | bytes 196616 | tf_op jit(solution)/shard_map/scalars/ppermute | solution.py:370
  70.0 4.7 %collective-permute-start.22 = (bf16[64,512]{1,0:T(8,128)(2,1)S(1)}, bf16[64,512]{1,0:T(8,128)(2,1)S(1)}, u32[]{:S(2)}, u32[]{:S(2)}) collective-permute-start(bf16[64,512]{1,0:T(8,128)(2,1)S(1)} %get-tuple-element.77), channel_id=1, source_target_pairs={{0,2},{1,3},{2,0},{3,1},{4,6},{5,7},{6,4},{7,5},{8,10},{9,11},{10,... | collective-permute-start | bytes 196616 | tf_op jit(solution)/shard_map/scalars/ppermute | solution.py:370
  72.3 8.3 %collective-permute-start.25 = (bf16[64,512]{1,0:T(8,128)(2,1)S(1)}, bf16[64,512]{1,0:T(8,128)(2,1)S(1)}, u32[]{:S(2)}, u32[]{:S(2)}) collective-permute-start(bf16[64,512]{1,0:T(8,128)(2,1)S(1)} %get-tuple-element.74), channel_id=1, source_target_pairs={{0,6},{1,7},{2,4},{3,5},{4,2},{5,3},{6,0},{7,1},{8,14},{9,15},{10,... | collective-permute-start | bytes 196616 | tf_op jit(solution)/shard_map/scalars/ppermute | solution.py:370
  74.6 7.9 %collective-permute-start.26 = (bf16[64,512]{1,0:T(8,128)(2,1)S(1)}, bf16[64,512]{1,0:T(8,128)(2,1)S(1)}, u32[]{:S(2)}, u32[]{:S(2)}) collective-permute-start(bf16[64,512]{1,0:T(8,128)(2,1)S(1)} %get-tuple-element.73), channel_id=1, source_target_pairs={{0,4},{1,5},{2,6},{3,7},{4,0},{5,1},{6,2},{7,3},{8,12},{9,13},{10,... | collective-permute-start | bytes 196616 | tf_op jit(solution)/shard_map/scalars/ppermute | solution.py:370
  74.7 7.8 %collective-permute-start.27 = (bf16[64,512]{1,0:T(8,128)(2,1)S(1)}, bf16[64,512]{1,0:T(8,128)(2,1)S(1)}, u32[]{:S(2)}, u32[]{:S(2)}) collective-permute-start(bf16[64,512]{1,0:T(8,128)(2,1)S(1)} %get-tuple-element.72), channel_id=1, source_target_pairs={{0,2},{1,3},{2,0},{3,1},{4,6},{5,7},{6,4},{7,5},{8,10},{9,11},{10,... | collective-permute-start | bytes 196616 | tf_op jit(solution)/shard_map/scalars/ppermute | solution.py:370
  77.2 5.4 %collective-permute-start.28 = (f32[8,512]{1,0:T(8,128)S(1)}, f32[8,512]{1,0:T(8,128)S(1)}, u32[]{:S(2)}, u32[]{:S(2)}) collective-permute-start(f32[8,512]{1,0:T(8,128)S(1)} %add.19.refs_14_), channel_id=1, source_target_pairs={{0,8},{8,0},{16,24},{24,16},{1,9},{9,1},{17,25},{25,17},{2,10},{10... | collective-permute-start | bytes 49160 | tf_op jit(solution)/shard_map/scalars/ppermute | solution.py:493
  79.2 3.7 %collective-permute-start.29 = (f32[8,512]{1,0:T(8,128)S(1)}, f32[8,512]{1,0:T(8,128)S(1)}, u32[]{:S(2)}, u32[]{:S(2)}) collective-permute-start(f32[8,512]{1,0:T(8,128)S(1)} %add.19.refs_14_), channel_id=1, source_target_pairs={{0,16},{8,24},{16,0},{24,8},{1,17},{9,25},{17,1},{25,9},{2,18},{10... | collective-permute-start | bytes 49160 | tf_op jit(solution)/shard_map/scalars/ppermute | solution.py:493
  80.7 3.2 %collective-permute-start.30 = (f32[8,512]{1,0:T(8,128)S(1)}, f32[8,512]{1,0:T(8,128)S(1)}, u32[]{:S(2)}, u32[]{:S(2)}) collective-permute-start(f32[8,512]{1,0:T(8,128)S(1)} %add.19.refs_14_), channel_id=1, source_target_pairs={{0,24},{8,16},{16,8},{24,0},{1,25},{9,17},{17,9},{25,1},{2,26},{10... | collective-permute-start | bytes 49160 | tf_op jit(solution)/shard_map/scalars/ppermute | solution.py:493

commit v10 on v8

--- a/solution.py
+++ b/solution.py
@@ -360,7 +360,7 @@
         return jnp.concatenate([held] + [got[k] for k in range(1, count)])
 
     with jax.named_scope("first"):
-        parts = 2 if size % 256 == 0 else 1
+        parts = 4 if size % 256 == 0 else 1
         block = jax.ShapeDtypeStruct((size, size), jnp.bfloat16)
         rounded, *edges = call(
             round_kernel,

time: 86.7 us -> 86.8 us (level)
  Pallas kernels: 21.8 us -> 19.9 us
  starting transfers between devices: 36.9 us -> 38.3 us
    pallas_call x11, Pallas kernels: 21.8 us -> 19.9 us  [call(): pl.pallas_call(kernel, out_shape=out_shape, in_specs=[SMEM] * len(scalars...]
    ppermute x4, starting transfers between devices: 4.49 us -> 5.88 us  [low_sum(): lax.ppermute(send, 'term', pairs_low(ranks)).astype(jnp.float32)]
  transfers between devices with their start and end apart: 31 -> 31, of which waited for: 13 -> 14; matrix products, arithmetic and copies ran while one was open for 1% -> 1% of each run, Pallas kernels for 21% -> 19%
where the time goes in v10:
time: 86.8 us; the launch traced here: 86.6 us
  starting transfers between devices  38.3 us (44%)
  waiting for transfers between devices  26 us (30%)
  Pallas kernels  19.9 us (23%)
  local copies, waits for them, and re-layouts  1.03 us (1%)
  between operations  0.92 us (1%)
    pallas_call x11, Pallas kernels, call(): pl.pallas_call(kernel, out_shape=out_shape, in_specs=[SMEM] * len(scalars...  19.9 us
    ppermute x12, starting transfers between devices, high_parts(): lax.ppermute(total[k].astype(jnp.bfloat16), 'term', pairs_high(ranks, low...  16.8 us
    ppermute x6, starting transfers between devices, gather_high(): lax.ppermute(held, 'term', pairs_high(ranks, low, k))  8.91 us
    ppermute x12, waiting for transfers between devices, high_parts(): lax.ppermute(total[k].astype(jnp.bfloat16), 'term', pairs_high(ranks, low...  7.88 us
    ppermute x4, waiting for transfers between devices, low_sum(): lax.ppermute(send, 'term', pairs_low(ranks)).astype(jnp.float32)  6.56 us
    ppermute x4, starting transfers between devices, low_sum(): lax.ppermute(send, 'term', pairs_low(ranks)).astype(jnp.float32)  5.88 us
    ppermute x2, waiting for transfers between devices, on_device(): theirs = lax.ppermute(mine, 'term', pairs_low(ranks)) if low > 1 else mine  5.13 us
    ppermute x6, waiting for transfers between devices, gather_high(): lax.ppermute(held, 'term', pairs_high(ranks, low, k))  4.6 us
  transfers between devices with their start and end apart: 31, of which 14 were waited for; matrix products, arithmetic and copies ran while one was open for 1% of the time, Pallas kernels for 19%

profile of v10, /device:TPU:0, one launch (start us, length us, event | category | flops | bytes accessed | tf_op | source)
XLA Modules:
  0.0 86.6 jit_solution(13213262214102607931)
XLA Ops:
  0.6 1.6 %first.3 = (bf16[2,512,512]{2,1,0:T(8,128)(2,1)S(1)}, bf16[512,512]{1,0:T(8,128)(2,1)S(1)}, bf16[512,512]{1,0:T(8,128)(2,1)S(1)}) custom-call(s32[2]{0:T(128)} %size_ref.9, f32[2,512,512]{2,1,0:T(8,128)} %vector_ref.3), custom_call_target="tpu_custom_call" | custom-call | flops 1048576 | bytes 4096 | tf_op jit(solution)/shard_map/first/pallas_call | solution.py:304
  2.3 0.5 collective-permute-start
  2.8 0.7 collective-permute-start.5
  3.5 0.8 collective-permute-done.refs_0_
  4.3 4.4 %first.4 = (bf16[4,64,512]{2,1,0:T(8,128)(2,1)S(1)}, f32[4,64,512]{2,1,0:T(8,128)S(1)}, bf16[4,512,512]{2,1,0:T(8,128)(2,1)S(1)}, bf16[4,512,512]{2,1,0:T(8,128)(2,1)S(1)}, f32[2,64,512]{2,1,0:T(8,128)S(1)}) custom-call(bf16[2,512,512]{2,1,0:T(8,128)(2,1)S(1)} %get-tuple-element.33.own, bf16[512,512]{1,0:T(8,128)(2,1)S(1)} %collective-permute-done.refs_0_, ...), custom_call_target="tpu_custom_call" | custom-call | flops 2147483648 | bytes 8388608 | tf_op jit(solution)/shard_map/first/pallas_call | solution.py:304
  8.7 3.0 %collective-permute-start.1 = (bf16[4,64,512]{2,1,0:T(8,128)(2,1)S(1)}, bf16[4,64,512]{2,1,0:T(8,128)(2,1)S(1)}, u32[]{:S(2)}, u32[]{:S(2)}) collective-permute-start(bf16[4,64,512]{2,1,0:T(8,128)(2,1)S(1)} %get-tuple-element.37), channel_id=1, source_target_pairs={{0,1},{1,0},{2,3},{3,2},{4,5},{5,4},{6,7},{7,6},{8,9},{9,8},{10,11... | collective-permute-start | bytes 786440 | tf_op jit(solution)/shard_map/first/ppermute | solution.py:348
  11.7 3.1 %first.5 = (bf16[4,64,512]{2,1,0:T(8,128)(2,1)S(1)}, f32[4,64,512]{2,1,0:T(8,128)S(1)}, bf16[4,512,512]{2,1,0:T(8,128)(2,1)S(1)}, bf16[4,512,512]{2,1,0:T(8,128)(2,1)S(1)}) custom-call(bf16[2,512,512]{2,1,0:T(8,128)(2,1)S(1)} %get-tuple-element.33.own, bf16[512,512]{1,0:T(8,128)(2,1)S(1)} %collective-permute-done.5.refs_0_, s32[4]{0:T(128)} %shift_ref.5, ...), custom_call_target="tpu_custom_call" | custom-call | flops 2147483648 | bytes 8388608 | tf_op jit(solution)/shard_map/first/pallas_call | solution.py:304
  14.9 2.9 %collective-permute-done.1 = bf16[4,64,512]{2,1,0:T(8,128)(2,1)S(1)} collective-permute-done((bf16[4,64,512]{2,1,0:T(8,128)(2,1)S(1)}, bf16[4,64,512]{2,1,0:T(8,128)(2,1)S(1)}, u32[]{:S(2)}, u32[]{:S(2)}) %collective-permute-start.1) | collective-permute-done | bytes 262176 | tf_op jit(solution)/shard_map/first/ppermute | solution.py:348
  17.9 4.6 %collective-permute-start.2 = (bf16[64,512]{1,0:T(8,128)(2,1)S(1)}, bf16[64,512]{1,0:T(8,128)(2,1)S(1)}, u32[]{:S(2)}, u32[]{:S(2)}) collective-permute-start(bf16[64,512]{1,0:T(8,128)(2,1)S(1)} %get-tuple-element.87), channel_id=1, source_target_pairs={{0,6},{1,7},{2,4},{3,5},{4,2},{5,3},{6,0},{7,1},{8,14},{9,15},{10,... | collective-permute-start | bytes 196616 | tf_op jit(solution)/shard_map/gather/ppermute | solution.py:354
  22.5 0.6 collective-permute-start.4
  23.3 3.8 %collective-permute-start.7 = (bf16[64,512]{1,0:T(8,128)(2,1)S(1)}, bf16[64,512]{1,0:T(8,128)(2,1)S(1)}, u32[]{:S(2)}, u32[]{:S(2)}) collective-permute-start(bf16[64,512]{1,0:T(8,128)(2,1)S(1)} %get-tuple-element.84), channel_id=1, source_target_pairs={{0,6},{1,7},{2,4},{3,5},{4,2},{5,3},{6,0},{7,1},{8,14},{9,15},{10,... | collective-permute-start | bytes 196616 | tf_op jit(solution)/shard_map/gather/ppermute | solution.py:354
  27.2 0.6 collective-permute-start.9
  27.8 1.2 %collective-permute-done.3.refs_2_ = bf16[64,512]{1,0:T(8,128)(2,1)S(1)} collective-permute-done((bf16[64,512]{1,0:T(8,128)(2,1)S(1)}, bf16[64,512]{1,0:T(8,128)(2,1)S(1)}, u32[]{:S(2)}, u32[]{:S(2)}) %collective-permute-start.3) | collective-permute-done | bytes 65568 | tf_op jit(solution)/shard_map/gather/ppermute | solution.py:354
  29.0 0.7 gather.2
  29.7 2.6 %collective-permute-start.12 = (bf16[1,64,512]{2,1,0:T(8,128)(2,1)S(1)}, bf16[1,64,512]{2,1,0:T(8,128)(2,1)S(1)}, u32[]{:S(2)}, u32[]{:S(2)}) collective-permute-start(bf16[1,64,512]{2,1,0:T(8,128)(2,1)S(1)} %bitcast.42), channel_id=1, source_target_pairs={{0,6},{1,7},{2,4},{3,5},{4,2},{5,3},{6,0},{7,1},{8,14},{9,15},{10,... | collective-permute-start | bytes 196616 | tf_op jit(solution)/shard_map/gather/ppermute | solution.py:359
  32.3 1.8 %collective-permute-start.10 = (bf16[1,64,512]{2,1,0:T(8,128)(2,1)S(1)}, bf16[1,64,512]{2,1,0:T(8,128)(2,1)S(1)}, u32[]{:S(2)}, u32[]{:S(2)}) collective-permute-start(bf16[1,64,512]{2,1,0:T(8,128)(2,1)S(1)} %bitcast.44), channel_id=1, source_target_pairs={{0,2},{1,3},{2,0},{3,1},{4,6},{5,7},{6,4},{7,5},{8,10},{9,11},{10,... | collective-permute-start | bytes 196616 | tf_op jit(solution)/shard_map/gather/ppermute | solution.py:359
  34.2 0.4 collective-permute-done.8.refs_2_
  34.6 0.7 gather.3
  35.3 2.3 %collective-permute-start.16 = (bf16[1,64,512]{2,1,0:T(8,128)(2,1)S(1)}, bf16[1,64,512]{2,1,0:T(8,128)(2,1)S(1)}, u32[]{:S(2)}, u32[]{:S(2)}) collective-permute-start(bf16[1,64,512]{2,1,0:T(8,128)(2,1)S(1)} %bitcast.46), channel_id=1, source_target_pairs={{0,6},{1,7},{2,4},{3,5},{4,2},{5,3},{6,0},{7,1},{8,14},{9,15},{10,... | collective-permute-start | bytes 196616 | tf_op jit(solution)/shard_map/gather/ppermute | solution.py:359
  37.6 2.1 %collective-permute-start.14 = (bf16[1,64,512]{2,1,0:T(8,128)(2,1)S(1)}, bf16[1,64,512]{2,1,0:T(8,128)(2,1)S(1)}, u32[]{:S(2)}, u32[]{:S(2)}) collective-permute-start(bf16[1,64,512]{2,1,0:T(8,128)(2,1)S(1)} %bitcast.48), channel_id=1, source_target_pairs={{0,2},{1,3},{2,0},{3,1},{4,6},{5,7},{6,4},{7,5},{8,10},{9,11},{10,... | collective-permute-start | bytes 196616 | tf_op jit(solution)/shard_map/gather/ppermute | solution.py:359
  39.7 0.5 collective-permute-done.11
  40.3 1.4 %collective-permute-start.13 = (bf16[4,64,512]{2,1,0:T(8,128)(2,1)S(1)}, bf16[4,64,512]{2,1,0:T(8,128)(2,1)S(1)}, u32[]{:S(2)}, u32[]{:S(2)}) collective-permute-start(bf16[4,64,512]{2,1,0:T(8,128)(2,1)S(1)} %get-tuple-element.81.mine), channel_id=1, source_target_pairs={{0,1},{1,0},{2,3},{3,2},{4,5},{5,4},{6,7},{7,6},{8,9},{9,8},{10,11... | collective-permute-start | bytes 786440 | tf_op jit(solution)/shard_map/gather/ppermute | solution.py:413
  41.7 0.2 collective-permute-done.16
  42.0 3.9 %collective-permute-done.15 = bf16[1,64,512]{2,1,0:T(8,128)(2,1)S(1)} collective-permute-done((bf16[1,64,512]{2,1,0:T(8,128)(2,1)S(1)}, bf16[1,64,512]{2,1,0:T(8,128)(2,1)S(1)}, u32[]{:S(2)}, u32[]{:S(2)}) %collective-permute-start.15) | collective-permute-done | bytes 65568 | tf_op jit(solution)/shard_map/gather/ppermute | solution.py:359
  45.9 1.4 %collective-permute-start.17 = (bf16[4,64,512]{2,1,0:T(8,128)(2,1)S(1)}, bf16[4,64,512]{2,1,0:T(8,128)(2,1)S(1)}, u32[]{:S(2)}, u32[]{:S(2)}) collective-permute-start(bf16[4,64,512]{2,1,0:T(8,128)(2,1)S(1)} %get-tuple-element.76.refs_0_), channel_id=1, source_target_pairs={{0,1},{1,0},{2,3},{3,2},{4,5},{5,4},{6,7},{7,6},{8,9},{9,8},{10,11... | collective-permute-start | bytes 786440 | tf_op jit(solution)/shard_map/gather/ppermute | solution.py:413
  47.3 1.8 %collective-permute-done.13.theirs = bf16[4,64,512]{2,1,0:T(8,128)(2,1)S(1)} collective-permute-done((bf16[4,64,512]{2,1,0:T(8,128)(2,1)S(1)}, bf16[4,64,512]{2,1,0:T(8,128)(2,1)S(1)}, u32[]{:S(2)}, u32[]{:S(2)}) %collective-permute-start.13) | collective-permute-done | bytes 262176 | tf_op jit(solution)/shard_map/gather/ppermute | solution.py:413
  49.2 0.7 second.5
  49.9 0.9 %copy-done = f32[2,512,512]{2,1,0:T(8,128)S(1)} copy-done((f32[2,512,512]{2,1,0:T(8,128)S(1)}, f32[2,512,512]{2,1,0:T(8,128)}, u32[]{:S(2)}) %copy-start) | copy-done | bytes 2097176
  50.8 1.0 %second.6 = f32[8,512]{1,0:T(8,128)S(1)} custom-call(s32[2]{0:T(128)S(1)} %copy-done.1, f32[2,512,512]{2,1,0:T(8,128)S(1)} %copy-done, bf16[512,512]{1,0:T(8,128)(2,1)S(1)} %get-tuple-element.51.block.first_block), custom_call_target="tpu_custom_call" | custom-call | flops 1 | tf_op jit(solution)/shard_map/second/pallas_call | solution.py:304
  51.8 3.3 %collective-permute-done.17.refs_1_ = bf16[4,64,512]{2,1,0:T(8,128)(2,1)S(1)} collective-permute-done((bf16[4,64,512]{2,1,0:T(8,128)(2,1)S(1)}, bf16[4,64,512]{2,1,0:T(8,128)(2,1)S(1)}, u32[]{:S(2)}, u32[]{:S(2)}) %collective-permute-start.17) | collective-permute-done | bytes 262176 | tf_op jit(solution)/shard_map/gather/ppermute | solution.py:413
  55.2 0.9 %collective-permute-start.23 = (bf16[2,4,64,512]{3,2,1,0:T(8,128)(2,1)S(1)}, bf16[2,4,64,512]{3,2,1,0:T(8,128)(2,1)S(1)}, u32[]{:S(2)}, u32[]{:S(2)}) collective-permute-start(bf16[2,4,64,512]{3,2,1,0:T(8,128)(2,1)S(1)} %pad_maximum_fusion.1), channel_id=1, source_target_pairs={{8,16},{16,8},{9,17},{17,9},{10,18},{18,10},{11,19},{19,11},{12,20... | collective-permute-start | bytes 1572872 | tf_op jit(solution)/shard_map/second/ppermute | solution.py:343
  56.1 0.9 %collective-permute-done.18.refs_2_ = bf16[2,4,64,512]{3,2,1,0:T(8,128)(2,1)S(1)} collective-permute-done((bf16[2,4,64,512]{3,2,1,0:T(8,128)(2,1)S(1)}, bf16[2,4,64,512]{3,2,1,0:T(8,128)(2,1)S(1)}, u32[]{:S(2)}, u32[]{:S(2)}) %collective-permute-start.18) | collective-permute-done | bytes 524320 | tf_op jit(solution)/shard_map/second/ppermute | solution.py:343
  57.1 3.7 %second.7 = (bf16[4,64,512]{2,1,0:T(8,128)(2,1)S(1)}, f32[4,64,512]{2,1,0:T(8,128)S(1)}, bf16[2,512,512]{2,1,0:T(8,128)(2,1)S(1)}) custom-call(s32[4]{0:T(128)S(1)} %copy-done.4, f32[512,512]{1,0:T(8,128)S(1)} %get-tuple-element.50.acc_ref, bf16[512,512]{1,0:T(8,128)(2,1)S(1)} %get-tuple-element.51.block.first_block, ...), custom_call_target="tpu_custom_call" | custom-call | flops 1073741824 | bytes 4194304 | tf_op jit(solution)/shard_map/second/pallas_call | solution.py:304
  60.8 1.0 %second.8 = f32[8,512]{1,0:T(8,128)S(1)} custom-call(s32[2]{0:T(128)S(1)} %copy-done.1, f32[2,512,512]{2,1,0:T(8,128)S(1)} %copy-done, bf16[2,512,512]{2,1,0:T(8,128)(2,1)S(1)} %get-tuple-element.58.block.own), custom_call_target="tpu_custom_call" | custom-call | flops 1 | tf_op jit(solution)/shard_map/second/pallas_call | solution.py:304
  61.8 1.5 %second.9 = (bf16[4,64,512]{2,1,0:T(8,128)(2,1)S(1)}, f32[4,64,512]{2,1,0:T(8,128)S(1)}) custom-call(s32[4]{0:T(128)S(1)} %copy-done.4, bf16[2,512,512]{2,1,0:T(8,128)(2,1)S(1)} %get-tuple-element.58.block.own, bf16[4,512,512]{2,1,0:T(8,128)(2,1)S(1)} %get-tuple-element.59.left, bf16[4,512,512]{2,1,0:T(8,128)(2,1)S(1)} %get-tuple-element.60.right, ...), custom_call_target="tpu_custom_call" | custom-call | flops 2147483648 | bytes 8388608 | tf_op jit(solution)/shard_map/second/pallas_call | solution.py:304
  63.3 2.8 %collective-permute-start.24 = (bf16[4,64,512]{2,1,0:T(8,128)(2,1)S(1)}, bf16[4,64,512]{2,1,0:T(8,128)(2,1)S(1)}, u32[]{:S(2)}, u32[]{:S(2)}) collective-permute-start(bf16[4,64,512]{2,1,0:T(8,128)(2,1)S(1)} %get-tuple-element.62), channel_id=1, source_target_pairs={{0,1},{1,0},{2,3},{3,2},{4,5},{5,4},{6,7},{7,6},{8,9},{9,8},{10,11... | collective-permute-start | bytes 786440 | tf_op jit(solution)/shard_map/second/ppermute | solution.py:348
  66.1 3.7 %collective-permute-done.19 = bf16[4,64,512]{2,1,0:T(8,128)(2,1)S(1)} collective-permute-done((bf16[4,64,512]{2,1,0:T(8,128)(2,1)S(1)}, bf16[4,64,512]{2,1,0:T(8,128)(2,1)S(1)}, u32[]{:S(2)}, u32[]{:S(2)}) %collective-permute-start.19) | collective-permute-done | bytes 262176 | tf_op jit(solution)/shard_map/second/ppermute | solution.py:348
  69.8 0.1 fusion.3
  69.9 1.6 %collective-permute-start.20 = (bf16[64,512]{1,0:T(8,128)(2,1)S(1)}, bf16[64,512]{1,0:T(8,128)(2,1)S(1)}, u32[]{:S(2)}, u32[]{:S(2)}) collective-permute-start(bf16[64,512]{1,0:T(8,128)(2,1)S(1)} %get-tuple-element.79), channel_id=1, source_target_pairs={{0,6},{1,7},{2,4},{3,5},{4,2},{5,3},{6,0},{7,1},{8,14},{9,15},{10,... | collective-permute-start | bytes 196616 | tf_op jit(solution)/shard_map/scalars/ppermute | solution.py:354
  71.5 2.8 %collective-permute-start.22 = (bf16[64,512]{1,0:T(8,128)(2,1)S(1)}, bf16[64,512]{1,0:T(8,128)(2,1)S(1)}, u32[]{:S(2)}, u32[]{:S(2)}) collective-permute-start(bf16[64,512]{1,0:T(8,128)(2,1)S(1)} %get-tuple-element.77), channel_id=1, source_target_pairs={{0,2},{1,3},{2,0},{3,1},{4,6},{5,7},{6,4},{7,5},{8,10},{9,11},{10,... | collective-permute-start | bytes 196616 | tf_op jit(solution)/shard_map/scalars/ppermute | solution.py:354
  74.5 1.6 %collective-permute-start.25 = (bf16[64,512]{1,0:T(8,128)(2,1)S(1)}, bf16[64,512]{1,0:T(8,128)(2,1)S(1)}, u32[]{:S(2)}, u32[]{:S(2)}) collective-permute-start(bf16[64,512]{1,0:T(8,128)(2,1)S(1)} %get-tuple-element.74), channel_id=1, source_target_pairs={{0,6},{1,7},{2,4},{3,5},{4,2},{5,3},{6,0},{7,1},{8,14},{9,15},{10,... | collective-permute-start | bytes 196616 | tf_op jit(solution)/shard_map/scalars/ppermute | solution.py:354
  76.2 2.3 %collective-permute-done.22.refs_9_ = bf16[64,512]{1,0:T(8,128)(2,1)S(1)} collective-permute-done((bf16[64,512]{1,0:T(8,128)(2,1)S(1)}, bf16[64,512]{1,0:T(8,128)(2,1)S(1)}, u32[]{:S(2)}, u32[]{:S(2)}) %collective-permute-start.22) | collective-permute-done | bytes 65568 | tf_op jit(solution)/shard_map/scalars/ppermute | solution.py:354
  78.5 0.9 %collective-permute-start.27 = (bf16[64,512]{1,0:T(8,128)(2,1)S(1)}, bf16[64,512]{1,0:T(8,128)(2,1)S(1)}, u32[]{:S(2)}, u32[]{:S(2)}) collective-permute-start(bf16[64,512]{1,0:T(8,128)(2,1)S(1)} %get-tuple-element.72), channel_id=1, source_target_pairs={{0,2},{1,3},{2,0},{3,1},{4,6},{5,7},{6,4},{7,5},{8,10},{9,11},{10,... | collective-permute-start | bytes 196616 | tf_op jit(solution)/shard_map/scalars/ppermute | solution.py:354
  79.5 1.4 %collective-permute-start.29 = (f32[8,512]{1,0:T(8,128)S(1)}, f32[8,512]{1,0:T(8,128)S(1)}, u32[]{:S(2)}, u32[]{:S(2)}) collective-permute-start(f32[8,512]{1,0:T(8,128)S(1)} %add.19.refs_14_), channel_id=1, source_target_pairs={{0,16},{8,24},{16,0},{24,8},{1,17},{9,25},{17,1},{25,9},{2,18},{10... | collective-permute-start | bytes 49160 | tf_op jit(solution)/shard_map/scalars/ppermute | solution.py:477
  80.9 0.2 collective-permute-done.25.refs_11_
  81.1 0.2 collective-permute-start.30
  81.3 3.8 %collective-permute-done.26.refs_12_ = bf16[64,512]{1,0:T(8,128)(2,1)S(1)} collective-permute-done((bf16[64,512]{1,0:T(8,128)(2,1)S(1)}, bf16[64,512]{1,0:T(8,128)(2,1)S(1)}, u32[]{:S(2)}, u32[]{:S(2)}) %collective-permute-start.26) | collective-permute-done | bytes 65568 | tf_op jit(solution)/shard_map/scalars/ppermute | solution.py:354
  85.1 1.5 %scalars.1 = (f32[2,64,512]{2,1,0:T(8,128)}, f32[2,64,512]{2,1,0:T(8,128)}) custom-call(s32[2]{0:T(128)S(1)} %copy-done.1, f32[2,64,512]{2,1,0:T(8,128)S(1)} %get-tuple-element.35.start, f32[64,512]{1,0:T(8,128)S(1)} %get-tuple-element.38.refs_0_, f32[64,512]{1,0:T(8,128)S(1)} %get-tuple-element.42.refs_1_, f32[64,512]{1,0:T(8,128)S(1)} %get-tuple-element.43.refs_2_, ...), custom_call_target="tpu_custom_call" | custom-call | flops 1048576 | bytes 4096 | tf_op jit(solution)/shard_map/scalars/pallas_call | solution.py:304
  (52 shorter events, 1.0 us)
Async XLA Ops:
  2.3 2.1 %collective-permute-start = (bf16[512,512]{1,0:T(8,128)(2,1)S(1)}, bf16[512,512]{1,0:T(8,128)(2,1)S(1)}, u32[]{:S(2)}, u32[]{:S(2)}) collective-permute-start(bf16[512,512]{1,0:T(8,128)(2,1)S(1)} %get-tuple-element.34), channel_id=1, source_target_pairs={{0,8},{8,0},{16,24},{24,16},{1,9},{9,1},{17,25},{25,17},{2,10},{10... | collective-permute-start | bytes 1572872 | tf_op jit(solution)/shard_map/first/ppermute | solution.py:343
  2.8 8.9 %collective-permute-start.5 = (bf16[512,512]{1,0:T(8,128)(2,1)S(1)}, bf16[512,512]{1,0:T(8,128)(2,1)S(1)}, u32[]{:S(2)}, u32[]{:S(2)}) collective-permute-start(bf16[512,512]{1,0:T(8,128)(2,1)S(1)} %get-tuple-element.39), channel_id=1, source_target_pairs={{8,16},{16,8},{9,17},{17,9},{10,18},{18,10},{11,19},{19,11},{12,20... | collective-permute-start | bytes 1572872 | tf_op jit(solution)/shard_map/first/ppermute | solution.py:343
  8.7 9.0 %collective-permute-start.1 = (bf16[4,64,512]{2,1,0:T(8,128)(2,1)S(1)}, bf16[4,64,512]{2,1,0:T(8,128)(2,1)S(1)}, u32[]{:S(2)}, u32[]{:S(2)}) collective-permute-start(bf16[4,64,512]{2,1,0:T(8,128)(2,1)S(1)} %get-tuple-element.37), channel_id=1, source_target_pairs={{0,1},{1,0},{2,3},{3,2},{4,5},{5,4},{6,7},{7,6},{8,9},{9,8},{10,11... | collective-permute-start | bytes 786440 | tf_op jit(solution)/shard_map/first/ppermute | solution.py:348
  14.8 8.4 %collective-permute-start.6 = (bf16[4,64,512]{2,1,0:T(8,128)(2,1)S(1)}, bf16[4,64,512]{2,1,0:T(8,128)(2,1)S(1)}, u32[]{:S(2)}, u32[]{:S(2)}) collective-permute-start(bf16[4,64,512]{2,1,0:T(8,128)(2,1)S(1)} %get-tuple-element.41), channel_id=1, source_target_pairs={{0,1},{1,0},{2,3},{3,2},{4,5},{5,4},{6,7},{7,6},{8,9},{9,8},{10,11... | collective-permute-start | bytes 786440 | tf_op jit(solution)/shard_map/first/ppermute | solution.py:348
  17.7 11.2 %copy-start.1 = (s32[2]{0:T(128)S(1)}, s32[2]{0:T(128)}, u32[]{:S(2)}) copy-start(s32[2]{0:T(128)} %size_ref.9) | copy-start | bytes 28
  17.7 11.2 %copy-start.2 = (f32[2,512]{1,0:T(2,128)S(1)}, f32[2,512]{1,0:T(2,128)}, u32[]{:S(2)}) copy-start(f32[2,512]{1,0:T(2,128)} %left_row.3) | copy-start | bytes 12292
  17.8 11.3 %copy-start.3 = (f32[2,512]{1,0:T(2,128)S(1)}, f32[2,512]{1,0:T(2,128)}, u32[]{:S(2)}) copy-start(f32[2,512]{1,0:T(2,128)} %right_row.3) | copy-start | bytes 12292
  17.9 9.3 %collective-permute-start.2 = (bf16[64,512]{1,0:T(8,128)(2,1)S(1)}, bf16[64,512]{1,0:T(8,128)(2,1)S(1)}, u32[]{:S(2)}, u32[]{:S(2)}) collective-permute-start(bf16[64,512]{1,0:T(8,128)(2,1)S(1)} %get-tuple-element.87), channel_id=1, source_target_pairs={{0,6},{1,7},{2,4},{3,5},{4,2},{5,3},{6,0},{7,1},{8,14},{9,15},{10,... | collective-permute-start | bytes 196616 | tf_op jit(solution)/shard_map/gather/ppermute | solution.py:354
  22.5 6.5 %collective-permute-start.3 = (bf16[64,512]{1,0:T(8,128)(2,1)S(1)}, bf16[64,512]{1,0:T(8,128)(2,1)S(1)}, u32[]{:S(2)}, u32[]{:S(2)}) collective-permute-start(bf16[64,512]{1,0:T(8,128)(2,1)S(1)} %get-tuple-element.86), channel_id=1, source_target_pairs={{0,4},{1,5},{2,6},{3,7},{4,0},{5,1},{6,2},{7,3},{8,12},{9,13},{10,... | collective-permute-start | bytes 196616 | tf_op jit(solution)/shard_map/gather/ppermute | solution.py:354
  22.5 6.5 %collective-permute-start.4 = (bf16[64,512]{1,0:T(8,128)(2,1)S(1)}, bf16[64,512]{1,0:T(8,128)(2,1)S(1)}, u32[]{:S(2)}, u32[]{:S(2)}) collective-permute-start(bf16[64,512]{1,0:T(8,128)(2,1)S(1)} %get-tuple-element.85), channel_id=1, source_target_pairs={{0,2},{1,3},{2,0},{3,1},{4,6},{5,7},{6,4},{7,5},{8,10},{9,11},{10,... | collective-permute-start | bytes 196616 | tf_op jit(solution)/shard_map/gather/ppermute | solution.py:354
  23.2 25.9 %copy-start.4 = (s32[4]{0:T(128)S(1)}, s32[4]{0:T(128)}, u32[]{:S(2)}) copy-start(s32[4]{0:T(128)} %shift_ref.5) | copy-start | bytes 52
  23.3 9.1 %collective-permute-start.7 = (bf16[64,512]{1,0:T(8,128)(2,1)S(1)}, bf16[64,512]{1,0:T(8,128)(2,1)S(1)}, u32[]{:S(2)}, u32[]{:S(2)}) collective-permute-start(bf16[64,512]{1,0:T(8,128)(2,1)S(1)} %get-tuple-element.84), channel_id=1, source_target_pairs={{0,6},{1,7},{2,4},{3,5},{4,2},{5,3},{6,0},{7,1},{8,14},{9,15},{10,... | collective-permute-start | bytes 196616 | tf_op jit(solution)/shard_map/gather/ppermute | solution.py:354
  27.1 7.5 %collective-permute-start.8 = (bf16[64,512]{1,0:T(8,128)(2,1)S(1)}, bf16[64,512]{1,0:T(8,128)(2,1)S(1)}, u32[]{:S(2)}, u32[]{:S(2)}) collective-permute-start(bf16[64,512]{1,0:T(8,128)(2,1)S(1)} %get-tuple-element.83), channel_id=1, source_target_pairs={{0,4},{1,5},{2,6},{3,7},{4,0},{5,1},{6,2},{7,3},{8,12},{9,13},{10,... | collective-permute-start | bytes 196616 | tf_op jit(solution)/shard_map/gather/ppermute | solution.py:354
  27.2 7.4 %collective-permute-start.9 = (bf16[64,512]{1,0:T(8,128)(2,1)S(1)}, bf16[64,512]{1,0:T(8,128)(2,1)S(1)}, u32[]{:S(2)}, u32[]{:S(2)}) collective-permute-start(bf16[64,512]{1,0:T(8,128)(2,1)S(1)} %get-tuple-element.82), channel_id=1, source_target_pairs={{0,2},{1,3},{2,0},{3,1},{4,6},{5,7},{6,4},{7,5},{8,10},{9,11},{10,... | collective-permute-start | bytes 196616 | tf_op jit(solution)/shard_map/gather/ppermute | solution.py:354
  29.7 7.9 %collective-permute-start.12 = (bf16[1,64,512]{2,1,0:T(8,128)(2,1)S(1)}, bf16[1,64,512]{2,1,0:T(8,128)(2,1)S(1)}, u32[]{:S(2)}, u32[]{:S(2)}) collective-permute-start(bf16[1,64,512]{2,1,0:T(8,128)(2,1)S(1)} %bitcast.42), channel_id=1, source_target_pairs={{0,6},{1,7},{2,4},{3,5},{4,2},{5,3},{6,0},{7,1},{8,14},{9,15},{10,... | collective-permute-start | bytes 196616 | tf_op jit(solution)/shard_map/gather/ppermute | solution.py:359
  32.3 7.9 %collective-permute-start.11 = (bf16[1,64,512]{2,1,0:T(8,128)(2,1)S(1)}, bf16[1,64,512]{2,1,0:T(8,128)(2,1)S(1)}, u32[]{:S(2)}, u32[]{:S(2)}) collective-permute-start(bf16[1,64,512]{2,1,0:T(8,128)(2,1)S(1)} %bitcast.43), channel_id=1, source_target_pairs={{0,4},{1,5},{2,6},{3,7},{4,0},{5,1},{6,2},{7,3},{8,12},{9,13},{10,... | collective-permute-start | bytes 196616 | tf_op jit(solution)/shard_map/gather/ppermute | solution.py:359
  32.3 7.9 %collective-permute-start.10 = (bf16[1,64,512]{2,1,0:T(8,128)(2,1)S(1)}, bf16[1,64,512]{2,1,0:T(8,128)(2,1)S(1)}, u32[]{:S(2)}, u32[]{:S(2)}) collective-permute-start(bf16[1,64,512]{2,1,0:T(8,128)(2,1)S(1)} %bitcast.44), channel_id=1, source_target_pairs={{0,2},{1,3},{2,0},{3,1},{4,6},{5,7},{6,4},{7,5},{8,10},{9,11},{10,... | collective-permute-start | bytes 196616 | tf_op jit(solution)/shard_map/gather/ppermute | solution.py:359
  35.3 6.7 %collective-permute-start.16 = (bf16[1,64,512]{2,1,0:T(8,128)(2,1)S(1)}, bf16[1,64,512]{2,1,0:T(8,128)(2,1)S(1)}, u32[]{:S(2)}, u32[]{:S(2)}) collective-permute-start(bf16[1,64,512]{2,1,0:T(8,128)(2,1)S(1)} %bitcast.46), channel_id=1, source_target_pairs={{0,6},{1,7},{2,4},{3,5},{4,2},{5,3},{6,0},{7,1},{8,14},{9,15},{10,... | collective-permute-start | bytes 196616 | tf_op jit(solution)/shard_map/gather/ppermute | solution.py:359
  37.6 8.2 %collective-permute-start.15 = (bf16[1,64,512]{2,1,0:T(8,128)(2,1)S(1)}, bf16[1,64,512]{2,1,0:T(8,128)(2,1)S(1)}, u32[]{:S(2)}, u32[]{:S(2)}) collective-permute-start(bf16[1,64,512]{2,1,0:T(8,128)(2,1)S(1)} %bitcast.47), channel_id=1, source_target_pairs={{0,4},{1,5},{2,6},{3,7},{4,0},{5,1},{6,2},{7,3},{8,12},{9,13},{10,... | collective-permute-start | bytes 196616 | tf_op jit(solution)/shard_map/gather/ppermute | solution.py:359
  37.6 8.2 %collective-permute-start.14 = (bf16[1,64,512]{2,1,0:T(8,128)(2,1)S(1)}, bf16[1,64,512]{2,1,0:T(8,128)(2,1)S(1)}, u32[]{:S(2)}, u32[]{:S(2)}) collective-permute-start(bf16[1,64,512]{2,1,0:T(8,128)(2,1)S(1)} %bitcast.48), channel_id=1, source_target_pairs={{0,2},{1,3},{2,0},{3,1},{4,6},{5,7},{6,4},{7,5},{8,10},{9,11},{10,... | collective-permute-start | bytes 196616 | tf_op jit(solution)/shard_map/gather/ppermute | solution.py:359
  40.3 8.9 %collective-permute-start.13 = (bf16[4,64,512]{2,1,0:T(8,128)(2,1)S(1)}, bf16[4,64,512]{2,1,0:T(8,128)(2,1)S(1)}, u32[]{:S(2)}, u32[]{:S(2)}) collective-permute-start(bf16[4,64,512]{2,1,0:T(8,128)(2,1)S(1)} %get-tuple-element.81.mine), channel_id=1, source_target_pairs={{0,1},{1,0},{2,3},{3,2},{4,5},{5,4},{6,7},{7,6},{8,9},{9,8},{10,11... | collective-permute-start | bytes 786440 | tf_op jit(solution)/shard_map/gather/ppermute | solution.py:413
  45.9 9.2 %collective-permute-start.17 = (bf16[4,64,512]{2,1,0:T(8,128)(2,1)S(1)}, bf16[4,64,512]{2,1,0:T(8,128)(2,1)S(1)}, u32[]{:S(2)}, u32[]{:S(2)}) collective-permute-start(bf16[4,64,512]{2,1,0:T(8,128)(2,1)S(1)} %get-tuple-element.76.refs_0_), channel_id=1, source_target_pairs={{0,1},{1,0},{2,3},{3,2},{4,5},{5,4},{6,7},{7,6},{8,9},{9,8},{10,11... | collective-permute-start | bytes 786440 | tf_op jit(solution)/shard_map/gather/ppermute | solution.py:413
  49.2 1.6 %copy-start = (f32[2,512,512]{2,1,0:T(8,128)S(1)}, f32[2,512,512]{2,1,0:T(8,128)}, u32[]{:S(2)}) copy-start(f32[2,512,512]{2,1,0:T(8,128)} %vector_ref.3) | copy-start | bytes 6291460
  55.1 1.9 %collective-permute-start.18 = (bf16[2,4,64,512]{3,2,1,0:T(8,128)(2,1)S(1)}, bf16[2,4,64,512]{3,2,1,0:T(8,128)(2,1)S(1)}, u32[]{:S(2)}, u32[]{:S(2)}) collective-permute-start(bf16[2,4,64,512]{3,2,1,0:T(8,128)(2,1)S(1)} %pad_maximum_fusion), channel_id=1, source_target_pairs={{0,8},{8,0},{16,24},{24,16},{1,9},{9,1},{17,25},{25,17},{2,10},{10... | collective-permute-start | bytes 1572872 | tf_op jit(solution)/shard_map/second/ppermute | solution.py:343
  55.2 6.6 %collective-permute-start.23 = (bf16[2,4,64,512]{3,2,1,0:T(8,128)(2,1)S(1)}, bf16[2,4,64,512]{3,2,1,0:T(8,128)(2,1)S(1)}, u32[]{:S(2)}, u32[]{:S(2)}) collective-permute-start(bf16[2,4,64,512]{3,2,1,0:T(8,128)(2,1)S(1)} %pad_maximum_fusion.1), channel_id=1, source_target_pairs={{8,16},{16,8},{9,17},{17,9},{10,18},{18,10},{11,19},{19,11},{12,20... | collective-permute-start | bytes 1572872 | tf_op jit(solution)/shard_map/second/ppermute | solution.py:343
  60.7 9.1 %collective-permute-start.19 = (bf16[4,64,512]{2,1,0:T(8,128)(2,1)S(1)}, bf16[4,64,512]{2,1,0:T(8,128)(2,1)S(1)}, u32[]{:S(2)}, u32[]{:S(2)}) collective-permute-start(bf16[4,64,512]{2,1,0:T(8,128)(2,1)S(1)} %get-tuple-element.55), channel_id=1, source_target_pairs={{0,1},{1,0},{2,3},{3,2},{4,5},{5,4},{6,7},{7,6},{8,9},{9,8},{10,11... | collective-permute-start | bytes 786440 | tf_op jit(solution)/shard_map/second/ppermute | solution.py:348
  63.3 11.0 %collective-permute-start.24 = (bf16[4,64,512]{2,1,0:T(8,128)(2,1)S(1)}, bf16[4,64,512]{2,1,0:T(8,128)(2,1)S(1)}, u32[]{:S(2)}, u32[]{:S(2)}) collective-permute-start(bf16[4,64,512]{2,1,0:T(8,128)(2,1)S(1)} %get-tuple-element.62), channel_id=1, source_target_pairs={{0,1},{1,0},{2,3},{3,2},{4,5},{5,4},{6,7},{7,6},{8,9},{9,8},{10,11... | collective-permute-start | bytes 786440 | tf_op jit(solution)/shard_map/second/ppermute | solution.py:348
  69.9 9.5 %collective-permute-start.20 = (bf16[64,512]{1,0:T(8,128)(2,1)S(1)}, bf16[64,512]{1,0:T(8,128)(2,1)S(1)}, u32[]{:S(2)}, u32[]{:S(2)}) collective-permute-start(bf16[64,512]{1,0:T(8,128)(2,1)S(1)} %get-tuple-element.79), channel_id=1, source_target_pairs={{0,6},{1,7},{2,4},{3,5},{4,2},{5,3},{6,0},{7,1},{8,14},{9,15},{10,... | collective-permute-start | bytes 196616 | tf_op jit(solution)/shard_map/scalars/ppermute | solution.py:354
  71.5 8.0 %collective-permute-start.21 = (bf16[64,512]{1,0:T(8,128)(2,1)S(1)}, bf16[64,512]{1,0:T(8,128)(2,1)S(1)}, u32[]{:S(2)}, u32[]{:S(2)}) collective-permute-start(bf16[64,512]{1,0:T(8,128)(2,1)S(1)} %get-tuple-element.78), channel_id=1, source_target_pairs={{0,4},{1,5},{2,6},{3,7},{4,0},{5,1},{6,2},{7,3},{8,12},{9,13},{10,... | collective-permute-start | bytes 196616 | tf_op jit(solution)/shard_map/scalars/ppermute | solution.py:354
  71.5 7.0 %collective-permute-start.22 = (bf16[64,512]{1,0:T(8,128)(2,1)S(1)}, bf16[64,512]{1,0:T(8,128)(2,1)S(1)}, u32[]{:S(2)}, u32[]{:S(2)}) collective-permute-start(bf16[64,512]{1,0:T(8,128)(2,1)S(1)} %get-tuple-element.77), channel_id=1, source_target_pairs={{0,2},{1,3},{2,0},{3,1},{4,6},{5,7},{6,4},{7,5},{8,10},{9,11},{10,... | collective-permute-start | bytes 196616 | tf_op jit(solution)/shard_map/scalars/ppermute | solution.py:354
  74.5 6.6 %collective-permute-start.25 = (bf16[64,512]{1,0:T(8,128)(2,1)S(1)}, bf16[64,512]{1,0:T(8,128)(2,1)S(1)}, u32[]{:S(2)}, u32[]{:S(2)}) collective-permute-start(bf16[64,512]{1,0:T(8,128)(2,1)S(1)} %get-tuple-element.74), channel_id=1, source_target_pairs={{0,6},{1,7},{2,4},{3,5},{4,2},{5,3},{6,0},{7,1},{8,14},{9,15},{10,... | collective-permute-start | bytes 196616 | tf_op jit(solution)/shard_map/scalars/ppermute | solution.py:354
  76.1 8.9 %collective-permute-start.26 = (bf16[64,512]{1,0:T(8,128)(2,1)S(1)}, bf16[64,512]{1,0:T(8,128)(2,1)S(1)}, u32[]{:S(2)}, u32[]{:S(2)}) collective-permute-start(bf16[64,512]{1,0:T(8,128)(2,1)S(1)} %get-tuple-element.73), channel_id=1, source_target_pairs={{0,4},{1,5},{2,6},{3,7},{4,0},{5,1},{6,2},{7,3},{8,12},{9,13},{10,... | collective-permute-start | bytes 196616 | tf_op jit(solution)/shard_map/scalars/ppermute | solution.py:354
  78.5 6.5 %collective-permute-start.27 = (bf16[64,512]{1,0:T(8,128)(2,1)S(1)}, bf16[64,512]{1,0:T(8,128)(2,1)S(1)}, u32[]{:S(2)}, u32[]{:S(2)}) collective-permute-start(bf16[64,512]{1,0:T(8,128)(2,1)S(1)} %get-tuple-element.72), channel_id=1, source_target_pairs={{0,2},{1,3},{2,0},{3,1},{4,6},{5,7},{6,4},{7,5},{8,10},{9,11},{10,... | collective-permute-start | bytes 196616 | tf_op jit(solution)/shard_map/scalars/ppermute | solution.py:354
  79.4 5.7 %collective-permute-start.28 = (f32[8,512]{1,0:T(8,128)S(1)}, f32[8,512]{1,0:T(8,128)S(1)}, u32[]{:S(2)}, u32[]{:S(2)}) collective-permute-start(f32[8,512]{1,0:T(8,128)S(1)} %add.19.refs_14_), channel_id=1, source_target_pairs={{0,8},{8,0},{16,24},{24,16},{1,9},{9,1},{17,25},{25,17},{2,10},{10... | collective-permute-start | bytes 49160 | tf_op jit(solution)/shard_map/scalars/ppermute | solution.py:477
  79.5 5.6 %collective-permute-start.29 = (f32[8,512]{1,0:T(8,128)S(1)}, f32[8,512]{1,0:T(8,128)S(1)}, u32[]{:S(2)}, u32[]{:S(2)}) collective-permute-start(f32[8,512]{1,0:T(8,128)S(1)} %add.19.refs_14_), channel_id=1, source_target_pairs={{0,16},{8,24},{16,0},{24,8},{1,17},{9,25},{17,1},{25,9},{2,18},{10... | collective-permute-start | bytes 49160 | tf_op jit(solution)/shard_map/scalars/ppermute | solution.py:477
  81.1 4.0 %collective-permute-start.30 = (f32[8,512]{1,0:T(8,128)S(1)}, f32[8,512]{1,0:T(8,128)S(1)}, u32[]{:S(2)}, u32[]{:S(2)}) collective-permute-start(f32[8,512]{1,0:T(8,128)S(1)} %add.19.refs_14_), channel_id=1, source_target_pairs={{0,24},{8,16},{16,8},{24,0},{1,25},{9,17},{17,9},{25,1},{2,26},{10... | collective-permute-start | bytes 49160 | tf_op jit(solution)/shard_map/scalars/ppermute | solution.py:477
